TPU v7x, 32 devices: a whole 2x2x4 slice. The times are simulated.
32 devices in a mesh: ctx: 16 (over z, x, core), dp: 2 (over y).
Axes of the slice: x: 2, y: 2, z: 4, core: 2. Of those that a mesh axis runs over, the one named last changes fastest.
Arguments:
- hidden_in: bfloat16 [8192, 8192], P(('dp', 'ctx')), parts along dimension 0, may hold values from -32 to 32
- segment_ids: int32 [8192], P('dp'), parts along dimension 0, may hold values from 1023 to 4095, as said below
- w_query: bfloat16 [8192, 512], P('ctx'), may hold values from -0.0625 to 0.0625
- w_key: bfloat16 [8192, 128], P('ctx'), may hold values from -0.0625 to 0.0625
- w_value: bfloat16 [8192, 128], P('ctx'), may hold values from -0.0625 to 0.0625
- w_out: bfloat16 [512, 8192], P(None, 'ctx'), may hold values from -0.25 to 0.25
Outputs:
- attended: bfloat16 [8192, 8192], P(('dp', 'ctx')), parts along dimension 0
There are 2 independent parts, one for each index of `dp`. A program takes and returns all parts, laid end to end along the dimension named above; an argument that names none is the same for every part. Nothing has to cross between parts.
Inputs may be any that keep to these rules, and one draw needn't show every extreme that they name: `segment_ids`: A token's id is the position in sequence order of the last token of its document, so ids never fall along the sequence and tokens share an id exactly when they share a document; every document holds 1 to 1024 tokens, and the first one exactly 1024. Stored in the same block order as hidden_in.
All inputs are finite; a program needn't handle non-finite values.
Results may differ from a plain program's by a relative error of at most 0.034.
Values may be sent and summed in bfloat16 or wider, within the bound.
No kernel may reach another device: no remote copies, remote signals or barrier semaphores. Data moves between devices by JAX's collectives and lax.ppermute only.
A program may use at most 128 MiB of HBM per device.

v0:
```python
import math

import jax
import jax.numpy as jnp
from jax import lax
from jax.sharding import PartitionSpec as P

REACH = 8


ROPE_BASE = 500000.0


def passed_along(value, axis, steps):
    count = lax.axis_size(axis)
    leading, last = (max(0, -steps), min(count, count - steps))
    return lax.ppermute(value, axis, [(source, source + steps) for source in range(leading, last)])


def rotate(rows_in, positions):
    half_dim = rows_in.shape[-1] // 2
    frequency = ROPE_BASE ** (-(jnp.arange(half_dim, dtype=jnp.float32) * 2.0) / rows_in.shape[-1])
    angles = positions.astype(jnp.float32)[:, None] * frequency[None, :]
    cosine = jnp.cos(angles)[:, None, :]
    sine_part = jnp.sin(angles)[:, None, :]
    front_part = rows_in[..., :half_dim]
    back_part = rows_in[..., half_dim:]
    return jnp.concatenate(
        [front_part * cosine - back_part * sine_part, back_part * cosine + front_part * sine_part],
        axis=-1,
    )


def storage_block(seq_block, cycle_size):
    return jnp.where(
        seq_block < cycle_size, 2 * seq_block, 2 * (2 * cycle_size - 1 - seq_block) + 1
    )


def window_meta(last_block, block_len, seg_blocks, cycle_size):
    blocks_in = last_block - REACH + jnp.arange(REACH + 1, dtype=jnp.int32)
    inside = blocks_in >= 0
    seg_rows = seg_blocks[storage_block(jnp.maximum(blocks_in, 0), cycle_size)]
    key_seg = jnp.where(inside[:, None], seg_rows, -1).reshape(-1)
    key_pos = (
        blocks_in[:, None] * block_len + jnp.arange(block_len, dtype=jnp.int32)[None, :]
    ).reshape(-1)
    return (key_seg, key_pos)


def attend(query_part, window, query_pos, key_pos, query_seg, key_seg, head_dim):
    key_part = window[:, :head_dim]
    value_part = window[:, head_dim:]
    scores = jnp.einsum(
        "qhd,kd->hqk", query_part, key_part, preferred_element_type=jnp.float32
    ) / math.sqrt(head_dim)
    allowed = (query_seg[:, None] == key_seg[None, :]) & (key_pos[None, :] <= query_pos[:, None])
    scores = jnp.where(allowed[None], scores, -1e30)
    row_peak = jnp.max(scores, axis=-1, keepdims=True)
    exp_terms = jnp.exp(scores - row_peak)
    weights = (exp_terms / jnp.sum(exp_terms, axis=-1, keepdims=True)).astype(jnp.bfloat16)
    mixed_part = jnp.einsum("hqk,kd->qhd", weights, value_part, preferred_element_type=jnp.float32)
    return mixed_part.reshape(mixed_part.shape[0], -1).astype(jnp.bfloat16)


def on_device(hidden_in, segment_ids, w_query, w_key, w_value, w_out):
    cycle_size = lax.axis_size("ctx")
    my_index = lax.axis_index("ctx")
    block_len = hidden_in.shape[0] // 2
    query_width = w_query.shape[1]
    head_dim = w_key.shape[1]
    head_count = query_width // head_dim
    row_count = hidden_in.shape[0]
    portions = (
        lax.all_gather(w_query, "ctx", axis=0, tiled=True),
        lax.all_gather(w_key, "ctx", axis=0, tiled=True),
        lax.all_gather(w_value, "ctx", axis=0, tiled=True),
    )
    query_sum, key_sum, value_sum = tuple(
        (jnp.dot(hidden_in, portion, preferred_element_type=jnp.float32) for portion in portions)
    )
    late_block = 2 * cycle_size - 1 - my_index
    offsets = jnp.arange(block_len, dtype=jnp.int32)
    own_pos = jnp.concatenate([my_index * block_len + offsets, late_block * block_len + offsets])
    queries = rotate(query_sum.reshape(row_count, head_count, head_dim), own_pos).astype(
        jnp.bfloat16
    )
    key_rows = (
        rotate(key_sum.reshape(row_count, 1, head_dim), own_pos)
        .reshape(row_count, head_dim)
        .astype(jnp.bfloat16)
    )
    value_rows = value_sum.astype(jnp.bfloat16)
    joined_kv = jnp.concatenate([key_rows, value_rows], axis=1)
    early_list = [joined_kv[:block_len]]
    late_list = [joined_kv[block_len:]]
    at_top = my_index == cycle_size - 1
    for repeat_index in range(REACH):
        from_below = passed_along(early_list[-1], "ctx", 1)
        from_above = passed_along(late_list[-1], "ctx", -1)
        late_list.append(jnp.where(at_top, early_list[-1], from_above))
        early_list.append(from_below)
    early_window = jnp.concatenate(early_list[::-1], axis=0)
    late_window = jnp.concatenate(late_list[::-1], axis=0)
    seg_blocks = segment_ids.reshape(2 * cycle_size, block_len)
    early_seg, early_pos = window_meta(my_index, block_len, seg_blocks, cycle_size)
    late_seg, late_pos = window_meta(late_block, block_len, seg_blocks, cycle_size)
    early_out = attend(
        queries[:block_len],
        early_window,
        own_pos[:block_len],
        early_pos,
        seg_blocks[2 * my_index],
        early_seg,
        head_dim,
    )
    late_out = attend(
        queries[block_len:],
        late_window,
        own_pos[block_len:],
        late_pos,
        seg_blocks[2 * my_index + 1],
        late_seg,
        head_dim,
    )
    mixed_rows = jnp.concatenate([early_out, late_out], axis=0)
    result = jnp.dot(
        mixed_rows,
        lax.all_gather(w_out, "ctx", axis=1, tiled=True),
        preferred_element_type=jnp.float32,
    )
    return result.astype(jnp.bfloat16)


def solution(mesh):
    in_specs = (
        P(("dp", "ctx"), None),
        P("dp"),
        P("ctx", None),
        P("ctx", None),
        P("ctx", None),
        P(None, "ctx"),
    )
    out_specs = P(("dp", "ctx"), None)
    return jax.shard_map(
        on_device, mesh=mesh, in_specs=in_specs, out_specs=out_specs, check_vma=False
    )
```

profile of v0, /device:TPU:19, one launch (start us, length us, event | category | flops | bytes accessed | tf_op | source)
XLA Modules:
  0.0 267.9 jit_solution(17487832789576290161)
XLA Ops:
  9.4 40.4 %all-gather.5.cloned.1.call-done = bf16[8192,128]{1,0:T(8,128)(2,1)} async-done(((bf16[512,128]{1,0:T(8,128)(2,1)}), bf16[8192,128]{1,0:T(8,128)(2,1)}) %all-gather.5.cloned.1.call-update) | async-done | bytes 2097168 | tf_op jit(solution)/shard_map/all_gather | solution.py:76
  49.8 4.4 %convolution_bitcast_fusion = f32[256,1,128]{0,2,1:T(8,128)S(1)} fusion(bf16[256,8192]{1,0:T(8,128)(2,1)} %param.6, bf16[8192,128]{1,0:T(8,128)(2,1)} %all-gather.5.cloned.1.call-done), kind=kOutput, calls=%fused_computation.21 | convolution fusion | flops 536870912 | bytes 6422528 | tf_op jit(solution)/shard_map/dot_general | solution.py:80
  54.5 37.6 %all-gather.7.cloned.1.call-done = bf16[8192,128]{1,0:T(8,128)(2,1)} async-done(((bf16[512,128]{1,0:T(8,128)(2,1)}), bf16[8192,128]{1,0:T(8,128)(2,1)}) %all-gather.7.cloned.1.call-update) | async-done | bytes 2097168 | tf_op jit(solution)/shard_map/all_gather | solution.py:77
  92.1 4.4 %convolution_convert_fusion.1 = bf16[256,128]{0,1:T(8,128)(2,1)S(1)} fusion(bf16[256,8192]{1,0:T(8,128)(2,1)} %param.6, bf16[8192,128]{1,0:T(8,128)(2,1)} %all-gather.7.cloned.1.call-done), kind=kOutput, calls=%fused_computation.22 | convolution fusion | flops 536903680 | bytes 6356992 | tf_op jit(solution)/shard_map/dot_general | solution.py:80
  96.5 2.2 collective-permute-start.8
  98.7 4.4 %collective-permute-done.8 = bf16[128,256]{0,1:T(8,128)(2,1)S(1)} collective-permute-done((bf16[128,256]{0,1:T(8,128)(2,1)S(1)}, bf16[128,256]{0,1:T(8,128)(2,1)S(1)}, u32[]{:S(2)}, u32[]{:S(2)}) %collective-permute-start.8) | collective-permute-done | bytes 65568 | tf_op jit(solution)/shard_map/ppermute | solution.py:17
  103.2 1.9 collective-permute-start
  105.7 2.6 collective-permute-done
  108.3 5.5 %collective-permute-start.1 = (bf16[128,256]{0,1:T(8,128)(2,1)S(1)}, bf16[128,256]{0,1:T(8,128)(2,1)S(1)}, u32[]{:S(2)}, u32[]{:S(2)}) collective-permute-start(bf16[128,256]{0,1:T(8,128)(2,1)S(1)} %collective-permute-done), channel_id=1, source_target_pairs={{0,2},{2,4},{4,6},{6,8},{8,10},{10,12},{12,14},{14,16},{16,18},{18... | collective-permute-start | bytes 196616 | tf_op jit(solution)/shard_map/ppermute | solution.py:17
  113.9 3.9 %collective-permute-done.1 = bf16[128,256]{0,1:T(8,128)(2,1)S(1)} collective-permute-done((bf16[128,256]{0,1:T(8,128)(2,1)S(1)}, bf16[128,256]{0,1:T(8,128)(2,1)S(1)}, u32[]{:S(2)}, u32[]{:S(2)}) %collective-permute-start.1) | collective-permute-done | bytes 65568 | tf_op jit(solution)/shard_map/ppermute | solution.py:17
  117.8 5.6 %collective-permute-start.2 = (bf16[128,256]{0,1:T(8,128)(2,1)S(1)}, bf16[128,256]{0,1:T(8,128)(2,1)S(1)}, u32[]{:S(2)}, u32[]{:S(2)}) collective-permute-start(bf16[128,256]{0,1:T(8,128)(2,1)S(1)} %collective-permute-done.1), channel_id=1, source_target_pairs={{0,2},{2,4},{4,6},{6,8},{8,10},{10,12},{12,14},{14,16},{16,18},{18... | collective-permute-start | bytes 196616 | tf_op jit(solution)/shard_map/ppermute | solution.py:17
  124.7 5.2 %collective-permute-start.3 = (bf16[128,256]{0,1:T(8,128)(2,1)S(1)}, bf16[128,256]{0,1:T(8,128)(2,1)S(1)}, u32[]{:S(2)}, u32[]{:S(2)}) collective-permute-start(bf16[128,256]{0,1:T(8,128)(2,1)S(1)} %collective-permute-done.2), channel_id=1, source_target_pairs={{0,2},{2,4},{4,6},{6,8},{8,10},{10,12},{12,14},{14,16},{16,18},{18... | collective-permute-start | bytes 196616 | tf_op jit(solution)/shard_map/ppermute | solution.py:17
  131.1 5.7 %collective-permute-start.4 = (bf16[128,256]{0,1:T(8,128)(2,1)S(1)}, bf16[128,256]{0,1:T(8,128)(2,1)S(1)}, u32[]{:S(2)}, u32[]{:S(2)}) collective-permute-start(bf16[128,256]{0,1:T(8,128)(2,1)S(1)} %collective-permute-done.3), channel_id=1, source_target_pairs={{0,2},{2,4},{4,6},{6,8},{8,10},{10,12},{12,14},{14,16},{16,18},{18... | collective-permute-start | bytes 196616 | tf_op jit(solution)/shard_map/ppermute | solution.py:17
  136.9 3.9 %collective-permute-done.4 = bf16[128,256]{0,1:T(8,128)(2,1)S(1)} collective-permute-done((bf16[128,256]{0,1:T(8,128)(2,1)S(1)}, bf16[128,256]{0,1:T(8,128)(2,1)S(1)}, u32[]{:S(2)}, u32[]{:S(2)}) %collective-permute-start.4) | collective-permute-done | bytes 65568 | tf_op jit(solution)/shard_map/ppermute | solution.py:17
  140.8 5.6 %collective-permute-start.5 = (bf16[128,256]{0,1:T(8,128)(2,1)S(1)}, bf16[128,256]{0,1:T(8,128)(2,1)S(1)}, u32[]{:S(2)}, u32[]{:S(2)}) collective-permute-start(bf16[128,256]{0,1:T(8,128)(2,1)S(1)} %collective-permute-done.4), channel_id=1, source_target_pairs={{0,2},{2,4},{4,6},{6,8},{8,10},{10,12},{12,14},{14,16},{16,18},{18... | collective-permute-start | bytes 196616 | tf_op jit(solution)/shard_map/ppermute | solution.py:17
  146.4 3.5 %collective-permute-done.5 = bf16[128,256]{0,1:T(8,128)(2,1)S(1)} collective-permute-done((bf16[128,256]{0,1:T(8,128)(2,1)S(1)}, bf16[128,256]{0,1:T(8,128)(2,1)S(1)}, u32[]{:S(2)}, u32[]{:S(2)}) %collective-permute-start.5) | collective-permute-done | bytes 65568 | tf_op jit(solution)/shard_map/ppermute | solution.py:17
  149.9 5.6 %collective-permute-start.6 = (bf16[128,256]{0,1:T(8,128)(2,1)S(1)}, bf16[128,256]{0,1:T(8,128)(2,1)S(1)}, u32[]{:S(2)}, u32[]{:S(2)}) collective-permute-start(bf16[128,256]{0,1:T(8,128)(2,1)S(1)} %collective-permute-done.5), channel_id=1, source_target_pairs={{0,2},{2,4},{4,6},{6,8},{8,10},{10,12},{12,14},{14,16},{16,18},{18... | collective-permute-start | bytes 196616 | tf_op jit(solution)/shard_map/ppermute | solution.py:17
  156.8 5.2 %collective-permute-start.7 = (bf16[128,256]{0,1:T(8,128)(2,1)S(1)}, bf16[128,256]{0,1:T(8,128)(2,1)S(1)}, u32[]{:S(2)}, u32[]{:S(2)}) collective-permute-start(bf16[128,256]{0,1:T(8,128)(2,1)S(1)} %collective-permute-done.6), channel_id=1, source_target_pairs={{0,2},{2,4},{4,6},{6,8},{8,10},{10,12},{12,14},{14,16},{16,18},{18... | collective-permute-start | bytes 196616 | tf_op jit(solution)/shard_map/ppermute | solution.py:17
  162.6 1.9 collective-permute-start.9
  165.9 4.6 %collective-permute-done.9 = bf16[128,256]{0,1:T(8,128)(2,1)S(1)} collective-permute-done((bf16[128,256]{0,1:T(8,128)(2,1)S(1)}, bf16[128,256]{0,1:T(8,128)(2,1)S(1)}, u32[]{:S(2)}, u32[]{:S(2)}) %collective-permute-start.9) | collective-permute-done | bytes 65568 | tf_op jit(solution)/shard_map/ppermute | solution.py:17
  170.5 1.9 collective-permute-start.10
  172.5 4.5 %collective-permute-done.10 = bf16[128,256]{0,1:T(8,128)(2,1)S(1)} collective-permute-done((bf16[128,256]{0,1:T(8,128)(2,1)S(1)}, bf16[128,256]{0,1:T(8,128)(2,1)S(1)}, u32[]{:S(2)}, u32[]{:S(2)}) %collective-permute-start.10) | collective-permute-done | bytes 65568 | tf_op jit(solution)/shard_map/ppermute | solution.py:17
  177.0 1.9 collective-permute-start.11
  179.0 4.5 %collective-permute-done.11 = bf16[128,256]{0,1:T(8,128)(2,1)S(1)} collective-permute-done((bf16[128,256]{0,1:T(8,128)(2,1)S(1)}, bf16[128,256]{0,1:T(8,128)(2,1)S(1)}, u32[]{:S(2)}, u32[]{:S(2)}) %collective-permute-start.11) | collective-permute-done | bytes 65568 | tf_op jit(solution)/shard_map/ppermute | solution.py:17
  185.5 5.9 %collective-permute-done.12 = bf16[128,256]{0,1:T(8,128)(2,1)S(1)} collective-permute-done((bf16[128,256]{0,1:T(8,128)(2,1)S(1)}, bf16[128,256]{0,1:T(8,128)(2,1)S(1)}, u32[]{:S(2)}, u32[]{:S(2)}) %collective-permute-start.12) | collective-permute-done | bytes 65568 | tf_op jit(solution)/shard_map/ppermute | solution.py:17
  194.2 5.5 %collective-permute-done.13 = bf16[128,256]{0,1:T(8,128)(2,1)S(1)} collective-permute-done((bf16[128,256]{0,1:T(8,128)(2,1)S(1)}, bf16[128,256]{0,1:T(8,128)(2,1)S(1)}, u32[]{:S(2)}, u32[]{:S(2)}) %collective-permute-start.13) | collective-permute-done | bytes 65568 | tf_op jit(solution)/shard_map/ppermute | solution.py:17
  202.2 4.7 %collective-permute-done.14 = bf16[128,256]{0,1:T(8,128)(2,1)S(1)} collective-permute-done((bf16[128,256]{0,1:T(8,128)(2,1)S(1)}, bf16[128,256]{0,1:T(8,128)(2,1)S(1)}, u32[]{:S(2)}, u32[]{:S(2)}) %collective-permute-start.14) | collective-permute-done | bytes 65568 | tf_op jit(solution)/shard_map/ppermute | solution.py:17
  206.9 2.1 collective-permute-start.15
  209.0 4.3 %collective-permute-done.15 = bf16[128,256]{0,1:T(8,128)(2,1)S(1)} collective-permute-done((bf16[128,256]{0,1:T(8,128)(2,1)S(1)}, bf16[128,256]{0,1:T(8,128)(2,1)S(1)}, u32[]{:S(2)}, u32[]{:S(2)}) %collective-permute-start.15) | collective-permute-done | bytes 65568 | tf_op jit(solution)/shard_map/ppermute | solution.py:17
  213.6 7.3 %fusion.62 = f32[256,512]{1,0:T(8,128)S(1)} fusion(bf16[256,8192]{1,0:T(8,128)(2,1)} %param.6, bf16[8192,512]{1,0:T(8,128)(2,1)} %all-gather.9.cloned.1.call-done), kind=kOutput, calls=%fused_computation.120 | convolution fusion | flops 2147483648 | bytes 13107200 | tf_op jit(solution)/shard_map/dot_general | solution.py:80
  226.2 27.3 %all-gather.11.cloned.1.call-done = bf16[512,8192]{1,0:T(8,128)(2,1)} async-done(((bf16[512,512]{1,0:T(8,128)(2,1)}), bf16[512,8192]{1,0:T(8,128)(2,1)}) %all-gather.11.cloned.1.call-update) | async-done | bytes 8388624 | tf_op jit(solution)/shard_map/all_gather | solution.py:129
  253.6 7.8 %convolution_convert_fusion = bf16[256,8192]{1,0:T(8,128)(2,1)} fusion(bf16[512,8192]{1,0:T(8,128)(2,1)} %all-gather.11.cloned.1.call-done, bf16[128,512]{0,1:T(8,128)(2,1)S(1)} %bitcast.100, bf16[128,512]{0,1:T(8,128)(2,1)S(1)} %bitcast.99), kind=kOutput, calls=%fused_computation.4 | convolution fusion | flops 2150105088 | bytes 12845056 | tf_op jit(solution)/shard_map/dot_general | solution.py:127
  (73 shorter events, 22.4 us)
Async XLA Ops:
  6.5 43.2 %all-gather.5.cloned.1.call-start = ((), (), s32[]{:S(2)}) async-start(), calls=%async_computation | async-start | bytes 2228224 | tf_op jit(solution)/shard_map/all_gather | solution.py:76
  7.3 84.9 %all-gather.7.cloned.1.call-start = ((), (), s32[]{:S(2)}) async-start(), calls=%async_computation.1 | async-start | bytes 2228224 | tf_op jit(solution)/shard_map/all_gather | solution.py:77
  8.0 205.6 %all-gather.9.cloned.1.call-start = ((), (), s32[]{:S(2)}) async-start(), calls=%async_computation.2 | async-start | bytes 8912896 | tf_op jit(solution)/shard_map/all_gather | solution.py:75
  8.7 244.8 %all-gather.11.cloned.1.call-start = ((), (), s32[]{:S(2)}) async-start(), calls=%async_computation.3 | async-start | bytes 8912896 | tf_op jit(solution)/shard_map/all_gather | solution.py:129
  54.5 50.6 %copy-start = (s32[4096]{0:T(1024)S(1)}, s32[4096]{0:T(1024)}, u32[]{:S(2)}) copy-start(s32[4096]{0:T(1024)} %param.7) | copy-start | bytes 49156
  96.5 6.6 %collective-permute-start.8 = (bf16[128,256]{0,1:T(8,128)(2,1)S(1)}, bf16[128,256]{0,1:T(8,128)(2,1)S(1)}, u32[]{:S(2)}, u32[]{:S(2)}) collective-permute-start(bf16[128,256]{0,1:T(8,128)(2,1)S(1)} %pad_maximum_fusion.1), channel_id=1, source_target_pairs={{2,0},{4,2},{6,4},{8,6},{10,8},{12,10},{14,12},{16,14},{18,16},{20... | collective-permute-start | bytes 196616 | tf_op jit(solution)/shard_map/ppermute | solution.py:17
  103.2 5.1 %collective-permute-start = (bf16[128,256]{0,1:T(8,128)(2,1)S(1)}, bf16[128,256]{0,1:T(8,128)(2,1)S(1)}, u32[]{:S(2)}, u32[]{:S(2)}) collective-permute-start(bf16[128,256]{0,1:T(8,128)(2,1)S(1)} %get-tuple-element.6), channel_id=1, source_target_pairs={{0,2},{2,4},{4,6},{6,8},{8,10},{10,12},{12,14},{14,16},{16,18},{18... | collective-permute-start | bytes 196616 | tf_op jit(solution)/shard_map/ppermute | solution.py:17
  108.3 9.4 %collective-permute-start.1 = (bf16[128,256]{0,1:T(8,128)(2,1)S(1)}, bf16[128,256]{0,1:T(8,128)(2,1)S(1)}, u32[]{:S(2)}, u32[]{:S(2)}) collective-permute-start(bf16[128,256]{0,1:T(8,128)(2,1)S(1)} %collective-permute-done), channel_id=1, source_target_pairs={{0,2},{2,4},{4,6},{6,8},{8,10},{10,12},{12,14},{14,16},{16,18},{18... | collective-permute-start | bytes 196616 | tf_op jit(solution)/shard_map/ppermute | solution.py:17
  117.8 6.9 %collective-permute-start.2 = (bf16[128,256]{0,1:T(8,128)(2,1)S(1)}, bf16[128,256]{0,1:T(8,128)(2,1)S(1)}, u32[]{:S(2)}, u32[]{:S(2)}) collective-permute-start(bf16[128,256]{0,1:T(8,128)(2,1)S(1)} %collective-permute-done.1), channel_id=1, source_target_pairs={{0,2},{2,4},{4,6},{6,8},{8,10},{10,12},{12,14},{14,16},{16,18},{18... | collective-permute-start | bytes 196616 | tf_op jit(solution)/shard_map/ppermute | solution.py:17
  124.7 6.5 %collective-permute-start.3 = (bf16[128,256]{0,1:T(8,128)(2,1)S(1)}, bf16[128,256]{0,1:T(8,128)(2,1)S(1)}, u32[]{:S(2)}, u32[]{:S(2)}) collective-permute-start(bf16[128,256]{0,1:T(8,128)(2,1)S(1)} %collective-permute-done.2), channel_id=1, source_target_pairs={{0,2},{2,4},{4,6},{6,8},{8,10},{10,12},{12,14},{14,16},{16,18},{18... | collective-permute-start | bytes 196616 | tf_op jit(solution)/shard_map/ppermute | solution.py:17
  131.1 9.6 %collective-permute-start.4 = (bf16[128,256]{0,1:T(8,128)(2,1)S(1)}, bf16[128,256]{0,1:T(8,128)(2,1)S(1)}, u32[]{:S(2)}, u32[]{:S(2)}) collective-permute-start(bf16[128,256]{0,1:T(8,128)(2,1)S(1)} %collective-permute-done.3), channel_id=1, source_target_pairs={{0,2},{2,4},{4,6},{6,8},{8,10},{10,12},{12,14},{14,16},{16,18},{18... | collective-permute-start | bytes 196616 | tf_op jit(solution)/shard_map/ppermute | solution.py:17
  140.8 9.2 %collective-permute-start.5 = (bf16[128,256]{0,1:T(8,128)(2,1)S(1)}, bf16[128,256]{0,1:T(8,128)(2,1)S(1)}, u32[]{:S(2)}, u32[]{:S(2)}) collective-permute-start(bf16[128,256]{0,1:T(8,128)(2,1)S(1)} %collective-permute-done.4), channel_id=1, source_target_pairs={{0,2},{2,4},{4,6},{6,8},{8,10},{10,12},{12,14},{14,16},{16,18},{18... | collective-permute-start | bytes 196616 | tf_op jit(solution)/shard_map/ppermute | solution.py:17
  149.9 6.9 %collective-permute-start.6 = (bf16[128,256]{0,1:T(8,128)(2,1)S(1)}, bf16[128,256]{0,1:T(8,128)(2,1)S(1)}, u32[]{:S(2)}, u32[]{:S(2)}) collective-permute-start(bf16[128,256]{0,1:T(8,128)(2,1)S(1)} %collective-permute-done.5), channel_id=1, source_target_pairs={{0,2},{2,4},{4,6},{6,8},{8,10},{10,12},{12,14},{14,16},{16,18},{18... | collective-permute-start | bytes 196616 | tf_op jit(solution)/shard_map/ppermute | solution.py:17
  156.8 8.9 %collective-permute-start.7 = (bf16[128,256]{0,1:T(8,128)(2,1)S(1)}, bf16[128,256]{0,1:T(8,128)(2,1)S(1)}, u32[]{:S(2)}, u32[]{:S(2)}) collective-permute-start(bf16[128,256]{0,1:T(8,128)(2,1)S(1)} %collective-permute-done.6), channel_id=1, source_target_pairs={{0,2},{2,4},{4,6},{6,8},{8,10},{10,12},{12,14},{14,16},{16,18},{18... | collective-permute-start | bytes 196616 | tf_op jit(solution)/shard_map/ppermute | solution.py:17
  162.6 7.9 %collective-permute-start.9 = (bf16[128,256]{0,1:T(8,128)(2,1)S(1)}, bf16[128,256]{0,1:T(8,128)(2,1)S(1)}, u32[]{:S(2)}, u32[]{:S(2)}) collective-permute-start(bf16[128,256]{0,1:T(8,128)(2,1)S(1)} %get-tuple-element.5), channel_id=1, source_target_pairs={{2,0},{4,2},{6,4},{8,6},{10,8},{12,10},{14,12},{16,14},{18,16},{20... | collective-permute-start | bytes 196616 | tf_op jit(solution)/shard_map/ppermute | solution.py:17
  170.5 6.5 %collective-permute-start.10 = (bf16[128,256]{0,1:T(8,128)(2,1)S(1)}, bf16[128,256]{0,1:T(8,128)(2,1)S(1)}, u32[]{:S(2)}, u32[]{:S(2)}) collective-permute-start(bf16[128,256]{0,1:T(8,128)(2,1)S(1)} %get-tuple-element.14), channel_id=1, source_target_pairs={{2,0},{4,2},{6,4},{8,6},{10,8},{12,10},{14,12},{16,14},{18,16},{20... | collective-permute-start | bytes 196616 | tf_op jit(solution)/shard_map/ppermute | solution.py:17
  177.0 6.5 %collective-permute-start.11 = (bf16[128,256]{0,1:T(8,128)(2,1)S(1)}, bf16[128,256]{0,1:T(8,128)(2,1)S(1)}, u32[]{:S(2)}, u32[]{:S(2)}) collective-permute-start(bf16[128,256]{0,1:T(8,128)(2,1)S(1)} %broadcast_select_fusion.4), channel_id=1, source_target_pairs={{2,0},{4,2},{6,4},{8,6},{10,8},{12,10},{14,12},{16,14},{18,16},{20... | collective-permute-start | bytes 196616 | tf_op jit(solution)/shard_map/ppermute | solution.py:17
  183.5 7.9 %collective-permute-start.12 = (bf16[128,256]{0,1:T(8,128)(2,1)S(1)}, bf16[128,256]{0,1:T(8,128)(2,1)S(1)}, u32[]{:S(2)}, u32[]{:S(2)}) collective-permute-start(bf16[128,256]{0,1:T(8,128)(2,1)S(1)} %broadcast_select_fusion.3), channel_id=1, source_target_pairs={{2,0},{4,2},{6,4},{8,6},{10,8},{12,10},{14,12},{16,14},{18,16},{20... | collective-permute-start | bytes 196616 | tf_op jit(solution)/shard_map/ppermute | solution.py:17
  191.4 8.3 %collective-permute-start.13 = (bf16[128,256]{0,1:T(8,128)(2,1)S(1)}, bf16[128,256]{0,1:T(8,128)(2,1)S(1)}, u32[]{:S(2)}, u32[]{:S(2)}) collective-permute-start(bf16[128,256]{0,1:T(8,128)(2,1)S(1)} %broadcast_select_fusion.2), channel_id=1, source_target_pairs={{2,0},{4,2},{6,4},{8,6},{10,8},{12,10},{14,12},{16,14},{18,16},{20... | collective-permute-start | bytes 196616 | tf_op jit(solution)/shard_map/ppermute | solution.py:17
  199.7 7.2 %collective-permute-start.14 = (bf16[128,256]{0,1:T(8,128)(2,1)S(1)}, bf16[128,256]{0,1:T(8,128)(2,1)S(1)}, u32[]{:S(2)}, u32[]{:S(2)}) collective-permute-start(bf16[128,256]{0,1:T(8,128)(2,1)S(1)} %broadcast_select_fusion.1), channel_id=1, source_target_pairs={{2,0},{4,2},{6,4},{8,6},{10,8},{12,10},{14,12},{16,14},{18,16},{20... | collective-permute-start | bytes 196616 | tf_op jit(solution)/shard_map/ppermute | solution.py:17
  206.9 6.5 %collective-permute-start.15 = (bf16[128,256]{0,1:T(8,128)(2,1)S(1)}, bf16[128,256]{0,1:T(8,128)(2,1)S(1)}, u32[]{:S(2)}, u32[]{:S(2)}) collective-permute-start(bf16[128,256]{0,1:T(8,128)(2,1)S(1)} %broadcast_select_fusion), channel_id=1, source_target_pairs={{2,0},{4,2},{6,4},{8,6},{10,8},{12,10},{14,12},{16,14},{18,16},{20... | collective-permute-start | bytes 196616 | tf_op jit(solution)/shard_map/ppermute | solution.py:17
Sparse Core Ops, SparseCore 0:
  9.5 40.2 all-gather.4
  51.9 40.1 all-gather.6
  94.3 78.0 all-gather.8
  174.4 79.0 all-gather.10
where the time goes:
time: 272 us; the launch traced here: 268 us
  waiting for transfers between devices  165 us (61%)
  starting transfers between devices  56.1 us (21%)
  matrix products  28.3 us (10%)
  between operations  13.6 us (5%)
  other arithmetic  3.19 us (1%)
    ppermute x16, waiting for transfers between devices, passed_along(): lax.ppermute(value, axis, [(source, source + steps) for source in range(l...  56.8 us
    ppermute x16, starting transfers between devices, passed_along(): lax.ppermute(value, axis, [(source, source + steps) for source in range(l...  56 us
    all_gather x1, waiting for transfers between devices, on_device(): lax.all_gather(w_key, 'ctx', axis=0, tiled=True)  40.4 us
    all_gather x1, waiting for transfers between devices, on_device(): lax.all_gather(w_value, 'ctx', axis=0, tiled=True)  37.6 us
    all_gather x1, waiting for transfers between devices, on_device(): lax.all_gather(w_out, 'ctx', axis=1, tiled=True)  27.3 us
    dot_general x3, matrix products, on_device(): jnp.dot(hidden_in, portion, preferred_element_type=jnp.float32)  16 us
    dot_general x1, matrix products, on_device(): jnp.dot(mixed_rows, lax.all_gather(w_out, 'ctx', axis=1, tiled=True), pre...  7.77 us
  transfers between devices with their start and end apart: 20, of which 19 were waited for; matrix products, arithmetic and copies ran while one was open for 10% of the time, Pallas kernels for 0%

commit v1 on v0

v1 whole, which is shorter than its diff:
```python
import functools
import math

import jax
import jax.numpy as jnp
from jax import lax
from jax.experimental import pallas as pl
from jax.experimental.pallas import tpu as pltpu
from jax.sharding import PartitionSpec as P

REACH = 8
ROPE_BASE = 500000.0
RING_LIMIT = 16
VMEM_LIMIT = 16 * 1024 * 1024


def chip_at(place, chips):
    place = place % chips
    return jnp.where(place < chips // 2, 2 * place, 2 * (chips - 1 - place) + 1)


def static_chip_at(place, chips):
    place %= chips
    return 2 * place if place < chips // 2 else 2 * (chips - 1 - place) + 1


def ring_pairs(chips):
    pairs = []
    for place in range(chips):
        here = static_chip_at(place, chips)
        pairs.append((2 * here, 2 * static_chip_at(place + 1, chips)))
        pairs.append((2 * here + 1, 2 * static_chip_at(place - 1, chips) + 1))
    return pairs


def core_swap(value, count):
    return lax.ppermute(value, "ctx", [(i, i ^ 1) for i in range(count)])


def plane_swap(value):
    return lax.ppermute(value, "dp", [(0, 1), (1, 0)])


def pair_device(pair, count):
    return 2 * pair if pair < count // 2 else 2 * (count - 1 - pair) + 1


def after(value, *others):
    return lax.optimization_barrier((value, *others))[0]


def shard_owners(me, count):
    chips = count // 2
    half = chips // 2
    core, chip = me % 2, me // 2
    place = jnp.where(chip % 2 == 0, chip // 2, chips - 1 - chip // 2)
    way = jnp.where(core == 0, -1, 1)
    owners = [me]
    for step in range(1, half + 1):
        source = chip_at(place + way * step + chips, chips)
        owners.append(2 * source + core)
        if step < half:
            owners.append(2 * source + 1 - core)
    return owners


def params(**settings):
    return pltpu.CompilerParams(vmem_limit_bytes=VMEM_LIMIT, **settings)


def in_vmem(*arrays):
    return [pltpu.with_memory_space_constraint(array, pltpu.VMEM) for array in arrays]


def in_hbm(*arrays):
    return [pltpu.with_memory_space_constraint(array, pltpu.HBM) for array in arrays]


IN_VMEM = pl.BlockSpec(memory_space=pltpu.VMEM)
IN_HBM = pl.BlockSpec(memory_space=pl.ANY)
IN_SMEM = pl.BlockSpec(memory_space=pltpu.SMEM)


def rotate_kernel(head_dim, kept_ref, came_ref, cos_ref, sin_ref, joined_ref, query_ref):
    cosine, sine = cos_ref[...], sin_ref[...]

    def rotated(column):
        span = pl.ds(column, head_dim)
        part = kept_ref[:, span] + came_ref[:, span]
        return (part * cosine + pltpu.roll(part, head_dim // 2, 1) * sine).astype(jnp.bfloat16)

    joined_ref[:, :head_dim] = rotated(0)
    values = pl.ds(head_dim, head_dim)
    joined_ref[:, values] = (kept_ref[:, values] + came_ref[:, values]).astype(jnp.bfloat16)
    for column in range(0, query_ref.shape[1], head_dim):
        query_ref[:, pl.ds(column, head_dim)] = rotated(2 * head_dim + column)


def rotate_sums(kept, came, positions, head_dim):
    rows, columns = kept.shape
    frequency = ROPE_BASE ** (
        -(jnp.arange(head_dim // 2, dtype=jnp.float32) * 2.0) / head_dim
    )
    angles = positions.astype(jnp.float32)[:, None] * frequency[None, :]
    cosine, sine = jnp.cos(angles), jnp.sin(angles)
    cosine = jnp.concatenate([cosine, cosine], axis=1)
    sine = jnp.concatenate([-sine, sine], axis=1)
    return pl.pallas_call(
        functools.partial(rotate_kernel, head_dim),
        out_shape=(
            pltpu.VMEM((rows, 2 * head_dim), jnp.bfloat16),
            pltpu.VMEM((rows, columns - 2 * head_dim), jnp.bfloat16),
        ),
        in_specs=[IN_VMEM] * 4,
        out_specs=(IN_VMEM, IN_VMEM),
        compiler_params=params(),
        name="rotate_sums",
    )(*in_vmem(kept, came, cosine, sine))


def attend_kernel(
    head_dim, reach, query_ref, key_seg_ref, query_seg_ref, *refs
):
    windows, mixed_ref = refs[:-1], refs[-1]
    rows = query_ref.shape[0]
    query_seg = query_seg_ref[...]
    base = lax.broadcasted_iota(jnp.int32, (rows, rows), 0)
    offset = lax.broadcasted_iota(jnp.int32, (rows, rows), 1)
    allowed = []
    for piece in range(reach + 1):
        same = query_seg == key_seg_ref[:, pl.ds(piece * rows, rows)]
        if piece == reach:
            same = same & (offset <= base)
        allowed.append(same)
    for column in range(0, query_ref.shape[1], head_dim):
        span = pl.ds(column, head_dim)
        query = query_ref[:, span]
        scores = []
        for piece in range(reach + 1):
            score = lax.dot_general(
                query,
                windows[piece][:, :head_dim],
                (((1,), (1,)), ((), ())),
                preferred_element_type=jnp.float32,
            ) / math.sqrt(head_dim)
            scores.append(jnp.where(allowed[piece], score, -1e30))
        peak = scores[0]
        for score in scores[1:]:
            peak = jnp.maximum(peak, score)
        peak = jnp.max(peak, axis=1, keepdims=True)
        terms = [jnp.exp(score - peak) for score in scores]
        total = terms[0]
        for term in terms[1:]:
            total = total + term
        inverse = 1.0 / jnp.sum(total, axis=1, keepdims=True)
        mixed = jnp.zeros((rows, head_dim), jnp.float32)
        for piece in range(reach + 1):
            mixed += jnp.dot(
                (terms[piece] * inverse).astype(jnp.bfloat16),
                windows[piece][:, head_dim:],
                preferred_element_type=jnp.float32,
            )
        mixed_ref[:, span] = mixed.astype(jnp.bfloat16)


def attend(queries, windows, key_seg, query_seg, head_dim):
    reach = len(windows) - 1
    rows = queries.shape[0]
    kernel = functools.partial(attend_kernel, head_dim, reach)
    return pl.pallas_call(
        kernel,
        out_shape=pltpu.VMEM(queries.shape, jnp.bfloat16),
        in_specs=[IN_VMEM] * (3 + len(windows)),
        out_specs=IN_VMEM,
        compiler_params=params(),
        name="attend",
    )(*in_vmem(queries, key_seg.reshape(1, -1), query_seg.reshape(rows, 1), *windows))


def join_projections_kernel(plane_ref, *refs):
    own, beside, (near_out, common_out, far_out, sems) = refs[:3], refs[3:6], refs[6:]
    q_half, kv_half = near_out.shape[2], common_out.shape[2] // 2
    near = pl.ds(pl.multiple_of(plane_ref[0] * q_half, q_half), q_half)
    far = pl.ds(pl.multiple_of((1 - plane_ref[0]) * q_half, q_half), q_half)
    moves = [(own[0].at[:, far], far_out.at[0])]
    for slot, (query_ref, key_ref, value_ref) in enumerate((own, beside)):
        moves += [
            (query_ref.at[:, near], near_out.at[slot]),
            (key_ref, common_out.at[slot, :, :kv_half]),
            (value_ref, common_out.at[slot, :, kv_half:]),
        ]
    copies = [
        pltpu.make_async_copy(source, target, sems.at[place])
        for place, (source, target) in enumerate(moves)
    ]
    for copy in copies:
        copy.start()
    for copy in copies:
        copy.wait()


def join_projections(plane, own, beside):
    query, key, value = own
    depth, q_half = query.shape[0], query.shape[1] // 2
    shapes = ((2, depth, q_half), (2, depth, 2 * key.shape[1]), (1, depth, q_half))
    return pl.pallas_call(
        join_projections_kernel,
        in_specs=[IN_SMEM] + [IN_HBM] * 3 + [IN_VMEM] * 3,
        out_specs=[IN_VMEM] * 3,
        scratch_shapes=[pltpu.SemaphoreType.DMA((7,))],
        out_shape=[pltpu.VMEM(shape, jnp.bfloat16) for shape in shapes],
        compiler_params=params(),
        name="join_projections",
    )(plane, *in_hbm(*own), *in_vmem(*beside))


def project_kernel(slots, groups, first, last, index_ref, *refs):
    sources, refs = refs[:2], refs[2:]
    refs, (tokens, sems) = refs[:-2], refs[-2:]
    rows, depth = tokens.shape[1:]
    copies = []
    for place in range(len(slots)):
        column = pl.multiple_of(index_ref[1 + place] * depth, depth)
        for side in range(2):
            entry = 2 * place + side
            copy = pltpu.make_async_copy(
                sources[side].at[:, pl.ds(column, depth)], tokens.at[entry], sems.at[entry]
            )
            copy.start()
            copies.append(copy)
    held_weights = groups * (1 + slots[-1][0])
    weights, refs = refs[:held_weights], refs[held_weights:]
    total_ref, refs = (None, refs) if first else (refs[0], refs[1:])
    block = rows // 2
    width = weights[0].shape[-1]
    out_ref = refs[2] if last else refs[0]
    for copy in copies:
        copy.wait()
    for side in range(2):
        for group in range(groups):
            columns = pl.ds(group * width, width)
            total = None if first else total_ref[side, :, columns]
            for place, (step, slot) in enumerate(slots):
                product = jnp.dot(
                    tokens[2 * place + side],
                    weights[groups * step + group][slot],
                    preferred_element_type=jnp.float32,
                )
                total = product if total is None else total + product
            out_ref[side, :, columns] = total
    if last:
        kept_ref, sent_ref, held = refs
        mine = pl.multiple_of(index_ref[0] * block, block)
        others = pl.multiple_of((1 - index_ref[0]) * block, block)
        kept_ref[:block] = held[0, pl.ds(mine, block), :]
        kept_ref[block:] = held[1, pl.ds(mine, block), :]
        sent_ref[:block] = held[1, pl.ds(others, block), :]
        sent_ref[block:] = held[0, pl.ds(others, block), :]


def project(index, tokens, steps, total, last):
    groups = len(steps[0][1])
    slots = [(i, slot) for i, (used, _) in enumerate(steps) for slot in range(used)]
    rows = tokens[0].shape[0]
    depth = steps[0][1][0].shape[1]
    columns = sum(part.shape[2] for part in steps[0][1])
    operands = in_hbm(tokens[0]) + in_vmem(tokens[1], *(part for _, parts in steps for part in parts))
    if total is not None:
        operands += in_vmem(total)
    specs = [IN_SMEM, IN_HBM] + [IN_VMEM] * (len(operands) - 1)
    shapes = ((rows, columns), (rows, columns)) if last else ((2, rows, columns),)
    out = pl.pallas_call(
        functools.partial(project_kernel, slots, groups, total is None, last),
        in_specs=specs,
        out_specs=[IN_VMEM] * len(shapes),
        scratch_shapes=([pltpu.VMEM((2, rows, columns), jnp.float32)] if last else [])
        + [
            pltpu.VMEM((2 * len(slots), rows, depth), jnp.bfloat16),
            pltpu.SemaphoreType.DMA((2 * len(slots),)),
        ],
        out_shape=[pltpu.VMEM(shape, jnp.float32) for shape in shapes],
        compiler_params=params(),
        name="project",
    )(index, *operands)
    return out if last else out[0]


def columns_kernel(places, index_ref, mixed_ref, returned_ref, *refs):
    weights = list(refs[: sum(places)])
    out_ref, send_ref, held, sems = refs[-4:]
    block = mixed_ref.shape[0] // 2
    half = mixed_ref.shape[1] // 2
    width = weights[0].shape[-1]
    mine = pl.ds(pl.multiple_of(index_ref[0] * block, block), block)
    others = pl.ds(pl.multiple_of((1 - index_ref[0]) * block, block), block)
    near = pl.ds(pl.multiple_of(index_ref[1] * half, half), half)
    far = pl.ds(pl.multiple_of((1 - index_ref[1]) * half, half), half)
    rows_in = jnp.concatenate([mixed_ref[...], returned_ref[...]], axis=0)
    copies = []
    for place, parts in enumerate(places):
        if parts == 1:
            whole = weights.pop(0)
            low, high = whole[near, :], whole[far, :]
        else:
            low, high = weights.pop(0)[...], weights.pop(0)[...]
        weight = jnp.concatenate([low, high], axis=0)
        value = jnp.dot(rows_in, weight, preferred_element_type=jnp.float32)
        value = value.astype(jnp.bfloat16)
        columns = pl.ds(place * width, width)
        held[mine, columns] = value[:block]
        held[others, columns] = value[3 * block :]
        send_ref[mine, columns] = value[block : 2 * block]
        send_ref[others, columns] = value[2 * block : 3 * block]
        column = pl.multiple_of(index_ref[2 + place] * width, width)
        copy = pltpu.make_async_copy(
            held.at[:, columns], out_ref.at[:, pl.ds(column, width)], sems.at[place]
        )
        copy.start()
        copies.append(copy)
    for copy in copies:
        copy.wait()


def columns_of(index, mixed, returned, shards, result, width):
    rows = mixed.shape[0]
    out_cols = shards[0][0].shape[-1]
    operands = in_vmem(mixed, returned, *(part for shard in shards for part in shard))
    specs = [IN_SMEM] + [IN_VMEM] * len(operands)
    if result is not None:
        operands += in_hbm(result)
        specs.append(IN_HBM)
    sent = (rows, len(shards) * out_cols)
    return pl.pallas_call(
        functools.partial(columns_kernel, [len(shard) for shard in shards]),
        in_specs=specs,
        out_specs=[IN_HBM, IN_VMEM],
        scratch_shapes=[
            pltpu.VMEM(sent, jnp.bfloat16),
            pltpu.SemaphoreType.DMA((len(shards),)),
        ],
        out_shape=[pltpu.HBM((rows, width), jnp.bfloat16), pltpu.VMEM(sent, jnp.bfloat16)],
        input_output_aliases={} if result is None else {len(operands): 0},
        compiler_params=params(),
        name="columns_of",
    )(index, *operands)


def place_kernel(width, owners_ref, came_ref, _, out_ref, sems):
    copies = []
    for place in range(came_ref.shape[1] // width):
        column = pl.multiple_of(owners_ref[place] * width, width)
        copy = pltpu.make_async_copy(
            came_ref.at[:, pl.ds(place * width, width)],
            out_ref.at[:, pl.ds(column, width)],
            sems.at[place],
        )
        copy.start()
        copies.append(copy)
    for copy in copies:
        copy.wait()


def place_columns(owners, came, result, out_cols):
    return pl.pallas_call(
        functools.partial(place_kernel, out_cols),
        in_specs=[IN_SMEM, IN_VMEM, IN_HBM],
        out_specs=IN_HBM,
        scratch_shapes=[pltpu.SemaphoreType.DMA((came.shape[1] // out_cols,))],
        out_shape=pltpu.HBM(result.shape, result.dtype),
        input_output_aliases={2: 0},
        compiler_params=params(),
        name="place_columns",
    )(owners, *in_vmem(came), *in_hbm(result))


def on_device(hidden_in, segment_ids, w_query, w_key, w_value, w_out):
    count = lax.axis_size("ctx")
    me = lax.axis_index("ctx")
    plane = lax.axis_index("dp")
    core, chip = me % 2, me // 2
    rows, width = hidden_in.shape
    block = rows // 2
    head_dim = w_key.shape[1]
    q_rows, out_cols = w_out.shape
    q_half = q_rows // 2

    ringed = count <= RING_LIMIT
    if ringed:
        depth = w_query.shape[0]
        plane_index = plane.reshape(1).astype(jnp.int32)
        pairs = ring_pairs(count // 2)
        half = count // 4
        owners = shard_owners(me, count)

        def ring(value):
            return lax.ppermute(value, "ctx", pairs)

        own = (w_query, w_key, w_value)
        beside = tuple(core_swap(part, count) for part in own)
        near, common, own_far = join_projections(plane_index, own, beside)
        steps = [(1, (common, near, own_far))]
        other = core_swap(after(hidden_in, near), count)

        def add_projections(total, begin, end):
            place = 0 if begin == 0 else 2 * begin - 1
            used = sum(step[0] for step in steps[begin:end])
            index = jnp.stack([core, *owners[place : place + used]]).astype(jnp.int32)
            return project(index, (hidden_in, other), steps[begin:end], total, end == half + 1)

        total = None
        for step in range(1, half + 1):
            if step == half:
                near, common = near[:1], common[:1]
            if step > 2:
                near = after(near, steps[step - 2][1][2])
            near = ring(near)
            if step == 2:
                beside_near = lax.dynamic_slice(w_out, (plane * q_half, 0), (q_half, out_cols))
                beside_near = core_swap(after(beside_near, near), count)
            if step == 4:
                total = add_projections(None, 0, 2)
                common = after(common, total)
            common = ring(after(common, near))
            steps.append((near.shape[0], (common, near, plane_swap(near))))

        total = add_projections(total, 2, 3)
        out_near = after(beside_near, near, steps[half - 1][1][0], steps[half - 1][1][2])
        out_whole = after(w_out, common, total)
        shards = [(w_out,)]
        for step in range(1, half + 1):
            if step == 2:
                out_near = after(out_near, steps[half][1][2])
            if step > 2:
                out_near = after(out_near, shards[-1][1])
            if step < half:
                out_near = ring(out_near)
            out_whole = ring(out_whole)
            shards.append((out_whole,))
            if step < half:
                shards.append((out_near, plane_swap(out_near)))
        total = add_projections(total, 3, 4)
        kept, sent = add_projections(total, 4, 5)
        came = core_swap(sent, count)
    else:
        gathered = lax.all_gather(
            jnp.concatenate([w_key, w_value, w_query], axis=1), "ctx", axis=0, tiled=True
        )
        ordered = jnp.where(core == 0, hidden_in, jnp.roll(hidden_in, block, axis=0))
        pair_tokens = jnp.concatenate([ordered[:block], core_swap(ordered[block:], count)], axis=0)
        kept = jnp.dot(pair_tokens, gathered, preferred_element_type=jnp.float32)
        came = jnp.zeros_like(kept)

    if ringed:
        came = after(came, shards[1][0], shards[2][0])
    pair = jnp.where(core == 0, chip, count - 1 - chip)
    pair_pos = pair * rows + jnp.arange(rows, dtype=jnp.int32)
    joined, queries = rotate_sums(kept, came, pair_pos, head_dim)

    reach = REACH * block // rows
    windows = [joined]
    for back in range(1, reach + 1):
        sends = [
            (pair_device(m, count), pair_device(m + back, count)) for m in range(count - back)
        ]
        windows.append(lax.ppermute(joined, "ctx", sends))

    seg_blocks = segment_ids.reshape(2 * count, block)
    seq_block = pair * 2 - 2 * reach + jnp.arange(2 * reach + 2, dtype=jnp.int32)
    clipped = jnp.maximum(seq_block, 0)
    stored = jnp.where(clipped < count, 2 * clipped, 2 * (2 * count - 1 - clipped) + 1)
    seg_rows = seg_blocks[stored]
    key_seg = jnp.where(seq_block[:, None] >= 0, seg_rows, -1).reshape(-1)
    if ringed:
        queries = after(queries, shards[3][0], shards[4][0])
    mixed = attend(queries, windows[::-1], key_seg, seg_rows[-2:].reshape(-1), head_dim)

    returned = core_swap(mixed, count)
    if not ringed:
        kinds = (mixed[:block], returned[block:])
        own_rows = jnp.where(
            core == 0, jnp.concatenate(kinds, axis=0), jnp.concatenate(kinds[::-1], axis=0)
        )
        gathered = lax.all_gather(w_out, "ctx", axis=1, tiled=True)
        return jnp.dot(own_rows, gathered, preferred_element_type=jnp.float32).astype(jnp.bfloat16)

    returned = after(returned, shards[5][0], shards[6][0])
    other_owners = shard_owners(me ^ 1, count)
    arrivals = []
    result = None
    for begin, end in ((0, 5), (5, len(shards))):
        index = jnp.stack([core, plane, *owners[begin:end]]).astype(jnp.int32)
        result, sent = columns_of(index, mixed, returned, shards[begin:end], result, width)
        arrivals.append((other_owners[begin:end], core_swap(sent, count)))
    for senders, came in arrivals:
        result = place_columns(jnp.stack(senders).astype(jnp.int32), came, result, out_cols)
    return result


def solution(mesh):
    in_specs = (
        P(("dp", "ctx"), None),
        P("dp"),
        P("ctx", None),
        P("ctx", None),
        P("ctx", None),
        P(None, "ctx"),
    )
    out_specs = P(("dp", "ctx"), None)
    return jax.shard_map(
        on_device, mesh=mesh, in_specs=in_specs, out_specs=out_specs, check_vma=False
    )
```

time: 272 us -> 161 us (0.59)
  the two profiles are of different devices: /device:TPU:19 before, /device:TPU:9 now
where the time goes in v1:
time: 161 us; the launch traced here: 159 us
  waiting for transfers between devices  59 us (37%)
  starting transfers between devices  38.2 us (24%)
  Pallas kernels  33.8 us (21%)
  local copies, waits for them, and re-layouts  25.7 us (16%)
  other arithmetic  2.33 us (1%)
    ppermute x15, waiting for transfers between devices, ring(): return lax.ppermute(value, 'ctx', pairs)  40 us
    unnamed x61, local copies, waits for them, and re-layouts  19.5 us
    pallas_call x4, Pallas kernels, project(): pl.pallas_call(functools.partial(project_kernel, slots, groups, total is...  18.4 us
    ppermute x9, starting transfers between devices, core_swap(): return lax.ppermute(value, 'ctx', [(i, i ^ 1) for i in range(count)])  17.8 us
    ppermute x7, waiting for transfers between devices, plane_swap(): return lax.ppermute(value, 'dp', [(0, 1), (1, 0)])  14.1 us
    pallas_call x2, Pallas kernels, columns_of(): pl.pallas_call(functools.partial(columns_kernel, [len(shard) for shard in...  7.7 us
    ppermute x7, starting transfers between devices, plane_swap(): return lax.ppermute(value, 'dp', [(0, 1), (1, 0)])  6.95 us
    ppermute x15, starting transfers between devices, ring(): return lax.ppermute(value, 'ctx', pairs)  6.87 us
  transfers between devices with their start and end apart: 35, of which 16 were waited for; matrix products, arithmetic and copies ran while one was open for 5% of the time, Pallas kernels for 20%

profile of v1, /device:TPU:9, one launch (start us, length us, event | category | flops | bytes accessed | tf_op | source)
XLA Modules:
  0.0 159.5 jit_solution(3242508100247690264)
XLA Ops:
  1.2 1.4 collective-permute-done.1.refs_4_
  5.0 8.3 %collective-permute-done.4.refs_6_ = bf16[2,512,256]{2,1,0:T(8,128)(2,1)S(1)} collective-permute-done((bf16[2,512,256]{2,1,0:T(8,128)(2,1)S(1)}, bf16[2,512,256]{2,1,0:T(8,128)(2,1)S(1)}, u32[]{:S(2)}, u32[]{:S(2)}) %collective-permute-start.4) | collective-permute-done | bytes 524320 | tf_op jit(solution)/shard_map/ppermute | solution.py:396
  14.2 1.4 collective-permute-start.6
  17.7 4.0 %collective-permute-done.5.refs_5_ = bf16[2,512,256]{2,1,0:T(8,128)(2,1)S(1)} collective-permute-done((bf16[2,512,256]{2,1,0:T(8,128)(2,1)S(1)}, bf16[2,512,256]{2,1,0:T(8,128)(2,1)S(1)}, u32[]{:S(2)}, u32[]{:S(2)}) %collective-permute-start.5) | collective-permute-done | bytes 524320 | tf_op jit(solution)/shard_map/ppermute | solution.py:396
  21.7 5.6 %collective-permute-done.6.refs_3_ = bf16[2,512,256]{2,1,0:T(8,128)(2,1)S(1)} collective-permute-done((bf16[2,512,256]{2,1,0:T(8,128)(2,1)S(1)}, bf16[2,512,256]{2,1,0:T(8,128)(2,1)S(1)}, u32[]{:S(2)}, u32[]{:S(2)}) %collective-permute-start.6) | collective-permute-done | bytes 524320 | tf_op jit(solution)/shard_map/ppermute | solution.py:396
  29.0 1.4 collective-permute-start.9
  32.4 3.3 %collective-permute-done.7.refs_2_ = bf16[2,512,256]{2,1,0:T(8,128)(2,1)S(1)} collective-permute-done((bf16[2,512,256]{2,1,0:T(8,128)(2,1)S(1)}, bf16[2,512,256]{2,1,0:T(8,128)(2,1)S(1)}, u32[]{:S(2)}, u32[]{:S(2)}) %collective-permute-start.7) | collective-permute-done | bytes 524320 | tf_op jit(solution)/shard_map/ppermute | solution.py:396
  35.6 5.7 %collective-permute-done.9.refs_3_ = bf16[2,512,256]{2,1,0:T(8,128)(2,1)} collective-permute-done((bf16[2,512,256]{2,1,0:T(8,128)(2,1)S(1)}, bf16[2,512,256]{2,1,0:T(8,128)(2,1)}, u32[]{:S(2)}, u32[]{:S(2)}) %collective-permute-start.9) | collective-permute-done | bytes 524320 | tf_op jit(solution)/shard_map/ppermute | solution.py:396
  41.4 1.7 %slice.15 = bf16[1,512,256]{2,1,0:T(8,128)(2,1)} slice(bf16[2,512,256]{2,1,0:T(8,128)(2,1)} %collective-permute-done.9.refs_3_), slice={[0:1], [0:512], [0:256]} | slice | bytes 524288 | tf_op jit(solution)/shard_map/slice | solution.py:413
  43.8 1.4 collective-permute-start.12
  46.5 3.2 %collective-permute-done.10.refs_2_ = bf16[2,512,256]{2,1,0:T(8,128)(2,1)S(1)} collective-permute-done((bf16[2,512,256]{2,1,0:T(8,128)(2,1)S(1)}, bf16[2,512,256]{2,1,0:T(8,128)(2,1)S(1)}, u32[]{:S(2)}, u32[]{:S(2)}) %collective-permute-start.10) | collective-permute-done | bytes 524320 | tf_op jit(solution)/shard_map/ppermute | solution.py:396
  55.6 4.8 %project.4.refs_5_ = f32[2,256,768]{2,1,0:T(8,128)S(1)} custom-call(s32[4]{0:T(128)S(1)} %pad_add_fusion.2.index_ref, bf16[256,8192]{1,0:T(8,128)(2,1)} %refs_0_.10, bf16[256,8192]{1,0:T(8,128)(2,1)} %collective-permute-done.3.refs_1_, bf16[2,512,256]{2,1,0:T(8,128)(2,1)S(1)} %copy-done.10, bf16[2,512,256]{2,1,0:T(8,128)(2,1)S(1)} %get-tuple-element.32.refs_3_, ...), custom_call_target="tpu_custom_call" | custom-call | tf_op jit(solution)/shard_map/project/pallas_call | solution.py:272
  60.5 1.7 %constant_dynamic-slice_fusion = bf16[256,512]{1,0:T(8,128)(2,1)} fusion(bf16[512,512]{1,0:T(8,128)(2,1)} %refs_0_.11, s32[]{:T(128)S(6)} %select_n.171), kind=kLoop, calls=%fused_computation.20 | loop fusion | bytes 524292 | tf_op jit(solution)/shard_map/dynamic_slice | solution.py:418
  62.2 5.1 %collective-permute-start.18 = (bf16[256,512]{1,0:T(8,128)(2,1)}, bf16[256,512]{1,0:T(8,128)(2,1)}, u32[]{:S(2)}, u32[]{:S(2)}) collective-permute-start(bf16[256,512]{1,0:T(8,128)(2,1)} %constant_dynamic-slice_fusion), channel_id=1, source_target_pairs={{0,2},{2,0},{4,6},{6,4},{8,10},{10,8},{12,14},{14,12},{16,18},{18,... | collective-permute-start | bytes 786440 | tf_op jit(solution)/shard_map/ppermute | solution.py:37
  70.5 4.3 %project.5.refs_5_ = f32[2,256,768]{2,1,0:T(8,128)S(1)} custom-call(s32[3]{0:T(128)S(1)} %pad_add_fusion.4.index_ref, bf16[256,8192]{1,0:T(8,128)(2,1)} %refs_0_.10, bf16[256,8192]{1,0:T(8,128)(2,1)} %collective-permute-done.3.refs_1_, bf16[2,512,256]{2,1,0:T(8,128)(2,1)S(1)} %copy-done.6, bf16[2,512,256]{2,1,0:T(8,128)(2,1)S(1)} %copy-done.4, ...), custom_call_target="tpu_custom_call" | custom-call | tf_op jit(solution)/shard_map/project/pallas_call | solution.py:272
  77.6 4.6 %project.6.refs_5_ = f32[2,256,768]{2,1,0:T(8,128)S(1)} custom-call(s32[3]{0:T(128)S(1)} %pad_add_fusion.3.index_ref, bf16[256,8192]{1,0:T(8,128)(2,1)} %refs_0_.10, bf16[256,8192]{1,0:T(8,128)(2,1)} %collective-permute-done.3.refs_1_, bf16[2,512,256]{2,1,0:T(8,128)(2,1)S(1)} %copy-done.2, bf16[2,512,256]{2,1,0:T(8,128)(2,1)} %collective-permute-done.9.refs_3_, ...), custom_call_target="tpu_custom_call" | custom-call | tf_op jit(solution)/shard_map/project/pallas_call | solution.py:272
  82.2 4.8 %project.7 = (f32[256,768]{1,0:T(8,128)S(1)}, f32[256,768]{1,0:T(8,128)}) custom-call(s32[2]{0:T(128)S(1)} %pad_add_fusion.1.index_ref, bf16[256,8192]{1,0:T(8,128)(2,1)} %refs_0_.10, bf16[256,8192]{1,0:T(8,128)(2,1)} %collective-permute-done.3.refs_1_, bf16[1,512,256]{2,1,0:T(8,128)(2,1)} %collective-permute-done.13.refs_2_, ...), custom_call_target="tpu_custom_call" | custom-call | tf_op jit(solution)/shard_map/project/pallas_call | solution.py:272
  87.0 3.1 %collective-permute-start.16 = (f32[256,768]{1,0:T(8,128)}, f32[256,768]{1,0:T(8,128)S(1)}, u32[]{:S(2)}, u32[]{:S(2)}) collective-permute-start(f32[256,768]{1,0:T(8,128)} %get-tuple-element.44), channel_id=1, source_target_pairs={{0,2},{2,0},{4,6},{6,4},{8,10},{10,8},{12,14},{14,12},{16,18},{18,... | collective-permute-start | bytes 2359304 | tf_op jit(solution)/shard_map/ppermute | solution.py:37
  91.1 4.6 %collective-permute-done.21.refs_5_ = bf16[256,512]{1,0:T(8,128)(2,1)} collective-permute-done((bf16[256,512]{1,0:T(8,128)(2,1)S(1)}, bf16[256,512]{1,0:T(8,128)(2,1)}, u32[]{:S(2)}, u32[]{:S(2)}) %collective-permute-start.21) | collective-permute-done | bytes 262176 | tf_op jit(solution)/shard_map/ppermute | solution.py:396
  96.1 5.2 %collective-permute-done.20.refs_4_ = bf16[512,512]{1,0:T(8,128)(2,1)S(1)} collective-permute-done((bf16[512,512]{1,0:T(8,128)(2,1)S(1)}, bf16[512,512]{1,0:T(8,128)(2,1)S(1)}, u32[]{:S(2)}, u32[]{:S(2)}) %collective-permute-start.20) | collective-permute-done | bytes 524320 | tf_op jit(solution)/shard_map/ppermute | solution.py:396
  106.8 2.1 %collective-permute-start.24 = (bf16[256,256]{1,0:T(8,128)(2,1)S(1)}, bf16[256,256]{1,0:T(8,128)(2,1)S(1)}, u32[]{:S(2)}, u32[]{:S(2)}) collective-permute-start(bf16[256,256]{1,0:T(8,128)(2,1)S(1)} %get-tuple-element.52.refs_4_), channel_id=1, source_target_pairs={{0,8},{4,12},{8,16},{12,20},{16,24},{20,28},{24,30},{28,26},{30,22... | collective-permute-start | bytes 393224 | tf_op jit(solution)/shard_map/ppermute | solution.py:465
  108.9 1.9 %collective-permute-start.25 = (bf16[256,256]{1,0:T(8,128)(2,1)S(1)}, bf16[256,256]{1,0:T(8,128)(2,1)S(1)}, u32[]{:S(2)}, u32[]{:S(2)}) collective-permute-start(bf16[256,256]{1,0:T(8,128)(2,1)S(1)} %get-tuple-element.52.refs_4_), channel_id=1, source_target_pairs={{0,4},{4,8},{8,12},{12,16},{16,20},{20,24},{24,28},{28,30},{30,26}... | collective-permute-start | bytes 393224 | tf_op jit(solution)/shard_map/ppermute | solution.py:465
  112.4 1.5 collective-permute-start.29
  114.5 2.3 %collective-permute-done.24.refs_2_ = bf16[256,256]{1,0:T(8,128)(2,1)S(1)} collective-permute-done((bf16[256,256]{1,0:T(8,128)(2,1)S(1)}, bf16[256,256]{1,0:T(8,128)(2,1)S(1)}, u32[]{:S(2)}, u32[]{:S(2)}) %collective-permute-start.24) | collective-permute-done | bytes 131104 | tf_op jit(solution)/shard_map/ppermute | solution.py:465
  117.7 3.2 %attend.1.mixed_ref = bf16[256,512]{1,0:T(8,128)(2,1)S(1)} custom-call(bf16[256,512]{1,0:T(8,128)(2,1)S(1)} %copy-done.26, s32[1,1280]{1,0:T(1,128)S(1)} %bitcast.29, s32[256,1]{1,0:T(8,128)S(1)} %copy.10.query_seg_ref, bf16[256,256]{1,0:T(8,128)(2,1)S(1)} %collective-permute-done.22.refs_0_, bf16[256,256]{1,0:T(8,128)(2,1)S(1)} %collective-permute-done.23.refs_1_, ...), custom_call_target="tpu_custom_call" | custom-call | tf_op jit(solution)/shard_map/attend/pallas_call | solution.py:170
  120.9 6.2 %collective-permute-start.26 = (bf16[256,512]{1,0:T(8,128)(2,1)S(1)}, bf16[256,512]{1,0:T(8,128)(2,1)S(1)}, u32[]{:S(2)}, u32[]{:S(2)}) collective-permute-start(bf16[256,512]{1,0:T(8,128)(2,1)S(1)} %attend.1.mixed_ref), channel_id=1, source_target_pairs={{0,2},{2,0},{4,6},{6,4},{8,10},{10,8},{12,14},{14,12},{16,18},{18,... | collective-permute-start | bytes 786440 | tf_op jit(solution)/shard_map/ppermute | solution.py:37
  128.4 6.9 %collective-permute-done.32.refs_3_ = bf16[256,512]{1,0:T(8,128)(2,1)S(1)} collective-permute-done((bf16[256,512]{1,0:T(8,128)(2,1)}, bf16[256,512]{1,0:T(8,128)(2,1)S(1)}, u32[]{:S(2)}, u32[]{:S(2)}) %collective-permute-start.32) | collective-permute-done | bytes 262176 | tf_op jit(solution)/shard_map/ppermute | solution.py:41
  137.3 4.6 %columns_of.2 = (bf16[256,8192]{1,0:T(8,128)(2,1)}, bf16[256,2560]{1,0:T(8,128)(2,1)}) custom-call(s32[7]{0:T(128)S(1)} %stack.111.index_ref, bf16[256,512]{1,0:T(8,128)(2,1)S(1)} %attend.1.mixed_ref, bf16[256,512]{1,0:T(8,128)(2,1)S(1)} %collective-permute-done.26.returned_ref, bf16[512,512]{1,0:T(8,128)(2,1)} %refs_0_.11, ...), custom_call_target="tpu_custom_call" | custom-call | tf_op jit(solution)/shard_map/columns_of/pallas_call | solution.py:333
  143.7 7.1 %collective-permute-done.30.refs_2_ = bf16[256,512]{1,0:T(8,128)(2,1)S(1)} collective-permute-done((bf16[256,512]{1,0:T(8,128)(2,1)}, bf16[256,512]{1,0:T(8,128)(2,1)S(1)}, u32[]{:S(2)}, u32[]{:S(2)}) %collective-permute-start.30) | collective-permute-done | bytes 262176 | tf_op jit(solution)/shard_map/ppermute | solution.py:41
  151.8 3.1 %columns_of.3 = (bf16[256,8192]{1,0:T(8,128)(2,1)}, bf16[256,1536]{1,0:T(8,128)(2,1)}) custom-call(s32[5]{0:T(128)S(1)} %stack.101.index_ref, bf16[256,512]{1,0:T(8,128)(2,1)S(1)} %attend.1.mixed_ref, bf16[256,512]{1,0:T(8,128)(2,1)S(1)} %collective-permute-done.26.returned_ref, ...), custom_call_target="tpu_custom_call", output_to_operand_aliasing={{0}: (7, {})} | custom-call | tf_op jit(solution)/shard_map/columns_of/pallas_call | solution.py:333
  156.0 1.6 %place_columns.2._ = bf16[256,8192]{1,0:T(8,128)(2,1)} custom-call(s32[5]{0:T(128)S(1)} %stack.117.owners_ref, bf16[256,2560]{1,0:T(8,128)(2,1)S(1)} %collective-permute-done.34.came_ref, bf16[256,8192]{1,0:T(8,128)(2,1)} %get-tuple-element.58._), custom_call_target="tpu_custom_call", output_to_operand_aliasing={{}: (2, {})} | custom-call | tf_op jit(solution)/shard_map/place_columns/pallas_call | solution.py:364
  158.0 1.4 place_columns.3
  (132 shorter events, 41.5 us)
Async XLA Ops:
  4.7 45.8 %collective-permute-start.3 = (bf16[256,8192]{1,0:T(8,128)(2,1)}, bf16[256,8192]{1,0:T(8,128)(2,1)}, u32[]{:S(2)}, u32[]{:S(2)}) collective-permute-start(bf16[256,8192]{1,0:T(8,128)(2,1)} %refs_0_.10), channel_id=1, source_target_pairs={{0,2},{2,0},{4,6},{6,4},{8,10},{10,8},{12,14},{14,12},{16,18},{18,... | collective-permute-start | bytes 12582920 | tf_op jit(solution)/shard_map/ppermute | solution.py:37
  5.0 8.3 %collective-permute-start.4 = (bf16[2,512,256]{2,1,0:T(8,128)(2,1)S(1)}, bf16[2,512,256]{2,1,0:T(8,128)(2,1)S(1)}, u32[]{:S(2)}, u32[]{:S(2)}) collective-permute-start(bf16[2,512,256]{2,1,0:T(8,128)(2,1)S(1)} %get-tuple-element.32.refs_3_), channel_id=1, source_target_pairs={{0,8},{2,6},{8,16},{10,2},{16,24},{18,10},{24,28},{26,18},{28,20},... | collective-permute-start | bytes 1572872 | tf_op jit(solution)/shard_map/ppermute | solution.py:396
  13.4 8.3 %collective-permute-start.5 = (bf16[2,512,256]{2,1,0:T(8,128)(2,1)S(1)}, bf16[2,512,256]{2,1,0:T(8,128)(2,1)S(1)}, u32[]{:S(2)}, u32[]{:S(2)}) collective-permute-start(bf16[2,512,256]{2,1,0:T(8,128)(2,1)S(1)} %get-tuple-element.35.refs_2_), channel_id=1, source_target_pairs={{0,8},{2,6},{8,16},{10,2},{16,24},{18,10},{24,28},{26,18},{28,20},... | collective-permute-start | bytes 1572872 | tf_op jit(solution)/shard_map/ppermute | solution.py:396
  14.2 13.1 %collective-permute-start.6 = (bf16[2,512,256]{2,1,0:T(8,128)(2,1)S(1)}, bf16[2,512,256]{2,1,0:T(8,128)(2,1)S(1)}, u32[]{:S(2)}, u32[]{:S(2)}) collective-permute-start(bf16[2,512,256]{2,1,0:T(8,128)(2,1)S(1)} %collective-permute-done.4.refs_6_), channel_id=1, source_target_pairs={{0,8},{2,6},{8,16},{10,2},{16,24},{18,10},{24,28},{26,18},{28,20},... | collective-permute-start | bytes 1572872 | tf_op jit(solution)/shard_map/ppermute | solution.py:396
  15.6 12.6 %collective-permute-start.8 = (bf16[2,512,256]{2,1,0:T(8,128)(2,1)S(1)}, bf16[2,512,256]{2,1,0:T(8,128)(2,1)S(1)}, u32[]{:S(2)}, u32[]{:S(2)}) collective-permute-start(bf16[2,512,256]{2,1,0:T(8,128)(2,1)S(1)} %collective-permute-done.4.refs_6_), channel_id=1, source_target_pairs={{0,1},{1,0},{2,3},{3,2},{4,5},{5,4},{6,7},{7,6},{8,9},{9,8},{10,11... | collective-permute-start | bytes 1572872 | tf_op jit(solution)/shard_map/ppermute | solution.py:41
  27.3 8.3 %collective-permute-start.7 = (bf16[2,512,256]{2,1,0:T(8,128)(2,1)S(1)}, bf16[2,512,256]{2,1,0:T(8,128)(2,1)S(1)}, u32[]{:S(2)}, u32[]{:S(2)}) collective-permute-start(bf16[2,512,256]{2,1,0:T(8,128)(2,1)S(1)} %collective-permute-done.5.refs_5_), channel_id=1, source_target_pairs={{0,8},{2,6},{8,16},{10,2},{16,24},{18,10},{24,28},{26,18},{28,20},... | collective-permute-start | bytes 1572872 | tf_op jit(solution)/shard_map/ppermute | solution.py:396
  29.0 12.4 %collective-permute-start.9 = (bf16[2,512,256]{2,1,0:T(8,128)(2,1)S(1)}, bf16[2,512,256]{2,1,0:T(8,128)(2,1)}, u32[]{:S(2)}, u32[]{:S(2)}) collective-permute-start(bf16[2,512,256]{2,1,0:T(8,128)(2,1)S(1)} %collective-permute-done.6.refs_3_), channel_id=1, source_target_pairs={{0,8},{2,6},{8,16},{10,2},{16,24},{18,10},{24,28},{26,18},{28,20},... | collective-permute-start | bytes 1572872 | tf_op jit(solution)/shard_map/ppermute | solution.py:396
  30.3 12.7 %collective-permute-start.11 = (bf16[2,512,256]{2,1,0:T(8,128)(2,1)S(1)}, bf16[2,512,256]{2,1,0:T(8,128)(2,1)S(1)}, u32[]{:S(2)}, u32[]{:S(2)}) collective-permute-start(bf16[2,512,256]{2,1,0:T(8,128)(2,1)S(1)} %collective-permute-done.6.refs_3_), channel_id=1, source_target_pairs={{0,1},{1,0},{2,3},{3,2},{4,5},{5,4},{6,7},{7,6},{8,9},{9,8},{10,11... | collective-permute-start | bytes 1572872 | tf_op jit(solution)/shard_map/ppermute | solution.py:41
  41.4 8.3 %collective-permute-start.10 = (bf16[2,512,256]{2,1,0:T(8,128)(2,1)S(1)}, bf16[2,512,256]{2,1,0:T(8,128)(2,1)S(1)}, u32[]{:S(2)}, u32[]{:S(2)}) collective-permute-start(bf16[2,512,256]{2,1,0:T(8,128)(2,1)S(1)} %collective-permute-done.7.refs_2_), channel_id=1, source_target_pairs={{0,8},{2,6},{8,16},{10,2},{16,24},{18,10},{24,28},{26,18},{28,20},... | collective-permute-start | bytes 1572872 | tf_op jit(solution)/shard_map/ppermute | solution.py:396
  43.8 16.6 %collective-permute-start.12 = (bf16[1,512,256]{2,1,0:T(8,128)(2,1)}, bf16[1,512,256]{2,1,0:T(8,128)(2,1)S(1)}, u32[]{:S(2)}, u32[]{:S(2)}) collective-permute-start(bf16[1,512,256]{2,1,0:T(8,128)(2,1)} %slice.15), channel_id=1, source_target_pairs={{0,8},{2,6},{8,16},{10,2},{16,24},{18,10},{24,28},{26,18},{28,20},... | collective-permute-start | bytes 786440 | tf_op jit(solution)/shard_map/ppermute | solution.py:396
  45.2 31.1 %collective-permute-start.15 = (bf16[2,512,256]{2,1,0:T(8,128)(2,1)}, bf16[2,512,256]{2,1,0:T(8,128)(2,1)}, u32[]{:S(2)}, u32[]{:S(2)}) collective-permute-start(bf16[2,512,256]{2,1,0:T(8,128)(2,1)} %collective-permute-done.9.refs_3_), channel_id=1, source_target_pairs={{0,1},{1,0},{2,3},{3,2},{4,5},{5,4},{6,7},{7,6},{8,9},{9,8},{10,11... | collective-permute-start | bytes 1572872 | tf_op jit(solution)/shard_map/ppermute | solution.py:41
  60.4 14.3 %collective-permute-start.13 = (bf16[1,512,256]{2,1,0:T(8,128)(2,1)}, bf16[1,512,256]{2,1,0:T(8,128)(2,1)}, u32[]{:S(2)}, u32[]{:S(2)}) collective-permute-start(bf16[1,512,256]{2,1,0:T(8,128)(2,1)} %slice.14), channel_id=1, source_target_pairs={{0,8},{2,6},{8,16},{10,2},{16,24},{18,10},{24,28},{26,18},{28,20},... | collective-permute-start | bytes 786440 | tf_op jit(solution)/shard_map/ppermute | solution.py:396
  62.2 14.1 %collective-permute-start.18 = (bf16[256,512]{1,0:T(8,128)(2,1)}, bf16[256,512]{1,0:T(8,128)(2,1)}, u32[]{:S(2)}, u32[]{:S(2)}) collective-permute-start(bf16[256,512]{1,0:T(8,128)(2,1)} %constant_dynamic-slice_fusion), channel_id=1, source_target_pairs={{0,2},{2,0},{4,6},{6,4},{8,10},{10,8},{12,14},{14,12},{16,18},{18,... | collective-permute-start | bytes 786440 | tf_op jit(solution)/shard_map/ppermute | solution.py:37
  74.8 15.6 %collective-permute-start.17 = (bf16[512,512]{1,0:T(8,128)(2,1)}, bf16[512,512]{1,0:T(8,128)(2,1)S(1)}, u32[]{:S(2)}, u32[]{:S(2)}) collective-permute-start(bf16[512,512]{1,0:T(8,128)(2,1)} %refs_0_.11), channel_id=1, source_target_pairs={{0,8},{2,6},{8,16},{10,2},{16,24},{18,10},{24,28},{26,18},{28,20},... | collective-permute-start | bytes 1572872 | tf_op jit(solution)/shard_map/ppermute | solution.py:396
  75.0 7.2 %collective-permute-start.14 = (bf16[1,512,256]{2,1,0:T(8,128)(2,1)}, bf16[1,512,256]{2,1,0:T(8,128)(2,1)S(1)}, u32[]{:S(2)}, u32[]{:S(2)}) collective-permute-start(bf16[1,512,256]{2,1,0:T(8,128)(2,1)} %copy-done.19), channel_id=1, source_target_pairs={{0,1},{1,0},{2,3},{3,2},{4,5},{5,4},{6,7},{7,6},{8,9},{9,8},{10,11... | collective-permute-start | bytes 786440 | tf_op jit(solution)/shard_map/ppermute | solution.py:41
  76.3 13.8 %collective-permute-start.19 = (bf16[256,512]{1,0:T(8,128)(2,1)}, bf16[256,512]{1,0:T(8,128)(2,1)S(1)}, u32[]{:S(2)}, u32[]{:S(2)}) collective-permute-start(bf16[256,512]{1,0:T(8,128)(2,1)} %collective-permute-done.18), channel_id=1, source_target_pairs={{0,8},{2,6},{8,16},{10,2},{16,24},{18,10},{24,28},{26,18},{28,20},... | collective-permute-start | bytes 786440 | tf_op jit(solution)/shard_map/ppermute | solution.py:396
  87.0 16.3 %collective-permute-start.16 = (f32[256,768]{1,0:T(8,128)}, f32[256,768]{1,0:T(8,128)S(1)}, u32[]{:S(2)}, u32[]{:S(2)}) collective-permute-start(f32[256,768]{1,0:T(8,128)} %get-tuple-element.44), channel_id=1, source_target_pairs={{0,2},{2,0},{4,6},{6,4},{8,10},{10,8},{12,14},{14,12},{16,18},{18,... | collective-permute-start | bytes 2359304 | tf_op jit(solution)/shard_map/ppermute | solution.py:37
  90.1 5.7 %collective-permute-start.21 = (bf16[256,512]{1,0:T(8,128)(2,1)S(1)}, bf16[256,512]{1,0:T(8,128)(2,1)}, u32[]{:S(2)}, u32[]{:S(2)}) collective-permute-start(bf16[256,512]{1,0:T(8,128)(2,1)S(1)} %collective-permute-done.19.refs_2_), channel_id=1, source_target_pairs={{0,8},{2,6},{8,16},{10,2},{16,24},{18,10},{24,28},{26,18},{28,20},... | collective-permute-start | bytes 786440 | tf_op jit(solution)/shard_map/ppermute | solution.py:396
  90.4 11.0 %collective-permute-start.20 = (bf16[512,512]{1,0:T(8,128)(2,1)S(1)}, bf16[512,512]{1,0:T(8,128)(2,1)S(1)}, u32[]{:S(2)}, u32[]{:S(2)}) collective-permute-start(bf16[512,512]{1,0:T(8,128)(2,1)S(1)} %collective-permute-done.17.refs_1_), channel_id=1, source_target_pairs={{0,8},{2,6},{8,16},{10,2},{16,24},{18,10},{24,28},{26,18},{28,20},... | collective-permute-start | bytes 1572872 | tf_op jit(solution)/shard_map/ppermute | solution.py:396
  95.8 13.2 %collective-permute-start.28 = (bf16[256,512]{1,0:T(8,128)(2,1)}, bf16[256,512]{1,0:T(8,128)(2,1)}, u32[]{:S(2)}, u32[]{:S(2)}) collective-permute-start(bf16[256,512]{1,0:T(8,128)(2,1)} %collective-permute-done.21.refs_5_), channel_id=1, source_target_pairs={{0,1},{1,0},{2,3},{3,2},{4,5},{5,4},{6,7},{7,6},{8,9},{9,8},{10,11... | collective-permute-start | bytes 786440 | tf_op jit(solution)/shard_map/ppermute | solution.py:41
  101.4 27.0 %collective-permute-start.27 = (bf16[512,512]{1,0:T(8,128)(2,1)S(1)}, bf16[512,512]{1,0:T(8,128)(2,1)S(1)}, u32[]{:S(2)}, u32[]{:S(2)}) collective-permute-start(bf16[512,512]{1,0:T(8,128)(2,1)S(1)} %collective-permute-done.20.refs_4_), channel_id=1, source_target_pairs={{0,8},{2,6},{8,16},{10,2},{16,24},{18,10},{24,28},{26,18},{28,20},... | collective-permute-start | bytes 1572872 | tf_op jit(solution)/shard_map/ppermute | solution.py:396
  104.2 8.2 %collective-permute-start.22 = (bf16[256,256]{1,0:T(8,128)(2,1)S(1)}, bf16[256,256]{1,0:T(8,128)(2,1)S(1)}, u32[]{:S(2)}, u32[]{:S(2)}) collective-permute-start(bf16[256,256]{1,0:T(8,128)(2,1)S(1)} %get-tuple-element.52.refs_4_), channel_id=1, source_target_pairs={{0,16},{4,20},{8,24},{12,28},{16,30},{20,26},{24,22},{28,18},{30,1... | collective-permute-start | bytes 393224 | tf_op jit(solution)/shard_map/ppermute | solution.py:465
  105.5 8.9 %collective-permute-start.23 = (bf16[256,256]{1,0:T(8,128)(2,1)S(1)}, bf16[256,256]{1,0:T(8,128)(2,1)S(1)}, u32[]{:S(2)}, u32[]{:S(2)}) collective-permute-start(bf16[256,256]{1,0:T(8,128)(2,1)S(1)} %get-tuple-element.52.refs_4_), channel_id=1, source_target_pairs={{0,12},{4,16},{8,20},{12,24},{16,28},{20,30},{24,26},{28,22},{30,1... | collective-permute-start | bytes 393224 | tf_op jit(solution)/shard_map/ppermute | solution.py:465
  106.8 10.0 %collective-permute-start.24 = (bf16[256,256]{1,0:T(8,128)(2,1)S(1)}, bf16[256,256]{1,0:T(8,128)(2,1)S(1)}, u32[]{:S(2)}, u32[]{:S(2)}) collective-permute-start(bf16[256,256]{1,0:T(8,128)(2,1)S(1)} %get-tuple-element.52.refs_4_), channel_id=1, source_target_pairs={{0,8},{4,12},{8,16},{12,20},{16,24},{20,28},{24,30},{28,26},{30,22... | collective-permute-start | bytes 393224 | tf_op jit(solution)/shard_map/ppermute | solution.py:465
  108.9 7.8 %collective-permute-start.25 = (bf16[256,256]{1,0:T(8,128)(2,1)S(1)}, bf16[256,256]{1,0:T(8,128)(2,1)S(1)}, u32[]{:S(2)}, u32[]{:S(2)}) collective-permute-start(bf16[256,256]{1,0:T(8,128)(2,1)S(1)} %get-tuple-element.52.refs_4_), channel_id=1, source_target_pairs={{0,4},{4,8},{8,12},{12,16},{16,20},{20,24},{24,28},{28,30},{30,26}... | collective-permute-start | bytes 393224 | tf_op jit(solution)/shard_map/ppermute | solution.py:465
  112.4 15.7 %collective-permute-start.29 = (bf16[256,512]{1,0:T(8,128)(2,1)}, bf16[256,512]{1,0:T(8,128)(2,1)S(1)}, u32[]{:S(2)}, u32[]{:S(2)}) collective-permute-start(bf16[256,512]{1,0:T(8,128)(2,1)} %collective-permute-done.21.refs_5_), channel_id=1, source_target_pairs={{0,8},{2,6},{8,16},{10,2},{16,24},{18,10},{24,28},{26,18},{28,20},... | collective-permute-start | bytes 786440 | tf_op jit(solution)/shard_map/ppermute | solution.py:396
  120.9 7.4 %collective-permute-start.26 = (bf16[256,512]{1,0:T(8,128)(2,1)S(1)}, bf16[256,512]{1,0:T(8,128)(2,1)S(1)}, u32[]{:S(2)}, u32[]{:S(2)}) collective-permute-start(bf16[256,512]{1,0:T(8,128)(2,1)S(1)} %attend.1.mixed_ref), channel_id=1, source_target_pairs={{0,2},{2,0},{4,6},{6,4},{8,10},{10,8},{12,14},{14,12},{16,18},{18,... | collective-permute-start | bytes 786440 | tf_op jit(solution)/shard_map/ppermute | solution.py:37
  127.2 8.1 %collective-permute-start.32 = (bf16[256,512]{1,0:T(8,128)(2,1)}, bf16[256,512]{1,0:T(8,128)(2,1)S(1)}, u32[]{:S(2)}, u32[]{:S(2)}) collective-permute-start(bf16[256,512]{1,0:T(8,128)(2,1)} %copy-done.27), channel_id=1, source_target_pairs={{0,1},{1,0},{2,3},{3,2},{4,5},{5,4},{6,7},{7,6},{8,9},{9,8},{10,11... | collective-permute-start | bytes 786440 | tf_op jit(solution)/shard_map/ppermute | solution.py:41
  128.4 22.5 %collective-permute-start.31 = (bf16[512,512]{1,0:T(8,128)(2,1)S(1)}, bf16[512,512]{1,0:T(8,128)(2,1)S(1)}, u32[]{:S(2)}, u32[]{:S(2)}) collective-permute-start(bf16[512,512]{1,0:T(8,128)(2,1)S(1)} %collective-permute-done.27.refs_0_), channel_id=1, source_target_pairs={{0,8},{2,6},{8,16},{10,2},{16,24},{18,10},{24,28},{26,18},{28,20},... | collective-permute-start | bytes 1572872 | tf_op jit(solution)/shard_map/ppermute | solution.py:396
  141.9 14.2 %collective-permute-start.34 = (bf16[256,2560]{1,0:T(8,128)(2,1)}, bf16[256,2560]{1,0:T(8,128)(2,1)S(1)}, u32[]{:S(2)}, u32[]{:S(2)}) collective-permute-start(bf16[256,2560]{1,0:T(8,128)(2,1)} %get-tuple-element.57), channel_id=1, source_target_pairs={{0,2},{2,0},{4,6},{6,4},{8,10},{10,8},{12,14},{14,12},{16,18},{18,... | collective-permute-start | bytes 3932168 | tf_op jit(solution)/shard_map/ppermute | solution.py:37
  142.8 8.1 %collective-permute-start.30 = (bf16[256,512]{1,0:T(8,128)(2,1)}, bf16[256,512]{1,0:T(8,128)(2,1)S(1)}, u32[]{:S(2)}, u32[]{:S(2)}) collective-permute-start(bf16[256,512]{1,0:T(8,128)(2,1)} %copy-done.23), channel_id=1, source_target_pairs={{0,1},{1,0},{2,3},{3,2},{4,5},{5,4},{6,7},{7,6},{8,9},{9,8},{10,11... | collective-permute-start | bytes 786440 | tf_op jit(solution)/shard_map/ppermute | solution.py:41
  155.0 3.0 %collective-permute-start.33 = (bf16[256,1536]{1,0:T(8,128)(2,1)}, bf16[256,1536]{1,0:T(8,128)(2,1)S(1)}, u32[]{:S(2)}, u32[]{:S(2)}) collective-permute-start(bf16[256,1536]{1,0:T(8,128)(2,1)} %get-tuple-element.56), channel_id=1, source_target_pairs={{0,2},{2,0},{4,6},{6,4},{8,10},{10,8},{12,14},{14,12},{16,18},{18,... | collective-permute-start | bytes 2359304 | tf_op jit(solution)/shard_map/ppermute | solution.py:37
  (33 other events, 230.0 us)

commit v2 on v1

v2 whole, which is shorter than its diff:
```python
import functools
import math

import jax
import jax.numpy as jnp
from jax import lax
from jax.experimental import pallas as pl
from jax.experimental.pallas import tpu as pltpu
from jax.sharding import PartitionSpec as P

REACH = 8
ROPE_BASE = 500000.0
RING_LIMIT = 16
VMEM_LIMIT = 16 * 1024 * 1024


def chip_at(place, chips):
    place = place % chips
    return jnp.where(place < chips // 2, 2 * place, 2 * (chips - 1 - place) + 1)


def static_chip_at(place, chips):
    place %= chips
    return 2 * place if place < chips // 2 else 2 * (chips - 1 - place) + 1


def ring_pairs(chips):
    pairs = []
    for place in range(chips):
        here = static_chip_at(place, chips)
        pairs.append((2 * here, 2 * static_chip_at(place + 1, chips)))
        pairs.append((2 * here + 1, 2 * static_chip_at(place - 1, chips) + 1))
    return pairs


def core_swap(value, count):
    return lax.ppermute(value, "ctx", [(i, i ^ 1) for i in range(count)])


def plane_swap(value):
    return lax.ppermute(value, "dp", [(0, 1), (1, 0)])


def row_device(row, column, count):
    pair = 2 * row + (column if row < count // 4 else 1 - column)
    return 2 * pair if pair < count // 2 else 2 * (count - 1 - pair) + 1


def after(value, *others):
    return lax.optimization_barrier((value, *others))[0]


def shard_owners(me, count):
    chips = count // 2
    half = chips // 2
    core, chip = me % 2, me // 2
    place = jnp.where(chip % 2 == 0, chip // 2, chips - 1 - chip // 2)
    way = jnp.where(core == 0, -1, 1)
    owners = [me]
    for step in range(1, half + 1):
        source = chip_at(place + way * step + chips, chips)
        owners.append(2 * source + core)
        if step < half:
            owners.append(2 * source + 1 - core)
    return owners


def params(**settings):
    return pltpu.CompilerParams(vmem_limit_bytes=VMEM_LIMIT, **settings)


def in_vmem(*arrays):
    return [pltpu.with_memory_space_constraint(array, pltpu.VMEM) for array in arrays]


def in_hbm(*arrays):
    return [pltpu.with_memory_space_constraint(array, pltpu.HBM) for array in arrays]


IN_VMEM = pl.BlockSpec(memory_space=pltpu.VMEM)
IN_HBM = pl.BlockSpec(memory_space=pl.ANY)
IN_SMEM = pl.BlockSpec(memory_space=pltpu.SMEM)


def rotate_kernel(head_dim, kept_ref, came_ref, cos_ref, sin_ref, joined_ref, query_ref):
    cosine, sine = cos_ref[...], sin_ref[...]

    def rotated(column):
        span = pl.ds(column, head_dim)
        part = kept_ref[:, span] + came_ref[:, span]
        return (part * cosine + pltpu.roll(part, head_dim // 2, 1) * sine).astype(jnp.bfloat16)

    joined_ref[:, :head_dim] = rotated(0)
    values = pl.ds(head_dim, head_dim)
    joined_ref[:, values] = (kept_ref[:, values] + came_ref[:, values]).astype(jnp.bfloat16)
    for column in range(0, query_ref.shape[1], head_dim):
        query_ref[:, pl.ds(column, head_dim)] = rotated(2 * head_dim + column)


def rotary_tables(positions, head_dim):
    frequency = ROPE_BASE ** (
        -(jnp.arange(head_dim // 2, dtype=jnp.float32) * 2.0) / head_dim
    )
    angles = positions.astype(jnp.float32)[:, None] * frequency[None, :]
    cosine, sine = jnp.cos(angles), jnp.sin(angles)
    return jnp.concatenate([cosine, cosine], axis=1), jnp.concatenate([-sine, sine], axis=1)


def rotate_sums(kept, came, cosine, sine):
    rows, columns = kept.shape
    head_dim = cosine.shape[1]
    return pl.pallas_call(
        functools.partial(rotate_kernel, head_dim),
        out_shape=(
            pltpu.VMEM((rows, 2 * head_dim), jnp.bfloat16),
            pltpu.VMEM((rows, columns - 2 * head_dim), jnp.bfloat16),
        ),
        in_specs=[IN_VMEM] * 4,
        out_specs=(IN_VMEM, IN_VMEM),
        compiler_params=params(),
        name="rotate_sums",
    )(*in_vmem(kept, came, cosine, sine))


def join_row_kernel(index_ref, own_ref, beside_ref, out_ref):
    odd = index_ref[2]
    out_ref[odd] = own_ref[...]
    out_ref[1 - odd] = beside_ref[...]


def join_row(index, own, beside):
    return pl.pallas_call(
        join_row_kernel,
        in_specs=[IN_SMEM, IN_VMEM, IN_VMEM],
        out_specs=IN_VMEM,
        out_shape=pltpu.VMEM((2, *own.shape), own.dtype),
        compiler_params=params(),
        name="join_row",
    )(index, *in_vmem(own, beside))


def attend_kernel(head_dim, reach, index_ref, query_ref, key_seg_ref, *refs):
    row_refs, (mixed_ref, window) = refs[:-2], refs[-2:]
    rows = query_ref.shape[0]
    for place, row_ref in enumerate(row_refs):
        window[2 * place : 2 * place + 2] = row_ref[...]
    odd = index_ref[2]
    own_seg = key_seg_ref[:, pl.ds(reach * rows, rows)]
    query_seg = jnp.transpose(jnp.broadcast_to(own_seg, (rows, rows)))
    base = lax.broadcasted_iota(jnp.int32, (rows, rows), 0)
    offset = lax.broadcasted_iota(jnp.int32, (rows, rows), 1)
    allowed = []
    for piece in range(reach + 1):
        same = query_seg == key_seg_ref[:, pl.ds(piece * rows, rows)]
        if piece == reach:
            same = same & (offset <= base)
        allowed.append(same)
    for column in range(0, query_ref.shape[1], head_dim):
        span = pl.ds(column, head_dim)
        query = query_ref[:, span]
        scores = []
        for piece in range(reach + 1):
            score = lax.dot_general(
                query,
                window[odd + piece, :, :head_dim],
                (((1,), (1,)), ((), ())),
                preferred_element_type=jnp.float32,
            ) / math.sqrt(head_dim)
            scores.append(jnp.where(allowed[piece], score, -1e30))
        peak = scores[0]
        for score in scores[1:]:
            peak = jnp.maximum(peak, score)
        peak = jnp.max(peak, axis=1, keepdims=True)
        terms = [jnp.exp(score - peak) for score in scores]
        total = terms[0]
        for term in terms[1:]:
            total = total + term
        inverse = 1.0 / jnp.sum(total, axis=1, keepdims=True)
        mixed = jnp.zeros((rows, head_dim), jnp.float32)
        for piece in range(reach + 1):
            mixed += jnp.dot(
                (terms[piece] * inverse).astype(jnp.bfloat16),
                window[odd + piece, :, head_dim:],
                preferred_element_type=jnp.float32,
            )
        mixed_ref[:, span] = mixed.astype(jnp.bfloat16)


def attend(index, queries, row_windows, key_seg, head_dim):
    reach = 2 * len(row_windows) - 2
    rows = queries.shape[0]
    return pl.pallas_call(
        functools.partial(attend_kernel, head_dim, reach),
        out_shape=pltpu.VMEM(queries.shape, jnp.bfloat16),
        in_specs=[IN_SMEM] + [IN_VMEM] * (2 + len(row_windows)),
        out_specs=IN_VMEM,
        scratch_shapes=[pltpu.VMEM((reach + 2, rows, 2 * head_dim), jnp.bfloat16)],
        compiler_params=params(),
        name="attend",
    )(index, *in_vmem(queries, key_seg, *row_windows))


def join_projections_kernel(plane_ref, *refs):
    own, beside, refs = refs[:3], refs[3:6], refs[6:]
    near_out, common_out, far_out, sems = refs
    q_half, kv_half = near_out.shape[2], common_out.shape[2] // 2
    near = pl.ds(pl.multiple_of(plane_ref[0] * q_half, q_half), q_half)
    far = pl.ds(pl.multiple_of((1 - plane_ref[0]) * q_half, q_half), q_half)
    moves = [(own[0].at[:, far], far_out.at[0])]
    for slot, (query_ref, key_ref, value_ref) in enumerate((own, beside)):
        moves += [
            (query_ref.at[:, near], near_out.at[slot]),
            (key_ref, common_out.at[slot, :, :kv_half]),
            (value_ref, common_out.at[slot, :, kv_half:]),
        ]
    copies = [
        pltpu.make_async_copy(source, target, sems.at[place])
        for place, (source, target) in enumerate(moves)
    ]
    for copy in copies:
        copy.start()
    for copy in copies:
        copy.wait()


def join_projections(plane, own, beside):
    query, key, _ = own
    depth, q_half = query.shape[0], query.shape[1] // 2
    shapes = (
        (2, depth, q_half),
        (2, depth, 2 * key.shape[1]),
        (1, depth, q_half),
    )
    return pl.pallas_call(
        join_projections_kernel,
        in_specs=[IN_SMEM] + [IN_HBM] * 3 + [IN_VMEM] * 3,
        out_specs=[IN_VMEM] * 3,
        scratch_shapes=[pltpu.SemaphoreType.DMA((7,))],
        out_shape=[pltpu.VMEM(shape, jnp.bfloat16) for shape in shapes],
        compiler_params=params(),
        name="join_projections",
    )(plane, *in_hbm(*own), *in_vmem(*beside))


def first_kernel(pair_ref, out_ref):
    out_ref[...] = pair_ref[:1]


def first_of(pair):
    return pl.pallas_call(
        first_kernel,
        in_specs=[IN_VMEM],
        out_specs=IN_VMEM,
        out_shape=pltpu.VMEM((1, *pair.shape[1:]), pair.dtype),
        compiler_params=params(),
        name="first_of",
    )(*in_vmem(pair))


def project_kernel(slots, base, groups, first, last, index_ref, own_ref, other_ref, *refs):
    refs, (tokens, sems) = refs[:-2], refs[-2:]
    rows, depth = tokens.shape[1:]
    spans = [
        pl.ds(pl.multiple_of(index_ref[3 + base + place] * depth, depth), depth)
        for place in range(len(slots))
    ]
    copies = [
        pltpu.make_async_copy(own_ref.at[:, span], tokens.at[place], sems.at[place])
        for place, span in enumerate(spans)
    ]
    for copy in copies:
        copy.start()
    held_weights = groups * (1 + slots[-1][0])
    weights, refs = refs[:held_weights], refs[held_weights:]
    total_ref, refs = (None, refs) if first else (refs[0], refs[1:])
    block = rows // 2
    width = weights[0].shape[-1]
    out_ref = refs[2] if last else refs[0]
    for side in (1, 0):
        if side == 0:
            for copy in copies:
                copy.wait()
        for group in range(groups):
            columns = pl.ds(group * width, width)
            total = None if first else total_ref[side, :, columns]
            for place, (step, slot) in enumerate(slots):
                product = jnp.dot(
                    tokens[place] if side == 0 else other_ref[:, spans[place]],
                    weights[groups * step + group][slot],
                    preferred_element_type=jnp.float32,
                )
                total = product if total is None else total + product
            out_ref[side, :, columns] = total
    if last:
        kept_ref, sent_ref, held = refs
        mine = pl.ds(pl.multiple_of(index_ref[0] * block, block), block)
        others = pl.ds(pl.multiple_of((1 - index_ref[0]) * block, block), block)
        kept_ref[:block] = held[0, mine, :]
        kept_ref[block:] = held[1, mine, :]
        sent_ref[:block] = held[1, others, :]
        sent_ref[block:] = held[0, others, :]


def project(index, base, tokens, steps, total, last):
    groups = len(steps[0][1])
    slots = [(i, slot) for i, (used, _) in enumerate(steps) for slot in range(used)]
    rows = tokens[0].shape[0]
    depth = steps[0][1][0].shape[1]
    columns = sum(part.shape[2] for part in steps[0][1])
    operands = in_hbm(tokens[0]) + in_vmem(tokens[1], *(part for _, parts in steps for part in parts))
    if total is not None:
        operands += in_vmem(total)
    shapes = ((rows, columns), (rows, columns)) if last else ((2, rows, columns),)
    out = pl.pallas_call(
        functools.partial(project_kernel, slots, base, groups, total is None, last),
        in_specs=[IN_SMEM, IN_HBM] + [IN_VMEM] * (len(operands) - 1),
        out_specs=[IN_VMEM] * len(shapes),
        scratch_shapes=([pltpu.VMEM((2, rows, columns), jnp.float32)] if last else [])
        + [
            pltpu.VMEM((len(slots), rows, depth), jnp.bfloat16),
            pltpu.SemaphoreType.DMA((len(slots),)),
        ],
        out_shape=[pltpu.VMEM(shape, jnp.float32) for shape in shapes],
        compiler_params=params(),
        name="project",
    )(index, *operands)
    return out if last else out[0]


def columns_kernel(shards, base, index_ref, mixed_ref, returned_ref, *refs):
    weights = refs[:shards]
    out_ref, send_ref, held, sems = refs[-4:]
    block = mixed_ref.shape[0] // 2
    half = mixed_ref.shape[1] // 2
    width = weights[0].shape[-1]
    mine = pl.ds(pl.multiple_of(index_ref[0] * block, block), block)
    others = pl.ds(pl.multiple_of((1 - index_ref[0]) * block, block), block)
    rows_in = jnp.concatenate([mixed_ref[...], returned_ref[...]], axis=0)
    near, far = rows_in[:, :half], rows_in[:, half:]
    low = index_ref[1] == 0
    rows_in = jnp.concatenate([jnp.where(low, near, far), jnp.where(low, far, near)], axis=1)
    copies = []
    for place in range(shards):
        value = jnp.dot(rows_in, weights[place][...], preferred_element_type=jnp.float32)
        value = value.astype(jnp.bfloat16)
        columns = pl.ds(place * width, width)
        held[mine, columns] = value[:block]
        held[others, columns] = value[3 * block :]
        send_ref[mine, columns] = value[block : 2 * block]
        send_ref[others, columns] = value[2 * block : 3 * block]
        column = pl.multiple_of(index_ref[3 + base + place] * width, width)
        copy = pltpu.make_async_copy(
            held.at[:, columns], out_ref.at[:, pl.ds(column, width)], sems.at[place]
        )
        copy.start()
        copies.append(copy)
    for copy in copies:
        copy.wait()


def columns_of(index, base, mixed, returned, shards, result, width):
    rows = mixed.shape[0]
    out_cols = shards[0].shape[1]
    operands = in_vmem(mixed, returned, *shards)
    specs = [IN_SMEM] + [IN_VMEM] * len(operands)
    if result is not None:
        operands += in_hbm(result)
        specs.append(IN_HBM)
    sent = (rows, len(shards) * out_cols)
    return pl.pallas_call(
        functools.partial(columns_kernel, len(shards), base),
        in_specs=specs,
        out_specs=[IN_HBM, IN_VMEM],
        scratch_shapes=[
            pltpu.VMEM(sent, jnp.bfloat16),
            pltpu.SemaphoreType.DMA((len(shards),)),
        ],
        out_shape=[pltpu.HBM((rows, width), jnp.bfloat16), pltpu.VMEM(sent, jnp.bfloat16)],
        input_output_aliases={} if result is None else {len(operands): 0},
        compiler_params=params(),
        name="columns_of",
    )(index, *operands)


def place_kernel(width, base, index_ref, came_ref, _, out_ref, sems):
    copies = []
    for place in range(came_ref.shape[1] // width):
        column = pl.multiple_of(index_ref[base + place] * width, width)
        copy = pltpu.make_async_copy(
            came_ref.at[:, pl.ds(place * width, width)],
            out_ref.at[:, pl.ds(column, width)],
            sems.at[place],
        )
        copy.start()
        copies.append(copy)
    for copy in copies:
        copy.wait()


def place_columns(index, base, came, result, out_cols):
    return pl.pallas_call(
        functools.partial(place_kernel, out_cols, base),
        in_specs=[IN_SMEM, IN_VMEM, IN_HBM],
        out_specs=IN_HBM,
        scratch_shapes=[pltpu.SemaphoreType.DMA((came.shape[1] // out_cols,))],
        out_shape=pltpu.HBM(result.shape, result.dtype),
        input_output_aliases={2: 0},
        compiler_params=params(),
        name="place_columns",
    )(index, *in_vmem(came), *in_hbm(result))


def on_device(hidden_in, segment_ids, w_query, w_key, w_value, w_out):
    count = lax.axis_size("ctx")
    me = lax.axis_index("ctx")
    plane = lax.axis_index("dp")
    core, chip = me % 2, me // 2
    rows, width = hidden_in.shape
    block = rows // 2
    head_dim = w_key.shape[1]
    q_rows, out_cols = w_out.shape
    q_half = q_rows // 2

    reach = REACH * block // rows
    pair = jnp.where(core == 0, chip, count - 1 - chip)
    pair_pos = pair * rows + jnp.arange(rows, dtype=jnp.int32)
    cosine, sine = rotary_tables(pair_pos, head_dim)
    seg_blocks = segment_ids.reshape(2 * count, block)
    seq_block = pair * 2 - 2 * reach + jnp.arange(2 * reach + 2, dtype=jnp.int32)
    clipped = jnp.maximum(seq_block, 0)
    stored = jnp.where(clipped < count, 2 * clipped, 2 * (2 * count - 1 - clipped) + 1)
    seg_rows = seg_blocks[stored]
    key_seg = jnp.where(seq_block[:, None] >= 0, seg_rows, -1).reshape(1, -1)
    tables = (cosine, sine, key_seg)
    index = [core, plane, pair % 2]

    ringed = count <= RING_LIMIT
    if ringed:
        plane_index = plane.reshape(1).astype(jnp.int32)
        pairs = ring_pairs(count // 2)
        half = count // 4
        owners = shard_owners(me, count)
        index += [*owners, *shard_owners(me ^ 1, count)]
        index = jnp.stack(index).astype(jnp.int32)

        def ring(value):
            return lax.ppermute(value, "ctx", pairs)

        own = (w_query, w_key, w_value)
        beside = tuple(core_swap(part, count) for part in own)
        near, common, own_far = join_projections(plane_index, own, beside)
        steps = [(1, (common, near, own_far))]

        def add_projections(total, begin, end):
            base = 0 if begin == 0 else 2 * begin - 1
            return project(index, base, (hidden_in, other), steps[begin:end], total, end == half + 1)

        out_flows = [w_out, None]
        shards = [w_out]
        total = None
        for step in range(1, half + 1):
            if step == 2:
                near, index, *tables = lax.optimization_barrier((near, index, *tables))
                other = core_swap(after(hidden_in, near), count)
                out_flows[1] = core_swap(after(w_out, near), count)
            if step == half:
                near = first_of(after(near, steps[step - 2][1][2]))
            near = ring(near)
            if step > 1:
                common = after(common, steps[step - 1][1][2])
            if step > 2:
                held = after(steps[step - 3][1][0], shards[-1])
                steps[step - 3] = (steps[step - 3][0], (held, *steps[step - 3][1][1:]))
                total = add_projections(total, step - 3, step - 2)
                common = after(common, total)
            if step == half:
                common = first_of(common)
            common = ring(after(common, near))
            steps.append((near.shape[0], (common, near, plane_swap(near))))
            turn = (step - 1) % 2
            out_flows[turn] = ring(after(out_flows[turn], near))
            shards.append(out_flows[turn])

        held = after(steps[half - 2][1][0], shards[-1])
        steps[half - 2] = (steps[half - 2][0], (held, *steps[half - 2][1][1:]))
        total = add_projections(total, half - 2, half - 1)
        total = add_projections(total, half - 1, half)
        for step in range(half + 1, 2 * half):
            turn = (step - 1) % 2
            out_flows[turn] = ring(after(out_flows[turn], common))
            shards.append(out_flows[turn])
        kept, sent = add_projections(total, half, half + 1)
        came = core_swap(sent, count)
    else:
        gathered = lax.all_gather(
            jnp.concatenate([w_key, w_value, w_query], axis=1), "ctx", axis=0, tiled=True
        )
        ordered = jnp.where(core == 0, hidden_in, jnp.roll(hidden_in, block, axis=0))
        pair_tokens = jnp.concatenate([ordered[:block], core_swap(ordered[block:], count)], axis=0)
        kept = jnp.dot(pair_tokens, gathered, preferred_element_type=jnp.float32)
        came = jnp.zeros_like(kept)

    cosine, sine, key_seg = tables
    joined, queries = rotate_sums(kept, came, cosine, sine)

    if not ringed:
        index = jnp.stack(index).astype(jnp.int32)
    sends = [(device, device ^ 2) for device in range(count)]
    own_row = join_row(index, joined, lax.ppermute(joined, "ctx", sends))
    row_count = count // 2
    windows = [own_row]
    for back in range(1, reach // 2 + 1):
        sends = [
            (row_device(row, column, count), row_device(row + back, column, count))
            for row in range(row_count - back)
            for column in range(2)
        ]
        windows.append(lax.ppermute(own_row, "ctx", sends))

    if ringed:
        queries = after(queries, shards[5], shards[6])
    mixed = attend(index, queries, windows[::-1], key_seg, head_dim)

    returned = core_swap(mixed, count)
    if not ringed:
        kinds = (mixed[:block], returned[block:])
        own_rows = jnp.where(
            core == 0, jnp.concatenate(kinds, axis=0), jnp.concatenate(kinds[::-1], axis=0)
        )
        gathered = lax.all_gather(w_out, "ctx", axis=1, tiled=True)
        return jnp.dot(own_rows, gathered, preferred_element_type=jnp.float32).astype(jnp.bfloat16)

    arrivals = []
    result = None
    for begin, end in ((0, 5), (5, len(shards))):
        result, sent = columns_of(index, begin, mixed, returned, shards[begin:end], result, width)
        arrivals.append((3 + len(shards) + begin, core_swap(sent, count)))
    for base, came in arrivals:
        result = place_columns(index, base, came, result, out_cols)
    return result


def solution(mesh):
    in_specs = (
        P(("dp", "ctx"), None),
        P("dp"),
        P("ctx", None),
        P("ctx", None),
        P("ctx", None),
        P(None, "ctx"),
    )
    out_specs = P(("dp", "ctx"), None)
    return jax.shard_map(
        on_device, mesh=mesh, in_specs=in_specs, out_specs=out_specs, check_vma=False
    )
```

time: 161 us -> 128 us (0.80)
  the two profiles are of different devices: /device:TPU:9 before, /device:TPU:19 now
where the time goes in v2:
time: 128 us; the launch traced here: 127 us
  waiting for transfers between devices  59.7 us (47%)
  starting transfers between devices  39.7 us (31%)
  Pallas kernels  26.3 us (21%)
    ppermute x15, waiting for transfers between devices, ring(): return lax.ppermute(value, 'ctx', pairs)  39.8 us
    ppermute x15, starting transfers between devices, ring(): return lax.ppermute(value, 'ctx', pairs)  15 us
    ppermute x2, starting transfers between devices, on_device(): windows.append(lax.ppermute(own_row, 'ctx', sends))  13.4 us
    pallas_call x5, Pallas kernels, project(): pl.pallas_call(functools.partial(project_kernel, slots, base, groups, tot...  12.3 us
    ppermute x2, waiting for transfers between devices, on_device(): windows.append(lax.ppermute(own_row, 'ctx', sends))  7.53 us
    ppermute x9, starting transfers between devices, core_swap(): return lax.ppermute(value, 'ctx', [(i, i ^ 1) for i in range(count)])  6.68 us
    ppermute x4, waiting for transfers between devices, plane_swap(): return lax.ppermute(value, 'dp', [(0, 1), (1, 0)])  6.5 us
    pallas_call x2, Pallas kernels, columns_of(): pl.pallas_call(functools.partial(columns_kernel, len(shards), base), in_s...  5.07 us
  transfers between devices with their start and end apart: 31, of which 19 were waited for; matrix products, arithmetic and copies ran while one was open for 1% of the time, Pallas kernels for 14%

profile of v2, /device:TPU:19, one launch (start us, length us, event | category | flops | bytes accessed | tf_op | source)
XLA Modules:
  0.0 127.4 jit_solution(15495073620727605324)
XLA Ops:
  4.0 1.3 %collective-permute-start.3 = (bf16[2,512,256]{2,1,0:T(8,128)(2,1)S(1)}, bf16[2,512,256]{2,1,0:T(8,128)(2,1)S(1)}, u32[]{:S(2)}, u32[]{:S(2)}) collective-permute-start(bf16[2,512,256]{2,1,0:T(8,128)(2,1)S(1)} %get-tuple-element.44.refs_1_), channel_id=1, source_target_pairs={{0,8},{2,6},{8,16},{10,2},{16,24},{18,10},{24,28},{26,18},{28,20},... | collective-permute-start | bytes 1572872 | tf_op jit(solution)/shard_map/ppermute | solution.py:447
  6.0 6.3 %collective-permute-done.3.refs_1_ = bf16[2,512,256]{2,1,0:T(8,128)(2,1)S(1)} collective-permute-done((bf16[2,512,256]{2,1,0:T(8,128)(2,1)S(1)}, bf16[2,512,256]{2,1,0:T(8,128)(2,1)S(1)}, u32[]{:S(2)}, u32[]{:S(2)}) %collective-permute-start.3) | collective-permute-done | bytes 524320 | tf_op jit(solution)/shard_map/ppermute | solution.py:447
  13.6 1.3 %collective-permute-start.7 = (bf16[2,512,256]{2,1,0:T(8,128)(2,1)S(1)}, bf16[2,512,256]{2,1,0:T(8,128)(2,1)S(1)}, u32[]{:S(2)}, u32[]{:S(2)}) collective-permute-start(bf16[2,512,256]{2,1,0:T(8,128)(2,1)S(1)} %collective-permute-done.3.refs_1_), channel_id=1, source_target_pairs={{0,8},{2,6},{8,16},{10,2},{16,24},{18,10},{24,28},{26,18},{28,20},... | collective-permute-start | bytes 1572872 | tf_op jit(solution)/shard_map/ppermute | solution.py:447
  16.6 5.3 %collective-permute-done.7.refs_1_ = bf16[2,512,256]{2,1,0:T(8,128)(2,1)S(1)} collective-permute-done((bf16[2,512,256]{2,1,0:T(8,128)(2,1)S(1)}, bf16[2,512,256]{2,1,0:T(8,128)(2,1)S(1)}, u32[]{:S(2)}, u32[]{:S(2)}) %collective-permute-start.7) | collective-permute-done | bytes 524320 | tf_op jit(solution)/shard_map/ppermute | solution.py:447
  24.5 3.1 %collective-permute-done.5.refs_0_ = bf16[2,512,256]{2,1,0:T(8,128)(2,1)S(1)} collective-permute-done((bf16[2,512,256]{2,1,0:T(8,128)(2,1)S(1)}, bf16[2,512,256]{2,1,0:T(8,128)(2,1)S(1)}, u32[]{:S(2)}, u32[]{:S(2)}) %collective-permute-start.5) | collective-permute-done | bytes 524320 | tf_op jit(solution)/shard_map/ppermute | solution.py:447
  29.6 3.5 %collective-permute-done.12.pair_ref.refs_1_ = bf16[2,512,256]{2,1,0:T(8,128)(2,1)S(1)} collective-permute-done((bf16[2,512,256]{2,1,0:T(8,128)(2,1)S(1)}, bf16[2,512,256]{2,1,0:T(8,128)(2,1)S(1)}, u32[]{:S(2)}, u32[]{:S(2)}) %collective-permute-start.12) | collective-permute-done | bytes 524320 | tf_op jit(solution)/shard_map/ppermute | solution.py:447
  34.4 5.1 %collective-permute-done.9.refs_2_ = bf16[2,512,256]{2,1,0:T(8,128)(2,1)S(1)} collective-permute-done((bf16[2,512,256]{2,1,0:T(8,128)(2,1)S(1)}, bf16[2,512,256]{2,1,0:T(8,128)(2,1)S(1)}, u32[]{:S(2)}, u32[]{:S(2)}) %collective-permute-start.9) | collective-permute-done | bytes 524320 | tf_op jit(solution)/shard_map/ppermute | solution.py:41
  39.6 1.3 %collective-permute-start.17 = (bf16[1,512,256]{2,1,0:T(8,128)(2,1)S(1)}, bf16[1,512,256]{2,1,0:T(8,128)(2,1)S(1)}, u32[]{:S(2)}, u32[]{:S(2)}) collective-permute-start(bf16[1,512,256]{2,1,0:T(8,128)(2,1)S(1)} %first_of.3), channel_id=1, source_target_pairs={{0,8},{2,6},{8,16},{10,2},{16,24},{18,10},{24,28},{26,18},{28,20},... | collective-permute-start | bytes 786440 | tf_op jit(solution)/shard_map/ppermute | solution.py:447
  41.2 3.2 %collective-permute-done.11.refs_2_ = bf16[512,512]{1,0:T(8,128)(2,1)S(1)} collective-permute-done((bf16[512,512]{1,0:T(8,128)(2,1)S(1)}, bf16[512,512]{1,0:T(8,128)(2,1)S(1)}, u32[]{:S(2)}, u32[]{:S(2)}) %collective-permute-start.11) | collective-permute-done | bytes 524320 | tf_op jit(solution)/shard_map/ppermute | solution.py:447
  44.4 5.6 %collective-permute-done.8.refs_0_ = bf16[2,512,256]{2,1,0:T(8,128)(2,1)S(1)} collective-permute-done((bf16[2,512,256]{2,1,0:T(8,128)(2,1)S(1)}, bf16[2,512,256]{2,1,0:T(8,128)(2,1)S(1)}, u32[]{:S(2)}, u32[]{:S(2)}) %collective-permute-start.8) | collective-permute-done | bytes 524320 | tf_op jit(solution)/shard_map/ppermute | solution.py:447
  51.2 2.0 %project.5.refs_3_ = f32[2,256,768]{2,1,0:T(8,128)S(1)} custom-call(s32[19]{0:T(128)S(1)} %stack.76.index_ref, bf16[256,8192]{1,0:T(8,128)(2,1)} %own_ref.9, bf16[256,8192]{1,0:T(8,128)(2,1)S(1)} %collective-permute-done.4.other_ref, bf16[2,512,256]{2,1,0:T(8,128)(2,1)S(1)} %get-tuple-element.55.refs_0_, bf16[2,512,256]{2,1,0:T(8,128)(2,1)S(1)} %get-tuple-element.44.refs_1_, ...), custom_call_target="tpu_custom_call" | custom-call | tf_op jit(solution)/shard_map/project/pallas_call | solution.py:314
  53.2 1.3 %collective-permute-start.13 = (bf16[2,512,256]{2,1,0:T(8,128)(2,1)S(1)}, bf16[2,512,256]{2,1,0:T(8,128)(2,1)S(1)}, u32[]{:S(2)}, u32[]{:S(2)}) collective-permute-start(bf16[2,512,256]{2,1,0:T(8,128)(2,1)S(1)} %collective-permute-done.8.refs_0_), channel_id=1, source_target_pairs={{0,8},{2,6},{8,16},{10,2},{16,24},{18,10},{24,28},{26,18},{28,20},... | collective-permute-start | bytes 1572872 | tf_op jit(solution)/shard_map/ppermute | solution.py:447
  55.3 3.1 %collective-permute-done.16.refs_3_ = bf16[512,512]{1,0:T(8,128)(2,1)S(1)} collective-permute-done((bf16[512,512]{1,0:T(8,128)(2,1)S(1)}, bf16[512,512]{1,0:T(8,128)(2,1)S(1)}, u32[]{:S(2)}, u32[]{:S(2)}) %collective-permute-start.16) | collective-permute-done | bytes 524320 | tf_op jit(solution)/shard_map/ppermute | solution.py:447
  58.4 2.8 %project.6.refs_3_ = f32[2,256,768]{2,1,0:T(8,128)S(1)} custom-call(s32[19]{0:T(128)S(1)} %stack.76.index_ref, bf16[256,8192]{1,0:T(8,128)(2,1)} %own_ref.9, bf16[256,8192]{1,0:T(8,128)(2,1)S(1)} %collective-permute-done.4.other_ref, bf16[2,512,256]{2,1,0:T(8,128)(2,1)S(1)} %collective-permute-done.5.refs_0_, ...), custom_call_target="tpu_custom_call" | custom-call | tf_op jit(solution)/shard_map/project/pallas_call | solution.py:314
  61.2 1.4 %collective-permute-done.14.refs_2_ = bf16[2,512,256]{2,1,0:T(8,128)(2,1)S(1)} collective-permute-done((bf16[2,512,256]{2,1,0:T(8,128)(2,1)S(1)}, bf16[2,512,256]{2,1,0:T(8,128)(2,1)S(1)}, u32[]{:S(2)}, u32[]{:S(2)}) %collective-permute-start.14) | collective-permute-done | bytes 524320 | tf_op jit(solution)/shard_map/ppermute | solution.py:41
  62.6 1.5 %collective-permute-done.13.pair_ref.refs_0_ = bf16[2,512,256]{2,1,0:T(8,128)(2,1)S(1)} collective-permute-done((bf16[2,512,256]{2,1,0:T(8,128)(2,1)S(1)}, bf16[2,512,256]{2,1,0:T(8,128)(2,1)S(1)}, u32[]{:S(2)}, u32[]{:S(2)}) %collective-permute-start.13) | collective-permute-done | bytes 524320 | tf_op jit(solution)/shard_map/ppermute | solution.py:447
  64.1 1.3 %collective-permute-start.18 = (bf16[1,512,256]{2,1,0:T(8,128)(2,1)S(1)}, bf16[1,512,256]{2,1,0:T(8,128)(2,1)S(1)}, u32[]{:S(2)}, u32[]{:S(2)}) collective-permute-start(bf16[1,512,256]{2,1,0:T(8,128)(2,1)S(1)} %first_of.2), channel_id=1, source_target_pairs={{0,8},{2,6},{8,16},{10,2},{16,24},{18,10},{24,28},{26,18},{28,20},... | collective-permute-start | bytes 786440 | tf_op jit(solution)/shard_map/ppermute | solution.py:447
  65.4 4.2 %collective-permute-done.20.refs_4_ = bf16[512,512]{1,0:T(8,128)(2,1)S(1)} collective-permute-done((bf16[512,512]{1,0:T(8,128)(2,1)S(1)}, bf16[512,512]{1,0:T(8,128)(2,1)S(1)}, u32[]{:S(2)}, u32[]{:S(2)}) %collective-permute-start.20) | collective-permute-done | bytes 524320 | tf_op jit(solution)/shard_map/ppermute | solution.py:447
  69.7 2.8 %project.7.refs_3_ = f32[2,256,768]{2,1,0:T(8,128)S(1)} custom-call(s32[19]{0:T(128)S(1)} %stack.76.index_ref, bf16[256,8192]{1,0:T(8,128)(2,1)} %own_ref.9, bf16[256,8192]{1,0:T(8,128)(2,1)S(1)} %collective-permute-done.4.other_ref, bf16[2,512,256]{2,1,0:T(8,128)(2,1)S(1)} %collective-permute-done.8.refs_0_, ...), custom_call_target="tpu_custom_call" | custom-call | tf_op jit(solution)/shard_map/project/pallas_call | solution.py:314
  72.4 2.8 %project.8.refs_3_ = f32[2,256,768]{2,1,0:T(8,128)S(1)} custom-call(s32[19]{0:T(128)S(1)} %stack.76.index_ref, bf16[256,8192]{1,0:T(8,128)(2,1)} %own_ref.9, bf16[256,8192]{1,0:T(8,128)(2,1)S(1)} %collective-permute-done.4.other_ref, bf16[2,512,256]{2,1,0:T(8,128)(2,1)S(1)} %collective-permute-done.13.pair_ref.refs_0_, ...), custom_call_target="tpu_custom_call" | custom-call | tf_op jit(solution)/shard_map/project/pallas_call | solution.py:314
  75.2 2.1 %project.9 = (f32[256,768]{1,0:T(8,128)S(1)}, f32[256,768]{1,0:T(8,128)S(1)}) custom-call(s32[19]{0:T(128)S(1)} %stack.76.index_ref, bf16[256,8192]{1,0:T(8,128)(2,1)} %own_ref.9, bf16[256,8192]{1,0:T(8,128)(2,1)S(1)} %collective-permute-done.4.other_ref, bf16[1,512,256]{2,1,0:T(8,128)(2,1)S(1)} %collective-permute-done.18.refs_0_, ...), custom_call_target="tpu_custom_call" | custom-call | tf_op jit(solution)/shard_map/project/pallas_call | solution.py:314
  80.7 4.5 %collective-permute-done.24.beside_ref = bf16[256,256]{1,0:T(8,128)(2,1)S(1)} collective-permute-done((bf16[256,256]{1,0:T(8,128)(2,1)S(1)}, bf16[256,256]{1,0:T(8,128)(2,1)S(1)}, u32[]{:S(2)}, u32[]{:S(2)}) %collective-permute-start.24) | collective-permute-done | bytes 131104 | tf_op jit(solution)/shard_map/ppermute | solution.py:509
  85.7 11.5 %collective-permute-start.25 = (bf16[2,256,256]{2,1,0:T(8,128)(2,1)S(1)}, bf16[2,256,256]{2,1,0:T(8,128)(2,1)S(1)}, u32[]{:S(2)}, u32[]{:S(2)}) collective-permute-start(bf16[2,256,256]{2,1,0:T(8,128)(2,1)S(1)} %join_row.1.refs_2_), channel_id=1, source_target_pairs={{0,16},{4,20},{8,24},{12,28},{16,26},{20,30},{24,18},{28,22},{26,1... | collective-permute-start | bytes 786440 | tf_op jit(solution)/shard_map/ppermute | solution.py:518
  97.2 1.9 %collective-permute-start.26 = (bf16[2,256,256]{2,1,0:T(8,128)(2,1)S(1)}, bf16[2,256,256]{2,1,0:T(8,128)(2,1)S(1)}, u32[]{:S(2)}, u32[]{:S(2)}) collective-permute-start(bf16[2,256,256]{2,1,0:T(8,128)(2,1)S(1)} %join_row.1.refs_2_), channel_id=1, source_target_pairs={{0,8},{4,12},{8,16},{12,20},{16,24},{20,28},{24,26},{28,30},{26,18... | collective-permute-start | bytes 786440 | tf_op jit(solution)/shard_map/ppermute | solution.py:518
  99.2 6.8 %collective-permute-done.25.refs_0_ = bf16[2,256,256]{2,1,0:T(8,128)(2,1)S(1)} collective-permute-done((bf16[2,256,256]{2,1,0:T(8,128)(2,1)S(1)}, bf16[2,256,256]{2,1,0:T(8,128)(2,1)S(1)}, u32[]{:S(2)}, u32[]{:S(2)}) %collective-permute-start.25) | collective-permute-done | bytes 262176 | tf_op jit(solution)/shard_map/ppermute | solution.py:518
  106.7 3.9 %attend.1.mixed_ref = bf16[256,512]{1,0:T(8,128)(2,1)S(1)} custom-call(s32[19]{0:T(128)S(1)} %stack.76.index_ref, bf16[256,512]{1,0:T(8,128)(2,1)S(1)} %get-tuple-element.75.query_ref, s32[1,1280]{1,0:T(1,128)S(1)} %bitcast.29, bf16[2,256,256]{2,1,0:T(8,128)(2,1)S(1)} %collective-permute-done.25.refs_0_, ...), custom_call_target="tpu_custom_call" | custom-call | tf_op jit(solution)/shard_map/attend/pallas_call | solution.py:192
  110.6 1.9 %collective-permute-start.27 = (bf16[256,512]{1,0:T(8,128)(2,1)S(1)}, bf16[256,512]{1,0:T(8,128)(2,1)S(1)}, u32[]{:S(2)}, u32[]{:S(2)}) collective-permute-start(bf16[256,512]{1,0:T(8,128)(2,1)S(1)} %attend.1.mixed_ref), channel_id=1, source_target_pairs={{0,2},{2,0},{4,6},{6,4},{8,10},{10,8},{12,14},{14,12},{16,18},{18,... | collective-permute-start | bytes 786440 | tf_op jit(solution)/shard_map/ppermute | solution.py:37
  113.7 2.8 %columns_of.2 = (bf16[256,8192]{1,0:T(8,128)(2,1)}, bf16[256,2560]{1,0:T(8,128)(2,1)S(1)}) custom-call(s32[19]{0:T(128)S(1)} %stack.76.index_ref, bf16[256,512]{1,0:T(8,128)(2,1)S(1)} %attend.1.mixed_ref, bf16[256,512]{1,0:T(8,128)(2,1)S(1)} %collective-permute-done.27.returned_ref, bf16[512,512]{1,0:T(8,128)(2,1)S(1)} %copy-done.1, ...), custom_call_target="tpu_custom_call" | custom-call | tf_op jit(solution)/shard_map/columns_of/pallas_call | solution.py:370
  116.9 3.9 %collective-permute-done.28.refs_2_ = bf16[512,512]{1,0:T(8,128)(2,1)S(1)} collective-permute-done((bf16[512,512]{1,0:T(8,128)(2,1)S(1)}, bf16[512,512]{1,0:T(8,128)(2,1)S(1)}, u32[]{:S(2)}, u32[]{:S(2)}) %collective-permute-start.28) | collective-permute-done | bytes 524320 | tf_op jit(solution)/shard_map/ppermute | solution.py:447
  120.8 2.3 %columns_of.3 = (bf16[256,8192]{1,0:T(8,128)(2,1)}, bf16[256,1536]{1,0:T(8,128)(2,1)S(1)}) custom-call(s32[19]{0:T(128)S(1)} %stack.76.index_ref, bf16[256,512]{1,0:T(8,128)(2,1)S(1)} %attend.1.mixed_ref, bf16[256,512]{1,0:T(8,128)(2,1)S(1)} %collective-permute-done.27.returned_ref, ...), custom_call_target="tpu_custom_call", output_to_operand_aliasing={{0}: (6, {})} | custom-call | tf_op jit(solution)/shard_map/columns_of/pallas_call | solution.py:370
  124.1 1.6 %place_columns.2._ = bf16[256,8192]{1,0:T(8,128)(2,1)} custom-call(s32[19]{0:T(128)S(1)} %stack.76.index_ref, bf16[256,2560]{1,0:T(8,128)(2,1)S(1)} %collective-permute-done.30.came_ref, bf16[256,8192]{1,0:T(8,128)(2,1)} %get-tuple-element.82._), custom_call_target="tpu_custom_call", output_to_operand_aliasing={{}: (2, {})} | custom-call | tf_op jit(solution)/shard_map/place_columns/pallas_call | solution.py:401
  126.0 1.4 %place_columns.3 = bf16[256,8192]{1,0:T(8,128)(2,1)} custom-call(s32[19]{0:T(128)S(1)} %stack.76.index_ref, bf16[256,1536]{1,0:T(8,128)(2,1)S(1)} %collective-permute-done.29.came_ref, bf16[256,8192]{1,0:T(8,128)(2,1)} %place_columns.2._), custom_call_target="tpu_custom_call", output_to_operand_aliasing={{}: (2, {})} | custom-call | tf_op jit(solution)/shard_map/place_columns/pallas_call | solution.py:401
  (60 shorter events, 23.3 us)
Async XLA Ops:
  0.0 2.8 %collective-permute-start = (bf16[512,512]{1,0:T(8,128)(2,1)}, bf16[512,512]{1,0:T(8,128)(2,1)S(1)}, u32[]{:S(2)}, u32[]{:S(2)}) collective-permute-start(bf16[512,512]{1,0:T(8,128)(2,1)} %refs_0_.2), channel_id=1, source_target_pairs={{0,2},{2,0},{4,6},{6,4},{8,10},{10,8},{12,14},{14,12},{16,18},{18,... | collective-permute-start | bytes 1572872 | tf_op jit(solution)/shard_map/ppermute | solution.py:37
  0.7 1.9 %collective-permute-start.1 = (bf16[512,128]{1,0:T(8,128)(2,1)}, bf16[512,128]{1,0:T(8,128)(2,1)S(1)}, u32[]{:S(2)}, u32[]{:S(2)}) collective-permute-start(bf16[512,128]{1,0:T(8,128)(2,1)} %refs_1_.1), channel_id=1, source_target_pairs={{0,2},{2,0},{4,6},{6,4},{8,10},{10,8},{12,14},{14,12},{16,18},{18,... | collective-permute-start | bytes 393224 | tf_op jit(solution)/shard_map/ppermute | solution.py:37
  0.8 2.1 %collective-permute-start.2 = (bf16[512,128]{1,0:T(8,128)(2,1)}, bf16[512,128]{1,0:T(8,128)(2,1)S(1)}, u32[]{:S(2)}, u32[]{:S(2)}) collective-permute-start(bf16[512,128]{1,0:T(8,128)(2,1)} %refs_2_.1), channel_id=1, source_target_pairs={{0,2},{2,0},{4,6},{6,4},{8,10},{10,8},{12,14},{14,12},{16,18},{18,... | collective-permute-start | bytes 393224 | tf_op jit(solution)/shard_map/ppermute | solution.py:37
  4.0 8.4 %collective-permute-start.3 = (bf16[2,512,256]{2,1,0:T(8,128)(2,1)S(1)}, bf16[2,512,256]{2,1,0:T(8,128)(2,1)S(1)}, u32[]{:S(2)}, u32[]{:S(2)}) collective-permute-start(bf16[2,512,256]{2,1,0:T(8,128)(2,1)S(1)} %get-tuple-element.44.refs_1_), channel_id=1, source_target_pairs={{0,8},{2,6},{8,16},{10,2},{16,24},{18,10},{24,28},{26,18},{28,20},... | collective-permute-start | bytes 1572872 | tf_op jit(solution)/shard_map/ppermute | solution.py:447
  12.4 38.9 %collective-permute-start.4 = (bf16[256,8192]{1,0:T(8,128)(2,1)}, bf16[256,8192]{1,0:T(8,128)(2,1)S(1)}, u32[]{:S(2)}, u32[]{:S(2)}) collective-permute-start(bf16[256,8192]{1,0:T(8,128)(2,1)} %own_ref.9), channel_id=1, source_target_pairs={{0,2},{2,0},{4,6},{6,4},{8,10},{10,8},{12,14},{14,12},{16,18},{18,... | collective-permute-start | bytes 12582920 | tf_op jit(solution)/shard_map/ppermute | solution.py:37
  13.6 8.3 %collective-permute-start.7 = (bf16[2,512,256]{2,1,0:T(8,128)(2,1)S(1)}, bf16[2,512,256]{2,1,0:T(8,128)(2,1)S(1)}, u32[]{:S(2)}, u32[]{:S(2)}) collective-permute-start(bf16[2,512,256]{2,1,0:T(8,128)(2,1)S(1)} %collective-permute-done.3.refs_1_), channel_id=1, source_target_pairs={{0,8},{2,6},{8,16},{10,2},{16,24},{18,10},{24,28},{26,18},{28,20},... | collective-permute-start | bytes 1572872 | tf_op jit(solution)/shard_map/ppermute | solution.py:447
  14.9 8.3 %collective-permute-start.10 = (bf16[512,512]{1,0:T(8,128)(2,1)}, bf16[512,512]{1,0:T(8,128)(2,1)S(1)}, u32[]{:S(2)}, u32[]{:S(2)}) collective-permute-start(bf16[512,512]{1,0:T(8,128)(2,1)} %refs_0_.3), channel_id=1, source_target_pairs={{0,2},{2,0},{4,6},{6,4},{8,10},{10,8},{12,14},{14,12},{16,18},{18,... | collective-permute-start | bytes 1572872 | tf_op jit(solution)/shard_map/ppermute | solution.py:37
  14.9 12.6 %collective-permute-start.5 = (bf16[2,512,256]{2,1,0:T(8,128)(2,1)S(1)}, bf16[2,512,256]{2,1,0:T(8,128)(2,1)S(1)}, u32[]{:S(2)}, u32[]{:S(2)}) collective-permute-start(bf16[2,512,256]{2,1,0:T(8,128)(2,1)S(1)} %get-tuple-element.55.refs_0_), channel_id=1, source_target_pairs={{0,8},{2,6},{8,16},{10,2},{16,24},{18,10},{24,28},{26,18},{28,20},... | collective-permute-start | bytes 1572872 | tf_op jit(solution)/shard_map/ppermute | solution.py:447
  15.3 13.5 %collective-permute-start.6 = (bf16[2,512,256]{2,1,0:T(8,128)(2,1)S(1)}, bf16[2,512,256]{2,1,0:T(8,128)(2,1)S(1)}, u32[]{:S(2)}, u32[]{:S(2)}) collective-permute-start(bf16[2,512,256]{2,1,0:T(8,128)(2,1)S(1)} %collective-permute-done.3.refs_1_), channel_id=1, source_target_pairs={{0,1},{1,0},{2,3},{3,2},{4,5},{5,4},{6,7},{7,6},{8,9},{9,8},{10,11... | collective-permute-start | bytes 1572872 | tf_op jit(solution)/shard_map/ppermute | solution.py:41
  21.9 11.2 %collective-permute-start.12 = (bf16[2,512,256]{2,1,0:T(8,128)(2,1)S(1)}, bf16[2,512,256]{2,1,0:T(8,128)(2,1)S(1)}, u32[]{:S(2)}, u32[]{:S(2)}) collective-permute-start(bf16[2,512,256]{2,1,0:T(8,128)(2,1)S(1)} %collective-permute-done.7.refs_1_), channel_id=1, source_target_pairs={{0,8},{2,6},{8,16},{10,2},{16,24},{18,10},{24,28},{26,18},{28,20},... | collective-permute-start | bytes 1572872 | tf_op jit(solution)/shard_map/ppermute | solution.py:447
  23.2 16.3 %collective-permute-start.9 = (bf16[2,512,256]{2,1,0:T(8,128)(2,1)S(1)}, bf16[2,512,256]{2,1,0:T(8,128)(2,1)S(1)}, u32[]{:S(2)}, u32[]{:S(2)}) collective-permute-start(bf16[2,512,256]{2,1,0:T(8,128)(2,1)S(1)} %collective-permute-done.7.refs_1_), channel_id=1, source_target_pairs={{0,1},{1,0},{2,3},{3,2},{4,5},{5,4},{6,7},{7,6},{8,9},{9,8},{10,11... | collective-permute-start | bytes 1572872 | tf_op jit(solution)/shard_map/ppermute | solution.py:41
  27.5 13.4 %collective-permute-start.15 = (bf16[512,512]{1,0:T(8,128)(2,1)}, bf16[512,512]{1,0:T(8,128)(2,1)S(1)}, u32[]{:S(2)}, u32[]{:S(2)}) collective-permute-start(bf16[512,512]{1,0:T(8,128)(2,1)} %refs_0_.3), channel_id=1, source_target_pairs={{0,8},{2,6},{8,16},{10,2},{16,24},{18,10},{24,28},{26,18},{28,20},... | collective-permute-start | bytes 1572872 | tf_op jit(solution)/shard_map/ppermute | solution.py:447
  28.8 15.6 %collective-permute-start.11 = (bf16[512,512]{1,0:T(8,128)(2,1)S(1)}, bf16[512,512]{1,0:T(8,128)(2,1)S(1)}, u32[]{:S(2)}, u32[]{:S(2)}) collective-permute-start(bf16[512,512]{1,0:T(8,128)(2,1)S(1)} %collective-permute-done.10), channel_id=1, source_target_pairs={{0,8},{2,6},{8,16},{10,2},{16,24},{18,10},{24,28},{26,18},{28,20},... | collective-permute-start | bytes 1572872 | tf_op jit(solution)/shard_map/ppermute | solution.py:447
  33.2 16.9 %collective-permute-start.8 = (bf16[2,512,256]{2,1,0:T(8,128)(2,1)S(1)}, bf16[2,512,256]{2,1,0:T(8,128)(2,1)S(1)}, u32[]{:S(2)}, u32[]{:S(2)}) collective-permute-start(bf16[2,512,256]{2,1,0:T(8,128)(2,1)S(1)} %collective-permute-done.5.refs_0_), channel_id=1, source_target_pairs={{0,8},{2,6},{8,16},{10,2},{16,24},{18,10},{24,28},{26,18},{28,20},... | collective-permute-start | bytes 1572872 | tf_op jit(solution)/shard_map/ppermute | solution.py:447
  39.6 15.0 %collective-permute-start.17 = (bf16[1,512,256]{2,1,0:T(8,128)(2,1)S(1)}, bf16[1,512,256]{2,1,0:T(8,128)(2,1)S(1)}, u32[]{:S(2)}, u32[]{:S(2)}) collective-permute-start(bf16[1,512,256]{2,1,0:T(8,128)(2,1)S(1)} %first_of.3), channel_id=1, source_target_pairs={{0,8},{2,6},{8,16},{10,2},{16,24},{18,10},{24,28},{26,18},{28,20},... | collective-permute-start | bytes 786440 | tf_op jit(solution)/shard_map/ppermute | solution.py:447
  40.9 17.5 %collective-permute-start.16 = (bf16[512,512]{1,0:T(8,128)(2,1)S(1)}, bf16[512,512]{1,0:T(8,128)(2,1)S(1)}, u32[]{:S(2)}, u32[]{:S(2)}) collective-permute-start(bf16[512,512]{1,0:T(8,128)(2,1)S(1)} %collective-permute-done.15.refs_1_), channel_id=1, source_target_pairs={{0,8},{2,6},{8,16},{10,2},{16,24},{18,10},{24,28},{26,18},{28,20},... | collective-permute-start | bytes 1572872 | tf_op jit(solution)/shard_map/ppermute | solution.py:447
  50.0 12.6 %collective-permute-start.14 = (bf16[2,512,256]{2,1,0:T(8,128)(2,1)S(1)}, bf16[2,512,256]{2,1,0:T(8,128)(2,1)S(1)}, u32[]{:S(2)}, u32[]{:S(2)}) collective-permute-start(bf16[2,512,256]{2,1,0:T(8,128)(2,1)S(1)} %collective-permute-done.12.pair_ref.refs_1_), channel_id=1, source_target_pairs={{0,1},{1,0},{2,3},{3,2},{4,5},{5,4},{6,7},{7,6},{8,9},{9,8},{10,11... | collective-permute-start | bytes 1572872 | tf_op jit(solution)/shard_map/ppermute | solution.py:41
  53.2 10.8 %collective-permute-start.13 = (bf16[2,512,256]{2,1,0:T(8,128)(2,1)S(1)}, bf16[2,512,256]{2,1,0:T(8,128)(2,1)S(1)}, u32[]{:S(2)}, u32[]{:S(2)}) collective-permute-start(bf16[2,512,256]{2,1,0:T(8,128)(2,1)S(1)} %collective-permute-done.8.refs_0_), channel_id=1, source_target_pairs={{0,8},{2,6},{8,16},{10,2},{16,24},{18,10},{24,28},{26,18},{28,20},... | collective-permute-start | bytes 1572872 | tf_op jit(solution)/shard_map/ppermute | solution.py:447
  54.6 15.1 %collective-permute-start.20 = (bf16[512,512]{1,0:T(8,128)(2,1)S(1)}, bf16[512,512]{1,0:T(8,128)(2,1)S(1)}, u32[]{:S(2)}, u32[]{:S(2)}) collective-permute-start(bf16[512,512]{1,0:T(8,128)(2,1)S(1)} %collective-permute-done.11.refs_2_), channel_id=1, source_target_pairs={{0,8},{2,6},{8,16},{10,2},{16,24},{18,10},{24,28},{26,18},{28,20},... | collective-permute-start | bytes 1572872 | tf_op jit(solution)/shard_map/ppermute | solution.py:447
  54.8 20.4 %collective-permute-start.19 = (bf16[1,512,256]{2,1,0:T(8,128)(2,1)S(1)}, bf16[1,512,256]{2,1,0:T(8,128)(2,1)S(1)}, u32[]{:S(2)}, u32[]{:S(2)}) collective-permute-start(bf16[1,512,256]{2,1,0:T(8,128)(2,1)S(1)} %collective-permute-done.17.refs_1_), channel_id=1, source_target_pairs={{0,1},{1,0},{2,3},{3,2},{4,5},{5,4},{6,7},{7,6},{8,9},{9,8},{10,11... | collective-permute-start | bytes 786440 | tf_op jit(solution)/shard_map/ppermute | solution.py:41
  64.1 11.2 %collective-permute-start.18 = (bf16[1,512,256]{2,1,0:T(8,128)(2,1)S(1)}, bf16[1,512,256]{2,1,0:T(8,128)(2,1)S(1)}, u32[]{:S(2)}, u32[]{:S(2)}) collective-permute-start(bf16[1,512,256]{2,1,0:T(8,128)(2,1)S(1)} %first_of.2), channel_id=1, source_target_pairs={{0,8},{2,6},{8,16},{10,2},{16,24},{18,10},{24,28},{26,18},{28,20},... | collective-permute-start | bytes 786440 | tf_op jit(solution)/shard_map/ppermute | solution.py:447
  75.2 38.5 %copy-start.1 = (bf16[512,512]{1,0:T(8,128)(2,1)S(1)}, bf16[512,512]{1,0:T(8,128)(2,1)}, u32[]{:S(2)}) copy-start(bf16[512,512]{1,0:T(8,128)(2,1)} %refs_0_.3) | copy-start | bytes 1572868
  77.3 2.8 %collective-permute-start.21 = (f32[256,768]{1,0:T(8,128)S(1)}, f32[256,768]{1,0:T(8,128)S(1)}, u32[]{:S(2)}, u32[]{:S(2)}) collective-permute-start(f32[256,768]{1,0:T(8,128)S(1)} %get-tuple-element.69), channel_id=1, source_target_pairs={{0,2},{2,0},{4,6},{6,4},{8,10},{10,8},{12,14},{14,12},{16,18},{18,... | collective-permute-start | bytes 2359304 | tf_op jit(solution)/shard_map/ppermute | solution.py:37
  78.2 20.9 %collective-permute-start.23 = (bf16[512,512]{1,0:T(8,128)(2,1)S(1)}, bf16[512,512]{1,0:T(8,128)(2,1)S(1)}, u32[]{:S(2)}, u32[]{:S(2)}) collective-permute-start(bf16[512,512]{1,0:T(8,128)(2,1)S(1)} %collective-permute-done.20.refs_4_), channel_id=1, source_target_pairs={{0,8},{2,6},{8,16},{10,2},{16,24},{18,10},{24,28},{26,18},{28,20},... | collective-permute-start | bytes 1572872 | tf_op jit(solution)/shard_map/ppermute | solution.py:447
  79.5 19.6 %collective-permute-start.22 = (bf16[512,512]{1,0:T(8,128)(2,1)S(1)}, bf16[512,512]{1,0:T(8,128)(2,1)S(1)}, u32[]{:S(2)}, u32[]{:S(2)}) collective-permute-start(bf16[512,512]{1,0:T(8,128)(2,1)S(1)} %collective-permute-done.16.refs_3_), channel_id=1, source_target_pairs={{0,8},{2,6},{8,16},{10,2},{16,24},{18,10},{24,28},{26,18},{28,20},... | collective-permute-start | bytes 1572872 | tf_op jit(solution)/shard_map/ppermute | solution.py:447
  80.4 4.8 %collective-permute-start.24 = (bf16[256,256]{1,0:T(8,128)(2,1)S(1)}, bf16[256,256]{1,0:T(8,128)(2,1)S(1)}, u32[]{:S(2)}, u32[]{:S(2)}) collective-permute-start(bf16[256,256]{1,0:T(8,128)(2,1)S(1)} %get-tuple-element.77.own_ref), channel_id=1, source_target_pairs={{0,4},{2,6},{4,0},{6,2},{8,12},{10,14},{12,8},{14,10},{16,20},{18,... | collective-permute-start | bytes 393224 | tf_op jit(solution)/shard_map/ppermute | solution.py:509
  85.7 20.3 %collective-permute-start.25 = (bf16[2,256,256]{2,1,0:T(8,128)(2,1)S(1)}, bf16[2,256,256]{2,1,0:T(8,128)(2,1)S(1)}, u32[]{:S(2)}, u32[]{:S(2)}) collective-permute-start(bf16[2,256,256]{2,1,0:T(8,128)(2,1)S(1)} %join_row.1.refs_2_), channel_id=1, source_target_pairs={{0,16},{4,20},{8,24},{12,28},{16,26},{20,30},{24,18},{28,22},{26,1... | collective-permute-start | bytes 786440 | tf_op jit(solution)/shard_map/ppermute | solution.py:518
  97.2 9.5 %collective-permute-start.26 = (bf16[2,256,256]{2,1,0:T(8,128)(2,1)S(1)}, bf16[2,256,256]{2,1,0:T(8,128)(2,1)S(1)}, u32[]{:S(2)}, u32[]{:S(2)}) collective-permute-start(bf16[2,256,256]{2,1,0:T(8,128)(2,1)S(1)} %join_row.1.refs_2_), channel_id=1, source_target_pairs={{0,8},{4,12},{8,16},{12,20},{16,24},{20,28},{24,26},{28,30},{26,18... | collective-permute-start | bytes 786440 | tf_op jit(solution)/shard_map/ppermute | solution.py:518
  110.6 3.1 %collective-permute-start.27 = (bf16[256,512]{1,0:T(8,128)(2,1)S(1)}, bf16[256,512]{1,0:T(8,128)(2,1)S(1)}, u32[]{:S(2)}, u32[]{:S(2)}) collective-permute-start(bf16[256,512]{1,0:T(8,128)(2,1)S(1)} %attend.1.mixed_ref), channel_id=1, source_target_pairs={{0,2},{2,0},{4,6},{6,4},{8,10},{10,8},{12,14},{14,12},{16,18},{18,... | collective-permute-start | bytes 786440 | tf_op jit(solution)/shard_map/ppermute | solution.py:37
  112.5 8.3 %collective-permute-start.28 = (bf16[512,512]{1,0:T(8,128)(2,1)S(1)}, bf16[512,512]{1,0:T(8,128)(2,1)S(1)}, u32[]{:S(2)}, u32[]{:S(2)}) collective-permute-start(bf16[512,512]{1,0:T(8,128)(2,1)S(1)} %collective-permute-done.22.refs_0_), channel_id=1, source_target_pairs={{0,8},{2,6},{8,16},{10,2},{16,24},{18,10},{24,28},{26,18},{28,20},... | collective-permute-start | bytes 1572872 | tf_op jit(solution)/shard_map/ppermute | solution.py:447
  116.5 7.6 %collective-permute-start.30 = (bf16[256,2560]{1,0:T(8,128)(2,1)S(1)}, bf16[256,2560]{1,0:T(8,128)(2,1)S(1)}, u32[]{:S(2)}, u32[]{:S(2)}) collective-permute-start(bf16[256,2560]{1,0:T(8,128)(2,1)S(1)} %get-tuple-element.81), channel_id=1, source_target_pairs={{0,2},{2,0},{4,6},{6,4},{8,10},{10,8},{12,14},{14,12},{16,18},{18,... | collective-permute-start | bytes 3932168 | tf_op jit(solution)/shard_map/ppermute | solution.py:37
  123.1 2.9 %collective-permute-start.29 = (bf16[256,1536]{1,0:T(8,128)(2,1)S(1)}, bf16[256,1536]{1,0:T(8,128)(2,1)S(1)}, u32[]{:S(2)}, u32[]{:S(2)}) collective-permute-start(bf16[256,1536]{1,0:T(8,128)(2,1)S(1)} %get-tuple-element.80), channel_id=1, source_target_pairs={{0,2},{2,0},{4,6},{6,4},{8,10},{10,8},{12,14},{14,12},{16,18},{18,... | collective-permute-start | bytes 2359304 | tf_op jit(solution)/shard_map/ppermute | solution.py:37
  (1 other events, 1.2 us)

commit v3 on v2

--- a/solution.py
+++ b/solution.py
@@ -82,19 +82,14 @@
 IN_SMEM = pl.BlockSpec(memory_space=pltpu.SMEM)
 
 
-def rotate_kernel(head_dim, kept_ref, came_ref, cos_ref, sin_ref, joined_ref, query_ref):
+def rotate_kernel(head_dim, heads, kept_ref, came_ref, cos_ref, sin_ref, out_ref):
     cosine, sine = cos_ref[...], sin_ref[...]
-
-    def rotated(column):
+    for column in range(0, kept_ref.shape[1], head_dim):
         span = pl.ds(column, head_dim)
         part = kept_ref[:, span] + came_ref[:, span]
-        return (part * cosine + pltpu.roll(part, head_dim // 2, 1) * sine).astype(jnp.bfloat16)
-
-    joined_ref[:, :head_dim] = rotated(0)
-    values = pl.ds(head_dim, head_dim)
-    joined_ref[:, values] = (kept_ref[:, values] + came_ref[:, values]).astype(jnp.bfloat16)
-    for column in range(0, query_ref.shape[1], head_dim):
-        query_ref[:, pl.ds(column, head_dim)] = rotated(2 * head_dim + column)
+        if column < heads * head_dim:
+            part = part * cosine + pltpu.roll(part, head_dim // 2, 1) * sine
+        out_ref[:, span] = part.astype(jnp.bfloat16)
 
 
 def rotary_tables(positions, head_dim):
@@ -106,17 +101,12 @@
     return jnp.concatenate([cosine, cosine], axis=1), jnp.concatenate([-sine, sine], axis=1)
 
 
-def rotate_sums(kept, came, cosine, sine):
-    rows, columns = kept.shape
-    head_dim = cosine.shape[1]
-    return pl.pallas_call(
-        functools.partial(rotate_kernel, head_dim),
-        out_shape=(
-            pltpu.VMEM((rows, 2 * head_dim), jnp.bfloat16),
-            pltpu.VMEM((rows, columns - 2 * head_dim), jnp.bfloat16),
-        ),
+def rotate_sums(heads, kept, came, cosine, sine):
+    return pl.pallas_call(
+        functools.partial(rotate_kernel, cosine.shape[1], heads),
+        out_shape=pltpu.VMEM(kept.shape, jnp.bfloat16),
         in_specs=[IN_VMEM] * 4,
-        out_specs=(IN_VMEM, IN_VMEM),
+        out_specs=IN_VMEM,
         compiler_params=params(),
         name="rotate_sums",
     )(*in_vmem(kept, came, cosine, sine))
@@ -200,19 +190,16 @@
     )(index, *in_vmem(queries, key_seg, *row_windows))
 
 
-def join_projections_kernel(plane_ref, *refs):
-    own, beside, refs = refs[:3], refs[3:6], refs[6:]
-    near_out, common_out, far_out, sems = refs
+def lay_out_kernel(plane_ref, query_ref, key_ref, value_ref, near_out, far_out, common_out, sems):
     q_half, kv_half = near_out.shape[2], common_out.shape[2] // 2
     near = pl.ds(pl.multiple_of(plane_ref[0] * q_half, q_half), q_half)
     far = pl.ds(pl.multiple_of((1 - plane_ref[0]) * q_half, q_half), q_half)
-    moves = [(own[0].at[:, far], far_out.at[0])]
-    for slot, (query_ref, key_ref, value_ref) in enumerate((own, beside)):
-        moves += [
-            (query_ref.at[:, near], near_out.at[slot]),
-            (key_ref, common_out.at[slot, :, :kv_half]),
-            (value_ref, common_out.at[slot, :, kv_half:]),
-        ]
+    moves = (
+        (key_ref, common_out.at[0, :, :kv_half]),
+        (value_ref, common_out.at[0, :, kv_half:]),
+        (query_ref.at[:, near], near_out.at[0]),
+        (query_ref.at[:, far], far_out.at[0]),
+    )
     copies = [
         pltpu.make_async_copy(source, target, sems.at[place])
         for place, (source, target) in enumerate(moves)
@@ -223,23 +210,34 @@
         copy.wait()
 
 
-def join_projections(plane, own, beside):
-    query, key, _ = own
+def lay_out(plane, query, key, value):
     depth, q_half = query.shape[0], query.shape[1] // 2
-    shapes = (
-        (2, depth, q_half),
-        (2, depth, 2 * key.shape[1]),
-        (1, depth, q_half),
-    )
-    return pl.pallas_call(
-        join_projections_kernel,
-        in_specs=[IN_SMEM] + [IN_HBM] * 3 + [IN_VMEM] * 3,
+    shapes = ((1, depth, q_half), (1, depth, q_half), (1, depth, 2 * key.shape[1]))
+    return pl.pallas_call(
+        lay_out_kernel,
+        in_specs=[IN_SMEM] + [IN_HBM] * 3,
         out_specs=[IN_VMEM] * 3,
-        scratch_shapes=[pltpu.SemaphoreType.DMA((7,))],
+        scratch_shapes=[pltpu.SemaphoreType.DMA((4,))],
         out_shape=[pltpu.VMEM(shape, jnp.bfloat16) for shape in shapes],
         compiler_params=params(),
-        name="join_projections",
-    )(plane, *in_hbm(*own), *in_vmem(*beside))
+        name="lay_out",
+    )(plane, *in_hbm(query, key, value))
+
+
+def both_kernel(first_ref, second_ref, out_ref):
+    out_ref[0] = first_ref[0]
+    out_ref[1] = second_ref[0]
+
+
+def both_of(first, second):
+    return pl.pallas_call(
+        both_kernel,
+        in_specs=[IN_VMEM] * 2,
+        out_specs=IN_VMEM,
+        out_shape=pltpu.VMEM((2, *first.shape[1:]), first.dtype),
+        compiler_params=params(),
+        name="both_of",
+    )(*in_vmem(first, second))
 
 
 def first_kernel(pair_ref, out_ref):
@@ -419,7 +417,6 @@
     block = rows // 2
     head_dim = w_key.shape[1]
     q_rows, out_cols = w_out.shape
-    q_half = q_rows // 2
 
     reach = REACH * block // rows
     pair = jnp.where(core == 0, chip, count - 1 - chip)
@@ -431,8 +428,21 @@
     stored = jnp.where(clipped < count, 2 * clipped, 2 * (2 * count - 1 - clipped) + 1)
     seg_rows = seg_blocks[stored]
     key_seg = jnp.where(seq_block[:, None] >= 0, seg_rows, -1).reshape(1, -1)
-    tables = (cosine, sine, key_seg)
+    tables = (cosine, sine, cosine, sine, key_seg)
     index = [core, plane, pair % 2]
+
+    def row_windows(joined):
+        sends = [(device, device ^ 2) for device in range(count)]
+        own_row = join_row(index, joined, lax.ppermute(joined, "ctx", sends))
+        windows = []
+        for back in range(1, reach // 2 + 1):
+            sends = [
+                (row_device(row, column, count), row_device(row + back, column, count))
+                for row in range(count // 2 - back)
+                for column in range(2)
+            ]
+            windows.append(lax.ppermute(own_row, "ctx", sends))
+        return own_row, windows
 
     ringed = count <= RING_LIMIT
     if ringed:
@@ -446,80 +456,72 @@
         def ring(value):
             return lax.ppermute(value, "ctx", pairs)
 
-        own = (w_query, w_key, w_value)
-        beside = tuple(core_swap(part, count) for part in own)
-        near, common, own_far = join_projections(plane_index, own, beside)
-        steps = [(1, (common, near, own_far))]
-
-        def add_projections(total, begin, end):
+        def add_projections(total, steps, begin, end, last=False):
             base = 0 if begin == 0 else 2 * begin - 1
-            return project(index, base, (hidden_in, other), steps[begin:end], total, end == half + 1)
-
-        out_flows = [w_out, None]
-        shards = [w_out]
-        total = None
+            return project(index, base, (hidden_in, other), steps[begin:end], total, last)
+
+        own_near, own_far, own_common = lay_out(plane_index, w_query, w_key, w_value)
+        common = both_of(own_common, core_swap(own_common, count))
+        common_steps = [(1, (own_common,))]
+        steps = [(1, (own_near, own_far))]
+        near = None
         for step in range(1, half + 1):
             if step == 2:
-                near, index, *tables = lax.optimization_barrier((near, index, *tables))
+                common, index, *tables = lax.optimization_barrier((common, index, *tables))
+                near = both_of(own_near, core_swap(after(own_near, common), count))
                 other = core_swap(after(hidden_in, near), count)
-                out_flows[1] = core_swap(after(w_out, near), count)
-            if step == half:
-                near = first_of(after(near, steps[step - 2][1][2]))
-            near = ring(near)
-            if step > 1:
-                common = after(common, steps[step - 1][1][2])
-            if step > 2:
-                held = after(steps[step - 3][1][0], shards[-1])
-                steps[step - 3] = (steps[step - 3][0], (held, *steps[step - 3][1][1:]))
-                total = add_projections(total, step - 3, step - 2)
-                common = after(common, total)
+                out_second = core_swap(after(w_out, near), count)
             if step == half:
                 common = first_of(common)
-            common = ring(after(common, near))
-            steps.append((near.shape[0], (common, near, plane_swap(near))))
+            common = ring(common)
+            common_steps.append((common.shape[0], (common,)))
+            if step > 1:
+                if step > 3:
+                    near = after(near, steps[step - 3][1][1])
+                near = ring(after(near, *common_steps[step - 1][1]))
+                steps.append((2, (near, plane_swap(near))))
+        cosine, sine, query_cosine, query_sine, key_seg = tables
+
+        total = add_projections(None, common_steps, 0, 3)
+        kept, sent = add_projections(total, common_steps, 3, half + 1, True)
+        joined = rotate_sums(1, kept, core_swap(sent, count), cosine, sine)
+        own_row, windows = row_windows(joined)
+
+        near = first_of(after(near, common, steps[half - 2][1][1]))
+        near = ring(near)
+        steps.append((1, (near, plane_swap(near))))
+        held = [after(w_out, *common_steps[half][1]), after(out_second, near)]
+        shards = [w_out]
+        waits = {3: (joined, steps[half - 1][1][1]), 4: (own_row,), 5: (*windows, steps[half][1][1])}
+        for step in range(1, 2 * half):
             turn = (step - 1) % 2
-            out_flows[turn] = ring(after(out_flows[turn], near))
-            shards.append(out_flows[turn])
-
-        held = after(steps[half - 2][1][0], shards[-1])
-        steps[half - 2] = (steps[half - 2][0], (held, *steps[half - 2][1][1:]))
-        total = add_projections(total, half - 2, half - 1)
-        total = add_projections(total, half - 1, half)
-        for step in range(half + 1, 2 * half):
-            turn = (step - 1) % 2
-            out_flows[turn] = ring(after(out_flows[turn], common))
-            shards.append(out_flows[turn])
-        kept, sent = add_projections(total, half, half + 1)
-        came = core_swap(sent, count)
+            held[turn] = ring(after(held[turn], *waits.get(step, ())))
+            shards.append(held[turn])
+        total = add_projections(None, steps, 0, 2)
+        total = add_projections(total, steps, 2, 3)
+        total = add_projections(total, steps, 3, 4)
+        kept, sent = add_projections(total, steps, 4, 5, True)
+        queries = rotate_sums(
+            q_rows // head_dim, kept, core_swap(sent, count), query_cosine, query_sine
+        )
+        queries = after(queries, shards[5])
     else:
+        index = jnp.stack(index).astype(jnp.int32)
+        cosine, sine, query_cosine, query_sine, key_seg = tables
         gathered = lax.all_gather(
             jnp.concatenate([w_key, w_value, w_query], axis=1), "ctx", axis=0, tiled=True
         )
         ordered = jnp.where(core == 0, hidden_in, jnp.roll(hidden_in, block, axis=0))
         pair_tokens = jnp.concatenate([ordered[:block], core_swap(ordered[block:], count)], axis=0)
-        kept = jnp.dot(pair_tokens, gathered, preferred_element_type=jnp.float32)
-        came = jnp.zeros_like(kept)
-
-    cosine, sine, key_seg = tables
-    joined, queries = rotate_sums(kept, came, cosine, sine)
-
-    if not ringed:
-        index = jnp.stack(index).astype(jnp.int32)
-    sends = [(device, device ^ 2) for device in range(count)]
-    own_row = join_row(index, joined, lax.ppermute(joined, "ctx", sends))
-    row_count = count // 2
-    windows = [own_row]
-    for back in range(1, reach // 2 + 1):
-        sends = [
-            (row_device(row, column, count), row_device(row + back, column, count))
-            for row in range(row_count - back)
-            for column in range(2)
-        ]
-        windows.append(lax.ppermute(own_row, "ctx", sends))
-
-    if ringed:
-        queries = after(queries, shards[5], shards[6])
-    mixed = attend(index, queries, windows[::-1], key_seg, head_dim)
+        sums = jnp.dot(pair_tokens, gathered, preferred_element_type=jnp.float32)
+        kv_sums, query_sums = sums[:, : 2 * head_dim], sums[:, 2 * head_dim :]
+        joined = rotate_sums(1, kv_sums, jnp.zeros_like(kv_sums), cosine, sine)
+        queries = rotate_sums(
+            q_rows // head_dim, query_sums, jnp.zeros_like(query_sums), query_cosine, query_sine
+        )
+        own_row, windows = row_windows(joined)
+
+    mixed = attend(index, queries, [*windows[::-1], own_row], key_seg, head_dim)
 
     returned = core_swap(mixed, count)
     if not ringed:

time: 128 us -> 135 us (1.055); the launches traced: 127 us -> 133 us
  waiting for transfers between devices: 59.7 us -> 62.9 us
  Pallas kernels: 26.3 us -> 29 us
    ppermute x3, waiting for transfers between devices: 12 us -> 0.53 us  [the longest x1 0.52 us: row_windows(): own_row = join_row(index, joined, lax.ppermute(joined, 'ctx', sends))]
    ppermute x15, waiting for transfers between devices: 39.8 us -> 48.5 us  [ring(): return lax.ppermute(value, 'ctx', pairs)]
    ppermute x4, waiting for transfers between devices: 6.5 us -> 11.6 us  [plane_swap(): return lax.ppermute(value, 'dp', [(0, 1), (1, 0)])]
    ppermute x9, starting transfers between devices: 6.68 us -> 11.4 us  [core_swap(): return lax.ppermute(value, 'ctx', [(i, i ^ 1) for i in range(count)])]
    ppermute x15, starting transfers between devices: 15 us -> 11.7 us  [ring(): return lax.ppermute(value, 'ctx', pairs)]
    pallas_call x5 -> x6, Pallas kernels: 12.3 us -> 14.7 us  [project(): pl.pallas_call(functools.partial(project_kernel, slots, base, groups, tot...]
  transfers between devices with their start and end apart: 31 -> 31, of which waited for: 19 -> 18; matrix products, arithmetic and copies ran while one was open for 1% -> 1% of each run, Pallas kernels for 14% -> 20%
where the time goes in v3:
time: 135 us; the launch traced here: 133 us
  waiting for transfers between devices  62.9 us (47%)
  starting transfers between devices  38.8 us (29%)
  Pallas kernels  29 us (21%)
    ppermute x15, waiting for transfers between devices, ring(): return lax.ppermute(value, 'ctx', pairs)  48.5 us
    pallas_call x6, Pallas kernels, project(): pl.pallas_call(functools.partial(project_kernel, slots, base, groups, tot...  14.7 us
    ppermute x2, starting transfers between devices, row_windows(): windows.append(lax.ppermute(own_row, 'ctx', sends))  12.8 us
    ppermute x15, starting transfers between devices, ring(): return lax.ppermute(value, 'ctx', pairs)  11.7 us
    ppermute x4, waiting for transfers between devices, plane_swap(): return lax.ppermute(value, 'dp', [(0, 1), (1, 0)])  11.6 us
    ppermute x9, starting transfers between devices, core_swap(): return lax.ppermute(value, 'ctx', [(i, i ^ 1) for i in range(count)])  11.4 us
    pallas_call x2, Pallas kernels, columns_of(): pl.pallas_call(functools.partial(columns_kernel, len(shards), base), in_s...  5.07 us
    pallas_call x1, Pallas kernels, attend(): pl.pallas_call(functools.partial(attend_kernel, head_dim, reach), out_sha...  3.88 us
  transfers between devices with their start and end apart: 31, of which 18 were waited for; matrix products, arithmetic and copies ran while one was open for 1% of the time, Pallas kernels for 20%

profile of v3, /device:TPU:19, one launch (start us, length us, event | category | flops | bytes accessed | tf_op | source)
XLA Modules:
  0.0 132.8 jit_solution(13788981203701028485)
XLA Ops:
  3.2 1.3 %collective-permute-start.1 = (bf16[2,512,256]{2,1,0:T(8,128)(2,1)S(1)}, bf16[2,512,256]{2,1,0:T(8,128)(2,1)S(1)}, u32[]{:S(2)}, u32[]{:S(2)}) collective-permute-start(bf16[2,512,256]{2,1,0:T(8,128)(2,1)S(1)} %both_of.2), channel_id=1, source_target_pairs={{0,8},{2,6},{8,16},{10,2},{16,24},{18,10},{24,28},{26,18},{28,20},... | collective-permute-start | bytes 1572872 | tf_op jit(solution)/shard_map/ppermute | solution.py:457
  5.3 6.3 %collective-permute-done.1.refs_1_ = bf16[2,512,256]{2,1,0:T(8,128)(2,1)S(1)} collective-permute-done((bf16[2,512,256]{2,1,0:T(8,128)(2,1)S(1)}, bf16[2,512,256]{2,1,0:T(8,128)(2,1)S(1)}, u32[]{:S(2)}, u32[]{:S(2)}) %collective-permute-start.1) | collective-permute-done | bytes 524320 | tf_op jit(solution)/shard_map/ppermute | solution.py:457
  16.0 6.8 %collective-permute-done.5.refs_2_ = bf16[2,512,256]{2,1,0:T(8,128)(2,1)S(1)} collective-permute-done((bf16[2,512,256]{2,1,0:T(8,128)(2,1)S(1)}, bf16[2,512,256]{2,1,0:T(8,128)(2,1)S(1)}, u32[]{:S(2)}, u32[]{:S(2)}) %collective-permute-start.5) | collective-permute-done | bytes 524320 | tf_op jit(solution)/shard_map/ppermute | solution.py:457
  22.8 5.6 %collective-permute-done.4.refs_2_ = bf16[2,512,256]{2,1,0:T(8,128)(2,1)S(1)} collective-permute-done((bf16[2,512,256]{2,1,0:T(8,128)(2,1)S(1)}, bf16[2,512,256]{2,1,0:T(8,128)(2,1)S(1)}, u32[]{:S(2)}, u32[]{:S(2)}) %collective-permute-start.4) | collective-permute-done | bytes 524320 | tf_op jit(solution)/shard_map/ppermute | solution.py:457
  31.2 9.6 %collective-permute-done.7.refs_3_ = bf16[2,512,256]{2,1,0:T(8,128)(2,1)S(1)} collective-permute-done((bf16[2,512,256]{2,1,0:T(8,128)(2,1)S(1)}, bf16[2,512,256]{2,1,0:T(8,128)(2,1)S(1)}, u32[]{:S(2)}, u32[]{:S(2)}) %collective-permute-start.7) | collective-permute-done | bytes 524320 | tf_op jit(solution)/shard_map/ppermute | solution.py:41
  40.8 2.8 %collective-permute-done.8.pair_ref.refs_0_ = bf16[2,512,256]{2,1,0:T(8,128)(2,1)S(1)} collective-permute-done((bf16[2,512,256]{2,1,0:T(8,128)(2,1)S(1)}, bf16[2,512,256]{2,1,0:T(8,128)(2,1)S(1)}, u32[]{:S(2)}, u32[]{:S(2)}) %collective-permute-start.8) | collective-permute-done | bytes 524320 | tf_op jit(solution)/shard_map/ppermute | solution.py:457
  45.4 9.3 %collective-permute-done.10.refs_1_ = bf16[1,512,256]{2,1,0:T(8,128)(2,1)S(1)} collective-permute-done((bf16[1,512,256]{2,1,0:T(8,128)(2,1)S(1)}, bf16[1,512,256]{2,1,0:T(8,128)(2,1)S(1)}, u32[]{:S(2)}, u32[]{:S(2)}) %collective-permute-start.10) | collective-permute-done | bytes 262176 | tf_op jit(solution)/shard_map/ppermute | solution.py:457
  54.7 1.3 collective-permute-start.16
  56.2 2.4 %collective-permute-start.24 = (bf16[512,512]{1,0:T(8,128)(2,1)S(1)}, bf16[512,512]{1,0:T(8,128)(2,1)S(1)}, u32[]{:S(2)}, u32[]{:S(2)}) collective-permute-start(bf16[512,512]{1,0:T(8,128)(2,1)S(1)} %copy-done.1), channel_id=1, source_target_pairs={{0,2},{2,0},{4,6},{6,4},{8,10},{10,8},{12,14},{14,12},{16,18},{18,... | collective-permute-start | bytes 1572872 | tf_op jit(solution)/shard_map/ppermute | solution.py:37
  58.7 3.3 %project.10.refs_2_ = f32[2,256,256]{2,1,0:T(8,128)S(1)} custom-call(s32[19]{0:T(128)S(1)} %stack.76.index_ref, bf16[256,8192]{1,0:T(8,128)(2,1)} %own_ref.11, bf16[256,8192]{1,0:T(8,128)(2,1)S(1)} %collective-permute-done.3.other_ref, bf16[1,512,256]{2,1,0:T(8,128)(2,1)S(1)} %get-tuple-element.37.first_ref.refs_0_, ...), custom_call_target="tpu_custom_call" | custom-call | tf_op jit(solution)/shard_map/project/pallas_call | solution.py:312
  62.0 2.5 %project.11 = (f32[256,256]{1,0:T(8,128)S(1)}, f32[256,256]{1,0:T(8,128)S(1)}) custom-call(s32[19]{0:T(128)S(1)} %stack.76.index_ref, bf16[256,8192]{1,0:T(8,128)(2,1)} %own_ref.11, bf16[256,8192]{1,0:T(8,128)(2,1)S(1)} %collective-permute-done.3.other_ref, bf16[2,512,256]{2,1,0:T(8,128)(2,1)S(1)} %collective-permute-done.8.pair_ref.refs_0_, ...), custom_call_target="tpu_custom_call" | custom-call | tf_op jit(solution)/shard_map/project/pallas_call | solution.py:312
  64.6 1.3 %collective-permute-start.12 = (bf16[1,512,256]{2,1,0:T(8,128)(2,1)S(1)}, bf16[1,512,256]{2,1,0:T(8,128)(2,1)S(1)}, u32[]{:S(2)}, u32[]{:S(2)}) collective-permute-start(bf16[1,512,256]{2,1,0:T(8,128)(2,1)S(1)} %first_of.3), channel_id=1, source_target_pairs={{0,8},{2,6},{8,16},{10,2},{16,24},{18,10},{24,28},{26,18},{28,20},... | collective-permute-start | bytes 786440 | tf_op jit(solution)/shard_map/ppermute | solution.py:457
  66.2 1.9 %collective-permute-done.14.refs_1_ = bf16[2,512,256]{2,1,0:T(8,128)(2,1)S(1)} collective-permute-done((bf16[2,512,256]{2,1,0:T(8,128)(2,1)S(1)}, bf16[2,512,256]{2,1,0:T(8,128)(2,1)S(1)}, u32[]{:S(2)}, u32[]{:S(2)}) %collective-permute-start.14) | collective-permute-done | bytes 524320 | tf_op jit(solution)/shard_map/ppermute | solution.py:41
  68.2 2.0 %collective-permute-done.12.refs_0_ = bf16[1,512,256]{2,1,0:T(8,128)(2,1)S(1)} collective-permute-done((bf16[1,512,256]{2,1,0:T(8,128)(2,1)S(1)}, bf16[1,512,256]{2,1,0:T(8,128)(2,1)S(1)}, u32[]{:S(2)}, u32[]{:S(2)}) %collective-permute-start.12) | collective-permute-done | bytes 262176 | tf_op jit(solution)/shard_map/ppermute | solution.py:457
  72.5 10.9 %collective-permute-start.21 = (bf16[2,256,256]{2,1,0:T(8,128)(2,1)S(1)}, bf16[2,256,256]{2,1,0:T(8,128)(2,1)S(1)}, u32[]{:S(2)}, u32[]{:S(2)}) collective-permute-start(bf16[2,256,256]{2,1,0:T(8,128)(2,1)S(1)} %join_row.1.refs_2_), channel_id=1, source_target_pairs={{0,16},{4,20},{8,24},{12,28},{16,26},{20,30},{24,18},{28,22},{26,1... | collective-permute-start | bytes 786440 | tf_op jit(solution)/shard_map/ppermute | solution.py:444
  83.4 1.9 %collective-permute-start.20 = (bf16[2,256,256]{2,1,0:T(8,128)(2,1)S(1)}, bf16[2,256,256]{2,1,0:T(8,128)(2,1)S(1)}, u32[]{:S(2)}, u32[]{:S(2)}) collective-permute-start(bf16[2,256,256]{2,1,0:T(8,128)(2,1)S(1)} %join_row.1.refs_2_), channel_id=1, source_target_pairs={{0,8},{4,12},{8,16},{12,20},{16,24},{20,28},{24,26},{28,30},{26,18... | collective-permute-start | bytes 786440 | tf_op jit(solution)/shard_map/ppermute | solution.py:444
  85.3 1.5 %collective-permute-start.25 = (bf16[512,512]{1,0:T(8,128)(2,1)S(1)}, bf16[512,512]{1,0:T(8,128)(2,1)S(1)}, u32[]{:S(2)}, u32[]{:S(2)}) collective-permute-start(bf16[512,512]{1,0:T(8,128)(2,1)S(1)} %collective-permute-done.24), channel_id=1, source_target_pairs={{0,8},{2,6},{8,16},{10,2},{16,24},{18,10},{24,28},{26,18},{28,20},... | collective-permute-start | bytes 1572872 | tf_op jit(solution)/shard_map/ppermute | solution.py:457
  86.8 2.6 %project.6.refs_2_ = f32[2,256,512]{2,1,0:T(8,128)S(1)} custom-call(s32[19]{0:T(128)S(1)} %stack.76.index_ref, bf16[256,8192]{1,0:T(8,128)(2,1)} %own_ref.11, bf16[256,8192]{1,0:T(8,128)(2,1)S(1)} %collective-permute-done.3.other_ref, bf16[1,512,256]{2,1,0:T(8,128)(2,1)S(1)} %get-tuple-element.41.first_ref.refs_0_, ...), custom_call_target="tpu_custom_call" | custom-call | tf_op jit(solution)/shard_map/project/pallas_call | solution.py:312
  89.5 2.2 %project.7.refs_2_ = f32[2,256,512]{2,1,0:T(8,128)S(1)} custom-call(s32[19]{0:T(128)S(1)} %stack.76.index_ref, bf16[256,8192]{1,0:T(8,128)(2,1)} %own_ref.11, bf16[256,8192]{1,0:T(8,128)(2,1)S(1)} %collective-permute-done.3.other_ref, bf16[2,512,256]{2,1,0:T(8,128)(2,1)S(1)} %collective-permute-done.6.refs_0_, ...), custom_call_target="tpu_custom_call" | custom-call | tf_op jit(solution)/shard_map/project/pallas_call | solution.py:312
  91.7 2.2 %project.8.refs_2_ = f32[2,256,512]{2,1,0:T(8,128)S(1)} custom-call(s32[19]{0:T(128)S(1)} %stack.76.index_ref, bf16[256,8192]{1,0:T(8,128)(2,1)} %own_ref.11, bf16[256,8192]{1,0:T(8,128)(2,1)S(1)} %collective-permute-done.3.other_ref, bf16[2,512,256]{2,1,0:T(8,128)(2,1)S(1)} %collective-permute-done.9.pair_ref.refs_0_, ...), custom_call_target="tpu_custom_call" | custom-call | tf_op jit(solution)/shard_map/project/pallas_call | solution.py:312
  93.9 1.9 %project.9 = (f32[256,512]{1,0:T(8,128)S(1)}, f32[256,512]{1,0:T(8,128)S(1)}) custom-call(s32[19]{0:T(128)S(1)} %stack.76.index_ref, bf16[256,8192]{1,0:T(8,128)(2,1)} %own_ref.11, bf16[256,8192]{1,0:T(8,128)(2,1)S(1)} %collective-permute-done.3.other_ref, bf16[1,512,256]{2,1,0:T(8,128)(2,1)S(1)} %collective-permute-done.12.refs_0_, ...), custom_call_target="tpu_custom_call" | custom-call | tf_op jit(solution)/shard_map/project/pallas_call | solution.py:312
  99.3 6.0 %collective-permute-done.22.refs_0_ = bf16[512,512]{1,0:T(8,128)(2,1)S(1)} collective-permute-done((bf16[512,512]{1,0:T(8,128)(2,1)S(1)}, bf16[512,512]{1,0:T(8,128)(2,1)S(1)}, u32[]{:S(2)}, u32[]{:S(2)}) %collective-permute-start.22) | collective-permute-done | bytes 524320 | tf_op jit(solution)/shard_map/ppermute | solution.py:457
  105.4 3.9 %attend.1.mixed_ref = bf16[256,512]{1,0:T(8,128)(2,1)S(1)} custom-call(s32[19]{0:T(128)S(1)} %stack.76.index_ref, bf16[256,512]{1,0:T(8,128)(2,1)S(1)} %rotate_sums.2.query_ref, s32[1,1280]{1,0:T(1,128)S(1)} %bitcast.29, bf16[2,256,256]{2,1,0:T(8,128)(2,1)S(1)} %collective-permute-done.21.refs_0_, bf16[2,256,256]{2,1,0:T(8,128)(2,1)S(1)} %collective-permute-done.20.refs_1_, ...), custom_call_target="tpu_custom_call" | custom-call | tf_op jit(solution)/shard_map/attend/pallas_call | solution.py:182
  109.3 1.3 %collective-permute-start.23 = (bf16[256,512]{1,0:T(8,128)(2,1)S(1)}, bf16[256,512]{1,0:T(8,128)(2,1)S(1)}, u32[]{:S(2)}, u32[]{:S(2)}) collective-permute-start(bf16[256,512]{1,0:T(8,128)(2,1)S(1)} %attend.1.mixed_ref), channel_id=1, source_target_pairs={{0,2},{2,0},{4,6},{6,4},{8,10},{10,8},{12,14},{14,12},{16,18},{18,... | collective-permute-start | bytes 786440 | tf_op jit(solution)/shard_map/ppermute | solution.py:37
  111.8 2.8 %columns_of.2 = (bf16[256,8192]{1,0:T(8,128)(2,1)}, bf16[256,2560]{1,0:T(8,128)(2,1)S(1)}) custom-call(s32[19]{0:T(128)S(1)} %stack.76.index_ref, bf16[256,512]{1,0:T(8,128)(2,1)S(1)} %attend.1.mixed_ref, bf16[256,512]{1,0:T(8,128)(2,1)S(1)} %collective-permute-done.23.returned_ref, bf16[512,512]{1,0:T(8,128)(2,1)S(1)} %copy-done.1, ...), custom_call_target="tpu_custom_call" | custom-call | tf_op jit(solution)/shard_map/columns_of/pallas_call | solution.py:368
  114.6 2.0 %collective-permute-start.30 = (bf16[256,2560]{1,0:T(8,128)(2,1)S(1)}, bf16[256,2560]{1,0:T(8,128)(2,1)S(1)}, u32[]{:S(2)}, u32[]{:S(2)}) collective-permute-start(bf16[256,2560]{1,0:T(8,128)(2,1)S(1)} %get-tuple-element.67), channel_id=1, source_target_pairs={{0,2},{2,0},{4,6},{6,4},{8,10},{10,8},{12,14},{14,12},{16,18},{18,... | collective-permute-start | bytes 3932168 | tf_op jit(solution)/shard_map/ppermute | solution.py:37
  116.6 2.8 %collective-permute-done.27.refs_1_ = bf16[512,512]{1,0:T(8,128)(2,1)S(1)} collective-permute-done((bf16[512,512]{1,0:T(8,128)(2,1)S(1)}, bf16[512,512]{1,0:T(8,128)(2,1)S(1)}, u32[]{:S(2)}, u32[]{:S(2)}) %collective-permute-start.27) | collective-permute-done | bytes 524320 | tf_op jit(solution)/shard_map/ppermute | solution.py:457
  119.3 5.6 %collective-permute-done.28.refs_2_ = bf16[512,512]{1,0:T(8,128)(2,1)S(1)} collective-permute-done((bf16[512,512]{1,0:T(8,128)(2,1)S(1)}, bf16[512,512]{1,0:T(8,128)(2,1)S(1)}, u32[]{:S(2)}, u32[]{:S(2)}) %collective-permute-start.28) | collective-permute-done | bytes 524320 | tf_op jit(solution)/shard_map/ppermute | solution.py:457
  125.0 2.3 %columns_of.3 = (bf16[256,8192]{1,0:T(8,128)(2,1)}, bf16[256,1536]{1,0:T(8,128)(2,1)S(1)}) custom-call(s32[19]{0:T(128)S(1)} %stack.76.index_ref, bf16[256,512]{1,0:T(8,128)(2,1)S(1)} %attend.1.mixed_ref, bf16[256,512]{1,0:T(8,128)(2,1)S(1)} %collective-permute-done.23.returned_ref, ...), custom_call_target="tpu_custom_call", output_to_operand_aliasing={{0}: (6, {})} | custom-call | tf_op jit(solution)/shard_map/columns_of/pallas_call | solution.py:368
  127.2 2.2 %collective-permute-start.29 = (bf16[256,1536]{1,0:T(8,128)(2,1)S(1)}, bf16[256,1536]{1,0:T(8,128)(2,1)S(1)}, u32[]{:S(2)}, u32[]{:S(2)}) collective-permute-start(bf16[256,1536]{1,0:T(8,128)(2,1)S(1)} %get-tuple-element.66), channel_id=1, source_target_pairs={{0,2},{2,0},{4,6},{6,4},{8,10},{10,8},{12,14},{14,12},{16,18},{18,... | collective-permute-start | bytes 2359304 | tf_op jit(solution)/shard_map/ppermute | solution.py:37
  129.4 1.6 %place_columns.2._ = bf16[256,8192]{1,0:T(8,128)(2,1)} custom-call(s32[19]{0:T(128)S(1)} %stack.76.index_ref, bf16[256,2560]{1,0:T(8,128)(2,1)S(1)} %collective-permute-done.30.came_ref, bf16[256,8192]{1,0:T(8,128)(2,1)} %get-tuple-element.68._), custom_call_target="tpu_custom_call", output_to_operand_aliasing={{}: (2, {})} | custom-call | tf_op jit(solution)/shard_map/place_columns/pallas_call | solution.py:399
  131.3 1.4 %place_columns.3 = bf16[256,8192]{1,0:T(8,128)(2,1)} custom-call(s32[19]{0:T(128)S(1)} %stack.76.index_ref, bf16[256,1536]{1,0:T(8,128)(2,1)S(1)} %collective-permute-done.29.came_ref, bf16[256,8192]{1,0:T(8,128)(2,1)} %place_columns.2._), custom_call_target="tpu_custom_call", output_to_operand_aliasing={{}: (2, {})} | custom-call | tf_op jit(solution)/shard_map/place_columns/pallas_call | solution.py:399
  (64 shorter events, 20.5 us)
Async XLA Ops:
  0.0 54.7 %copy-start.1 = (bf16[512,512]{1,0:T(8,128)(2,1)S(1)}, bf16[512,512]{1,0:T(8,128)(2,1)}, u32[]{:S(2)}) copy-start(bf16[512,512]{1,0:T(8,128)(2,1)} %refs_0_.1) | copy-start | bytes 1572868
  1.3 1.9 %collective-permute-start = (bf16[1,512,256]{2,1,0:T(8,128)(2,1)S(1)}, bf16[1,512,256]{2,1,0:T(8,128)(2,1)S(1)}, u32[]{:S(2)}, u32[]{:S(2)}) collective-permute-start(bf16[1,512,256]{2,1,0:T(8,128)(2,1)S(1)} %get-tuple-element.37.first_ref.refs_0_), channel_id=1, source_target_pairs={{0,2},{2,0},{4,6},{6,4},{8,10},{10,8},{12,14},{14,12},{16,18},{18,... | collective-permute-start | bytes 786440 | tf_op jit(solution)/shard_map/ppermute | solution.py:37
  3.2 8.4 %collective-permute-start.1 = (bf16[2,512,256]{2,1,0:T(8,128)(2,1)S(1)}, bf16[2,512,256]{2,1,0:T(8,128)(2,1)S(1)}, u32[]{:S(2)}, u32[]{:S(2)}) collective-permute-start(bf16[2,512,256]{2,1,0:T(8,128)(2,1)S(1)} %both_of.2), channel_id=1, source_target_pairs={{0,8},{2,6},{8,16},{10,2},{16,24},{18,10},{24,28},{26,18},{28,20},... | collective-permute-start | bytes 1572872 | tf_op jit(solution)/shard_map/ppermute | solution.py:457
  11.6 2.4 %collective-permute-start.2 = (bf16[1,512,256]{2,1,0:T(8,128)(2,1)S(1)}, bf16[1,512,256]{2,1,0:T(8,128)(2,1)S(1)}, u32[]{:S(2)}, u32[]{:S(2)}) collective-permute-start(bf16[1,512,256]{2,1,0:T(8,128)(2,1)S(1)} %get-tuple-element.41.first_ref.refs_0_), channel_id=1, source_target_pairs={{0,2},{2,0},{4,6},{6,4},{8,10},{10,8},{12,14},{14,12},{16,18},{18,... | collective-permute-start | bytes 786440 | tf_op jit(solution)/shard_map/ppermute | solution.py:37
  14.0 44.7 %collective-permute-start.3 = (bf16[256,8192]{1,0:T(8,128)(2,1)}, bf16[256,8192]{1,0:T(8,128)(2,1)S(1)}, u32[]{:S(2)}, u32[]{:S(2)}) collective-permute-start(bf16[256,8192]{1,0:T(8,128)(2,1)} %own_ref.11), channel_id=1, source_target_pairs={{0,2},{2,0},{4,6},{6,4},{8,10},{10,8},{12,14},{14,12},{16,18},{18,... | collective-permute-start | bytes 12582920 | tf_op jit(solution)/shard_map/ppermute | solution.py:37
  14.4 8.3 %collective-permute-start.5 = (bf16[2,512,256]{2,1,0:T(8,128)(2,1)S(1)}, bf16[2,512,256]{2,1,0:T(8,128)(2,1)S(1)}, u32[]{:S(2)}, u32[]{:S(2)}) collective-permute-start(bf16[2,512,256]{2,1,0:T(8,128)(2,1)S(1)} %collective-permute-done.1.refs_1_), channel_id=1, source_target_pairs={{0,8},{2,6},{8,16},{10,2},{16,24},{18,10},{24,28},{26,18},{28,20},... | collective-permute-start | bytes 1572872 | tf_op jit(solution)/shard_map/ppermute | solution.py:457
  15.7 12.6 %collective-permute-start.4 = (bf16[2,512,256]{2,1,0:T(8,128)(2,1)S(1)}, bf16[2,512,256]{2,1,0:T(8,128)(2,1)S(1)}, u32[]{:S(2)}, u32[]{:S(2)}) collective-permute-start(bf16[2,512,256]{2,1,0:T(8,128)(2,1)S(1)} %both_of.3), channel_id=1, source_target_pairs={{0,8},{2,6},{8,16},{10,2},{16,24},{18,10},{24,28},{26,18},{28,20},... | collective-permute-start | bytes 1572872 | tf_op jit(solution)/shard_map/ppermute | solution.py:457
  28.4 12.4 %collective-permute-start.7 = (bf16[2,512,256]{2,1,0:T(8,128)(2,1)S(1)}, bf16[2,512,256]{2,1,0:T(8,128)(2,1)S(1)}, u32[]{:S(2)}, u32[]{:S(2)}) collective-permute-start(bf16[2,512,256]{2,1,0:T(8,128)(2,1)S(1)} %collective-permute-done.4.refs_2_), channel_id=1, source_target_pairs={{0,1},{1,0},{2,3},{3,2},{4,5},{5,4},{6,7},{7,6},{8,9},{9,8},{10,11... | collective-permute-start | bytes 1572872 | tf_op jit(solution)/shard_map/ppermute | solution.py:41
  29.6 11.2 %collective-permute-start.6 = (bf16[2,512,256]{2,1,0:T(8,128)(2,1)S(1)}, bf16[2,512,256]{2,1,0:T(8,128)(2,1)S(1)}, u32[]{:S(2)}, u32[]{:S(2)}) collective-permute-start(bf16[2,512,256]{2,1,0:T(8,128)(2,1)S(1)} %collective-permute-done.4.refs_2_), channel_id=1, source_target_pairs={{0,8},{2,6},{8,16},{10,2},{16,24},{18,10},{24,28},{26,18},{28,20},... | collective-permute-start | bytes 1572872 | tf_op jit(solution)/shard_map/ppermute | solution.py:457
  30.9 12.6 %collective-permute-start.8 = (bf16[2,512,256]{2,1,0:T(8,128)(2,1)S(1)}, bf16[2,512,256]{2,1,0:T(8,128)(2,1)S(1)}, u32[]{:S(2)}, u32[]{:S(2)}) collective-permute-start(bf16[2,512,256]{2,1,0:T(8,128)(2,1)S(1)} %collective-permute-done.5.refs_2_), channel_id=1, source_target_pairs={{0,8},{2,6},{8,16},{10,2},{16,24},{18,10},{24,28},{26,18},{28,20},... | collective-permute-start | bytes 1572872 | tf_op jit(solution)/shard_map/ppermute | solution.py:457
  43.6 12.4 %collective-permute-start.9 = (bf16[2,512,256]{2,1,0:T(8,128)(2,1)S(1)}, bf16[2,512,256]{2,1,0:T(8,128)(2,1)S(1)}, u32[]{:S(2)}, u32[]{:S(2)}) collective-permute-start(bf16[2,512,256]{2,1,0:T(8,128)(2,1)S(1)} %collective-permute-done.6.refs_0_), channel_id=1, source_target_pairs={{0,8},{2,6},{8,16},{10,2},{16,24},{18,10},{24,28},{26,18},{28,20},... | collective-permute-start | bytes 1572872 | tf_op jit(solution)/shard_map/ppermute | solution.py:457
  44.9 9.8 %collective-permute-start.10 = (bf16[1,512,256]{2,1,0:T(8,128)(2,1)S(1)}, bf16[1,512,256]{2,1,0:T(8,128)(2,1)S(1)}, u32[]{:S(2)}, u32[]{:S(2)}) collective-permute-start(bf16[1,512,256]{2,1,0:T(8,128)(2,1)S(1)} %first_of.2), channel_id=1, source_target_pairs={{0,8},{2,6},{8,16},{10,2},{16,24},{18,10},{24,28},{26,18},{28,20},... | collective-permute-start | bytes 786440 | tf_op jit(solution)/shard_map/ppermute | solution.py:457
  45.2 19.4 %collective-permute-start.11 = (bf16[2,512,256]{2,1,0:T(8,128)(2,1)S(1)}, bf16[2,512,256]{2,1,0:T(8,128)(2,1)S(1)}, u32[]{:S(2)}, u32[]{:S(2)}) collective-permute-start(bf16[2,512,256]{2,1,0:T(8,128)(2,1)S(1)} %collective-permute-done.6.refs_0_), channel_id=1, source_target_pairs={{0,1},{1,0},{2,3},{3,2},{4,5},{5,4},{6,7},{7,6},{8,9},{9,8},{10,11... | collective-permute-start | bytes 1572872 | tf_op jit(solution)/shard_map/ppermute | solution.py:41
  54.7 11.5 %collective-permute-start.16 = (bf16[512,512]{1,0:T(8,128)(2,1)S(1)}, bf16[512,512]{1,0:T(8,128)(2,1)S(1)}, u32[]{:S(2)}, u32[]{:S(2)}) collective-permute-start(bf16[512,512]{1,0:T(8,128)(2,1)S(1)} %copy-done.1), channel_id=1, source_target_pairs={{0,8},{2,6},{8,16},{10,2},{16,24},{18,10},{24,28},{26,18},{28,20},... | collective-permute-start | bytes 1572872 | tf_op jit(solution)/shard_map/ppermute | solution.py:457
  56.0 12.1 %collective-permute-start.14 = (bf16[2,512,256]{2,1,0:T(8,128)(2,1)S(1)}, bf16[2,512,256]{2,1,0:T(8,128)(2,1)S(1)}, u32[]{:S(2)}, u32[]{:S(2)}) collective-permute-start(bf16[2,512,256]{2,1,0:T(8,128)(2,1)S(1)} %collective-permute-done.9.pair_ref.refs_0_), channel_id=1, source_target_pairs={{0,1},{1,0},{2,3},{3,2},{4,5},{5,4},{6,7},{7,6},{8,9},{9,8},{10,11... | collective-permute-start | bytes 1572872 | tf_op jit(solution)/shard_map/ppermute | solution.py:41
  56.2 11.9 %collective-permute-start.24 = (bf16[512,512]{1,0:T(8,128)(2,1)S(1)}, bf16[512,512]{1,0:T(8,128)(2,1)S(1)}, u32[]{:S(2)}, u32[]{:S(2)}) collective-permute-start(bf16[512,512]{1,0:T(8,128)(2,1)S(1)} %copy-done.1), channel_id=1, source_target_pairs={{0,2},{2,0},{4,6},{6,4},{8,10},{10,8},{12,14},{14,12},{16,18},{18,... | collective-permute-start | bytes 1572872 | tf_op jit(solution)/shard_map/ppermute | solution.py:37
  64.5 1.6 %collective-permute-start.17 = (f32[256,256]{1,0:T(8,128)S(1)}, f32[256,256]{1,0:T(8,128)S(1)}, u32[]{:S(2)}, u32[]{:S(2)}) collective-permute-start(f32[256,256]{1,0:T(8,128)S(1)} %get-tuple-element.55), channel_id=1, source_target_pairs={{0,2},{2,0},{4,6},{6,4},{8,10},{10,8},{12,14},{14,12},{16,18},{18,... | collective-permute-start | bytes 786440 | tf_op jit(solution)/shard_map/ppermute | solution.py:37
  64.6 5.6 %collective-permute-start.12 = (bf16[1,512,256]{2,1,0:T(8,128)(2,1)S(1)}, bf16[1,512,256]{2,1,0:T(8,128)(2,1)S(1)}, u32[]{:S(2)}, u32[]{:S(2)}) collective-permute-start(bf16[1,512,256]{2,1,0:T(8,128)(2,1)S(1)} %first_of.3), channel_id=1, source_target_pairs={{0,8},{2,6},{8,16},{10,2},{16,24},{18,10},{24,28},{26,18},{28,20},... | collective-permute-start | bytes 786440 | tf_op jit(solution)/shard_map/ppermute | solution.py:457
  68.1 28.6 %collective-permute-start.18 = (bf16[512,512]{1,0:T(8,128)(2,1)S(1)}, bf16[512,512]{1,0:T(8,128)(2,1)S(1)}, u32[]{:S(2)}, u32[]{:S(2)}) collective-permute-start(bf16[512,512]{1,0:T(8,128)(2,1)S(1)} %collective-permute-done.16.refs_1_), channel_id=1, source_target_pairs={{0,8},{2,6},{8,16},{10,2},{16,24},{18,10},{24,28},{26,18},{28,20},... | collective-permute-start | bytes 1572872 | tf_op jit(solution)/shard_map/ppermute | solution.py:457
  68.2 3.8 %collective-permute-start.19 = (bf16[256,256]{1,0:T(8,128)(2,1)S(1)}, bf16[256,256]{1,0:T(8,128)(2,1)S(1)}, u32[]{:S(2)}, u32[]{:S(2)}) collective-permute-start(bf16[256,256]{1,0:T(8,128)(2,1)S(1)} %rotate_sums.3.own_ref), channel_id=1, source_target_pairs={{0,4},{2,6},{4,0},{6,2},{8,12},{10,14},{12,8},{14,10},{16,20},{18,... | collective-permute-start | bytes 393224 | tf_op jit(solution)/shard_map/ppermute | solution.py:436
  70.2 23.6 %collective-permute-start.13 = (bf16[1,512,256]{2,1,0:T(8,128)(2,1)S(1)}, bf16[1,512,256]{2,1,0:T(8,128)(2,1)S(1)}, u32[]{:S(2)}, u32[]{:S(2)}) collective-permute-start(bf16[1,512,256]{2,1,0:T(8,128)(2,1)S(1)} %collective-permute-done.12.refs_0_), channel_id=1, source_target_pairs={{0,1},{1,0},{2,3},{3,2},{4,5},{5,4},{6,7},{7,6},{8,9},{9,8},{10,11... | collective-permute-start | bytes 786440 | tf_op jit(solution)/shard_map/ppermute | solution.py:41
  72.5 24.2 %collective-permute-start.21 = (bf16[2,256,256]{2,1,0:T(8,128)(2,1)S(1)}, bf16[2,256,256]{2,1,0:T(8,128)(2,1)S(1)}, u32[]{:S(2)}, u32[]{:S(2)}) collective-permute-start(bf16[2,256,256]{2,1,0:T(8,128)(2,1)S(1)} %join_row.1.refs_2_), channel_id=1, source_target_pairs={{0,16},{4,20},{8,24},{12,28},{16,26},{20,30},{24,18},{28,22},{26,1... | collective-permute-start | bytes 786440 | tf_op jit(solution)/shard_map/ppermute | solution.py:444
  83.4 13.3 %collective-permute-start.20 = (bf16[2,256,256]{2,1,0:T(8,128)(2,1)S(1)}, bf16[2,256,256]{2,1,0:T(8,128)(2,1)S(1)}, u32[]{:S(2)}, u32[]{:S(2)}) collective-permute-start(bf16[2,256,256]{2,1,0:T(8,128)(2,1)S(1)} %join_row.1.refs_2_), channel_id=1, source_target_pairs={{0,8},{4,12},{8,16},{12,20},{16,24},{20,28},{24,26},{28,30},{26,18... | collective-permute-start | bytes 786440 | tf_op jit(solution)/shard_map/ppermute | solution.py:444
  85.3 12.6 %collective-permute-start.25 = (bf16[512,512]{1,0:T(8,128)(2,1)S(1)}, bf16[512,512]{1,0:T(8,128)(2,1)S(1)}, u32[]{:S(2)}, u32[]{:S(2)}) collective-permute-start(bf16[512,512]{1,0:T(8,128)(2,1)S(1)} %collective-permute-done.24), channel_id=1, source_target_pairs={{0,8},{2,6},{8,16},{10,2},{16,24},{18,10},{24,28},{26,18},{28,20},... | collective-permute-start | bytes 1572872 | tf_op jit(solution)/shard_map/ppermute | solution.py:457
  95.8 3.4 %collective-permute-start.15 = (f32[256,512]{1,0:T(8,128)S(1)}, f32[256,512]{1,0:T(8,128)S(1)}, u32[]{:S(2)}, u32[]{:S(2)}) collective-permute-start(f32[256,512]{1,0:T(8,128)S(1)} %get-tuple-element.50), channel_id=1, source_target_pairs={{0,2},{2,0},{4,6},{6,4},{8,10},{10,8},{12,14},{14,12},{16,18},{18,... | collective-permute-start | bytes 1572872 | tf_op jit(solution)/shard_map/ppermute | solution.py:37
  96.7 8.7 %collective-permute-start.22 = (bf16[512,512]{1,0:T(8,128)(2,1)S(1)}, bf16[512,512]{1,0:T(8,128)(2,1)S(1)}, u32[]{:S(2)}, u32[]{:S(2)}) collective-permute-start(bf16[512,512]{1,0:T(8,128)(2,1)S(1)} %collective-permute-done.18.refs_3_), channel_id=1, source_target_pairs={{0,8},{2,6},{8,16},{10,2},{16,24},{18,10},{24,28},{26,18},{28,20},... | collective-permute-start | bytes 1572872 | tf_op jit(solution)/shard_map/ppermute | solution.py:457
  97.9 13.1 %collective-permute-start.26 = (bf16[512,512]{1,0:T(8,128)(2,1)S(1)}, bf16[512,512]{1,0:T(8,128)(2,1)S(1)}, u32[]{:S(2)}, u32[]{:S(2)}) collective-permute-start(bf16[512,512]{1,0:T(8,128)(2,1)S(1)} %collective-permute-done.25.refs_2_), channel_id=1, source_target_pairs={{0,8},{2,6},{8,16},{10,2},{16,24},{18,10},{24,28},{26,18},{28,20},... | collective-permute-start | bytes 1572872 | tf_op jit(solution)/shard_map/ppermute | solution.py:457
  109.3 2.5 %collective-permute-start.23 = (bf16[256,512]{1,0:T(8,128)(2,1)S(1)}, bf16[256,512]{1,0:T(8,128)(2,1)S(1)}, u32[]{:S(2)}, u32[]{:S(2)}) collective-permute-start(bf16[256,512]{1,0:T(8,128)(2,1)S(1)} %attend.1.mixed_ref), channel_id=1, source_target_pairs={{0,2},{2,0},{4,6},{6,4},{8,10},{10,8},{12,14},{14,12},{16,18},{18,... | collective-permute-start | bytes 786440 | tf_op jit(solution)/shard_map/ppermute | solution.py:37
  111.0 8.3 %collective-permute-start.27 = (bf16[512,512]{1,0:T(8,128)(2,1)S(1)}, bf16[512,512]{1,0:T(8,128)(2,1)S(1)}, u32[]{:S(2)}, u32[]{:S(2)}) collective-permute-start(bf16[512,512]{1,0:T(8,128)(2,1)S(1)} %collective-permute-done.26.refs_4_), channel_id=1, source_target_pairs={{0,8},{2,6},{8,16},{10,2},{16,24},{18,10},{24,28},{26,18},{28,20},... | collective-permute-start | bytes 1572872 | tf_op jit(solution)/shard_map/ppermute | solution.py:457
  111.0 13.9 %collective-permute-start.28 = (bf16[512,512]{1,0:T(8,128)(2,1)S(1)}, bf16[512,512]{1,0:T(8,128)(2,1)S(1)}, u32[]{:S(2)}, u32[]{:S(2)}) collective-permute-start(bf16[512,512]{1,0:T(8,128)(2,1)S(1)} %collective-permute-done.22.refs_0_), channel_id=1, source_target_pairs={{0,8},{2,6},{8,16},{10,2},{16,24},{18,10},{24,28},{26,18},{28,20},... | collective-permute-start | bytes 1572872 | tf_op jit(solution)/shard_map/ppermute | solution.py:457
  114.6 14.8 %collective-permute-start.30 = (bf16[256,2560]{1,0:T(8,128)(2,1)S(1)}, bf16[256,2560]{1,0:T(8,128)(2,1)S(1)}, u32[]{:S(2)}, u32[]{:S(2)}) collective-permute-start(bf16[256,2560]{1,0:T(8,128)(2,1)S(1)} %get-tuple-element.67), channel_id=1, source_target_pairs={{0,2},{2,0},{4,6},{6,4},{8,10},{10,8},{12,14},{14,12},{16,18},{18,... | collective-permute-start | bytes 3932168 | tf_op jit(solution)/shard_map/ppermute | solution.py:37
  127.2 4.1 %collective-permute-start.29 = (bf16[256,1536]{1,0:T(8,128)(2,1)S(1)}, bf16[256,1536]{1,0:T(8,128)(2,1)S(1)}, u32[]{:S(2)}, u32[]{:S(2)}) collective-permute-start(bf16[256,1536]{1,0:T(8,128)(2,1)S(1)} %get-tuple-element.66), channel_id=1, source_target_pairs={{0,2},{2,0},{4,6},{6,4},{8,10},{10,8},{12,14},{14,12},{16,18},{18,... | collective-permute-start | bytes 2359304 | tf_op jit(solution)/shard_map/ppermute | solution.py:37
  (1 other events, 2.4 us)

commit v4 on v3

--- a/solution.py
+++ b/solution.py
@@ -12,6 +12,65 @@
 ROPE_BASE = 500000.0
 RING_LIMIT = 16
 VMEM_LIMIT = 16 * 1024 * 1024
+HALVED = True
+PLAN = (
+    "first0",
+    "near0",
+    "near1",
+    "common0",
+    "tables0",
+    "second0 near1",
+    "tokens0 near1 common0",
+    "other0",
+    "near2",
+    "common1 near1",
+    "far1",
+    "first1 near2",
+    "near3",
+    "common2 near2 far1",
+    "far2",
+    "second1 near3",
+    "cross1",
+    "queries1 first1",
+    "near4 far2",
+    "common3 near3 far2 queries1",
+    "far3",
+    "first2 near4",
+    "queries2 second1",
+    "common4 near4 queries2",
+    "keys1",
+    "far4",
+    "keys2 first2",
+    "second2 near4",
+    "cross2 far4",
+    "first3 common4",
+    "second3 common4",
+    "keys3",
+    "queries3",
+    "queries4 first3",
+    "row0 second3",
+    "row1",
+    "row2",
+    "cross3",
+    "first4 row0",
+    "mixed0",
+    "mixed1",
+    "columns0",
+    "place0",
+    "columns1",
+    "place1",
+)
+MICROS = {}
+PROJECTIONS = {
+    "keys1": (0, 2, False),
+    "keys2": (2, 4, False),
+    "keys3": (4, 5, True),
+    "queries1": (0, 2, False),
+    "queries2": (2, 3, False),
+    "queries3": (3, 4, False),
+    "queries4": (4, 5, True),
+}
+COLUMNS = {"columns0": (0, 5), "columns1": (5, 8)}
 
 
 def chip_at(place, chips):
@@ -75,6 +134,10 @@
 
 def in_hbm(*arrays):
     return [pltpu.with_memory_space_constraint(array, pltpu.HBM) for array in arrays]
+
+
+def estimate(micros):
+    return pl.CostEstimate(flops=int(micros * 1.1535e9), bytes_accessed=0, transcendentals=0)
 
 
 IN_VMEM = pl.BlockSpec(memory_space=pltpu.VMEM)
@@ -176,7 +239,7 @@
         mixed_ref[:, span] = mixed.astype(jnp.bfloat16)
 
 
-def attend(index, queries, row_windows, key_seg, head_dim):
+def attend(index, queries, row_windows, key_seg, head_dim, micros):
     reach = 2 * len(row_windows) - 2
     rows = queries.shape[0]
     return pl.pallas_call(
@@ -186,6 +249,7 @@
         out_specs=IN_VMEM,
         scratch_shapes=[pltpu.VMEM((reach + 2, rows, 2 * head_dim), jnp.bfloat16)],
         compiler_params=params(),
+        cost_estimate=estimate(micros),
         name="attend",
     )(index, *in_vmem(queries, key_seg, *row_windows))
 
@@ -224,6 +288,27 @@
     )(plane, *in_hbm(query, key, value))
 
 
+def rows_near_kernel(plane_ref, weight_ref, out_ref, sem):
+    half = out_ref.shape[0]
+    near = pl.ds(pl.multiple_of(plane_ref[0] * half, half), half)
+    copy = pltpu.make_async_copy(weight_ref.at[near, :], out_ref, sem)
+    copy.start()
+    copy.wait()
+
+
+def rows_near_of(plane, weight):
+    rows, columns = weight.shape
+    return pl.pallas_call(
+        rows_near_kernel,
+        in_specs=[IN_SMEM, IN_HBM],
+        out_specs=IN_VMEM,
+        scratch_shapes=[pltpu.SemaphoreType.DMA],
+        out_shape=pltpu.VMEM((rows // 2, columns), weight.dtype),
+        compiler_params=params(),
+        name="rows_near",
+    )(plane, *in_hbm(weight))
+
+
 def both_kernel(first_ref, second_ref, out_ref):
     out_ref[0] = first_ref[0]
     out_ref[1] = second_ref[0]
@@ -255,35 +340,44 @@
     )(*in_vmem(pair))
 
 
+def bring_kernel(source_ref, out_ref, sem):
+    copy = pltpu.make_async_copy(source_ref, out_ref, sem)
+    copy.start()
+    copy.wait()
+
+
+def bring(tokens, micros):
+    return pl.pallas_call(
+        bring_kernel,
+        in_specs=[IN_HBM],
+        out_specs=IN_VMEM,
+        scratch_shapes=[pltpu.SemaphoreType.DMA],
+        out_shape=pltpu.VMEM(tokens.shape, tokens.dtype),
+        compiler_params=params(),
+        cost_estimate=estimate(micros),
+        name="bring",
+    )(*in_hbm(tokens))
+
+
 def project_kernel(slots, base, groups, first, last, index_ref, own_ref, other_ref, *refs):
-    refs, (tokens, sems) = refs[:-2], refs[-2:]
-    rows, depth = tokens.shape[1:]
+    held_weights = groups * (1 + slots[-1][0])
+    weights, refs = refs[:held_weights], refs[held_weights:]
+    total_ref, refs = (None, refs) if first else (refs[0], refs[1:])
+    rows = own_ref.shape[0]
+    depth, width = weights[0].shape[-2:]
+    block = rows // 2
     spans = [
         pl.ds(pl.multiple_of(index_ref[3 + base + place] * depth, depth), depth)
         for place in range(len(slots))
     ]
-    copies = [
-        pltpu.make_async_copy(own_ref.at[:, span], tokens.at[place], sems.at[place])
-        for place, span in enumerate(spans)
-    ]
-    for copy in copies:
-        copy.start()
-    held_weights = groups * (1 + slots[-1][0])
-    weights, refs = refs[:held_weights], refs[held_weights:]
-    total_ref, refs = (None, refs) if first else (refs[0], refs[1:])
-    block = rows // 2
-    width = weights[0].shape[-1]
     out_ref = refs[2] if last else refs[0]
-    for side in (1, 0):
-        if side == 0:
-            for copy in copies:
-                copy.wait()
+    for side, source_ref in enumerate((own_ref, other_ref)):
         for group in range(groups):
             columns = pl.ds(group * width, width)
             total = None if first else total_ref[side, :, columns]
             for place, (step, slot) in enumerate(slots):
                 product = jnp.dot(
-                    tokens[place] if side == 0 else other_ref[:, spans[place]],
+                    source_ref[:, spans[place]],
                     weights[groups * step + group][slot],
                     preferred_element_type=jnp.float32,
                 )
@@ -299,47 +393,48 @@
         sent_ref[block:] = held[0, others, :]
 
 
-def project(index, base, tokens, steps, total, last):
+def project(index, base, tokens, steps, total, last, micros):
     groups = len(steps[0][1])
     slots = [(i, slot) for i, (used, _) in enumerate(steps) for slot in range(used)]
     rows = tokens[0].shape[0]
-    depth = steps[0][1][0].shape[1]
     columns = sum(part.shape[2] for part in steps[0][1])
-    operands = in_hbm(tokens[0]) + in_vmem(tokens[1], *(part for _, parts in steps for part in parts))
+    operands = in_vmem(*tokens, *(part for _, parts in steps for part in parts))
     if total is not None:
         operands += in_vmem(total)
     shapes = ((rows, columns), (rows, columns)) if last else ((2, rows, columns),)
     out = pl.pallas_call(
         functools.partial(project_kernel, slots, base, groups, total is None, last),
-        in_specs=[IN_SMEM, IN_HBM] + [IN_VMEM] * (len(operands) - 1),
+        in_specs=[IN_SMEM] + [IN_VMEM] * len(operands),
         out_specs=[IN_VMEM] * len(shapes),
-        scratch_shapes=([pltpu.VMEM((2, rows, columns), jnp.float32)] if last else [])
-        + [
-            pltpu.VMEM((len(slots), rows, depth), jnp.bfloat16),
-            pltpu.SemaphoreType.DMA((len(slots),)),
-        ],
+        scratch_shapes=[pltpu.VMEM((2, rows, columns), jnp.float32)] if last else [],
         out_shape=[pltpu.VMEM(shape, jnp.float32) for shape in shapes],
         compiler_params=params(),
+        cost_estimate=estimate(micros),
         name="project",
     )(index, *operands)
     return out if last else out[0]
 
 
-def columns_kernel(shards, base, index_ref, mixed_ref, returned_ref, *refs):
-    weights = refs[:shards]
+def columns_kernel(places, base, index_ref, mixed_ref, returned_ref, *refs):
+    weights = list(refs[: sum(places)])
     out_ref, send_ref, held, sems = refs[-4:]
     block = mixed_ref.shape[0] // 2
     half = mixed_ref.shape[1] // 2
     width = weights[0].shape[-1]
     mine = pl.ds(pl.multiple_of(index_ref[0] * block, block), block)
     others = pl.ds(pl.multiple_of((1 - index_ref[0]) * block, block), block)
+    near = pl.ds(pl.multiple_of(index_ref[1] * half, half), half)
+    far = pl.ds(pl.multiple_of((1 - index_ref[1]) * half, half), half)
     rows_in = jnp.concatenate([mixed_ref[...], returned_ref[...]], axis=0)
-    near, far = rows_in[:, :half], rows_in[:, half:]
-    low = index_ref[1] == 0
-    rows_in = jnp.concatenate([jnp.where(low, near, far), jnp.where(low, far, near)], axis=1)
     copies = []
-    for place in range(shards):
-        value = jnp.dot(rows_in, weights[place][...], preferred_element_type=jnp.float32)
+    for place, parts in enumerate(places):
+        if parts == 1:
+            whole = weights.pop(0)
+            low, high = whole[near, :], whole[far, :]
+        else:
+            low, high = weights.pop(0)[...], weights.pop(0)[...]
+        weight = jnp.concatenate([low, high], axis=0)
+        value = jnp.dot(rows_in, weight, preferred_element_type=jnp.float32)
         value = value.astype(jnp.bfloat16)
         columns = pl.ds(place * width, width)
         held[mine, columns] = value[:block]
@@ -356,17 +451,17 @@
         copy.wait()
 
 
-def columns_of(index, base, mixed, returned, shards, result, width):
+def columns_of(index, base, mixed, returned, shards, result, width, micros):
     rows = mixed.shape[0]
-    out_cols = shards[0].shape[1]
-    operands = in_vmem(mixed, returned, *shards)
+    out_cols = shards[0][0].shape[-1]
+    operands = in_vmem(mixed, returned, *(part for shard in shards for part in shard))
     specs = [IN_SMEM] + [IN_VMEM] * len(operands)
     if result is not None:
         operands += in_hbm(result)
         specs.append(IN_HBM)
     sent = (rows, len(shards) * out_cols)
     return pl.pallas_call(
-        functools.partial(columns_kernel, len(shards), base),
+        functools.partial(columns_kernel, [len(shard) for shard in shards], base),
         in_specs=specs,
         out_specs=[IN_HBM, IN_VMEM],
         scratch_shapes=[
@@ -376,6 +471,7 @@
         out_shape=[pltpu.HBM((rows, width), jnp.bfloat16), pltpu.VMEM(sent, jnp.bfloat16)],
         input_output_aliases={} if result is None else {len(operands): 0},
         compiler_params=params(),
+        cost_estimate=estimate(micros),
         name="columns_of",
     )(index, *operands)
 
@@ -461,50 +557,133 @@
             return project(index, base, (hidden_in, other), steps[begin:end], total, last)
 
         own_near, own_far, own_common = lay_out(plane_index, w_query, w_key, w_value)
-        common = both_of(own_common, core_swap(own_common, count))
+        done = {"w_out": w_out}
         common_steps = [(1, (own_common,))]
-        steps = [(1, (own_near, own_far))]
-        near = None
-        for step in range(1, half + 1):
-            if step == 2:
-                common, index, *tables = lax.optimization_barrier((common, index, *tables))
-                near = both_of(own_near, core_swap(after(own_near, common), count))
-                other = core_swap(after(hidden_in, near), count)
-                out_second = core_swap(after(w_out, near), count)
-            if step == half:
-                common = first_of(common)
-            common = ring(common)
-            common_steps.append((common.shape[0], (common,)))
-            if step > 1:
-                if step > 3:
-                    near = after(near, steps[step - 3][1][1])
-                near = ring(after(near, *common_steps[step - 1][1]))
-                steps.append((2, (near, plane_swap(near))))
+        query_steps = [(1, (own_near, own_far))]
+        sent_sums = {}
+        outputs = {}
+
+        def run(name, *ties):
+            nonlocal index, cosine, sine, query_cosine, query_sine, key_seg
+
+            def tied(value):
+                return after(value, *(done[tie] for tie in ties)) if ties else value
+
+            kind, step = name[:-1], int(name[-1])
+            micros = MICROS.get(kind, 2)
+            if name == "tables0":
+                first, index, cosine, sine, query_cosine, query_sine, key_seg = (
+                    lax.optimization_barrier(
+                        (done["common0"], index, cosine, sine, query_cosine, query_sine, key_seg)
+                    )
+                )
+                done["common0"] = value = first
+            elif name == "common0":
+                value = both_of(own_common, core_swap(tied(own_common), count))
+            elif name == "near0":
+                value = both_of(own_near, core_swap(tied(own_near), count))
+            elif name == "other0":
+                value = core_swap(tied(done["tokens0"]), count)
+            elif name == "tokens0":
+                value = bring(tied(hidden_in), micros)
+            elif name == "second0":
+                rows_near = w_out
+                if HALVED:
+                    rows_near = own_rows_near
+                value = core_swap(tied(rows_near), count)
+            elif name == "first0":
+                value = w_out
+            elif kind in ("common", "near"):
+                value = done[f"{kind}{step - 1}"]
+                value = ring(tied(first_of(value) if step == half else value))
+                if kind == "common":
+                    common_steps.append((value.shape[0], (value,)))
+            elif kind == "far":
+                near = done[f"near{step}"]
+                value = plane_swap(tied(near))
+                query_steps.append((near.shape[0], (near, value)))
+            elif kind in ("first", "second"):
+                value = ring(tied(done[f"{kind}{step - 1}"]))
+            elif kind == "cross":
+                value = plane_swap(tied(done[f"second{step}"]))
+            elif kind in ("keys", "queries"):
+                begin, end, last = PROJECTIONS[name]
+                steps = list(common_steps if kind == "keys" else query_steps)
+                if ties:
+                    used, parts = steps[begin]
+                    steps[begin] = (used, (tied(parts[0]), *parts[1:]))
+                value = project(
+                    index,
+                    0 if begin == 0 else 2 * begin - 1,
+                    (done["tokens0"], done["other0"]),
+                    steps[begin:end],
+                    done.get(f"{kind}{step - 1}"),
+                    last,
+                    micros,
+                )
+                if last:
+                    kept, sent = value
+                    came = core_swap(sent, count)
+                    if kind == "keys":
+                        value = rotate_sums(1, kept, came, cosine, sine)
+                    else:
+                        value = rotate_sums(
+                            q_rows // head_dim, kept, came, query_cosine, query_sine
+                        )
+            elif name == "row0":
+                sends = [(device, device ^ 2) for device in range(count)]
+                joined = done["keys3"]
+                value = join_row(index, joined, lax.ppermute(tied(joined), "ctx", sends))
+            elif kind == "row":
+                sends = [
+                    (row_device(row, column, count), row_device(row + step, column, count))
+                    for row in range(count // 2 - step)
+                    for column in range(2)
+                ]
+                value = lax.ppermute(tied(done["row0"]), "ctx", sends)
+            elif name == "mixed0":
+                windows = [done["row2"], done["row1"], done["row0"]]
+                value = attend(index, tied(done["queries4"]), windows, key_seg, head_dim, micros)
+            elif name == "mixed1":
+                value = core_swap(done["mixed0"], count)
+            elif kind == "columns":
+                begin, end = COLUMNS[name]
+                shards = [(w_out,)]
+                for turn in range(1, half + 1):
+                    if f"first{turn}" in done:
+                        shards.append((done[f"first{turn}"],))
+                    if f"second{turn}" in done:
+                        pair = (done[f"second{turn}"],)
+                        if HALVED:
+                            pair += (done[f"cross{turn}"],)
+                        shards.append(pair)
+                result, sent = columns_of(
+                    index,
+                    begin,
+                    done["mixed0"],
+                    tied(done["mixed1"]),
+                    shards[begin:end],
+                    outputs.get("result"),
+                    width,
+                    micros,
+                )
+                outputs["result"] = result
+                value = core_swap(sent, count)
+            elif kind == "place":
+                begin, _ = COLUMNS[f"columns{step}"]
+                value = place_columns(
+                    index, 3 + 2 * half + begin, done[f"columns{step}"], outputs["result"], out_cols
+                )
+                outputs["result"] = value
+            done[name] = value
+
+        own_rows_near = None
         cosine, sine, query_cosine, query_sine, key_seg = tables
-
-        total = add_projections(None, common_steps, 0, 3)
-        kept, sent = add_projections(total, common_steps, 3, half + 1, True)
-        joined = rotate_sums(1, kept, core_swap(sent, count), cosine, sine)
-        own_row, windows = row_windows(joined)
-
-        near = first_of(after(near, common, steps[half - 2][1][1]))
-        near = ring(near)
-        steps.append((1, (near, plane_swap(near))))
-        held = [after(w_out, *common_steps[half][1]), after(out_second, near)]
-        shards = [w_out]
-        waits = {3: (joined, steps[half - 1][1][1]), 4: (own_row,), 5: (*windows, steps[half][1][1])}
-        for step in range(1, 2 * half):
-            turn = (step - 1) % 2
-            held[turn] = ring(after(held[turn], *waits.get(step, ())))
-            shards.append(held[turn])
-        total = add_projections(None, steps, 0, 2)
-        total = add_projections(total, steps, 2, 3)
-        total = add_projections(total, steps, 3, 4)
-        kept, sent = add_projections(total, steps, 4, 5, True)
-        queries = rotate_sums(
-            q_rows // head_dim, kept, core_swap(sent, count), query_cosine, query_sine
-        )
-        queries = after(queries, shards[5])
+        if HALVED:
+            own_rows_near = rows_near_of(plane_index, w_out)
+        for entry in PLAN:
+            run(*entry.split())
+        return outputs["result"]
     else:
         index = jnp.stack(index).astype(jnp.int32)
         cosine, sine, query_cosine, query_sine, key_seg = tables
@@ -521,25 +700,14 @@
         )
         own_row, windows = row_windows(joined)
 
-    mixed = attend(index, queries, [*windows[::-1], own_row], key_seg, head_dim)
-
+    mixed = attend(index, queries, [*windows[::-1], own_row], key_seg, head_dim, 4)
     returned = core_swap(mixed, count)
-    if not ringed:
-        kinds = (mixed[:block], returned[block:])
-        own_rows = jnp.where(
-            core == 0, jnp.concatenate(kinds, axis=0), jnp.concatenate(kinds[::-1], axis=0)
-        )
-        gathered = lax.all_gather(w_out, "ctx", axis=1, tiled=True)
-        return jnp.dot(own_rows, gathered, preferred_element_type=jnp.float32).astype(jnp.bfloat16)
-
-    arrivals = []
-    result = None
-    for begin, end in ((0, 5), (5, len(shards))):
-        result, sent = columns_of(index, begin, mixed, returned, shards[begin:end], result, width)
-        arrivals.append((3 + len(shards) + begin, core_swap(sent, count)))
-    for base, came in arrivals:
-        result = place_columns(index, base, came, result, out_cols)
-    return result
+    kinds = (mixed[:block], returned[block:])
+    own_rows = jnp.where(
+        core == 0, jnp.concatenate(kinds, axis=0), jnp.concatenate(kinds[::-1], axis=0)
+    )
+    gathered = lax.all_gather(w_out, "ctx", axis=1, tiled=True)
+    return jnp.dot(own_rows, gathered, preferred_element_type=jnp.float32).astype(jnp.bfloat16)
 
 
 def solution(mesh):

time: 135 us -> 124 us (0.919); the launches traced: 133 us -> 123 us
  starting transfers between devices: 38.8 us -> 33.9 us
  Pallas kernels: 29 us -> 25.8 us
    ppermute x15, waiting for transfers between devices: 48.5 us -> 34 us  [ring(): return lax.ppermute(value, 'ctx', pairs)]
    ppermute x3, waiting for transfers between devices: 0.53 us -> 11.1 us  [the longest x2 7.32 us: run(): value = lax.ppermute(tied(done['row0']), 'ctx', sends)]
    ppermute x3, starting transfers between devices: 12.8 us -> 3.91 us  [the longest x2 3.84 us: run(): value = lax.ppermute(tied(done['row0']), 'ctx', sends)]
    pallas_call x6 -> x7, Pallas kernels: 14.7 us -> 8.38 us  [project(): pl.pallas_call(functools.partial(project_kernel, slots, base, groups, tot...]
    ppermute x4 -> x7, starting transfers between devices: 2.93 us -> 7.74 us  [plane_swap(): return lax.ppermute(value, 'dp', [(0, 1), (1, 0)])]
    pallas_call x2 -> x4, Pallas kernels: 5.07 us -> 8.24 us  [the longest x2 5.08 us: columns_of(): pl.pallas_call(functools.partial(columns_kernel, [len(shard) for shard in...]
    ppermute x9, waiting for transfers between devices: 2.33 us -> 4.8 us  [core_swap(): return lax.ppermute(value, 'ctx', [(i, i ^ 1) for i in range(count)])]
    ppermute x15, starting transfers between devices: 11.7 us -> 9.58 us  [ring(): return lax.ppermute(value, 'ctx', pairs)]
  transfers between devices with their start and end apart: 31 -> 34, of which waited for: 18 -> 21; matrix products, arithmetic and copies ran while one was open for 1% -> 1% of each run, Pallas kernels for 20% -> 13%
where the time goes in v4:
time: 124 us; the launch traced here: 123 us
  waiting for transfers between devices  61.6 us (50%)
  starting transfers between devices  33.9 us (27%)
  Pallas kernels  25.8 us (21%)
    ppermute x15, waiting for transfers between devices, ring(): return lax.ppermute(value, 'ctx', pairs)  34 us
    ppermute x9, starting transfers between devices, core_swap(): return lax.ppermute(value, 'ctx', [(i, i ^ 1) for i in range(count)])  12.7 us
    ppermute x7, waiting for transfers between devices, plane_swap(): return lax.ppermute(value, 'dp', [(0, 1), (1, 0)])  11.7 us
    ppermute x15, starting transfers between devices, ring(): return lax.ppermute(value, 'ctx', pairs)  9.58 us
    pallas_call x7, Pallas kernels, project(): pl.pallas_call(functools.partial(project_kernel, slots, base, groups, tot...  8.38 us
    ppermute x7, starting transfers between devices, plane_swap(): return lax.ppermute(value, 'dp', [(0, 1), (1, 0)])  7.74 us
    ppermute x2, waiting for transfers between devices, run(): value = lax.ppermute(tied(done['row0']), 'ctx', sends)  7.32 us
    pallas_call x2, Pallas kernels, columns_of(): pl.pallas_call(functools.partial(columns_kernel, [len(shard) for shard in...  5.08 us
  transfers between devices with their start and end apart: 34, of which 21 were waited for; matrix products, arithmetic and copies ran while one was open for 1% of the time, Pallas kernels for 13%

profile of v4, /device:TPU:19, one launch (start us, length us, event | category | flops | bytes accessed | tf_op | source)
XLA Modules:
  0.0 123.4 jit_solution(14394274307264626838)
XLA Ops:
  3.5 1.3 %collective-permute-start.2 = (bf16[2,512,256]{2,1,0:T(8,128)(2,1)S(1)}, bf16[2,512,256]{2,1,0:T(8,128)(2,1)S(1)}, u32[]{:S(2)}, u32[]{:S(2)}) collective-permute-start(bf16[2,512,256]{2,1,0:T(8,128)(2,1)S(1)} %both_of.3), channel_id=1, source_target_pairs={{0,8},{2,6},{8,16},{10,2},{16,24},{18,10},{24,28},{26,18},{28,20},... | collective-permute-start | bytes 1572872 | tf_op jit(solution)/shard_map/ppermute | solution.py:553
  5.7 6.3 %collective-permute-done.2.refs_2_ = bf16[2,512,256]{2,1,0:T(8,128)(2,1)S(1)} collective-permute-done((bf16[2,512,256]{2,1,0:T(8,128)(2,1)S(1)}, bf16[2,512,256]{2,1,0:T(8,128)(2,1)S(1)}, u32[]{:S(2)}, u32[]{:S(2)}) %collective-permute-start.2) | collective-permute-done | bytes 524320 | tf_op jit(solution)/shard_map/ppermute | solution.py:553
  11.9 2.2 %bring.1.own_ref = bf16[256,8192]{1,0:T(8,128)(2,1)S(1)} custom-call(bf16[256,8192]{1,0:T(8,128)(2,1)} %source_ref), custom_call_target="tpu_custom_call" | custom-call | flops 2307000064 | tf_op jit(solution)/shard_map/bring/pallas_call | solution.py:350
  15.4 1.3 %collective-permute-start.4 = (bf16[2,512,256]{2,1,0:T(8,128)(2,1)S(1)}, bf16[2,512,256]{2,1,0:T(8,128)(2,1)S(1)}, u32[]{:S(2)}, u32[]{:S(2)}) collective-permute-start(bf16[2,512,256]{2,1,0:T(8,128)(2,1)S(1)} %collective-permute-done.2.refs_2_), channel_id=1, source_target_pairs={{0,8},{2,6},{8,16},{10,2},{16,24},{18,10},{24,28},{26,18},{28,20},... | collective-permute-start | bytes 1572872 | tf_op jit(solution)/shard_map/ppermute | solution.py:553
  18.2 5.5 %collective-permute-done.4.refs_0_ = bf16[2,512,256]{2,1,0:T(8,128)(2,1)S(1)} collective-permute-done((bf16[2,512,256]{2,1,0:T(8,128)(2,1)S(1)}, bf16[2,512,256]{2,1,0:T(8,128)(2,1)S(1)}, u32[]{:S(2)}, u32[]{:S(2)}) %collective-permute-start.4) | collective-permute-done | bytes 524320 | tf_op jit(solution)/shard_map/ppermute | solution.py:553
  23.7 1.3 %collective-permute-start.8 = (bf16[512,512]{1,0:T(8,128)(2,1)S(1)}, bf16[512,512]{1,0:T(8,128)(2,1)S(1)}, u32[]{:S(2)}, u32[]{:S(2)}) collective-permute-start(bf16[512,512]{1,0:T(8,128)(2,1)S(1)} %copy-done.1), channel_id=1, source_target_pairs={{0,8},{2,6},{8,16},{10,2},{16,24},{18,10},{24,28},{26,18},{28,20},... | collective-permute-start | bytes 1572872 | tf_op jit(solution)/shard_map/ppermute | solution.py:553
  25.3 5.0 %collective-permute-done.11.refs_3_ = bf16[2,512,256]{2,1,0:T(8,128)(2,1)S(1)} collective-permute-done((bf16[2,512,256]{2,1,0:T(8,128)(2,1)S(1)}, bf16[2,512,256]{2,1,0:T(8,128)(2,1)S(1)}, u32[]{:S(2)}, u32[]{:S(2)}) %collective-permute-start.11) | collective-permute-done | bytes 524320 | tf_op jit(solution)/shard_map/ppermute | solution.py:100
  32.5 2.4 %collective-permute-done.8.refs_1_ = bf16[512,512]{1,0:T(8,128)(2,1)S(1)} collective-permute-done((bf16[512,512]{1,0:T(8,128)(2,1)S(1)}, bf16[512,512]{1,0:T(8,128)(2,1)S(1)}, u32[]{:S(2)}, u32[]{:S(2)}) %collective-permute-start.8) | collective-permute-done | bytes 524320 | tf_op jit(solution)/shard_map/ppermute | solution.py:553
  35.9 4.7 %collective-permute-done.5.pair_ref.refs_0_ = bf16[2,512,256]{2,1,0:T(8,128)(2,1)S(1)} collective-permute-done((bf16[2,512,256]{2,1,0:T(8,128)(2,1)S(1)}, bf16[2,512,256]{2,1,0:T(8,128)(2,1)S(1)}, u32[]{:S(2)}, u32[]{:S(2)}) %collective-permute-start.5) | collective-permute-done | bytes 524320 | tf_op jit(solution)/shard_map/ppermute | solution.py:553
  40.6 3.2 %collective-permute-done.6.refs_1_ = bf16[2,512,256]{2,1,0:T(8,128)(2,1)S(1)} collective-permute-done((bf16[2,512,256]{2,1,0:T(8,128)(2,1)S(1)}, bf16[2,512,256]{2,1,0:T(8,128)(2,1)S(1)}, u32[]{:S(2)}, u32[]{:S(2)}) %collective-permute-start.6) | collective-permute-done | bytes 524320 | tf_op jit(solution)/shard_map/ppermute | solution.py:100
  43.8 1.5 %project.7.refs_2_ = f32[2,256,512]{2,1,0:T(8,128)S(1)} custom-call(s32[19]{0:T(128)S(1)} %stack.76.index_ref, bf16[256,8192]{1,0:T(8,128)(2,1)S(1)} %bring.1.own_ref, bf16[256,8192]{1,0:T(8,128)(2,1)S(1)} %collective-permute-done.3.other_ref, bf16[1,512,256]{2,1,0:T(8,128)(2,1)S(1)} %get-tuple-element.53.first_ref.refs_0_, ...), custom_call_target="tpu_custom_call" | custom-call | flops 2307000064 | tf_op jit(solution)/shard_map/project/pallas_call | solution.py:405
  47.8 1.6 %collective-permute-done.7.refs_0_ = bf16[1,512,256]{2,1,0:T(8,128)(2,1)S(1)} collective-permute-done((bf16[1,512,256]{2,1,0:T(8,128)(2,1)S(1)}, bf16[1,512,256]{2,1,0:T(8,128)(2,1)S(1)}, u32[]{:S(2)}, u32[]{:S(2)}) %collective-permute-start.7) | collective-permute-done | bytes 262176 | tf_op jit(solution)/shard_map/ppermute | solution.py:553
  51.5 6.2 %collective-permute-done.15.refs_2_ = bf16[256,512]{1,0:T(8,128)(2,1)S(1)} collective-permute-done((bf16[256,512]{1,0:T(8,128)(2,1)S(1)}, bf16[256,512]{1,0:T(8,128)(2,1)S(1)}, u32[]{:S(2)}, u32[]{:S(2)}) %collective-permute-start.15) | collective-permute-done | bytes 262176 | tf_op jit(solution)/shard_map/ppermute | solution.py:553
  61.6 1.8 %collective-permute-done.9.refs_4_ = bf16[512,512]{1,0:T(8,128)(2,1)S(1)} collective-permute-done((bf16[512,512]{1,0:T(8,128)(2,1)S(1)}, bf16[512,512]{1,0:T(8,128)(2,1)S(1)}, u32[]{:S(2)}, u32[]{:S(2)}) %collective-permute-start.9) | collective-permute-done | bytes 524320 | tf_op jit(solution)/shard_map/ppermute | solution.py:553
  64.5 1.7 %collective-permute-done.16.refs_0_ = bf16[1,512,256]{2,1,0:T(8,128)(2,1)S(1)} collective-permute-done((bf16[1,512,256]{2,1,0:T(8,128)(2,1)S(1)}, bf16[1,512,256]{2,1,0:T(8,128)(2,1)S(1)}, u32[]{:S(2)}, u32[]{:S(2)}) %collective-permute-start.16) | collective-permute-done | bytes 262176 | tf_op jit(solution)/shard_map/ppermute | solution.py:553
  70.9 1.3 %collective-permute-start.21 = (f32[256,256]{1,0:T(8,128)S(1)}, f32[256,256]{1,0:T(8,128)S(1)}, u32[]{:S(2)}, u32[]{:S(2)}) collective-permute-start(f32[256,256]{1,0:T(8,128)S(1)} %get-tuple-element.69), channel_id=1, source_target_pairs={{0,2},{2,0},{4,6},{6,4},{8,10},{10,8},{12,14},{14,12},{16,18},{18,... | collective-permute-start | bytes 786440 | tf_op jit(solution)/shard_map/ppermute | solution.py:96
  72.2 2.4 %collective-permute-done.17.refs_0_ = bf16[512,512]{1,0:T(8,128)(2,1)S(1)} collective-permute-done((bf16[512,512]{1,0:T(8,128)(2,1)S(1)}, bf16[512,512]{1,0:T(8,128)(2,1)S(1)}, u32[]{:S(2)}, u32[]{:S(2)}) %collective-permute-start.17) | collective-permute-done | bytes 524320 | tf_op jit(solution)/shard_map/ppermute | solution.py:553
  75.7 2.5 %collective-permute-start.20 = (f32[256,512]{1,0:T(8,128)S(1)}, f32[256,512]{1,0:T(8,128)S(1)}, u32[]{:S(2)}, u32[]{:S(2)}) collective-permute-start(f32[256,512]{1,0:T(8,128)S(1)} %get-tuple-element.63), channel_id=1, source_target_pairs={{0,2},{2,0},{4,6},{6,4},{8,10},{10,8},{12,14},{14,12},{16,18},{18,... | collective-permute-start | bytes 1572872 | tf_op jit(solution)/shard_map/ppermute | solution.py:96
  78.4 3.8 %collective-permute-done.24.beside_ref = bf16[256,256]{1,0:T(8,128)(2,1)S(1)} collective-permute-done((bf16[256,256]{1,0:T(8,128)(2,1)S(1)}, bf16[256,256]{1,0:T(8,128)(2,1)S(1)}, u32[]{:S(2)}, u32[]{:S(2)}) %collective-permute-start.24) | collective-permute-done | bytes 131104 | tf_op jit(solution)/shard_map/ppermute | solution.py:636
  82.8 1.9 %collective-permute-start.25 = (bf16[2,256,256]{2,1,0:T(8,128)(2,1)S(1)}, bf16[2,256,256]{2,1,0:T(8,128)(2,1)S(1)}, u32[]{:S(2)}, u32[]{:S(2)}) collective-permute-start(bf16[2,256,256]{2,1,0:T(8,128)(2,1)S(1)} %join_row.1.refs_2_), channel_id=1, source_target_pairs={{0,16},{4,20},{8,24},{12,28},{16,26},{20,30},{24,18},{28,22},{26,1... | collective-permute-start | bytes 786440 | tf_op jit(solution)/shard_map/ppermute | solution.py:643
  84.7 1.9 %collective-permute-start.26 = (bf16[2,256,256]{2,1,0:T(8,128)(2,1)S(1)}, bf16[2,256,256]{2,1,0:T(8,128)(2,1)S(1)}, u32[]{:S(2)}, u32[]{:S(2)}) collective-permute-start(bf16[2,256,256]{2,1,0:T(8,128)(2,1)S(1)} %join_row.1.refs_2_), channel_id=1, source_target_pairs={{0,8},{4,12},{8,16},{12,20},{16,24},{20,28},{24,26},{28,30},{26,18... | collective-permute-start | bytes 786440 | tf_op jit(solution)/shard_map/ppermute | solution.py:643
  86.6 1.4 %collective-permute-start.30 = (bf16[256,512]{1,0:T(8,128)(2,1)S(1)}, bf16[256,512]{1,0:T(8,128)(2,1)S(1)}, u32[]{:S(2)}, u32[]{:S(2)}) collective-permute-start(bf16[256,512]{1,0:T(8,128)(2,1)S(1)} %collective-permute-done.15.refs_2_), channel_id=1, source_target_pairs={{0,1},{1,0},{2,3},{3,2},{4,5},{5,4},{6,7},{7,6},{8,9},{9,8},{10,11... | collective-permute-start | bytes 786440 | tf_op jit(solution)/shard_map/ppermute | solution.py:100
  88.4 7.0 %collective-permute-done.25.refs_0_ = bf16[2,256,256]{2,1,0:T(8,128)(2,1)S(1)} collective-permute-done((bf16[2,256,256]{2,1,0:T(8,128)(2,1)S(1)}, bf16[2,256,256]{2,1,0:T(8,128)(2,1)S(1)}, u32[]{:S(2)}, u32[]{:S(2)}) %collective-permute-start.25) | collective-permute-done | bytes 262176 | tf_op jit(solution)/shard_map/ppermute | solution.py:643
  95.7 3.9 %attend.1.mixed_ref = bf16[256,512]{1,0:T(8,128)(2,1)S(1)} custom-call(s32[19]{0:T(128)S(1)} %stack.76.index_ref, bf16[256,512]{1,0:T(8,128)(2,1)S(1)} %rotate_sums.2.query_ref, s32[1,1280]{1,0:T(1,128)S(1)} %bitcast.29, bf16[2,256,256]{2,1,0:T(8,128)(2,1)S(1)} %collective-permute-done.25.refs_0_, bf16[2,256,256]{2,1,0:T(8,128)(2,1)S(1)} %collective-permute-done.26.refs_1_, ...), custom_call_target="tpu_custom_call" | custom-call | flops 2307000064 | tf_op jit(solution)/shard_map/attend/pallas_call | solution.py:245
  99.6 4.3 %collective-permute-start.27 = (bf16[256,512]{1,0:T(8,128)(2,1)S(1)}, bf16[256,512]{1,0:T(8,128)(2,1)S(1)}, u32[]{:S(2)}, u32[]{:S(2)}) collective-permute-start(bf16[256,512]{1,0:T(8,128)(2,1)S(1)} %attend.1.mixed_ref), channel_id=1, source_target_pairs={{0,2},{2,0},{4,6},{6,4},{8,10},{10,8},{12,14},{14,12},{16,18},{18,... | collective-permute-start | bytes 786440 | tf_op jit(solution)/shard_map/ppermute | solution.py:96
  105.1 2.8 %columns_of.2 = (bf16[256,8192]{1,0:T(8,128)(2,1)}, bf16[256,2560]{1,0:T(8,128)(2,1)S(1)}) custom-call(s32[19]{0:T(128)S(1)} %stack.76.index_ref, bf16[256,512]{1,0:T(8,128)(2,1)S(1)} %attend.1.mixed_ref, bf16[256,512]{1,0:T(8,128)(2,1)S(1)} %collective-permute-done.27.returned_ref, bf16[512,512]{1,0:T(8,128)(2,1)S(1)} %copy-done.2, ...), custom_call_target="tpu_custom_call" | custom-call | flops 2307000064 | tf_op jit(solution)/shard_map/columns_of/pallas_call | solution.py:463
  109.6 1.4 %collective-permute-done.32.came_ref = bf16[256,2560]{1,0:T(8,128)(2,1)S(1)} collective-permute-done((bf16[256,2560]{1,0:T(8,128)(2,1)S(1)}, bf16[256,2560]{1,0:T(8,128)(2,1)S(1)}, u32[]{:S(2)}, u32[]{:S(2)}) %collective-permute-start.32) | collective-permute-done | bytes 1310752 | tf_op jit(solution)/shard_map/ppermute | solution.py:96
  111.0 1.6 %place_columns.2.refs_4_ = bf16[256,8192]{1,0:T(8,128)(2,1)} custom-call(s32[19]{0:T(128)S(1)} %stack.76.index_ref, bf16[256,2560]{1,0:T(8,128)(2,1)S(1)} %collective-permute-done.32.came_ref, bf16[256,8192]{1,0:T(8,128)(2,1)} %get-tuple-element.78._), custom_call_target="tpu_custom_call", output_to_operand_aliasing={{}: (2, {})} | custom-call | tf_op jit(solution)/shard_map/place_columns/pallas_call | solution.py:495
  112.7 3.5 %collective-permute-done.28.refs_2_ = bf16[256,512]{1,0:T(8,128)(2,1)S(1)} collective-permute-done((bf16[256,512]{1,0:T(8,128)(2,1)S(1)}, bf16[256,512]{1,0:T(8,128)(2,1)S(1)}, u32[]{:S(2)}, u32[]{:S(2)}) %collective-permute-start.28) | collective-permute-done | bytes 262176 | tf_op jit(solution)/shard_map/ppermute | solution.py:100
  116.7 2.3 %columns_of.3 = (bf16[256,8192]{1,0:T(8,128)(2,1)}, bf16[256,1536]{1,0:T(8,128)(2,1)S(1)}) custom-call(s32[19]{0:T(128)S(1)} %stack.76.index_ref, bf16[256,512]{1,0:T(8,128)(2,1)S(1)} %attend.1.mixed_ref, bf16[256,512]{1,0:T(8,128)(2,1)S(1)} %collective-permute-done.27.returned_ref, ...), custom_call_target="tpu_custom_call", output_to_operand_aliasing={{0}: (7, {})} | custom-call | flops 2307000064 | tf_op jit(solution)/shard_map/columns_of/pallas_call | solution.py:463
  120.0 1.9 %collective-permute-done.33.came_ref = bf16[256,1536]{1,0:T(8,128)(2,1)S(1)} collective-permute-done((bf16[256,1536]{1,0:T(8,128)(2,1)S(1)}, bf16[256,1536]{1,0:T(8,128)(2,1)S(1)}, u32[]{:S(2)}, u32[]{:S(2)}) %collective-permute-start.33) | collective-permute-done | bytes 786464 | tf_op jit(solution)/shard_map/ppermute | solution.py:96
  121.9 1.4 %place_columns.3 = bf16[256,8192]{1,0:T(8,128)(2,1)} custom-call(s32[19]{0:T(128)S(1)} %stack.76.index_ref, bf16[256,1536]{1,0:T(8,128)(2,1)S(1)} %collective-permute-done.33.came_ref, bf16[256,8192]{1,0:T(8,128)(2,1)} %get-tuple-element.80._), custom_call_target="tpu_custom_call", output_to_operand_aliasing={{}: (2, {})} | custom-call | tf_op jit(solution)/shard_map/place_columns/pallas_call | solution.py:495
  (75 shorter events, 31.3 us)
Async XLA Ops:
  1.2 4.4 %collective-permute-start = (bf16[1,512,256]{2,1,0:T(8,128)(2,1)S(1)}, bf16[1,512,256]{2,1,0:T(8,128)(2,1)S(1)}, u32[]{:S(2)}, u32[]{:S(2)}) collective-permute-start(bf16[1,512,256]{2,1,0:T(8,128)(2,1)S(1)} %get-tuple-element.43.first_ref.refs_0_), channel_id=1, source_target_pairs={{0,2},{2,0},{4,6},{6,4},{8,10},{10,8},{12,14},{14,12},{16,18},{18,... | collective-permute-start | bytes 786440 | tf_op jit(solution)/shard_map/ppermute | solution.py:96
  3.5 8.4 %collective-permute-start.2 = (bf16[2,512,256]{2,1,0:T(8,128)(2,1)S(1)}, bf16[2,512,256]{2,1,0:T(8,128)(2,1)S(1)}, u32[]{:S(2)}, u32[]{:S(2)}) collective-permute-start(bf16[2,512,256]{2,1,0:T(8,128)(2,1)S(1)} %both_of.3), channel_id=1, source_target_pairs={{0,8},{2,6},{8,16},{10,2},{16,24},{18,10},{24,28},{26,18},{28,20},... | collective-permute-start | bytes 1572872 | tf_op jit(solution)/shard_map/ppermute | solution.py:553
  14.1 29.7 %collective-permute-start.3 = (bf16[256,8192]{1,0:T(8,128)(2,1)S(1)}, bf16[256,8192]{1,0:T(8,128)(2,1)S(1)}, u32[]{:S(2)}, u32[]{:S(2)}) collective-permute-start(bf16[256,8192]{1,0:T(8,128)(2,1)S(1)} %bring.1.own_ref), channel_id=1, source_target_pairs={{0,2},{2,0},{4,6},{6,4},{8,10},{10,8},{12,14},{14,12},{16,18},{18,... | collective-permute-start | bytes 12582920 | tf_op jit(solution)/shard_map/ppermute | solution.py:96
  15.4 8.3 %collective-permute-start.4 = (bf16[2,512,256]{2,1,0:T(8,128)(2,1)S(1)}, bf16[2,512,256]{2,1,0:T(8,128)(2,1)S(1)}, u32[]{:S(2)}, u32[]{:S(2)}) collective-permute-start(bf16[2,512,256]{2,1,0:T(8,128)(2,1)S(1)} %collective-permute-done.2.refs_2_), channel_id=1, source_target_pairs={{0,8},{2,6},{8,16},{10,2},{16,24},{18,10},{24,28},{26,18},{28,20},... | collective-permute-start | bytes 1572872 | tf_op jit(solution)/shard_map/ppermute | solution.py:553
  16.7 13.6 %collective-permute-start.11 = (bf16[2,512,256]{2,1,0:T(8,128)(2,1)S(1)}, bf16[2,512,256]{2,1,0:T(8,128)(2,1)S(1)}, u32[]{:S(2)}, u32[]{:S(2)}) collective-permute-start(bf16[2,512,256]{2,1,0:T(8,128)(2,1)S(1)} %collective-permute-done.2.refs_2_), channel_id=1, source_target_pairs={{0,1},{1,0},{2,3},{3,2},{4,5},{5,4},{6,7},{7,6},{8,9},{9,8},{10,11... | collective-permute-start | bytes 1572872 | tf_op jit(solution)/shard_map/ppermute | solution.py:100
  17.9 13.6 %collective-permute-start.10 = (bf16[2,512,256]{2,1,0:T(8,128)(2,1)S(1)}, bf16[2,512,256]{2,1,0:T(8,128)(2,1)S(1)}, u32[]{:S(2)}, u32[]{:S(2)}) collective-permute-start(bf16[2,512,256]{2,1,0:T(8,128)(2,1)S(1)} %both_of.2), channel_id=1, source_target_pairs={{0,8},{2,6},{8,16},{10,2},{16,24},{18,10},{24,28},{26,18},{28,20},... | collective-permute-start | bytes 1572872 | tf_op jit(solution)/shard_map/ppermute | solution.py:553
  23.7 11.2 %collective-permute-start.8 = (bf16[512,512]{1,0:T(8,128)(2,1)S(1)}, bf16[512,512]{1,0:T(8,128)(2,1)S(1)}, u32[]{:S(2)}, u32[]{:S(2)}) collective-permute-start(bf16[512,512]{1,0:T(8,128)(2,1)S(1)} %copy-done.1), channel_id=1, source_target_pairs={{0,8},{2,6},{8,16},{10,2},{16,24},{18,10},{24,28},{26,18},{28,20},... | collective-permute-start | bytes 1572872 | tf_op jit(solution)/shard_map/ppermute | solution.py:553
  25.0 15.6 %collective-permute-start.5 = (bf16[2,512,256]{2,1,0:T(8,128)(2,1)S(1)}, bf16[2,512,256]{2,1,0:T(8,128)(2,1)S(1)}, u32[]{:S(2)}, u32[]{:S(2)}) collective-permute-start(bf16[2,512,256]{2,1,0:T(8,128)(2,1)S(1)} %collective-permute-done.4.refs_0_), channel_id=1, source_target_pairs={{0,8},{2,6},{8,16},{10,2},{16,24},{18,10},{24,28},{26,18},{28,20},... | collective-permute-start | bytes 1572872 | tf_op jit(solution)/shard_map/ppermute | solution.py:553
  30.3 13.5 %collective-permute-start.6 = (bf16[2,512,256]{2,1,0:T(8,128)(2,1)S(1)}, bf16[2,512,256]{2,1,0:T(8,128)(2,1)S(1)}, u32[]{:S(2)}, u32[]{:S(2)}) collective-permute-start(bf16[2,512,256]{2,1,0:T(8,128)(2,1)S(1)} %collective-permute-done.4.refs_0_), channel_id=1, source_target_pairs={{0,1},{1,0},{2,3},{3,2},{4,5},{5,4},{6,7},{7,6},{8,9},{9,8},{10,11... | collective-permute-start | bytes 1572872 | tf_op jit(solution)/shard_map/ppermute | solution.py:100
  31.6 14.6 %collective-permute-start.12 = (bf16[2,512,256]{2,1,0:T(8,128)(2,1)S(1)}, bf16[2,512,256]{2,1,0:T(8,128)(2,1)S(1)}, u32[]{:S(2)}, u32[]{:S(2)}) collective-permute-start(bf16[2,512,256]{2,1,0:T(8,128)(2,1)S(1)} %collective-permute-done.10.refs_1_), channel_id=1, source_target_pairs={{0,8},{2,6},{8,16},{10,2},{16,24},{18,10},{24,28},{26,18},{28,20},... | collective-permute-start | bytes 1572872 | tf_op jit(solution)/shard_map/ppermute | solution.py:553
  35.0 12.5 %collective-permute-start.14 = (bf16[256,512]{1,0:T(8,128)(2,1)S(1)}, bf16[256,512]{1,0:T(8,128)(2,1)S(1)}, u32[]{:S(2)}, u32[]{:S(2)}) collective-permute-start(bf16[256,512]{1,0:T(8,128)(2,1)S(1)} %rows_near.1), channel_id=1, source_target_pairs={{0,2},{2,0},{4,6},{6,4},{8,10},{10,8},{12,14},{14,12},{16,18},{18,... | collective-permute-start | bytes 786440 | tf_op jit(solution)/shard_map/ppermute | solution.py:96
  43.8 5.5 %collective-permute-start.7 = (bf16[1,512,256]{2,1,0:T(8,128)(2,1)S(1)}, bf16[1,512,256]{2,1,0:T(8,128)(2,1)S(1)}, u32[]{:S(2)}, u32[]{:S(2)}) collective-permute-start(bf16[1,512,256]{2,1,0:T(8,128)(2,1)S(1)} %first_of.2), channel_id=1, source_target_pairs={{0,8},{2,6},{8,16},{10,2},{16,24},{18,10},{24,28},{26,18},{28,20},... | collective-permute-start | bytes 786440 | tf_op jit(solution)/shard_map/ppermute | solution.py:553
  46.2 12.8 %collective-permute-start.13 = (bf16[2,512,256]{2,1,0:T(8,128)(2,1)S(1)}, bf16[2,512,256]{2,1,0:T(8,128)(2,1)S(1)}, u32[]{:S(2)}, u32[]{:S(2)}) collective-permute-start(bf16[2,512,256]{2,1,0:T(8,128)(2,1)S(1)} %collective-permute-done.12.refs_0_), channel_id=1, source_target_pairs={{0,8},{2,6},{8,16},{10,2},{16,24},{18,10},{24,28},{26,18},{28,20},... | collective-permute-start | bytes 1572872 | tf_op jit(solution)/shard_map/ppermute | solution.py:553
  47.5 10.2 %collective-permute-start.15 = (bf16[256,512]{1,0:T(8,128)(2,1)S(1)}, bf16[256,512]{1,0:T(8,128)(2,1)S(1)}, u32[]{:S(2)}, u32[]{:S(2)}) collective-permute-start(bf16[256,512]{1,0:T(8,128)(2,1)S(1)} %collective-permute-done.14), channel_id=1, source_target_pairs={{0,8},{2,6},{8,16},{10,2},{16,24},{18,10},{24,28},{26,18},{28,20},... | collective-permute-start | bytes 786440 | tf_op jit(solution)/shard_map/ppermute | solution.py:553
  49.3 14.0 %collective-permute-start.9 = (bf16[512,512]{1,0:T(8,128)(2,1)S(1)}, bf16[512,512]{1,0:T(8,128)(2,1)S(1)}, u32[]{:S(2)}, u32[]{:S(2)}) collective-permute-start(bf16[512,512]{1,0:T(8,128)(2,1)S(1)} %collective-permute-done.8.refs_1_), channel_id=1, source_target_pairs={{0,8},{2,6},{8,16},{10,2},{16,24},{18,10},{24,28},{26,18},{28,20},... | collective-permute-start | bytes 1572872 | tf_op jit(solution)/shard_map/ppermute | solution.py:553
  50.3 16.9 %collective-permute-start.19 = (bf16[2,512,256]{2,1,0:T(8,128)(2,1)S(1)}, bf16[2,512,256]{2,1,0:T(8,128)(2,1)S(1)}, u32[]{:S(2)}, u32[]{:S(2)}) collective-permute-start(bf16[2,512,256]{2,1,0:T(8,128)(2,1)S(1)} %collective-permute-done.5.pair_ref.refs_0_), channel_id=1, source_target_pairs={{0,1},{1,0},{2,3},{3,2},{4,5},{5,4},{6,7},{7,6},{8,9},{9,8},{10,11... | collective-permute-start | bytes 1572872 | tf_op jit(solution)/shard_map/ppermute | solution.py:100
  59.1 7.1 %collective-permute-start.16 = (bf16[1,512,256]{2,1,0:T(8,128)(2,1)S(1)}, bf16[1,512,256]{2,1,0:T(8,128)(2,1)S(1)}, u32[]{:S(2)}, u32[]{:S(2)}) collective-permute-start(bf16[1,512,256]{2,1,0:T(8,128)(2,1)S(1)} %first_of.3), channel_id=1, source_target_pairs={{0,8},{2,6},{8,16},{10,2},{16,24},{18,10},{24,28},{26,18},{28,20},... | collective-permute-start | bytes 786440 | tf_op jit(solution)/shard_map/ppermute | solution.py:553
  60.1 9.6 %collective-permute-start.22 = (bf16[256,512]{1,0:T(8,128)(2,1)S(1)}, bf16[256,512]{1,0:T(8,128)(2,1)S(1)}, u32[]{:S(2)}, u32[]{:S(2)}) collective-permute-start(bf16[256,512]{1,0:T(8,128)(2,1)S(1)} %collective-permute-done.15.refs_2_), channel_id=1, source_target_pairs={{0,8},{2,6},{8,16},{10,2},{16,24},{18,10},{24,28},{26,18},{28,20},... | collective-permute-start | bytes 786440 | tf_op jit(solution)/shard_map/ppermute | solution.py:553
  60.4 14.3 %collective-permute-start.18 = (bf16[1,512,256]{2,1,0:T(8,128)(2,1)S(1)}, bf16[1,512,256]{2,1,0:T(8,128)(2,1)S(1)}, u32[]{:S(2)}, u32[]{:S(2)}) collective-permute-start(bf16[1,512,256]{2,1,0:T(8,128)(2,1)S(1)} %collective-permute-done.7.refs_0_), channel_id=1, source_target_pairs={{0,1},{1,0},{2,3},{3,2},{4,5},{5,4},{6,7},{7,6},{8,9},{9,8},{10,11... | collective-permute-start | bytes 786440 | tf_op jit(solution)/shard_map/ppermute | solution.py:100
  66.2 8.4 %collective-permute-start.17 = (bf16[512,512]{1,0:T(8,128)(2,1)S(1)}, bf16[512,512]{1,0:T(8,128)(2,1)S(1)}, u32[]{:S(2)}, u32[]{:S(2)}) collective-permute-start(bf16[512,512]{1,0:T(8,128)(2,1)S(1)} %collective-permute-done.9.refs_4_), channel_id=1, source_target_pairs={{0,8},{2,6},{8,16},{10,2},{16,24},{18,10},{24,28},{26,18},{28,20},... | collective-permute-start | bytes 1572872 | tf_op jit(solution)/shard_map/ppermute | solution.py:553
  69.7 8.6 %collective-permute-start.23 = (bf16[256,512]{1,0:T(8,128)(2,1)S(1)}, bf16[256,512]{1,0:T(8,128)(2,1)S(1)}, u32[]{:S(2)}, u32[]{:S(2)}) collective-permute-start(bf16[256,512]{1,0:T(8,128)(2,1)S(1)} %collective-permute-done.22.refs_5_), channel_id=1, source_target_pairs={{0,8},{2,6},{8,16},{10,2},{16,24},{18,10},{24,28},{26,18},{28,20},... | collective-permute-start | bytes 786440 | tf_op jit(solution)/shard_map/ppermute | solution.py:553
  70.9 7.3 %collective-permute-start.21 = (f32[256,256]{1,0:T(8,128)S(1)}, f32[256,256]{1,0:T(8,128)S(1)}, u32[]{:S(2)}, u32[]{:S(2)}) collective-permute-start(f32[256,256]{1,0:T(8,128)S(1)} %get-tuple-element.69), channel_id=1, source_target_pairs={{0,2},{2,0},{4,6},{6,4},{8,10},{10,8},{12,14},{14,12},{16,18},{18,... | collective-permute-start | bytes 786440 | tf_op jit(solution)/shard_map/ppermute | solution.py:96
  75.7 12.5 %collective-permute-start.20 = (f32[256,512]{1,0:T(8,128)S(1)}, f32[256,512]{1,0:T(8,128)S(1)}, u32[]{:S(2)}, u32[]{:S(2)}) collective-permute-start(f32[256,512]{1,0:T(8,128)S(1)} %get-tuple-element.63), channel_id=1, source_target_pairs={{0,2},{2,0},{4,6},{6,4},{8,10},{10,8},{12,14},{14,12},{16,18},{18,... | collective-permute-start | bytes 1572872 | tf_op jit(solution)/shard_map/ppermute | solution.py:96
  78.3 3.9 %collective-permute-start.24 = (bf16[256,256]{1,0:T(8,128)(2,1)S(1)}, bf16[256,256]{1,0:T(8,128)(2,1)S(1)}, u32[]{:S(2)}, u32[]{:S(2)}) collective-permute-start(bf16[256,256]{1,0:T(8,128)(2,1)S(1)} %rotate_sums.3.own_ref), channel_id=1, source_target_pairs={{0,4},{2,6},{4,0},{6,2},{8,12},{10,14},{12,8},{14,10},{16,20},{18,... | collective-permute-start | bytes 393224 | tf_op jit(solution)/shard_map/ppermute | solution.py:636
  82.8 12.6 %collective-permute-start.25 = (bf16[2,256,256]{2,1,0:T(8,128)(2,1)S(1)}, bf16[2,256,256]{2,1,0:T(8,128)(2,1)S(1)}, u32[]{:S(2)}, u32[]{:S(2)}) collective-permute-start(bf16[2,256,256]{2,1,0:T(8,128)(2,1)S(1)} %join_row.1.refs_2_), channel_id=1, source_target_pairs={{0,16},{4,20},{8,24},{12,28},{16,26},{20,30},{24,18},{28,22},{26,1... | collective-permute-start | bytes 786440 | tf_op jit(solution)/shard_map/ppermute | solution.py:643
  84.7 11.0 %collective-permute-start.26 = (bf16[2,256,256]{2,1,0:T(8,128)(2,1)S(1)}, bf16[2,256,256]{2,1,0:T(8,128)(2,1)S(1)}, u32[]{:S(2)}, u32[]{:S(2)}) collective-permute-start(bf16[2,256,256]{2,1,0:T(8,128)(2,1)S(1)} %join_row.1.refs_2_), channel_id=1, source_target_pairs={{0,8},{4,12},{8,16},{12,20},{16,24},{20,28},{24,26},{28,30},{26,18... | collective-permute-start | bytes 786440 | tf_op jit(solution)/shard_map/ppermute | solution.py:643
  86.6 17.3 %collective-permute-start.30 = (bf16[256,512]{1,0:T(8,128)(2,1)S(1)}, bf16[256,512]{1,0:T(8,128)(2,1)S(1)}, u32[]{:S(2)}, u32[]{:S(2)}) collective-permute-start(bf16[256,512]{1,0:T(8,128)(2,1)S(1)} %collective-permute-done.15.refs_2_), channel_id=1, source_target_pairs={{0,1},{1,0},{2,3},{3,2},{4,5},{5,4},{6,7},{7,6},{8,9},{9,8},{10,11... | collective-permute-start | bytes 786440 | tf_op jit(solution)/shard_map/ppermute | solution.py:100
  88.1 15.9 %collective-permute-start.31 = (bf16[256,512]{1,0:T(8,128)(2,1)S(1)}, bf16[256,512]{1,0:T(8,128)(2,1)S(1)}, u32[]{:S(2)}, u32[]{:S(2)}) collective-permute-start(bf16[256,512]{1,0:T(8,128)(2,1)S(1)} %collective-permute-done.22.refs_5_), channel_id=1, source_target_pairs={{0,1},{1,0},{2,3},{3,2},{4,5},{5,4},{6,7},{7,6},{8,9},{9,8},{10,11... | collective-permute-start | bytes 786440 | tf_op jit(solution)/shard_map/ppermute | solution.py:100
  99.6 5.5 %collective-permute-start.27 = (bf16[256,512]{1,0:T(8,128)(2,1)S(1)}, bf16[256,512]{1,0:T(8,128)(2,1)S(1)}, u32[]{:S(2)}, u32[]{:S(2)}) collective-permute-start(bf16[256,512]{1,0:T(8,128)(2,1)S(1)} %attend.1.mixed_ref), channel_id=1, source_target_pairs={{0,2},{2,0},{4,6},{6,4},{8,10},{10,8},{12,14},{14,12},{16,18},{18,... | collective-permute-start | bytes 786440 | tf_op jit(solution)/shard_map/ppermute | solution.py:96
  107.9 3.1 %collective-permute-start.32 = (bf16[256,2560]{1,0:T(8,128)(2,1)S(1)}, bf16[256,2560]{1,0:T(8,128)(2,1)S(1)}, u32[]{:S(2)}, u32[]{:S(2)}) collective-permute-start(bf16[256,2560]{1,0:T(8,128)(2,1)S(1)} %get-tuple-element.77), channel_id=1, source_target_pairs={{0,2},{2,0},{4,6},{6,4},{8,10},{10,8},{12,14},{14,12},{16,18},{18,... | collective-permute-start | bytes 3932168 | tf_op jit(solution)/shard_map/ppermute | solution.py:96
  108.4 8.3 %collective-permute-start.29 = (bf16[512,512]{1,0:T(8,128)(2,1)S(1)}, bf16[512,512]{1,0:T(8,128)(2,1)S(1)}, u32[]{:S(2)}, u32[]{:S(2)}) collective-permute-start(bf16[512,512]{1,0:T(8,128)(2,1)S(1)} %collective-permute-done.17.refs_0_), channel_id=1, source_target_pairs={{0,8},{2,6},{8,16},{10,2},{16,24},{18,10},{24,28},{26,18},{28,20},... | collective-permute-start | bytes 1572872 | tf_op jit(solution)/shard_map/ppermute | solution.py:553
  108.4 7.8 %collective-permute-start.28 = (bf16[256,512]{1,0:T(8,128)(2,1)S(1)}, bf16[256,512]{1,0:T(8,128)(2,1)S(1)}, u32[]{:S(2)}, u32[]{:S(2)}) collective-permute-start(bf16[256,512]{1,0:T(8,128)(2,1)S(1)} %collective-permute-done.23.refs_1_), channel_id=1, source_target_pairs={{0,1},{1,0},{2,3},{3,2},{4,5},{5,4},{6,7},{7,6},{8,9},{9,8},{10,11... | collective-permute-start | bytes 786440 | tf_op jit(solution)/shard_map/ppermute | solution.py:100
  (5 other events, 41.7 us)

commit v5 on v4

--- a/solution.py
+++ b/solution.py
@@ -37,7 +37,7 @@
     "far3",
     "first2 near4",
     "queries2 second1",
-    "common4 near4 queries2",
+    "common4 near4 queries2 far3",
     "keys1",
     "far4",
     "keys2 first2",
@@ -45,19 +45,19 @@
     "cross2 far4",
     "first3 common4",
     "second3 common4",
-    "keys3",
+    "keys3 cross1",
     "queries3",
     "queries4 first3",
-    "row0 second3",
+    "row0 second3 cross2",
     "row1",
     "row2",
     "cross3",
-    "first4 row0",
-    "mixed0",
+    "first4 row0 row1",
+    "mixed0 cross3",
     "mixed1",
-    "columns0",
+    "columns0 first4",
+    "columns1",
     "place0",
-    "columns1",
     "place1",
 )
 MICROS = {}

time: 124 us -> 122 us (0.984)
  waiting for transfers between devices: 61.6 us -> 53.6 us
  starting transfers between devices: 33.9 us -> 39.6 us
    ppermute x15, waiting for transfers between devices: 34 us -> 29.3 us  [ring(): return lax.ppermute(value, 'ctx', pairs)]
    ppermute x9, starting transfers between devices: 12.7 us -> 16.5 us  [core_swap(): return lax.ppermute(value, 'ctx', [(i, i ^ 1) for i in range(count)])]
    ppermute x9, waiting for transfers between devices: 4.8 us -> 2 us  [core_swap(): return lax.ppermute(value, 'ctx', [(i, i ^ 1) for i in range(count)])]
    ppermute x15, starting transfers between devices: 9.58 us -> 11.5 us  [ring(): return lax.ppermute(value, 'ctx', pairs)]
    ppermute x7, waiting for transfers between devices: 11.7 us -> 10.3 us  [plane_swap(): return lax.ppermute(value, 'dp', [(0, 1), (1, 0)])]
  transfers between devices with their start and end apart: 34 -> 34, of which waited for: 21 -> 17; matrix products, arithmetic and copies ran while one was open for 1% -> 1% of each run, Pallas kernels for 13% -> 15%
where the time goes in v5:
time: 122 us; the launch traced here: 121 us
  waiting for transfers between devices  53.6 us (44%)
  starting transfers between devices  39.6 us (32%)
  Pallas kernels  25.7 us (21%)
    ppermute x15, waiting for transfers between devices, ring(): return lax.ppermute(value, 'ctx', pairs)  29.3 us
    ppermute x9, starting transfers between devices, core_swap(): return lax.ppermute(value, 'ctx', [(i, i ^ 1) for i in range(count)])  16.5 us
    ppermute x15, starting transfers between devices, ring(): return lax.ppermute(value, 'ctx', pairs)  11.5 us
    ppermute x7, waiting for transfers between devices, plane_swap(): return lax.ppermute(value, 'dp', [(0, 1), (1, 0)])  10.3 us
    ppermute x2, waiting for transfers between devices, run(): value = lax.ppermute(tied(done['row0']), 'ctx', sends)  8.41 us
    pallas_call x7, Pallas kernels, project(): pl.pallas_call(functools.partial(project_kernel, slots, base, groups, tot...  8.37 us
    ppermute x7, starting transfers between devices, plane_swap(): return lax.ppermute(value, 'dp', [(0, 1), (1, 0)])  7.23 us
    pallas_call x2, Pallas kernels, columns_of(): pl.pallas_call(functools.partial(columns_kernel, [len(shard) for shard in...  5.08 us
  transfers between devices with their start and end apart: 34, of which 17 were waited for; matrix products, arithmetic and copies ran while one was open for 1% of the time, Pallas kernels for 15%

profile of v5, /device:TPU:19, one launch (start us, length us, event | category | flops | bytes accessed | tf_op | source)
XLA Modules:
  0.0 121.2 jit_solution(12681015049931003254)
XLA Ops:
  3.5 1.3 %collective-permute-start.2 = (bf16[2,512,256]{2,1,0:T(8,128)(2,1)S(1)}, bf16[2,512,256]{2,1,0:T(8,128)(2,1)S(1)}, u32[]{:S(2)}, u32[]{:S(2)}) collective-permute-start(bf16[2,512,256]{2,1,0:T(8,128)(2,1)S(1)} %both_of.3), channel_id=1, source_target_pairs={{0,8},{2,6},{8,16},{10,2},{16,24},{18,10},{24,28},{26,18},{28,20},... | collective-permute-start | bytes 1572872 | tf_op jit(solution)/shard_map/ppermute | solution.py:553
  5.7 6.3 %collective-permute-done.2.refs_2_ = bf16[2,512,256]{2,1,0:T(8,128)(2,1)S(1)} collective-permute-done((bf16[2,512,256]{2,1,0:T(8,128)(2,1)S(1)}, bf16[2,512,256]{2,1,0:T(8,128)(2,1)S(1)}, u32[]{:S(2)}, u32[]{:S(2)}) %collective-permute-start.2) | collective-permute-done | bytes 524320 | tf_op jit(solution)/shard_map/ppermute | solution.py:553
  11.9 2.2 %bring.1.own_ref = bf16[256,8192]{1,0:T(8,128)(2,1)S(1)} custom-call(bf16[256,8192]{1,0:T(8,128)(2,1)} %source_ref), custom_call_target="tpu_custom_call" | custom-call | flops 2307000064 | tf_op jit(solution)/shard_map/bring/pallas_call | solution.py:350
  14.1 1.3 %collective-permute-start.3 = (bf16[256,8192]{1,0:T(8,128)(2,1)S(1)}, bf16[256,8192]{1,0:T(8,128)(2,1)S(1)}, u32[]{:S(2)}, u32[]{:S(2)}) collective-permute-start(bf16[256,8192]{1,0:T(8,128)(2,1)S(1)} %bring.1.own_ref), channel_id=1, source_target_pairs={{0,2},{2,0},{4,6},{6,4},{8,10},{10,8},{12,14},{14,12},{16,18},{18,... | collective-permute-start | bytes 12582920 | tf_op jit(solution)/shard_map/ppermute | solution.py:96
  15.4 1.3 %collective-permute-start.4 = (bf16[2,512,256]{2,1,0:T(8,128)(2,1)S(1)}, bf16[2,512,256]{2,1,0:T(8,128)(2,1)S(1)}, u32[]{:S(2)}, u32[]{:S(2)}) collective-permute-start(bf16[2,512,256]{2,1,0:T(8,128)(2,1)S(1)} %collective-permute-done.2.refs_2_), channel_id=1, source_target_pairs={{0,8},{2,6},{8,16},{10,2},{16,24},{18,10},{24,28},{26,18},{28,20},... | collective-permute-start | bytes 1572872 | tf_op jit(solution)/shard_map/ppermute | solution.py:553
  18.2 5.5 %collective-permute-done.4.refs_0_ = bf16[2,512,256]{2,1,0:T(8,128)(2,1)S(1)} collective-permute-done((bf16[2,512,256]{2,1,0:T(8,128)(2,1)S(1)}, bf16[2,512,256]{2,1,0:T(8,128)(2,1)S(1)}, u32[]{:S(2)}, u32[]{:S(2)}) %collective-permute-start.4) | collective-permute-done | bytes 524320 | tf_op jit(solution)/shard_map/ppermute | solution.py:553
  23.7 1.3 %collective-permute-start.5 = (bf16[2,512,256]{2,1,0:T(8,128)(2,1)S(1)}, bf16[2,512,256]{2,1,0:T(8,128)(2,1)S(1)}, u32[]{:S(2)}, u32[]{:S(2)}) collective-permute-start(bf16[2,512,256]{2,1,0:T(8,128)(2,1)S(1)} %collective-permute-done.4.refs_0_), channel_id=1, source_target_pairs={{0,8},{2,6},{8,16},{10,2},{16,24},{18,10},{24,28},{26,18},{28,20},... | collective-permute-start | bytes 1572872 | tf_op jit(solution)/shard_map/ppermute | solution.py:553
  26.3 3.1 %collective-permute-done.10.refs_1_ = bf16[2,512,256]{2,1,0:T(8,128)(2,1)S(1)} collective-permute-done((bf16[2,512,256]{2,1,0:T(8,128)(2,1)S(1)}, bf16[2,512,256]{2,1,0:T(8,128)(2,1)S(1)}, u32[]{:S(2)}, u32[]{:S(2)}) %collective-permute-start.10) | collective-permute-done | bytes 524320 | tf_op jit(solution)/shard_map/ppermute | solution.py:553
  29.4 1.3 %collective-permute-start.8 = (bf16[512,512]{1,0:T(8,128)(2,1)S(1)}, bf16[512,512]{1,0:T(8,128)(2,1)S(1)}, u32[]{:S(2)}, u32[]{:S(2)}) collective-permute-start(bf16[512,512]{1,0:T(8,128)(2,1)S(1)} %copy-done.1), channel_id=1, source_target_pairs={{0,8},{2,6},{8,16},{10,2},{16,24},{18,10},{24,28},{26,18},{28,20},... | collective-permute-start | bytes 1572872 | tf_op jit(solution)/shard_map/ppermute | solution.py:553
  31.9 3.1 %collective-permute-done.5.pair_ref.refs_0_ = bf16[2,512,256]{2,1,0:T(8,128)(2,1)S(1)} collective-permute-done((bf16[2,512,256]{2,1,0:T(8,128)(2,1)S(1)}, bf16[2,512,256]{2,1,0:T(8,128)(2,1)S(1)}, u32[]{:S(2)}, u32[]{:S(2)}) %collective-permute-start.5) | collective-permute-done | bytes 524320 | tf_op jit(solution)/shard_map/ppermute | solution.py:553
  35.9 6.1 %collective-permute-done.6.refs_1_ = bf16[2,512,256]{2,1,0:T(8,128)(2,1)S(1)} collective-permute-done((bf16[2,512,256]{2,1,0:T(8,128)(2,1)S(1)}, bf16[2,512,256]{2,1,0:T(8,128)(2,1)S(1)}, u32[]{:S(2)}, u32[]{:S(2)}) %collective-permute-start.6) | collective-permute-done | bytes 524320 | tf_op jit(solution)/shard_map/ppermute | solution.py:100
  42.0 1.5 %project.7.refs_2_ = f32[2,256,512]{2,1,0:T(8,128)S(1)} custom-call(s32[19]{0:T(128)S(1)} %stack.76.index_ref, bf16[256,8192]{1,0:T(8,128)(2,1)S(1)} %bring.1.own_ref, bf16[256,8192]{1,0:T(8,128)(2,1)S(1)} %collective-permute-done.3.other_ref, bf16[1,512,256]{2,1,0:T(8,128)(2,1)S(1)} %get-tuple-element.56.first_ref.refs_0_, ...), custom_call_target="tpu_custom_call" | custom-call | flops 2307000064 | tf_op jit(solution)/shard_map/project/pallas_call | solution.py:405
  43.6 2.6 %collective-permute-done.12.refs_0_ = bf16[2,512,256]{2,1,0:T(8,128)(2,1)S(1)} collective-permute-done((bf16[2,512,256]{2,1,0:T(8,128)(2,1)S(1)}, bf16[2,512,256]{2,1,0:T(8,128)(2,1)S(1)}, u32[]{:S(2)}, u32[]{:S(2)}) %collective-permute-start.12) | collective-permute-done | bytes 524320 | tf_op jit(solution)/shard_map/ppermute | solution.py:553
  46.2 1.3 %collective-permute-start.13 = (bf16[2,512,256]{2,1,0:T(8,128)(2,1)S(1)}, bf16[2,512,256]{2,1,0:T(8,128)(2,1)S(1)}, u32[]{:S(2)}, u32[]{:S(2)}) collective-permute-start(bf16[2,512,256]{2,1,0:T(8,128)(2,1)S(1)} %collective-permute-done.12.refs_0_), channel_id=1, source_target_pairs={{0,8},{2,6},{8,16},{10,2},{16,24},{18,10},{24,28},{26,18},{28,20},... | collective-permute-start | bytes 1572872 | tf_op jit(solution)/shard_map/ppermute | solution.py:553
  49.0 1.3 %collective-permute-start.9 = (bf16[512,512]{1,0:T(8,128)(2,1)S(1)}, bf16[512,512]{1,0:T(8,128)(2,1)S(1)}, u32[]{:S(2)}, u32[]{:S(2)}) collective-permute-start(bf16[512,512]{1,0:T(8,128)(2,1)S(1)} %collective-permute-done.8.refs_1_), channel_id=1, source_target_pairs={{0,8},{2,6},{8,16},{10,2},{16,24},{18,10},{24,28},{26,18},{28,20},... | collective-permute-start | bytes 1572872 | tf_op jit(solution)/shard_map/ppermute | solution.py:553
  50.3 7.1 %collective-permute-done.15.refs_2_ = bf16[256,512]{1,0:T(8,128)(2,1)S(1)} collective-permute-done((bf16[256,512]{1,0:T(8,128)(2,1)S(1)}, bf16[256,512]{1,0:T(8,128)(2,1)S(1)}, u32[]{:S(2)}, u32[]{:S(2)}) %collective-permute-start.15) | collective-permute-done | bytes 262176 | tf_op jit(solution)/shard_map/ppermute | solution.py:553
  58.7 1.3 %collective-permute-start.21 = (bf16[256,512]{1,0:T(8,128)(2,1)S(1)}, bf16[256,512]{1,0:T(8,128)(2,1)S(1)}, u32[]{:S(2)}, u32[]{:S(2)}) collective-permute-start(bf16[256,512]{1,0:T(8,128)(2,1)S(1)} %collective-permute-done.15.refs_2_), channel_id=1, source_target_pairs={{0,8},{2,6},{8,16},{10,2},{16,24},{18,10},{24,28},{26,18},{28,20},... | collective-permute-start | bytes 786440 | tf_op jit(solution)/shard_map/ppermute | solution.py:553
  62.2 3.9 %collective-permute-done.19.refs_1_ = bf16[1,512,256]{2,1,0:T(8,128)(2,1)S(1)} collective-permute-done((bf16[1,512,256]{2,1,0:T(8,128)(2,1)S(1)}, bf16[1,512,256]{2,1,0:T(8,128)(2,1)S(1)}, u32[]{:S(2)}, u32[]{:S(2)}) %collective-permute-start.19) | collective-permute-done | bytes 262176 | tf_op jit(solution)/shard_map/ppermute | solution.py:100
  73.6 2.0 %collective-permute-start.25 = (f32[256,256]{1,0:T(8,128)S(1)}, f32[256,256]{1,0:T(8,128)S(1)}, u32[]{:S(2)}, u32[]{:S(2)}) collective-permute-start(f32[256,256]{1,0:T(8,128)S(1)} %get-tuple-element.76), channel_id=1, source_target_pairs={{0,2},{2,0},{4,6},{6,4},{8,10},{10,8},{12,14},{14,12},{16,18},{18,... | collective-permute-start | bytes 786440 | tf_op jit(solution)/shard_map/ppermute | solution.py:96
  75.5 1.5 %collective-permute-done.18.refs_0_ = bf16[512,512]{1,0:T(8,128)(2,1)S(1)} collective-permute-done((bf16[512,512]{1,0:T(8,128)(2,1)S(1)}, bf16[512,512]{1,0:T(8,128)(2,1)S(1)}, u32[]{:S(2)}, u32[]{:S(2)}) %collective-permute-start.18) | collective-permute-done | bytes 524320 | tf_op jit(solution)/shard_map/ppermute | solution.py:553
  78.1 3.4 %collective-permute-start.20 = (f32[256,512]{1,0:T(8,128)S(1)}, f32[256,512]{1,0:T(8,128)S(1)}, u32[]{:S(2)}, u32[]{:S(2)}) collective-permute-start(f32[256,512]{1,0:T(8,128)S(1)} %get-tuple-element.66), channel_id=1, source_target_pairs={{0,2},{2,0},{4,6},{6,4},{8,10},{10,8},{12,14},{14,12},{16,18},{18,... | collective-permute-start | bytes 1572872 | tf_op jit(solution)/shard_map/ppermute | solution.py:96
  82.0 3.6 %collective-permute-done.27.beside_ref = bf16[256,256]{1,0:T(8,128)(2,1)S(1)} collective-permute-done((bf16[256,256]{1,0:T(8,128)(2,1)S(1)}, bf16[256,256]{1,0:T(8,128)(2,1)S(1)}, u32[]{:S(2)}, u32[]{:S(2)}) %collective-permute-start.27) | collective-permute-done | bytes 131104 | tf_op jit(solution)/shard_map/ppermute | solution.py:636
  86.1 2.1 %collective-permute-start.29 = (bf16[2,256,256]{2,1,0:T(8,128)(2,1)S(1)}, bf16[2,256,256]{2,1,0:T(8,128)(2,1)S(1)}, u32[]{:S(2)}, u32[]{:S(2)}) collective-permute-start(bf16[2,256,256]{2,1,0:T(8,128)(2,1)S(1)} %join_row.1.refs_2_), channel_id=1, source_target_pairs={{0,8},{4,12},{8,16},{12,20},{16,24},{20,28},{24,26},{28,30},{26,18... | collective-permute-start | bytes 786440 | tf_op jit(solution)/shard_map/ppermute | solution.py:643
  88.6 1.9 %collective-permute-start.28 = (bf16[2,256,256]{2,1,0:T(8,128)(2,1)S(1)}, bf16[2,256,256]{2,1,0:T(8,128)(2,1)S(1)}, u32[]{:S(2)}, u32[]{:S(2)}) collective-permute-start(bf16[2,256,256]{2,1,0:T(8,128)(2,1)S(1)} %join_row.1.refs_2_), channel_id=1, source_target_pairs={{0,16},{4,20},{8,24},{12,28},{16,26},{20,30},{24,18},{28,22},{26,1... | collective-permute-start | bytes 786440 | tf_op jit(solution)/shard_map/ppermute | solution.py:643
  90.5 2.7 %collective-permute-done.29.refs_1_ = bf16[2,256,256]{2,1,0:T(8,128)(2,1)S(1)} collective-permute-done((bf16[2,256,256]{2,1,0:T(8,128)(2,1)S(1)}, bf16[2,256,256]{2,1,0:T(8,128)(2,1)S(1)}, u32[]{:S(2)}, u32[]{:S(2)}) %collective-permute-start.29) | collective-permute-done | bytes 262176 | tf_op jit(solution)/shard_map/ppermute | solution.py:643
  93.5 5.7 %collective-permute-done.28.refs_0_ = bf16[2,256,256]{2,1,0:T(8,128)(2,1)S(1)} collective-permute-done((bf16[2,256,256]{2,1,0:T(8,128)(2,1)S(1)}, bf16[2,256,256]{2,1,0:T(8,128)(2,1)S(1)}, u32[]{:S(2)}, u32[]{:S(2)}) %collective-permute-start.28) | collective-permute-done | bytes 262176 | tf_op jit(solution)/shard_map/ppermute | solution.py:643
  99.2 3.9 %attend.1.mixed_ref = bf16[256,512]{1,0:T(8,128)(2,1)S(1)} custom-call(s32[19]{0:T(128)S(1)} %stack.76.index_ref, bf16[256,512]{1,0:T(8,128)(2,1)S(1)} %rotate_sums.2.query_ref, s32[1,1280]{1,0:T(1,128)S(1)} %bitcast.29, bf16[2,256,256]{2,1,0:T(8,128)(2,1)S(1)} %collective-permute-done.28.refs_0_, bf16[2,256,256]{2,1,0:T(8,128)(2,1)S(1)} %collective-permute-done.29.refs_1_, ...), custom_call_target="tpu_custom_call" | custom-call | flops 2307000064 | tf_op jit(solution)/shard_map/attend/pallas_call | solution.py:245
  103.1 7.4 %collective-permute-start.30 = (bf16[256,512]{1,0:T(8,128)(2,1)S(1)}, bf16[256,512]{1,0:T(8,128)(2,1)S(1)}, u32[]{:S(2)}, u32[]{:S(2)}) collective-permute-start(bf16[256,512]{1,0:T(8,128)(2,1)S(1)} %attend.1.mixed_ref), channel_id=1, source_target_pairs={{0,2},{2,0},{4,6},{6,4},{8,10},{10,8},{12,14},{14,12},{16,18},{18,... | collective-permute-start | bytes 786440 | tf_op jit(solution)/shard_map/ppermute | solution.py:96
  111.7 2.8 %columns_of.2 = (bf16[256,8192]{1,0:T(8,128)(2,1)}, bf16[256,2560]{1,0:T(8,128)(2,1)S(1)}) custom-call(s32[19]{0:T(128)S(1)} %stack.76.index_ref, bf16[256,512]{1,0:T(8,128)(2,1)S(1)} %attend.1.mixed_ref, bf16[256,512]{1,0:T(8,128)(2,1)S(1)} %collective-permute-done.30.returned_ref, bf16[512,512]{1,0:T(8,128)(2,1)S(1)} %copy-done.2, ...), custom_call_target="tpu_custom_call" | custom-call | flops 2307000064 | tf_op jit(solution)/shard_map/columns_of/pallas_call | solution.py:463
  115.0 2.3 %columns_of.3 = (bf16[256,8192]{1,0:T(8,128)(2,1)}, bf16[256,1536]{1,0:T(8,128)(2,1)S(1)}) custom-call(s32[19]{0:T(128)S(1)} %stack.76.index_ref, bf16[256,512]{1,0:T(8,128)(2,1)S(1)} %attend.1.mixed_ref, bf16[256,512]{1,0:T(8,128)(2,1)S(1)} %collective-permute-done.30.returned_ref, ...), custom_call_target="tpu_custom_call", output_to_operand_aliasing={{0}: (7, {})} | custom-call | flops 2307000064 | tf_op jit(solution)/shard_map/columns_of/pallas_call | solution.py:463
  117.6 1.6 %place_columns.2._ = bf16[256,8192]{1,0:T(8,128)(2,1)} custom-call(s32[19]{0:T(128)S(1)} %stack.76.index_ref, bf16[256,2560]{1,0:T(8,128)(2,1)S(1)} %collective-permute-done.33.came_ref, bf16[256,8192]{1,0:T(8,128)(2,1)} %get-tuple-element.86._), custom_call_target="tpu_custom_call", output_to_operand_aliasing={{}: (2, {})} | custom-call | tf_op jit(solution)/shard_map/place_columns/pallas_call | solution.py:495
  119.6 1.4 %place_columns.3 = bf16[256,8192]{1,0:T(8,128)(2,1)} custom-call(s32[19]{0:T(128)S(1)} %stack.76.index_ref, bf16[256,1536]{1,0:T(8,128)(2,1)S(1)} %collective-permute-done.32.came_ref, bf16[256,8192]{1,0:T(8,128)(2,1)} %place_columns.2._), custom_call_target="tpu_custom_call", output_to_operand_aliasing={{}: (2, {})} | custom-call | tf_op jit(solution)/shard_map/place_columns/pallas_call | solution.py:495
  (75 shorter events, 26.1 us)
Async XLA Ops:
  1.2 4.4 %collective-permute-start = (bf16[1,512,256]{2,1,0:T(8,128)(2,1)S(1)}, bf16[1,512,256]{2,1,0:T(8,128)(2,1)S(1)}, u32[]{:S(2)}, u32[]{:S(2)}) collective-permute-start(bf16[1,512,256]{2,1,0:T(8,128)(2,1)S(1)} %get-tuple-element.46.first_ref.refs_0_), channel_id=1, source_target_pairs={{0,2},{2,0},{4,6},{6,4},{8,10},{10,8},{12,14},{14,12},{16,18},{18,... | collective-permute-start | bytes 786440 | tf_op jit(solution)/shard_map/ppermute | solution.py:96
  3.5 8.4 %collective-permute-start.2 = (bf16[2,512,256]{2,1,0:T(8,128)(2,1)S(1)}, bf16[2,512,256]{2,1,0:T(8,128)(2,1)S(1)}, u32[]{:S(2)}, u32[]{:S(2)}) collective-permute-start(bf16[2,512,256]{2,1,0:T(8,128)(2,1)S(1)} %both_of.3), channel_id=1, source_target_pairs={{0,8},{2,6},{8,16},{10,2},{16,24},{18,10},{24,28},{26,18},{28,20},... | collective-permute-start | bytes 1572872 | tf_op jit(solution)/shard_map/ppermute | solution.py:553
  14.1 27.9 %collective-permute-start.3 = (bf16[256,8192]{1,0:T(8,128)(2,1)S(1)}, bf16[256,8192]{1,0:T(8,128)(2,1)S(1)}, u32[]{:S(2)}, u32[]{:S(2)}) collective-permute-start(bf16[256,8192]{1,0:T(8,128)(2,1)S(1)} %bring.1.own_ref), channel_id=1, source_target_pairs={{0,2},{2,0},{4,6},{6,4},{8,10},{10,8},{12,14},{14,12},{16,18},{18,... | collective-permute-start | bytes 12582920 | tf_op jit(solution)/shard_map/ppermute | solution.py:96
  15.4 8.3 %collective-permute-start.4 = (bf16[2,512,256]{2,1,0:T(8,128)(2,1)S(1)}, bf16[2,512,256]{2,1,0:T(8,128)(2,1)S(1)}, u32[]{:S(2)}, u32[]{:S(2)}) collective-permute-start(bf16[2,512,256]{2,1,0:T(8,128)(2,1)S(1)} %collective-permute-done.2.refs_2_), channel_id=1, source_target_pairs={{0,8},{2,6},{8,16},{10,2},{16,24},{18,10},{24,28},{26,18},{28,20},... | collective-permute-start | bytes 1572872 | tf_op jit(solution)/shard_map/ppermute | solution.py:553
  16.7 12.6 %collective-permute-start.10 = (bf16[2,512,256]{2,1,0:T(8,128)(2,1)S(1)}, bf16[2,512,256]{2,1,0:T(8,128)(2,1)S(1)}, u32[]{:S(2)}, u32[]{:S(2)}) collective-permute-start(bf16[2,512,256]{2,1,0:T(8,128)(2,1)S(1)} %both_of.2), channel_id=1, source_target_pairs={{0,8},{2,6},{8,16},{10,2},{16,24},{18,10},{24,28},{26,18},{28,20},... | collective-permute-start | bytes 1572872 | tf_op jit(solution)/shard_map/ppermute | solution.py:553
  17.0 13.9 %collective-permute-start.11 = (bf16[2,512,256]{2,1,0:T(8,128)(2,1)S(1)}, bf16[2,512,256]{2,1,0:T(8,128)(2,1)S(1)}, u32[]{:S(2)}, u32[]{:S(2)}) collective-permute-start(bf16[2,512,256]{2,1,0:T(8,128)(2,1)S(1)} %collective-permute-done.2.refs_2_), channel_id=1, source_target_pairs={{0,1},{1,0},{2,3},{3,2},{4,5},{5,4},{6,7},{7,6},{8,9},{9,8},{10,11... | collective-permute-start | bytes 1572872 | tf_op jit(solution)/shard_map/ppermute | solution.py:100
  23.7 11.2 %collective-permute-start.5 = (bf16[2,512,256]{2,1,0:T(8,128)(2,1)S(1)}, bf16[2,512,256]{2,1,0:T(8,128)(2,1)S(1)}, u32[]{:S(2)}, u32[]{:S(2)}) collective-permute-start(bf16[2,512,256]{2,1,0:T(8,128)(2,1)S(1)} %collective-permute-done.4.refs_0_), channel_id=1, source_target_pairs={{0,8},{2,6},{8,16},{10,2},{16,24},{18,10},{24,28},{26,18},{28,20},... | collective-permute-start | bytes 1572872 | tf_op jit(solution)/shard_map/ppermute | solution.py:553
  25.0 17.0 %collective-permute-start.6 = (bf16[2,512,256]{2,1,0:T(8,128)(2,1)S(1)}, bf16[2,512,256]{2,1,0:T(8,128)(2,1)S(1)}, u32[]{:S(2)}, u32[]{:S(2)}) collective-permute-start(bf16[2,512,256]{2,1,0:T(8,128)(2,1)S(1)} %collective-permute-done.4.refs_0_), channel_id=1, source_target_pairs={{0,1},{1,0},{2,3},{3,2},{4,5},{5,4},{6,7},{7,6},{8,9},{9,8},{10,11... | collective-permute-start | bytes 1572872 | tf_op jit(solution)/shard_map/ppermute | solution.py:100
  29.4 12.7 %collective-permute-start.8 = (bf16[512,512]{1,0:T(8,128)(2,1)S(1)}, bf16[512,512]{1,0:T(8,128)(2,1)S(1)}, u32[]{:S(2)}, u32[]{:S(2)}) collective-permute-start(bf16[512,512]{1,0:T(8,128)(2,1)S(1)} %copy-done.1), channel_id=1, source_target_pairs={{0,8},{2,6},{8,16},{10,2},{16,24},{18,10},{24,28},{26,18},{28,20},... | collective-permute-start | bytes 1572872 | tf_op jit(solution)/shard_map/ppermute | solution.py:553
  30.9 15.3 %collective-permute-start.12 = (bf16[2,512,256]{2,1,0:T(8,128)(2,1)S(1)}, bf16[2,512,256]{2,1,0:T(8,128)(2,1)S(1)}, u32[]{:S(2)}, u32[]{:S(2)}) collective-permute-start(bf16[2,512,256]{2,1,0:T(8,128)(2,1)S(1)} %collective-permute-done.10.refs_1_), channel_id=1, source_target_pairs={{0,8},{2,6},{8,16},{10,2},{16,24},{18,10},{24,28},{26,18},{28,20},... | collective-permute-start | bytes 1572872 | tf_op jit(solution)/shard_map/ppermute | solution.py:553
  35.0 13.8 %collective-permute-start.14 = (bf16[256,512]{1,0:T(8,128)(2,1)S(1)}, bf16[256,512]{1,0:T(8,128)(2,1)S(1)}, u32[]{:S(2)}, u32[]{:S(2)}) collective-permute-start(bf16[256,512]{1,0:T(8,128)(2,1)S(1)} %rows_near.1), channel_id=1, source_target_pairs={{0,2},{2,0},{4,6},{6,4},{8,10},{10,8},{12,14},{14,12},{16,18},{18,... | collective-permute-start | bytes 786440 | tf_op jit(solution)/shard_map/ppermute | solution.py:96
  42.0 7.0 %collective-permute-start.7 = (bf16[1,512,256]{2,1,0:T(8,128)(2,1)S(1)}, bf16[1,512,256]{2,1,0:T(8,128)(2,1)S(1)}, u32[]{:S(2)}, u32[]{:S(2)}) collective-permute-start(bf16[1,512,256]{2,1,0:T(8,128)(2,1)S(1)} %first_of.2), channel_id=1, source_target_pairs={{0,8},{2,6},{8,16},{10,2},{16,24},{18,10},{24,28},{26,18},{28,20},... | collective-permute-start | bytes 786440 | tf_op jit(solution)/shard_map/ppermute | solution.py:553
  46.2 15.0 %collective-permute-start.13 = (bf16[2,512,256]{2,1,0:T(8,128)(2,1)S(1)}, bf16[2,512,256]{2,1,0:T(8,128)(2,1)S(1)}, u32[]{:S(2)}, u32[]{:S(2)}) collective-permute-start(bf16[2,512,256]{2,1,0:T(8,128)(2,1)S(1)} %collective-permute-done.12.refs_0_), channel_id=1, source_target_pairs={{0,8},{2,6},{8,16},{10,2},{16,24},{18,10},{24,28},{26,18},{28,20},... | collective-permute-start | bytes 1572872 | tf_op jit(solution)/shard_map/ppermute | solution.py:553
  47.5 13.8 %collective-permute-start.16 = (bf16[2,512,256]{2,1,0:T(8,128)(2,1)S(1)}, bf16[2,512,256]{2,1,0:T(8,128)(2,1)S(1)}, u32[]{:S(2)}, u32[]{:S(2)}) collective-permute-start(bf16[2,512,256]{2,1,0:T(8,128)(2,1)S(1)} %collective-permute-done.5.pair_ref.refs_0_), channel_id=1, source_target_pairs={{0,1},{1,0},{2,3},{3,2},{4,5},{5,4},{6,7},{7,6},{8,9},{9,8},{10,11... | collective-permute-start | bytes 1572872 | tf_op jit(solution)/shard_map/ppermute | solution.py:100
  48.7 8.7 %collective-permute-start.15 = (bf16[256,512]{1,0:T(8,128)(2,1)S(1)}, bf16[256,512]{1,0:T(8,128)(2,1)S(1)}, u32[]{:S(2)}, u32[]{:S(2)}) collective-permute-start(bf16[256,512]{1,0:T(8,128)(2,1)S(1)} %collective-permute-done.14), channel_id=1, source_target_pairs={{0,8},{2,6},{8,16},{10,2},{16,24},{18,10},{24,28},{26,18},{28,20},... | collective-permute-start | bytes 786440 | tf_op jit(solution)/shard_map/ppermute | solution.py:553
  49.0 18.4 %collective-permute-start.9 = (bf16[512,512]{1,0:T(8,128)(2,1)S(1)}, bf16[512,512]{1,0:T(8,128)(2,1)S(1)}, u32[]{:S(2)}, u32[]{:S(2)}) collective-permute-start(bf16[512,512]{1,0:T(8,128)(2,1)S(1)} %collective-permute-done.8.refs_1_), channel_id=1, source_target_pairs={{0,8},{2,6},{8,16},{10,2},{16,24},{18,10},{24,28},{26,18},{28,20},... | collective-permute-start | bytes 1572872 | tf_op jit(solution)/shard_map/ppermute | solution.py:553
  57.4 8.7 %collective-permute-start.19 = (bf16[1,512,256]{2,1,0:T(8,128)(2,1)S(1)}, bf16[1,512,256]{2,1,0:T(8,128)(2,1)S(1)}, u32[]{:S(2)}, u32[]{:S(2)}) collective-permute-start(bf16[1,512,256]{2,1,0:T(8,128)(2,1)S(1)} %collective-permute-done.7.refs_0_), channel_id=1, source_target_pairs={{0,1},{1,0},{2,3},{3,2},{4,5},{5,4},{6,7},{7,6},{8,9},{9,8},{10,11... | collective-permute-start | bytes 786440 | tf_op jit(solution)/shard_map/ppermute | solution.py:100
  58.7 7.5 %collective-permute-start.21 = (bf16[256,512]{1,0:T(8,128)(2,1)S(1)}, bf16[256,512]{1,0:T(8,128)(2,1)S(1)}, u32[]{:S(2)}, u32[]{:S(2)}) collective-permute-start(bf16[256,512]{1,0:T(8,128)(2,1)S(1)} %collective-permute-done.15.refs_2_), channel_id=1, source_target_pairs={{0,8},{2,6},{8,16},{10,2},{16,24},{18,10},{24,28},{26,18},{28,20},... | collective-permute-start | bytes 786440 | tf_op jit(solution)/shard_map/ppermute | solution.py:553
  61.3 7.4 %collective-permute-start.17 = (bf16[1,512,256]{2,1,0:T(8,128)(2,1)S(1)}, bf16[1,512,256]{2,1,0:T(8,128)(2,1)S(1)}, u32[]{:S(2)}, u32[]{:S(2)}) collective-permute-start(bf16[1,512,256]{2,1,0:T(8,128)(2,1)S(1)} %first_of.3), channel_id=1, source_target_pairs={{0,8},{2,6},{8,16},{10,2},{16,24},{18,10},{24,28},{26,18},{28,20},... | collective-permute-start | bytes 786440 | tf_op jit(solution)/shard_map/ppermute | solution.py:553
  61.6 11.1 %collective-permute-start.24 = (bf16[256,512]{1,0:T(8,128)(2,1)S(1)}, bf16[256,512]{1,0:T(8,128)(2,1)S(1)}, u32[]{:S(2)}, u32[]{:S(2)}) collective-permute-start(bf16[256,512]{1,0:T(8,128)(2,1)S(1)} %collective-permute-done.15.refs_2_), channel_id=1, source_target_pairs={{0,1},{1,0},{2,3},{3,2},{4,5},{5,4},{6,7},{7,6},{8,9},{9,8},{10,11... | collective-permute-start | bytes 786440 | tf_op jit(solution)/shard_map/ppermute | solution.py:100
  66.2 15.5 %collective-permute-start.26 = (bf16[256,512]{1,0:T(8,128)(2,1)S(1)}, bf16[256,512]{1,0:T(8,128)(2,1)S(1)}, u32[]{:S(2)}, u32[]{:S(2)}) collective-permute-start(bf16[256,512]{1,0:T(8,128)(2,1)S(1)} %collective-permute-done.21.refs_5_), channel_id=1, source_target_pairs={{0,1},{1,0},{2,3},{3,2},{4,5},{5,4},{6,7},{7,6},{8,9},{9,8},{10,11... | collective-permute-start | bytes 786440 | tf_op jit(solution)/shard_map/ppermute | solution.py:100
  68.7 8.4 %collective-permute-start.18 = (bf16[512,512]{1,0:T(8,128)(2,1)S(1)}, bf16[512,512]{1,0:T(8,128)(2,1)S(1)}, u32[]{:S(2)}, u32[]{:S(2)}) collective-permute-start(bf16[512,512]{1,0:T(8,128)(2,1)S(1)} %collective-permute-done.9.refs_4_), channel_id=1, source_target_pairs={{0,8},{2,6},{8,16},{10,2},{16,24},{18,10},{24,28},{26,18},{28,20},... | collective-permute-start | bytes 1572872 | tf_op jit(solution)/shard_map/ppermute | solution.py:553
  72.4 9.3 %collective-permute-start.22 = (bf16[256,512]{1,0:T(8,128)(2,1)S(1)}, bf16[256,512]{1,0:T(8,128)(2,1)S(1)}, u32[]{:S(2)}, u32[]{:S(2)}) collective-permute-start(bf16[256,512]{1,0:T(8,128)(2,1)S(1)} %collective-permute-done.21.refs_5_), channel_id=1, source_target_pairs={{0,8},{2,6},{8,16},{10,2},{16,24},{18,10},{24,28},{26,18},{28,20},... | collective-permute-start | bytes 786440 | tf_op jit(solution)/shard_map/ppermute | solution.py:553
  73.6 8.0 %collective-permute-start.25 = (f32[256,256]{1,0:T(8,128)S(1)}, f32[256,256]{1,0:T(8,128)S(1)}, u32[]{:S(2)}, u32[]{:S(2)}) collective-permute-start(f32[256,256]{1,0:T(8,128)S(1)} %get-tuple-element.76), channel_id=1, source_target_pairs={{0,2},{2,0},{4,6},{6,4},{8,10},{10,8},{12,14},{14,12},{16,18},{18,... | collective-permute-start | bytes 786440 | tf_op jit(solution)/shard_map/ppermute | solution.py:96
  78.1 15.1 %collective-permute-start.20 = (f32[256,512]{1,0:T(8,128)S(1)}, f32[256,512]{1,0:T(8,128)S(1)}, u32[]{:S(2)}, u32[]{:S(2)}) collective-permute-start(f32[256,512]{1,0:T(8,128)S(1)} %get-tuple-element.66), channel_id=1, source_target_pairs={{0,2},{2,0},{4,6},{6,4},{8,10},{10,8},{12,14},{14,12},{16,18},{18,... | collective-permute-start | bytes 1572872 | tf_op jit(solution)/shard_map/ppermute | solution.py:96
  81.7 3.9 %collective-permute-start.27 = (bf16[256,256]{1,0:T(8,128)(2,1)S(1)}, bf16[256,256]{1,0:T(8,128)(2,1)S(1)}, u32[]{:S(2)}, u32[]{:S(2)}) collective-permute-start(bf16[256,256]{1,0:T(8,128)(2,1)S(1)} %rotate_sums.3.own_ref), channel_id=1, source_target_pairs={{0,4},{2,6},{4,0},{6,2},{8,12},{10,14},{12,8},{14,10},{16,20},{18,... | collective-permute-start | bytes 393224 | tf_op jit(solution)/shard_map/ppermute | solution.py:636
  86.1 7.1 %collective-permute-start.29 = (bf16[2,256,256]{2,1,0:T(8,128)(2,1)S(1)}, bf16[2,256,256]{2,1,0:T(8,128)(2,1)S(1)}, u32[]{:S(2)}, u32[]{:S(2)}) collective-permute-start(bf16[2,256,256]{2,1,0:T(8,128)(2,1)S(1)} %join_row.1.refs_2_), channel_id=1, source_target_pairs={{0,8},{4,12},{8,16},{12,20},{16,24},{20,28},{24,26},{28,30},{26,18... | collective-permute-start | bytes 786440 | tf_op jit(solution)/shard_map/ppermute | solution.py:643
  88.2 5.3 %collective-permute-start.23 = (bf16[256,512]{1,0:T(8,128)(2,1)S(1)}, bf16[256,512]{1,0:T(8,128)(2,1)S(1)}, u32[]{:S(2)}, u32[]{:S(2)}) collective-permute-start(bf16[256,512]{1,0:T(8,128)(2,1)S(1)} %collective-permute-done.22.refs_1_), channel_id=1, source_target_pairs={{0,1},{1,0},{2,3},{3,2},{4,5},{5,4},{6,7},{7,6},{8,9},{9,8},{10,11... | collective-permute-start | bytes 786440 | tf_op jit(solution)/shard_map/ppermute | solution.py:100
  88.6 10.6 %collective-permute-start.28 = (bf16[2,256,256]{2,1,0:T(8,128)(2,1)S(1)}, bf16[2,256,256]{2,1,0:T(8,128)(2,1)S(1)}, u32[]{:S(2)}, u32[]{:S(2)}) collective-permute-start(bf16[2,256,256]{2,1,0:T(8,128)(2,1)S(1)} %join_row.1.refs_2_), channel_id=1, source_target_pairs={{0,16},{4,20},{8,24},{12,28},{16,26},{20,30},{24,18},{28,22},{26,1... | collective-permute-start | bytes 786440 | tf_op jit(solution)/shard_map/ppermute | solution.py:643
  93.3 17.3 %collective-permute-start.31 = (bf16[512,512]{1,0:T(8,128)(2,1)S(1)}, bf16[512,512]{1,0:T(8,128)(2,1)S(1)}, u32[]{:S(2)}, u32[]{:S(2)}) collective-permute-start(bf16[512,512]{1,0:T(8,128)(2,1)S(1)} %collective-permute-done.18.refs_0_), channel_id=1, source_target_pairs={{0,8},{2,6},{8,16},{10,2},{16,24},{18,10},{24,28},{26,18},{28,20},... | collective-permute-start | bytes 1572872 | tf_op jit(solution)/shard_map/ppermute | solution.py:553
  103.1 8.6 %collective-permute-start.30 = (bf16[256,512]{1,0:T(8,128)(2,1)S(1)}, bf16[256,512]{1,0:T(8,128)(2,1)S(1)}, u32[]{:S(2)}, u32[]{:S(2)}) collective-permute-start(bf16[256,512]{1,0:T(8,128)(2,1)S(1)} %attend.1.mixed_ref), channel_id=1, source_target_pairs={{0,2},{2,0},{4,6},{6,4},{8,10},{10,8},{12,14},{14,12},{16,18},{18,... | collective-permute-start | bytes 786440 | tf_op jit(solution)/shard_map/ppermute | solution.py:96
  114.5 3.1 %collective-permute-start.33 = (bf16[256,2560]{1,0:T(8,128)(2,1)S(1)}, bf16[256,2560]{1,0:T(8,128)(2,1)S(1)}, u32[]{:S(2)}, u32[]{:S(2)}) collective-permute-start(bf16[256,2560]{1,0:T(8,128)(2,1)S(1)} %get-tuple-element.85), channel_id=1, source_target_pairs={{0,2},{2,0},{4,6},{6,4},{8,10},{10,8},{12,14},{14,12},{16,18},{18,... | collective-permute-start | bytes 3932168 | tf_op jit(solution)/shard_map/ppermute | solution.py:96
  (5 other events, 48.2 us)

commit v6 on v5

--- a/solution.py
+++ b/solution.py
@@ -14,63 +14,72 @@
 VMEM_LIMIT = 16 * 1024 * 1024
 HALVED = True
 PLAN = (
-    "first0",
-    "near0",
-    "near1",
-    "common0",
-    "tables0",
-    "second0 near1",
-    "tokens0 near1 common0",
-    "other0",
-    "near2",
-    "common1 near1",
-    "far1",
-    "first1 near2",
-    "near3",
-    "common2 near2 far1",
-    "far2",
-    "second1 near3",
-    "cross1",
-    "queries1 first1",
-    "near4 far2",
-    "common3 near3 far2 queries1",
-    "far3",
-    "first2 near4",
-    "queries2 second1",
-    "common4 near4 queries2 far3",
-    "keys1",
-    "far4",
-    "keys2 first2",
-    "second2 near4",
-    "cross2 far4",
-    "first3 common4",
-    "second3 common4",
-    "keys3 cross1",
-    "queries3",
-    "queries4 first3",
-    "row0 second3 cross2",
-    "row1",
-    "row2",
-    "cross3",
-    "first4 row0 row1",
-    "mixed0 cross3",
-    "mixed1",
-    "columns0 first4",
-    "columns1",
-    "place0",
-    "place1",
+    "A0",
+    "N0",
+    "N1",
+    "C0",
+    "T0",
+    "B0 N1",
+    "H0 N1 C0",
+    "S0",
+    "N2",
+    "C1 N1",
+    "F1",
+    "A1",
+    "N3",
+    "C2 N2 F1",
+    "F2",
+    "B1 N3",
+    "X1",
+    "N4 F2",
+    "Q1 A1",
+    "C3 N3 F2 Q1",
+    "F3",
+    "A2 N4",
+    "F4",
+    "Q2 B1",
+    "C4 N4 Q2 F3",
+    "K1",
+    "K2 A2 Q2",
+    "B2 N4",
+    "X2 F4",
+    "A3 C4 K2",
+    "B3 C4",
+    "K3 X1",
+    "Q3 K3",
+    "Q4 A3",
+    "R0 X2",
+    "R1",
+    "R2",
+    "X3",
+    "A4 R0",
+    "M0 X3 R2",
+    "M1",
+    "W0 M0",
+    "W1 B3",
+    "W2",
+    "W3",
+    "O0",
+    "W4",
+    "O1",
 )
 MICROS = {}
 PROJECTIONS = {
-    "keys1": (0, 2, False),
-    "keys2": (2, 4, False),
-    "keys3": (4, 5, True),
-    "queries1": (0, 2, False),
-    "queries2": (2, 3, False),
-    "queries3": (3, 4, False),
-    "queries4": (4, 5, True),
+    "K1": (0, 2, False),
+    "K2": (2, 4, False),
+    "K3": (4, 5, True),
+    "Q1": (0, 2, False),
+    "Q2": (2, 3, False),
+    "Q3": (3, 4, False),
+    "Q4": (4, 5, True),
 }
-COLUMNS = {"columns0": (0, 5), "columns1": (5, 8)}
+COLUMNS = ((0, 1, 2, 3), (4,))
+
+
+def step_shards(turn, half):
+    if turn == 0 or turn == half:
+        return (f"A{turn}",)
+    return (f"A{turn}", f"B{turn}", f"X{turn}")
 
 
 def chip_at(place, chips):
@@ -208,6 +217,7 @@
         if piece == reach:
             same = same & (offset <= base)
         allowed.append(same)
+    scale = math.log2(math.e) / math.sqrt(head_dim)
     for column in range(0, query_ref.shape[1], head_dim):
         span = pl.ds(column, head_dim)
         query = query_ref[:, span]
@@ -218,24 +228,24 @@
                 window[odd + piece, :, :head_dim],
                 (((1,), (1,)), ((), ())),
                 preferred_element_type=jnp.float32,
-            ) / math.sqrt(head_dim)
+            )
             scores.append(jnp.where(allowed[piece], score, -1e30))
         peak = scores[0]
         for score in scores[1:]:
             peak = jnp.maximum(peak, score)
         peak = jnp.max(peak, axis=1, keepdims=True)
-        terms = [jnp.exp(score - peak) for score in scores]
+        terms = [jnp.exp2((score - peak) * scale) for score in scores]
         total = terms[0]
         for term in terms[1:]:
             total = total + term
-        inverse = 1.0 / jnp.sum(total, axis=1, keepdims=True)
         mixed = jnp.zeros((rows, head_dim), jnp.float32)
         for piece in range(reach + 1):
             mixed += jnp.dot(
-                (terms[piece] * inverse).astype(jnp.bfloat16),
+                terms[piece].astype(jnp.bfloat16),
                 window[odd + piece, :, head_dim:],
                 preferred_element_type=jnp.float32,
             )
+        mixed = mixed / jnp.sum(total, axis=1, keepdims=True)
         mixed_ref[:, span] = mixed.astype(jnp.bfloat16)
 
 
@@ -415,9 +425,9 @@
     return out if last else out[0]
 
 
-def columns_kernel(places, base, index_ref, mixed_ref, returned_ref, *refs):
-    weights = list(refs[: sum(places)])
-    out_ref, send_ref, held, sems = refs[-4:]
+def columns_kernel(entries, index_ref, mixed_ref, returned_ref, *refs):
+    weights = list(refs[: sum(parts for _, parts in entries)])
+    out_ref, held, sems = refs[-3:]
     block = mixed_ref.shape[0] // 2
     half = mixed_ref.shape[1] // 2
     width = weights[0].shape[-1]
@@ -425,23 +435,22 @@
     others = pl.ds(pl.multiple_of((1 - index_ref[0]) * block, block), block)
     near = pl.ds(pl.multiple_of(index_ref[1] * half, half), half)
     far = pl.ds(pl.multiple_of((1 - index_ref[1]) * half, half), half)
-    rows_in = jnp.concatenate([mixed_ref[...], returned_ref[...]], axis=0)
+    rows_in = jnp.concatenate([mixed_ref[:block], returned_ref[block:]], axis=0)
+    near_in, far_in = rows_in[:, :half], rows_in[:, half:]
     copies = []
-    for place, parts in enumerate(places):
+    for place, (owner, parts) in enumerate(entries):
         if parts == 1:
             whole = weights.pop(0)
             low, high = whole[near, :], whole[far, :]
         else:
             low, high = weights.pop(0)[...], weights.pop(0)[...]
-        weight = jnp.concatenate([low, high], axis=0)
-        value = jnp.dot(rows_in, weight, preferred_element_type=jnp.float32)
+        value = jnp.dot(near_in, low, preferred_element_type=jnp.float32)
+        value += jnp.dot(far_in, high, preferred_element_type=jnp.float32)
         value = value.astype(jnp.bfloat16)
         columns = pl.ds(place * width, width)
         held[mine, columns] = value[:block]
-        held[others, columns] = value[3 * block :]
-        send_ref[mine, columns] = value[block : 2 * block]
-        send_ref[others, columns] = value[2 * block : 3 * block]
-        column = pl.multiple_of(index_ref[3 + base + place] * width, width)
+        held[others, columns] = value[block:]
+        column = pl.multiple_of(index_ref[owner] * width, width)
         copy = pltpu.make_async_copy(
             held.at[:, columns], out_ref.at[:, pl.ds(column, width)], sems.at[place]
         )
@@ -451,57 +460,29 @@
         copy.wait()
 
 
-def columns_of(index, base, mixed, returned, shards, result, width, micros):
+def columns_of(index, mixed, returned, shards, result, width, micros):
     rows = mixed.shape[0]
-    out_cols = shards[0][0].shape[-1]
-    operands = in_vmem(mixed, returned, *(part for shard in shards for part in shard))
+    out_cols = shards[0][1][0].shape[-1]
+    entries = [(owner, len(parts)) for owner, parts in shards]
+    operands = in_vmem(mixed, returned, *(part for _, parts in shards for part in parts))
     specs = [IN_SMEM] + [IN_VMEM] * len(operands)
     if result is not None:
         operands += in_hbm(result)
         specs.append(IN_HBM)
-    sent = (rows, len(shards) * out_cols)
-    return pl.pallas_call(
-        functools.partial(columns_kernel, [len(shard) for shard in shards], base),
+    return pl.pallas_call(
+        functools.partial(columns_kernel, entries),
         in_specs=specs,
-        out_specs=[IN_HBM, IN_VMEM],
+        out_specs=IN_HBM,
         scratch_shapes=[
-            pltpu.VMEM(sent, jnp.bfloat16),
+            pltpu.VMEM((rows, len(shards) * out_cols), jnp.bfloat16),
             pltpu.SemaphoreType.DMA((len(shards),)),
         ],
-        out_shape=[pltpu.HBM((rows, width), jnp.bfloat16), pltpu.VMEM(sent, jnp.bfloat16)],
+        out_shape=pltpu.HBM((rows, width), jnp.bfloat16),
         input_output_aliases={} if result is None else {len(operands): 0},
         compiler_params=params(),
         cost_estimate=estimate(micros),
         name="columns_of",
     )(index, *operands)
-
-
-def place_kernel(width, base, index_ref, came_ref, _, out_ref, sems):
-    copies = []
-    for place in range(came_ref.shape[1] // width):
-        column = pl.multiple_of(index_ref[base + place] * width, width)
-        copy = pltpu.make_async_copy(
-            came_ref.at[:, pl.ds(place * width, width)],
-            out_ref.at[:, pl.ds(column, width)],
-            sems.at[place],
-        )
-        copy.start()
-        copies.append(copy)
-    for copy in copies:
-        copy.wait()
-
-
-def place_columns(index, base, came, result, out_cols):
-    return pl.pallas_call(
-        functools.partial(place_kernel, out_cols, base),
-        in_specs=[IN_SMEM, IN_VMEM, IN_HBM],
-        out_specs=IN_HBM,
-        scratch_shapes=[pltpu.SemaphoreType.DMA((came.shape[1] // out_cols,))],
-        out_shape=pltpu.HBM(result.shape, result.dtype),
-        input_output_aliases={2: 0},
-        compiler_params=params(),
-        name="place_columns",
-    )(index, *in_vmem(came), *in_hbm(result))
 
 
 def on_device(hidden_in, segment_ids, w_query, w_key, w_value, w_out):
@@ -560,8 +541,6 @@
         done = {"w_out": w_out}
         common_steps = [(1, (own_common,))]
         query_steps = [(1, (own_near, own_far))]
-        sent_sums = {}
-        outputs = {}
 
         def run(name, *ties):
             nonlocal index, cosine, sine, query_cosine, query_sine, key_seg
@@ -571,51 +550,51 @@
 
             kind, step = name[:-1], int(name[-1])
             micros = MICROS.get(kind, 2)
-            if name == "tables0":
+            if name == "T0":
                 first, index, cosine, sine, query_cosine, query_sine, key_seg = (
                     lax.optimization_barrier(
-                        (done["common0"], index, cosine, sine, query_cosine, query_sine, key_seg)
+                        (done["C0"], index, cosine, sine, query_cosine, query_sine, key_seg)
                     )
                 )
-                done["common0"] = value = first
-            elif name == "common0":
+                done["C0"] = value = first
+            elif name == "C0":
                 value = both_of(own_common, core_swap(tied(own_common), count))
-            elif name == "near0":
+            elif name == "N0":
                 value = both_of(own_near, core_swap(tied(own_near), count))
-            elif name == "other0":
-                value = core_swap(tied(done["tokens0"]), count)
-            elif name == "tokens0":
+            elif name == "S0":
+                value = core_swap(tied(done["H0"]), count)
+            elif name == "H0":
                 value = bring(tied(hidden_in), micros)
-            elif name == "second0":
+            elif name == "B0":
                 rows_near = w_out
                 if HALVED:
                     rows_near = own_rows_near
                 value = core_swap(tied(rows_near), count)
-            elif name == "first0":
+            elif name == "A0":
                 value = w_out
-            elif kind in ("common", "near"):
+            elif kind in ("C", "N"):
                 value = done[f"{kind}{step - 1}"]
                 value = ring(tied(first_of(value) if step == half else value))
-                if kind == "common":
+                if kind == "C":
                     common_steps.append((value.shape[0], (value,)))
-            elif kind == "far":
-                near = done[f"near{step}"]
+            elif kind == "F":
+                near = done[f"N{step}"]
                 value = plane_swap(tied(near))
                 query_steps.append((near.shape[0], (near, value)))
-            elif kind in ("first", "second"):
+            elif kind in ("A", "B"):
                 value = ring(tied(done[f"{kind}{step - 1}"]))
-            elif kind == "cross":
-                value = plane_swap(tied(done[f"second{step}"]))
-            elif kind in ("keys", "queries"):
+            elif kind == "X":
+                value = plane_swap(tied(done[f"B{step}"]))
+            elif kind in ("K", "Q"):
                 begin, end, last = PROJECTIONS[name]
-                steps = list(common_steps if kind == "keys" else query_steps)
+                steps = list(common_steps if kind == "K" else query_steps)
                 if ties:
                     used, parts = steps[begin]
                     steps[begin] = (used, (tied(parts[0]), *parts[1:]))
                 value = project(
                     index,
                     0 if begin == 0 else 2 * begin - 1,
-                    (done["tokens0"], done["other0"]),
+                    (done["H0"], done["S0"]),
                     steps[begin:end],
                     done.get(f"{kind}{step - 1}"),
                     last,
@@ -624,57 +603,56 @@
                 if last:
                     kept, sent = value
                     came = core_swap(sent, count)
-                    if kind == "keys":
+                    if kind == "K":
                         value = rotate_sums(1, kept, came, cosine, sine)
                     else:
                         value = rotate_sums(
                             q_rows // head_dim, kept, came, query_cosine, query_sine
                         )
-            elif name == "row0":
+            elif name == "R0":
                 sends = [(device, device ^ 2) for device in range(count)]
-                joined = done["keys3"]
+                joined = done["K3"]
                 value = join_row(index, joined, lax.ppermute(tied(joined), "ctx", sends))
-            elif kind == "row":
+            elif kind == "R":
                 sends = [
                     (row_device(row, column, count), row_device(row + step, column, count))
                     for row in range(count // 2 - step)
                     for column in range(2)
                 ]
-                value = lax.ppermute(tied(done["row0"]), "ctx", sends)
-            elif name == "mixed0":
-                windows = [done["row2"], done["row1"], done["row0"]]
-                value = attend(index, tied(done["queries4"]), windows, key_seg, head_dim, micros)
-            elif name == "mixed1":
-                value = core_swap(done["mixed0"], count)
-            elif kind == "columns":
-                begin, end = COLUMNS[name]
-                shards = [(w_out,)]
-                for turn in range(1, half + 1):
-                    if f"first{turn}" in done:
-                        shards.append((done[f"first{turn}"],))
-                    if f"second{turn}" in done:
-                        pair = (done[f"second{turn}"],)
-                        if HALVED:
-                            pair += (done[f"cross{turn}"],)
-                        shards.append(pair)
-                result, sent = columns_of(
+                value = lax.ppermute(tied(done["R0"]), "ctx", sends)
+            elif name == "M0":
+                windows = [done["R2"], done["R1"], done["R0"]]
+                value = attend(index, tied(done["Q4"]), windows, key_seg, head_dim, micros)
+            elif name == "M1":
+                value = core_swap(done["M0"], count)
+            elif kind == "W":
+                if step == 0:
+                    value = (core_swap(tied(w_out), count),)
+                else:
+                    value = [core_swap(tied(done[f"A{step}"]), count)]
+                    if step < half:
+                        value.append(core_swap(done[f"B{step}"], count))
+                        value.append(core_swap(done[f"X{step}"], count))
+            elif kind == "O":
+                shards = []
+                for turn in COLUMNS[step]:
+                    for base, held in (
+                        (3, [done[key] for key in step_shards(turn, half)]),
+                        (3 + 2 * half, done[f"W{turn}"]),
+                    ):
+                        place = base + (2 * turn - 1 if turn else 0)
+                        shards.append((place, held[:1]))
+                        if len(held) > 1:
+                            shards.append((place + 1, held[1:]))
+                value = columns_of(
                     index,
-                    begin,
-                    done["mixed0"],
-                    tied(done["mixed1"]),
-                    shards[begin:end],
-                    outputs.get("result"),
+                    done["M0"],
+                    tied(done["M1"]),
+                    shards,
+                    done.get("O0"),
                     width,
                     micros,
                 )
-                outputs["result"] = result
-                value = core_swap(sent, count)
-            elif kind == "place":
-                begin, _ = COLUMNS[f"columns{step}"]
-                value = place_columns(
-                    index, 3 + 2 * half + begin, done[f"columns{step}"], outputs["result"], out_cols
-                )
-                outputs["result"] = value
             done[name] = value
 
         own_rows_near = None
@@ -683,7 +661,7 @@
             own_rows_near = rows_near_of(plane_index, w_out)
         for entry in PLAN:
             run(*entry.split())
-        return outputs["result"]
+        return done["O1"]
     else:
         index = jnp.stack(index).astype(jnp.int32)
         cosine, sine, query_cosine, query_sine, key_seg = tables

time: 122 us -> 121 us (level)
  starting transfers between devices: 39.6 us -> 43.5 us
  Pallas kernels: 25.7 us -> 22.2 us
    ppermute x7, waiting for transfers between devices: 10.3 us -> 3.67 us  [plane_swap(): return lax.ppermute(value, 'dp', [(0, 1), (1, 0)])]
    ppermute x15, waiting for transfers between devices: 29.3 us -> 35.8 us  [ring(): return lax.ppermute(value, 'ctx', pairs)]
    pallas_call x4 -> x2, Pallas kernels: 8.15 us -> 5.16 us  [columns_of(): pl.pallas_call(functools.partial(columns_kernel, entries), in_specs=specs...]
    ppermute x9 -> x18, starting transfers between devices: 16.5 us -> 19.1 us  [core_swap(): return lax.ppermute(value, 'ctx', [(i, i ^ 1) for i in range(count)])]
    ppermute x2, waiting for transfers between devices: 8.41 us -> 6.95 us  [run(): value = lax.ppermute(tied(done['R0']), 'ctx', sends)]
    ppermute x9 -> x18, waiting for transfers between devices: 2 us -> 3.39 us  [core_swap(): return lax.ppermute(value, 'ctx', [(i, i ^ 1) for i in range(count)])]
    ppermute x15, starting transfers between devices: 11.5 us -> 12.8 us  [ring(): return lax.ppermute(value, 'ctx', pairs)]
  transfers between devices with their start and end apart: 34 -> 43, of which waited for: 17 -> 19; matrix products, arithmetic and copies ran while one was open for 1% -> 1% of each run, Pallas kernels for 15% -> 14%
where the time goes in v6:
time: 121 us; the launch traced here: 120 us
  waiting for transfers between devices  52.4 us (43%)
  starting transfers between devices  43.5 us (36%)
  Pallas kernels  22.2 us (18%)
    ppermute x15, waiting for transfers between devices, ring(): return lax.ppermute(value, 'ctx', pairs)  35.8 us
    ppermute x18, starting transfers between devices, core_swap(): return lax.ppermute(value, 'ctx', [(i, i ^ 1) for i in range(count)])  19.1 us
    ppermute x15, starting transfers between devices, ring(): return lax.ppermute(value, 'ctx', pairs)  12.8 us
    pallas_call x7, Pallas kernels, project(): pl.pallas_call(functools.partial(project_kernel, slots, base, groups, tot...  8.39 us
    ppermute x7, starting transfers between devices, plane_swap(): return lax.ppermute(value, 'dp', [(0, 1), (1, 0)])  7.74 us
    ppermute x2, waiting for transfers between devices, run(): value = lax.ppermute(tied(done['R0']), 'ctx', sends)  6.95 us
    pallas_call x2, Pallas kernels, columns_of(): pl.pallas_call(functools.partial(columns_kernel, entries), in_specs=specs...  5.16 us
    ppermute x2, starting transfers between devices, run(): value = lax.ppermute(tied(done['R0']), 'ctx', sends)  3.88 us
  transfers between devices with their start and end apart: 43, of which 19 were waited for; matrix products, arithmetic and copies ran while one was open for 1% of the time, Pallas kernels for 14%

profile of v6, /device:TPU:19, one launch (start us, length us, event | category | flops | bytes accessed | tf_op | source)
XLA Modules:
  0.0 120.4 jit_solution(12692492803915255803)
XLA Ops:
  3.5 1.3 %collective-permute-start.2 = (bf16[2,512,256]{2,1,0:T(8,128)(2,1)S(1)}, bf16[2,512,256]{2,1,0:T(8,128)(2,1)S(1)}, u32[]{:S(2)}, u32[]{:S(2)}) collective-permute-start(bf16[2,512,256]{2,1,0:T(8,128)(2,1)S(1)} %both_of.3), channel_id=1, source_target_pairs={{0,8},{2,6},{8,16},{10,2},{16,24},{18,10},{24,28},{26,18},{28,20},... | collective-permute-start | bytes 1572872 | tf_op jit(solution)/shard_map/ppermute | solution.py:534
  5.7 6.3 %collective-permute-done.2.refs_2_ = bf16[2,512,256]{2,1,0:T(8,128)(2,1)S(1)} collective-permute-done((bf16[2,512,256]{2,1,0:T(8,128)(2,1)S(1)}, bf16[2,512,256]{2,1,0:T(8,128)(2,1)S(1)}, u32[]{:S(2)}, u32[]{:S(2)}) %collective-permute-start.2) | collective-permute-done | bytes 524320 | tf_op jit(solution)/shard_map/ppermute | solution.py:534
  11.9 2.2 %bring.1.own_ref = bf16[256,8192]{1,0:T(8,128)(2,1)S(1)} custom-call(bf16[256,8192]{1,0:T(8,128)(2,1)} %source_ref), custom_call_target="tpu_custom_call" | custom-call | flops 2307000064 | tf_op jit(solution)/shard_map/bring/pallas_call | solution.py:360
  15.4 1.3 %collective-permute-start.4 = (bf16[2,512,256]{2,1,0:T(8,128)(2,1)S(1)}, bf16[2,512,256]{2,1,0:T(8,128)(2,1)S(1)}, u32[]{:S(2)}, u32[]{:S(2)}) collective-permute-start(bf16[2,512,256]{2,1,0:T(8,128)(2,1)S(1)} %collective-permute-done.2.refs_2_), channel_id=1, source_target_pairs={{0,8},{2,6},{8,16},{10,2},{16,24},{18,10},{24,28},{26,18},{28,20},... | collective-permute-start | bytes 1572872 | tf_op jit(solution)/shard_map/ppermute | solution.py:534
  18.4 5.4 %collective-permute-done.4.refs_0_ = bf16[2,512,256]{2,1,0:T(8,128)(2,1)S(1)} collective-permute-done((bf16[2,512,256]{2,1,0:T(8,128)(2,1)S(1)}, bf16[2,512,256]{2,1,0:T(8,128)(2,1)S(1)}, u32[]{:S(2)}, u32[]{:S(2)}) %collective-permute-start.4) | collective-permute-done | bytes 524320 | tf_op jit(solution)/shard_map/ppermute | solution.py:534
  23.7 1.3 %collective-permute-start.5 = (bf16[2,512,256]{2,1,0:T(8,128)(2,1)S(1)}, bf16[2,512,256]{2,1,0:T(8,128)(2,1)S(1)}, u32[]{:S(2)}, u32[]{:S(2)}) collective-permute-start(bf16[2,512,256]{2,1,0:T(8,128)(2,1)S(1)} %collective-permute-done.4.refs_0_), channel_id=1, source_target_pairs={{0,8},{2,6},{8,16},{10,2},{16,24},{18,10},{24,28},{26,18},{28,20},... | collective-permute-start | bytes 1572872 | tf_op jit(solution)/shard_map/ppermute | solution.py:534
  25.0 4.3 %collective-permute-done.10.refs_1_ = bf16[2,512,256]{2,1,0:T(8,128)(2,1)S(1)} collective-permute-done((bf16[2,512,256]{2,1,0:T(8,128)(2,1)S(1)}, bf16[2,512,256]{2,1,0:T(8,128)(2,1)S(1)}, u32[]{:S(2)}, u32[]{:S(2)}) %collective-permute-start.10) | collective-permute-done | bytes 524320 | tf_op jit(solution)/shard_map/ppermute | solution.py:534
  32.9 2.1 %collective-permute-done.8.refs_2_ = bf16[512,512]{1,0:T(8,128)(2,1)S(1)} collective-permute-done((bf16[512,512]{1,0:T(8,128)(2,1)S(1)}, bf16[512,512]{1,0:T(8,128)(2,1)S(1)}, u32[]{:S(2)}, u32[]{:S(2)}) %collective-permute-start.8) | collective-permute-done | bytes 524320 | tf_op jit(solution)/shard_map/ppermute | solution.py:534
  35.9 4.7 %collective-permute-done.5.pair_ref.refs_0_ = bf16[2,512,256]{2,1,0:T(8,128)(2,1)S(1)} collective-permute-done((bf16[2,512,256]{2,1,0:T(8,128)(2,1)S(1)}, bf16[2,512,256]{2,1,0:T(8,128)(2,1)S(1)}, u32[]{:S(2)}, u32[]{:S(2)}) %collective-permute-start.5) | collective-permute-done | bytes 524320 | tf_op jit(solution)/shard_map/ppermute | solution.py:534
  41.9 1.3 %collective-permute-start.7 = (bf16[1,512,256]{2,1,0:T(8,128)(2,1)S(1)}, bf16[1,512,256]{2,1,0:T(8,128)(2,1)S(1)}, u32[]{:S(2)}, u32[]{:S(2)}) collective-permute-start(bf16[1,512,256]{2,1,0:T(8,128)(2,1)S(1)} %first_of.2), channel_id=1, source_target_pairs={{0,8},{2,6},{8,16},{10,2},{16,24},{18,10},{24,28},{26,18},{28,20},... | collective-permute-start | bytes 786440 | tf_op jit(solution)/shard_map/ppermute | solution.py:534
  43.2 1.5 %project.7.refs_2_ = f32[2,256,512]{2,1,0:T(8,128)S(1)} custom-call(s32[19]{0:T(128)S(1)} %stack.76.index_ref, bf16[256,8192]{1,0:T(8,128)(2,1)S(1)} %bring.1.own_ref, bf16[256,8192]{1,0:T(8,128)(2,1)S(1)} %collective-permute-done.3.other_ref, bf16[1,512,256]{2,1,0:T(8,128)(2,1)S(1)} %get-tuple-element.52.first_ref.refs_0_, ...), custom_call_target="tpu_custom_call" | custom-call | flops 2307000064 | tf_op jit(solution)/shard_map/project/pallas_call | solution.py:415
  44.7 1.5 %collective-permute-done.12.refs_0_ = bf16[2,512,256]{2,1,0:T(8,128)(2,1)S(1)} collective-permute-done((bf16[2,512,256]{2,1,0:T(8,128)(2,1)S(1)}, bf16[2,512,256]{2,1,0:T(8,128)(2,1)S(1)}, u32[]{:S(2)}, u32[]{:S(2)}) %collective-permute-start.12) | collective-permute-done | bytes 524320 | tf_op jit(solution)/shard_map/ppermute | solution.py:534
  46.2 1.3 %collective-permute-start.13 = (bf16[2,512,256]{2,1,0:T(8,128)(2,1)S(1)}, bf16[2,512,256]{2,1,0:T(8,128)(2,1)S(1)}, u32[]{:S(2)}, u32[]{:S(2)}) collective-permute-start(bf16[2,512,256]{2,1,0:T(8,128)(2,1)S(1)} %collective-permute-done.12.refs_0_), channel_id=1, source_target_pairs={{0,8},{2,6},{8,16},{10,2},{16,24},{18,10},{24,28},{26,18},{28,20},... | collective-permute-start | bytes 1572872 | tf_op jit(solution)/shard_map/ppermute | solution.py:534
  49.0 1.3 %collective-permute-start.9 = (bf16[512,512]{1,0:T(8,128)(2,1)S(1)}, bf16[512,512]{1,0:T(8,128)(2,1)S(1)}, u32[]{:S(2)}, u32[]{:S(2)}) collective-permute-start(bf16[512,512]{1,0:T(8,128)(2,1)S(1)} %collective-permute-done.8.refs_2_), channel_id=1, source_target_pairs={{0,8},{2,6},{8,16},{10,2},{16,24},{18,10},{24,28},{26,18},{28,20},... | collective-permute-start | bytes 1572872 | tf_op jit(solution)/shard_map/ppermute | solution.py:534
  50.3 7.1 %collective-permute-done.15.refs_3_ = bf16[256,512]{1,0:T(8,128)(2,1)S(1)} collective-permute-done((bf16[256,512]{1,0:T(8,128)(2,1)S(1)}, bf16[256,512]{1,0:T(8,128)(2,1)S(1)}, u32[]{:S(2)}, u32[]{:S(2)}) %collective-permute-start.15) | collective-permute-done | bytes 262176 | tf_op jit(solution)/shard_map/ppermute | solution.py:534
  57.4 1.3 %collective-permute-start.23 = (bf16[256,512]{1,0:T(8,128)(2,1)S(1)}, bf16[256,512]{1,0:T(8,128)(2,1)S(1)}, u32[]{:S(2)}, u32[]{:S(2)}) collective-permute-start(bf16[256,512]{1,0:T(8,128)(2,1)S(1)} %collective-permute-done.15.refs_3_), channel_id=1, source_target_pairs={{0,8},{2,6},{8,16},{10,2},{16,24},{18,10},{24,28},{26,18},{28,20},... | collective-permute-start | bytes 786440 | tf_op jit(solution)/shard_map/ppermute | solution.py:534
  64.3 4.4 %collective-permute-done.17.refs_0_ = bf16[1,512,256]{2,1,0:T(8,128)(2,1)S(1)} collective-permute-done((bf16[1,512,256]{2,1,0:T(8,128)(2,1)S(1)}, bf16[1,512,256]{2,1,0:T(8,128)(2,1)S(1)}, u32[]{:S(2)}, u32[]{:S(2)}) %collective-permute-start.17) | collective-permute-done | bytes 262176 | tf_op jit(solution)/shard_map/ppermute | solution.py:534
  68.7 1.3 %collective-permute-start.18 = (bf16[512,512]{1,0:T(8,128)(2,1)S(1)}, bf16[512,512]{1,0:T(8,128)(2,1)S(1)}, u32[]{:S(2)}, u32[]{:S(2)}) collective-permute-start(bf16[512,512]{1,0:T(8,128)(2,1)S(1)} %collective-permute-done.9.refs_8_), channel_id=1, source_target_pairs={{0,8},{2,6},{8,16},{10,2},{16,24},{18,10},{24,28},{26,18},{28,20},... | collective-permute-start | bytes 1572872 | tf_op jit(solution)/shard_map/ppermute | solution.py:534
  70.0 1.4 %collective-permute-done.20.refs_4_ = bf16[256,512]{1,0:T(8,128)(2,1)S(1)} collective-permute-done((bf16[256,512]{1,0:T(8,128)(2,1)S(1)}, bf16[256,512]{1,0:T(8,128)(2,1)S(1)}, u32[]{:S(2)}, u32[]{:S(2)}) %collective-permute-start.20) | collective-permute-done | bytes 262176 | tf_op jit(solution)/shard_map/ppermute | solution.py:109
  72.2 1.8 %collective-permute-start.21 = (f32[256,256]{1,0:T(8,128)S(1)}, f32[256,256]{1,0:T(8,128)S(1)}, u32[]{:S(2)}, u32[]{:S(2)}) collective-permute-start(f32[256,256]{1,0:T(8,128)S(1)} %get-tuple-element.64), channel_id=1, source_target_pairs={{0,2},{2,0},{4,6},{6,4},{8,10},{10,8},{12,14},{14,12},{16,18},{18,... | collective-permute-start | bytes 786440 | tf_op jit(solution)/shard_map/ppermute | solution.py:105
  78.1 2.6 %collective-permute-start.22 = (f32[256,512]{1,0:T(8,128)S(1)}, f32[256,512]{1,0:T(8,128)S(1)}, u32[]{:S(2)}, u32[]{:S(2)}) collective-permute-start(f32[256,512]{1,0:T(8,128)S(1)} %get-tuple-element.69), channel_id=1, source_target_pairs={{0,2},{2,0},{4,6},{6,4},{8,10},{10,8},{12,14},{14,12},{16,18},{18,... | collective-permute-start | bytes 1572872 | tf_op jit(solution)/shard_map/ppermute | solution.py:105
  82.8 2.6 %collective-permute-done.27.beside_ref = bf16[256,256]{1,0:T(8,128)(2,1)S(1)} collective-permute-done((bf16[256,256]{1,0:T(8,128)(2,1)S(1)}, bf16[256,256]{1,0:T(8,128)(2,1)S(1)}, u32[]{:S(2)}, u32[]{:S(2)}) %collective-permute-start.27) | collective-permute-done | bytes 131104 | tf_op jit(solution)/shard_map/ppermute | solution.py:615
  86.0 2.0 %collective-permute-start.28 = (bf16[2,256,256]{2,1,0:T(8,128)(2,1)S(1)}, bf16[2,256,256]{2,1,0:T(8,128)(2,1)S(1)}, u32[]{:S(2)}, u32[]{:S(2)}) collective-permute-start(bf16[2,256,256]{2,1,0:T(8,128)(2,1)S(1)} %join_row.1.refs_2_), channel_id=1, source_target_pairs={{0,16},{4,20},{8,24},{12,28},{16,26},{20,30},{24,18},{28,22},{26,1... | collective-permute-start | bytes 786440 | tf_op jit(solution)/shard_map/ppermute | solution.py:622
  87.9 1.9 %collective-permute-start.29 = (bf16[2,256,256]{2,1,0:T(8,128)(2,1)S(1)}, bf16[2,256,256]{2,1,0:T(8,128)(2,1)S(1)}, u32[]{:S(2)}, u32[]{:S(2)}) collective-permute-start(bf16[2,256,256]{2,1,0:T(8,128)(2,1)S(1)} %join_row.1.refs_2_), channel_id=1, source_target_pairs={{0,8},{4,12},{8,16},{12,20},{16,24},{20,28},{24,26},{28,30},{26,18... | collective-permute-start | bytes 786440 | tf_op jit(solution)/shard_map/ppermute | solution.py:622
  89.9 3.0 %collective-permute-start.37 = (bf16[512,512]{1,0:T(8,128)(2,1)S(1)}, bf16[512,512]{1,0:T(8,128)(2,1)S(1)}, u32[]{:S(2)}, u32[]{:S(2)}) collective-permute-start(bf16[512,512]{1,0:T(8,128)(2,1)S(1)} %collective-permute-done.9.refs_8_), channel_id=1, source_target_pairs={{0,2},{2,0},{4,6},{6,4},{8,10},{10,8},{12,14},{14,12},{16,18},{18,... | collective-permute-start | bytes 1572872 | tf_op jit(solution)/shard_map/ppermute | solution.py:105
  92.8 4.7 %collective-permute-done.28.refs_0_ = bf16[2,256,256]{2,1,0:T(8,128)(2,1)S(1)} collective-permute-done((bf16[2,256,256]{2,1,0:T(8,128)(2,1)S(1)}, bf16[2,256,256]{2,1,0:T(8,128)(2,1)S(1)}, u32[]{:S(2)}, u32[]{:S(2)}) %collective-permute-start.28) | collective-permute-done | bytes 262176 | tf_op jit(solution)/shard_map/ppermute | solution.py:622
  98.0 2.2 %collective-permute-done.29.refs_1_ = bf16[2,256,256]{2,1,0:T(8,128)(2,1)S(1)} collective-permute-done((bf16[2,256,256]{2,1,0:T(8,128)(2,1)S(1)}, bf16[2,256,256]{2,1,0:T(8,128)(2,1)S(1)}, u32[]{:S(2)}, u32[]{:S(2)}) %collective-permute-start.29) | collective-permute-done | bytes 262176 | tf_op jit(solution)/shard_map/ppermute | solution.py:622
  100.2 6.6 %collective-permute-start.39 = (bf16[256,512]{1,0:T(8,128)(2,1)S(1)}, bf16[256,512]{1,0:T(8,128)(2,1)S(1)}, u32[]{:S(2)}, u32[]{:S(2)}) collective-permute-start(bf16[256,512]{1,0:T(8,128)(2,1)S(1)} %collective-permute-done.26.refs_10_), channel_id=1, source_target_pairs={{0,2},{2,0},{4,6},{6,4},{8,10},{10,8},{12,14},{14,12},{16,18},{18,... | collective-permute-start | bytes 786440 | tf_op jit(solution)/shard_map/ppermute | solution.py:105
  107.0 3.3 %attend.1.mixed_ref = bf16[256,512]{1,0:T(8,128)(2,1)S(1)} custom-call(s32[19]{0:T(128)S(1)} %stack.76.index_ref, bf16[256,512]{1,0:T(8,128)(2,1)S(1)} %rotate_sums.3.query_ref, s32[1,1280]{1,0:T(1,128)S(1)} %bitcast.29, bf16[2,256,256]{2,1,0:T(8,128)(2,1)S(1)} %collective-permute-done.28.refs_0_, bf16[2,256,256]{2,1,0:T(8,128)(2,1)S(1)} %collective-permute-done.29.refs_1_, ...), custom_call_target="tpu_custom_call" | custom-call | flops 2307000064 | tf_op jit(solution)/shard_map/attend/pallas_call | solution.py:255
  112.6 2.1 %collective-permute-done.42.refs_19_ = bf16[256,512]{1,0:T(8,128)(2,1)S(1)} collective-permute-done((bf16[256,512]{1,0:T(8,128)(2,1)S(1)}, bf16[256,512]{1,0:T(8,128)(2,1)S(1)}, u32[]{:S(2)}, u32[]{:S(2)}) %collective-permute-start.42) | collective-permute-done | bytes 262176 | tf_op jit(solution)/shard_map/ppermute | solution.py:105
  115.0 3.4 %columns_of.2.refs_2_ = bf16[256,8192]{1,0:T(8,128)(2,1)} custom-call(s32[19]{0:T(128)S(1)} %stack.76.index_ref, bf16[256,512]{1,0:T(8,128)(2,1)S(1)} %attend.1.mixed_ref, bf16[256,512]{1,0:T(8,128)(2,1)S(1)} %collective-permute-done.30.returned_ref, bf16[512,512]{1,0:T(8,128)(2,1)S(1)} %copy-done.2, bf16[512,512]{1,0:T(8,128)(2,1)S(1)} %collective-permute-done.33.refs_1_, ...), custom_call_target="tpu_custom_call" | custom-call | flops 2307000064 | tf_op jit(solution)/shard_map/columns_of/pallas_call | solution.py:472
  118.5 1.7 %columns_of.3 = bf16[256,8192]{1,0:T(8,128)(2,1)} custom-call(s32[19]{0:T(128)S(1)} %stack.76.index_ref, bf16[256,512]{1,0:T(8,128)(2,1)S(1)} %attend.1.mixed_ref, bf16[256,512]{1,0:T(8,128)(2,1)S(1)} %collective-permute-done.30.returned_ref, bf16[512,512]{1,0:T(8,128)(2,1)S(1)} %collective-permute-done.31.refs_0_, ...), custom_call_target="tpu_custom_call", output_to_operand_aliasing={{}: (5, {})} | custom-call | flops 2307000064 | tf_op jit(solution)/shard_map/columns_of/pallas_call | solution.py:472
  (91 shorter events, 30.5 us)
Async XLA Ops:
  3.5 8.4 %collective-permute-start.2 = (bf16[2,512,256]{2,1,0:T(8,128)(2,1)S(1)}, bf16[2,512,256]{2,1,0:T(8,128)(2,1)S(1)}, u32[]{:S(2)}, u32[]{:S(2)}) collective-permute-start(bf16[2,512,256]{2,1,0:T(8,128)(2,1)S(1)} %both_of.3), channel_id=1, source_target_pairs={{0,8},{2,6},{8,16},{10,2},{16,24},{18,10},{24,28},{26,18},{28,20},... | collective-permute-start | bytes 1572872 | tf_op jit(solution)/shard_map/ppermute | solution.py:534
  14.1 29.1 %collective-permute-start.3 = (bf16[256,8192]{1,0:T(8,128)(2,1)S(1)}, bf16[256,8192]{1,0:T(8,128)(2,1)S(1)}, u32[]{:S(2)}, u32[]{:S(2)}) collective-permute-start(bf16[256,8192]{1,0:T(8,128)(2,1)S(1)} %bring.1.own_ref), channel_id=1, source_target_pairs={{0,2},{2,0},{4,6},{6,4},{8,10},{10,8},{12,14},{14,12},{16,18},{18,... | collective-permute-start | bytes 12582920 | tf_op jit(solution)/shard_map/ppermute | solution.py:105
  15.4 8.3 %collective-permute-start.4 = (bf16[2,512,256]{2,1,0:T(8,128)(2,1)S(1)}, bf16[2,512,256]{2,1,0:T(8,128)(2,1)S(1)}, u32[]{:S(2)}, u32[]{:S(2)}) collective-permute-start(bf16[2,512,256]{2,1,0:T(8,128)(2,1)S(1)} %collective-permute-done.2.refs_2_), channel_id=1, source_target_pairs={{0,8},{2,6},{8,16},{10,2},{16,24},{18,10},{24,28},{26,18},{28,20},... | collective-permute-start | bytes 1572872 | tf_op jit(solution)/shard_map/ppermute | solution.py:534
  16.7 12.6 %collective-permute-start.10 = (bf16[2,512,256]{2,1,0:T(8,128)(2,1)S(1)}, bf16[2,512,256]{2,1,0:T(8,128)(2,1)S(1)}, u32[]{:S(2)}, u32[]{:S(2)}) collective-permute-start(bf16[2,512,256]{2,1,0:T(8,128)(2,1)S(1)} %both_of.2), channel_id=1, source_target_pairs={{0,8},{2,6},{8,16},{10,2},{16,24},{18,10},{24,28},{26,18},{28,20},... | collective-permute-start | bytes 1572872 | tf_op jit(solution)/shard_map/ppermute | solution.py:534
  17.0 13.8 %collective-permute-start.11 = (bf16[2,512,256]{2,1,0:T(8,128)(2,1)S(1)}, bf16[2,512,256]{2,1,0:T(8,128)(2,1)S(1)}, u32[]{:S(2)}, u32[]{:S(2)}) collective-permute-start(bf16[2,512,256]{2,1,0:T(8,128)(2,1)S(1)} %collective-permute-done.2.refs_2_), channel_id=1, source_target_pairs={{0,1},{1,0},{2,3},{3,2},{4,5},{5,4},{6,7},{7,6},{8,9},{9,8},{10,11... | collective-permute-start | bytes 1572872 | tf_op jit(solution)/shard_map/ppermute | solution.py:109
  18.2 16.8 %collective-permute-start.8 = (bf16[512,512]{1,0:T(8,128)(2,1)S(1)}, bf16[512,512]{1,0:T(8,128)(2,1)S(1)}, u32[]{:S(2)}, u32[]{:S(2)}) collective-permute-start(bf16[512,512]{1,0:T(8,128)(2,1)S(1)} %copy-done.1), channel_id=1, source_target_pairs={{0,8},{2,6},{8,16},{10,2},{16,24},{18,10},{24,28},{26,18},{28,20},... | collective-permute-start | bytes 1572872 | tf_op jit(solution)/shard_map/ppermute | solution.py:534
  23.7 16.9 %collective-permute-start.5 = (bf16[2,512,256]{2,1,0:T(8,128)(2,1)S(1)}, bf16[2,512,256]{2,1,0:T(8,128)(2,1)S(1)}, u32[]{:S(2)}, u32[]{:S(2)}) collective-permute-start(bf16[2,512,256]{2,1,0:T(8,128)(2,1)S(1)} %collective-permute-done.4.refs_0_), channel_id=1, source_target_pairs={{0,8},{2,6},{8,16},{10,2},{16,24},{18,10},{24,28},{26,18},{28,20},... | collective-permute-start | bytes 1572872 | tf_op jit(solution)/shard_map/ppermute | solution.py:534
  29.4 12.5 %collective-permute-start.6 = (bf16[2,512,256]{2,1,0:T(8,128)(2,1)S(1)}, bf16[2,512,256]{2,1,0:T(8,128)(2,1)S(1)}, u32[]{:S(2)}, u32[]{:S(2)}) collective-permute-start(bf16[2,512,256]{2,1,0:T(8,128)(2,1)S(1)} %collective-permute-done.4.refs_0_), channel_id=1, source_target_pairs={{0,1},{1,0},{2,3},{3,2},{4,5},{5,4},{6,7},{7,6},{8,9},{9,8},{10,11... | collective-permute-start | bytes 1572872 | tf_op jit(solution)/shard_map/ppermute | solution.py:109
  30.8 15.4 %collective-permute-start.12 = (bf16[2,512,256]{2,1,0:T(8,128)(2,1)S(1)}, bf16[2,512,256]{2,1,0:T(8,128)(2,1)S(1)}, u32[]{:S(2)}, u32[]{:S(2)}) collective-permute-start(bf16[2,512,256]{2,1,0:T(8,128)(2,1)S(1)} %collective-permute-done.10.refs_1_), channel_id=1, source_target_pairs={{0,8},{2,6},{8,16},{10,2},{16,24},{18,10},{24,28},{26,18},{28,20},... | collective-permute-start | bytes 1572872 | tf_op jit(solution)/shard_map/ppermute | solution.py:534
  35.0 13.8 %collective-permute-start.14 = (bf16[256,512]{1,0:T(8,128)(2,1)S(1)}, bf16[256,512]{1,0:T(8,128)(2,1)S(1)}, u32[]{:S(2)}, u32[]{:S(2)}) collective-permute-start(bf16[256,512]{1,0:T(8,128)(2,1)S(1)} %rows_near.1), channel_id=1, source_target_pairs={{0,2},{2,0},{4,6},{6,4},{8,10},{10,8},{12,14},{14,12},{16,18},{18,... | collective-permute-start | bytes 786440 | tf_op jit(solution)/shard_map/ppermute | solution.py:105
  41.9 7.1 %collective-permute-start.7 = (bf16[1,512,256]{2,1,0:T(8,128)(2,1)S(1)}, bf16[1,512,256]{2,1,0:T(8,128)(2,1)S(1)}, u32[]{:S(2)}, u32[]{:S(2)}) collective-permute-start(bf16[1,512,256]{2,1,0:T(8,128)(2,1)S(1)} %first_of.2), channel_id=1, source_target_pairs={{0,8},{2,6},{8,16},{10,2},{16,24},{18,10},{24,28},{26,18},{28,20},... | collective-permute-start | bytes 786440 | tf_op jit(solution)/shard_map/ppermute | solution.py:534
  46.2 15.1 %collective-permute-start.13 = (bf16[2,512,256]{2,1,0:T(8,128)(2,1)S(1)}, bf16[2,512,256]{2,1,0:T(8,128)(2,1)S(1)}, u32[]{:S(2)}, u32[]{:S(2)}) collective-permute-start(bf16[2,512,256]{2,1,0:T(8,128)(2,1)S(1)} %collective-permute-done.12.refs_0_), channel_id=1, source_target_pairs={{0,8},{2,6},{8,16},{10,2},{16,24},{18,10},{24,28},{26,18},{28,20},... | collective-permute-start | bytes 1572872 | tf_op jit(solution)/shard_map/ppermute | solution.py:534
  47.5 14.1 %collective-permute-start.16 = (bf16[2,512,256]{2,1,0:T(8,128)(2,1)S(1)}, bf16[2,512,256]{2,1,0:T(8,128)(2,1)S(1)}, u32[]{:S(2)}, u32[]{:S(2)}) collective-permute-start(bf16[2,512,256]{2,1,0:T(8,128)(2,1)S(1)} %collective-permute-done.5.pair_ref.refs_0_), channel_id=1, source_target_pairs={{0,1},{1,0},{2,3},{3,2},{4,5},{5,4},{6,7},{7,6},{8,9},{9,8},{10,11... | collective-permute-start | bytes 1572872 | tf_op jit(solution)/shard_map/ppermute | solution.py:109
  48.7 8.7 %collective-permute-start.15 = (bf16[256,512]{1,0:T(8,128)(2,1)S(1)}, bf16[256,512]{1,0:T(8,128)(2,1)S(1)}, u32[]{:S(2)}, u32[]{:S(2)}) collective-permute-start(bf16[256,512]{1,0:T(8,128)(2,1)S(1)} %collective-permute-done.14), channel_id=1, source_target_pairs={{0,8},{2,6},{8,16},{10,2},{16,24},{18,10},{24,28},{26,18},{28,20},... | collective-permute-start | bytes 786440 | tf_op jit(solution)/shard_map/ppermute | solution.py:534
  49.0 14.0 %collective-permute-start.9 = (bf16[512,512]{1,0:T(8,128)(2,1)S(1)}, bf16[512,512]{1,0:T(8,128)(2,1)S(1)}, u32[]{:S(2)}, u32[]{:S(2)}) collective-permute-start(bf16[512,512]{1,0:T(8,128)(2,1)S(1)} %collective-permute-done.8.refs_2_), channel_id=1, source_target_pairs={{0,8},{2,6},{8,16},{10,2},{16,24},{18,10},{24,28},{26,18},{28,20},... | collective-permute-start | bytes 1572872 | tf_op jit(solution)/shard_map/ppermute | solution.py:534
  57.4 16.7 %collective-permute-start.23 = (bf16[256,512]{1,0:T(8,128)(2,1)S(1)}, bf16[256,512]{1,0:T(8,128)(2,1)S(1)}, u32[]{:S(2)}, u32[]{:S(2)}) collective-permute-start(bf16[256,512]{1,0:T(8,128)(2,1)S(1)} %collective-permute-done.15.refs_3_), channel_id=1, source_target_pairs={{0,8},{2,6},{8,16},{10,2},{16,24},{18,10},{24,28},{26,18},{28,20},... | collective-permute-start | bytes 786440 | tf_op jit(solution)/shard_map/ppermute | solution.py:534
  58.7 15.4 %collective-permute-start.19 = (bf16[1,512,256]{2,1,0:T(8,128)(2,1)S(1)}, bf16[1,512,256]{2,1,0:T(8,128)(2,1)S(1)}, u32[]{:S(2)}, u32[]{:S(2)}) collective-permute-start(bf16[1,512,256]{2,1,0:T(8,128)(2,1)S(1)} %collective-permute-done.7.refs_0_), channel_id=1, source_target_pairs={{0,1},{1,0},{2,3},{3,2},{4,5},{5,4},{6,7},{7,6},{8,9},{9,8},{10,11... | collective-permute-start | bytes 786440 | tf_op jit(solution)/shard_map/ppermute | solution.py:109
  61.3 10.1 %collective-permute-start.20 = (bf16[256,512]{1,0:T(8,128)(2,1)S(1)}, bf16[256,512]{1,0:T(8,128)(2,1)S(1)}, u32[]{:S(2)}, u32[]{:S(2)}) collective-permute-start(bf16[256,512]{1,0:T(8,128)(2,1)S(1)} %collective-permute-done.15.refs_3_), channel_id=1, source_target_pairs={{0,1},{1,0},{2,3},{3,2},{4,5},{5,4},{6,7},{7,6},{8,9},{9,8},{10,11... | collective-permute-start | bytes 786440 | tf_op jit(solution)/shard_map/ppermute | solution.py:109
  61.6 7.1 %collective-permute-start.17 = (bf16[1,512,256]{2,1,0:T(8,128)(2,1)S(1)}, bf16[1,512,256]{2,1,0:T(8,128)(2,1)S(1)}, u32[]{:S(2)}, u32[]{:S(2)}) collective-permute-start(bf16[1,512,256]{2,1,0:T(8,128)(2,1)S(1)} %first_of.3), channel_id=1, source_target_pairs={{0,8},{2,6},{8,16},{10,2},{16,24},{18,10},{24,28},{26,18},{28,20},... | collective-permute-start | bytes 786440 | tf_op jit(solution)/shard_map/ppermute | solution.py:534
  68.7 8.3 %collective-permute-start.18 = (bf16[512,512]{1,0:T(8,128)(2,1)S(1)}, bf16[512,512]{1,0:T(8,128)(2,1)S(1)}, u32[]{:S(2)}, u32[]{:S(2)}) collective-permute-start(bf16[512,512]{1,0:T(8,128)(2,1)S(1)} %collective-permute-done.9.refs_8_), channel_id=1, source_target_pairs={{0,8},{2,6},{8,16},{10,2},{16,24},{18,10},{24,28},{26,18},{28,20},... | collective-permute-start | bytes 1572872 | tf_op jit(solution)/shard_map/ppermute | solution.py:534
  74.0 13.9 %collective-permute-start.35 = (bf16[256,512]{1,0:T(8,128)(2,1)S(1)}, bf16[256,512]{1,0:T(8,128)(2,1)S(1)}, u32[]{:S(2)}, u32[]{:S(2)}) collective-permute-start(bf16[256,512]{1,0:T(8,128)(2,1)S(1)} %collective-permute-done.15.refs_3_), channel_id=1, source_target_pairs={{0,2},{2,0},{4,6},{6,4},{8,10},{10,8},{12,14},{14,12},{16,18},{18,... | collective-permute-start | bytes 786440 | tf_op jit(solution)/shard_map/ppermute | solution.py:105
  74.1 7.5 %collective-permute-start.26 = (bf16[256,512]{1,0:T(8,128)(2,1)S(1)}, bf16[256,512]{1,0:T(8,128)(2,1)S(1)}, u32[]{:S(2)}, u32[]{:S(2)}) collective-permute-start(bf16[256,512]{1,0:T(8,128)(2,1)S(1)} %collective-permute-done.23.refs_9_), channel_id=1, source_target_pairs={{0,1},{1,0},{2,3},{3,2},{4,5},{5,4},{6,7},{7,6},{8,9},{9,8},{10,11... | collective-permute-start | bytes 786440 | tf_op jit(solution)/shard_map/ppermute | solution.py:109
  78.1 28.7 %collective-permute-start.22 = (f32[256,512]{1,0:T(8,128)S(1)}, f32[256,512]{1,0:T(8,128)S(1)}, u32[]{:S(2)}, u32[]{:S(2)}) collective-permute-start(f32[256,512]{1,0:T(8,128)S(1)} %get-tuple-element.69), channel_id=1, source_target_pairs={{0,2},{2,0},{4,6},{6,4},{8,10},{10,8},{12,14},{14,12},{16,18},{18,... | collective-permute-start | bytes 1572872 | tf_op jit(solution)/shard_map/ppermute | solution.py:105
  80.7 9.2 %collective-permute-start.36 = (bf16[256,512]{1,0:T(8,128)(2,1)S(1)}, bf16[256,512]{1,0:T(8,128)(2,1)S(1)}, u32[]{:S(2)}, u32[]{:S(2)}) collective-permute-start(bf16[256,512]{1,0:T(8,128)(2,1)S(1)} %collective-permute-done.20.refs_4_), channel_id=1, source_target_pairs={{0,2},{2,0},{4,6},{6,4},{8,10},{10,8},{12,14},{14,12},{16,18},{18,... | collective-permute-start | bytes 786440 | tf_op jit(solution)/shard_map/ppermute | solution.py:105
  81.6 11.3 %collective-permute-start.25 = (bf16[256,512]{1,0:T(8,128)(2,1)S(1)}, bf16[256,512]{1,0:T(8,128)(2,1)S(1)}, u32[]{:S(2)}, u32[]{:S(2)}) collective-permute-start(bf16[256,512]{1,0:T(8,128)(2,1)S(1)} %collective-permute-done.24.refs_15_), channel_id=1, source_target_pairs={{0,1},{1,0},{2,3},{3,2},{4,5},{5,4},{6,7},{7,6},{8,9},{9,8},{10,11... | collective-permute-start | bytes 786440 | tf_op jit(solution)/shard_map/ppermute | solution.py:109
  86.0 11.6 %collective-permute-start.28 = (bf16[2,256,256]{2,1,0:T(8,128)(2,1)S(1)}, bf16[2,256,256]{2,1,0:T(8,128)(2,1)S(1)}, u32[]{:S(2)}, u32[]{:S(2)}) collective-permute-start(bf16[2,256,256]{2,1,0:T(8,128)(2,1)S(1)} %join_row.1.refs_2_), channel_id=1, source_target_pairs={{0,16},{4,20},{8,24},{12,28},{16,26},{20,30},{24,18},{28,22},{26,1... | collective-permute-start | bytes 786440 | tf_op jit(solution)/shard_map/ppermute | solution.py:622
  87.9 12.3 %collective-permute-start.29 = (bf16[2,256,256]{2,1,0:T(8,128)(2,1)S(1)}, bf16[2,256,256]{2,1,0:T(8,128)(2,1)S(1)}, u32[]{:S(2)}, u32[]{:S(2)}) collective-permute-start(bf16[2,256,256]{2,1,0:T(8,128)(2,1)S(1)} %join_row.1.refs_2_), channel_id=1, source_target_pairs={{0,8},{4,12},{8,16},{12,20},{16,24},{20,28},{24,26},{28,30},{26,18... | collective-permute-start | bytes 786440 | tf_op jit(solution)/shard_map/ppermute | solution.py:622
  89.9 21.1 %collective-permute-start.37 = (bf16[512,512]{1,0:T(8,128)(2,1)S(1)}, bf16[512,512]{1,0:T(8,128)(2,1)S(1)}, u32[]{:S(2)}, u32[]{:S(2)}) collective-permute-start(bf16[512,512]{1,0:T(8,128)(2,1)S(1)} %collective-permute-done.9.refs_8_), channel_id=1, source_target_pairs={{0,2},{2,0},{4,6},{6,4},{8,10},{10,8},{12,14},{14,12},{16,18},{18,... | collective-permute-start | bytes 1572872 | tf_op jit(solution)/shard_map/ppermute | solution.py:105
  92.8 18.6 %collective-permute-start.31 = (bf16[512,512]{1,0:T(8,128)(2,1)S(1)}, bf16[512,512]{1,0:T(8,128)(2,1)S(1)}, u32[]{:S(2)}, u32[]{:S(2)}) collective-permute-start(bf16[512,512]{1,0:T(8,128)(2,1)S(1)} %collective-permute-done.18.refs_14_), channel_id=1, source_target_pairs={{0,8},{2,6},{8,16},{10,2},{16,24},{18,10},{24,28},{26,18},{28,20},... | collective-permute-start | bytes 1572872 | tf_op jit(solution)/shard_map/ppermute | solution.py:534
  97.6 12.7 %collective-permute-start.38 = (bf16[256,512]{1,0:T(8,128)(2,1)S(1)}, bf16[256,512]{1,0:T(8,128)(2,1)S(1)}, u32[]{:S(2)}, u32[]{:S(2)}) collective-permute-start(bf16[256,512]{1,0:T(8,128)(2,1)S(1)} %collective-permute-done.23.refs_9_), channel_id=1, source_target_pairs={{0,2},{2,0},{4,6},{6,4},{8,10},{10,8},{12,14},{14,12},{16,18},{18,... | collective-permute-start | bytes 786440 | tf_op jit(solution)/shard_map/ppermute | solution.py:105
  100.2 10.7 %collective-permute-start.39 = (bf16[256,512]{1,0:T(8,128)(2,1)S(1)}, bf16[256,512]{1,0:T(8,128)(2,1)S(1)}, u32[]{:S(2)}, u32[]{:S(2)}) collective-permute-start(bf16[256,512]{1,0:T(8,128)(2,1)S(1)} %collective-permute-done.26.refs_10_), channel_id=1, source_target_pairs={{0,2},{2,0},{4,6},{6,4},{8,10},{10,8},{12,14},{14,12},{16,18},{18,... | collective-permute-start | bytes 786440 | tf_op jit(solution)/shard_map/ppermute | solution.py:105
  111.4 7.1 %collective-permute-start.32 = (bf16[512,512]{1,0:T(8,128)(2,1)S(1)}, bf16[512,512]{1,0:T(8,128)(2,1)S(1)}, u32[]{:S(2)}, u32[]{:S(2)}) collective-permute-start(bf16[512,512]{1,0:T(8,128)(2,1)S(1)} %collective-permute-done.31.refs_0_), channel_id=1, source_target_pairs={{0,2},{2,0},{4,6},{6,4},{8,10},{10,8},{12,14},{14,12},{16,18},{18,... | collective-permute-start | bytes 1572872 | tf_op jit(solution)/shard_map/ppermute | solution.py:105
  (14 other events, 58.8 us)

commit v7 on v6

--- a/solution.py
+++ b/solution.py
@@ -20,8 +20,8 @@
     "C0",
     "T0",
     "B0 N1",
-    "H0 N1 C0",
-    "S0",
+    "H0 C0",
+    "S0 N1",
     "N2",
     "C1 N1",
     "F1",
@@ -55,8 +55,7 @@
     "A4 R0",
     "M0 X3 R2",
     "M1",
-    "W0 M0",
-    "W1 B3",
+    "W1 M0",
     "W2",
     "W3",
     "O0",
@@ -298,25 +297,22 @@
     )(plane, *in_hbm(query, key, value))
 
 
-def rows_near_kernel(plane_ref, weight_ref, out_ref, sem):
+def rows_near_kernel(plane_ref, weight_ref, out_ref):
     half = out_ref.shape[0]
     near = pl.ds(pl.multiple_of(plane_ref[0] * half, half), half)
-    copy = pltpu.make_async_copy(weight_ref.at[near, :], out_ref, sem)
-    copy.start()
-    copy.wait()
+    out_ref[...] = weight_ref[near, :]
 
 
 def rows_near_of(plane, weight):
     rows, columns = weight.shape
     return pl.pallas_call(
         rows_near_kernel,
-        in_specs=[IN_SMEM, IN_HBM],
+        in_specs=[IN_SMEM, IN_VMEM],
         out_specs=IN_VMEM,
-        scratch_shapes=[pltpu.SemaphoreType.DMA],
         out_shape=pltpu.VMEM((rows // 2, columns), weight.dtype),
         compiler_params=params(),
         name="rows_near",
-    )(plane, *in_hbm(weight))
+    )(plane, *in_vmem(weight))
 
 
 def both_kernel(first_ref, second_ref, out_ref):
@@ -566,10 +562,10 @@
             elif name == "H0":
                 value = bring(tied(hidden_in), micros)
             elif name == "B0":
-                rows_near = w_out
+                done["W0"] = (core_swap(tied(w_out), count),)
+                value = done["W0"][0]
                 if HALVED:
-                    rows_near = own_rows_near
-                value = core_swap(tied(rows_near), count)
+                    value = rows_near_of(plane_index, value)
             elif name == "A0":
                 value = w_out
             elif kind in ("C", "N"):
@@ -626,13 +622,10 @@
             elif name == "M1":
                 value = core_swap(done["M0"], count)
             elif kind == "W":
-                if step == 0:
-                    value = (core_swap(tied(w_out), count),)
-                else:
-                    value = [core_swap(tied(done[f"A{step}"]), count)]
-                    if step < half:
-                        value.append(core_swap(done[f"B{step}"], count))
-                        value.append(core_swap(done[f"X{step}"], count))
+                value = [core_swap(tied(done[f"A{step}"]), count)]
+                if step < half:
+                    value.append(core_swap(done[f"B{step}"], count))
+                    value.append(core_swap(done[f"X{step}"], count))
             elif kind == "O":
                 shards = []
                 for turn in COLUMNS[step]:
@@ -655,10 +648,7 @@
                 )
             done[name] = value
 
-        own_rows_near = None
         cosine, sine, query_cosine, query_sine, key_seg = tables
-        if HALVED:
-            own_rows_near = rows_near_of(plane_index, w_out)
         for entry in PLAN:
             run(*entry.split())
         return done["O1"]

time: 121 us -> 119 us (0.983)
  waiting for transfers between devices: 52.4 us -> 48.1 us
  starting transfers between devices: 43.5 us -> 47.6 us
    ppermute x2, waiting for transfers between devices: 6.95 us -> 4.12 us  [run(): value = lax.ppermute(tied(done['R0']), 'ctx', sends)]
    ppermute x18 -> x17, starting transfers between devices: 19.1 us -> 21.4 us  [core_swap(): return lax.ppermute(value, 'ctx', [(i, i ^ 1) for i in range(count)])]
    ppermute x15, starting transfers between devices: 12.8 us -> 14.5 us  [ring(): return lax.ppermute(value, 'ctx', pairs)]
    ppermute x15, waiting for transfers between devices: 35.8 us -> 34.6 us  [ring(): return lax.ppermute(value, 'ctx', pairs)]
    ppermute x18 -> x17, waiting for transfers between devices: 3.39 us -> 3.13 us  [core_swap(): return lax.ppermute(value, 'ctx', [(i, i ^ 1) for i in range(count)])]
  transfers between devices with their start and end apart: 43 -> 42, of which waited for: 19 -> 20; matrix products, arithmetic and copies ran while one was open for 1% -> 1% of each run, Pallas kernels for 14% -> 15%
where the time goes in v7:
time: 119 us
  waiting for transfers between devices  48.1 us (40%)
  starting transfers between devices  47.6 us (40%)
  Pallas kernels  21.3 us (18%)
    ppermute x15, waiting for transfers between devices, ring(): return lax.ppermute(value, 'ctx', pairs)  34.6 us
    ppermute x17, starting transfers between devices, core_swap(): return lax.ppermute(value, 'ctx', [(i, i ^ 1) for i in range(count)])  21.4 us
    ppermute x15, starting transfers between devices, ring(): return lax.ppermute(value, 'ctx', pairs)  14.5 us
    pallas_call x7, Pallas kernels, project(): pl.pallas_call(functools.partial(project_kernel, slots, base, groups, tot...  8.38 us
    ppermute x7, starting transfers between devices, plane_swap(): return lax.ppermute(value, 'dp', [(0, 1), (1, 0)])  7.73 us
    pallas_call x2, Pallas kernels, columns_of(): pl.pallas_call(functools.partial(columns_kernel, entries), in_specs=specs...  5.16 us
    ppermute x7, waiting for transfers between devices, plane_swap(): return lax.ppermute(value, 'dp', [(0, 1), (1, 0)])  4.22 us
    ppermute x2, waiting for transfers between devices, run(): value = lax.ppermute(tied(done['R0']), 'ctx', sends)  4.12 us
  transfers between devices with their start and end apart: 42, of which 20 were waited for; matrix products, arithmetic and copies ran while one was open for 1% of the time, Pallas kernels for 15%

profile of v7, /device:TPU:19, one launch (start us, length us, event | category | flops | bytes accessed | tf_op | source)
XLA Modules:
  0.0 119.1 jit_solution(1949154552194000214)
XLA Ops:
  3.5 1.3 %collective-permute-start.2 = (bf16[2,512,256]{2,1,0:T(8,128)(2,1)S(1)}, bf16[2,512,256]{2,1,0:T(8,128)(2,1)S(1)}, u32[]{:S(2)}, u32[]{:S(2)}) collective-permute-start(bf16[2,512,256]{2,1,0:T(8,128)(2,1)S(1)} %both_of.3), channel_id=1, source_target_pairs={{0,8},{2,6},{8,16},{10,2},{16,24},{18,10},{24,28},{26,18},{28,20},... | collective-permute-start | bytes 1572872 | tf_op jit(solution)/shard_map/ppermute | solution.py:530
  5.6 2.3 %bring.1.own_ref = bf16[256,8192]{1,0:T(8,128)(2,1)S(1)} custom-call(bf16[256,8192]{1,0:T(8,128)(2,1)} %source_ref), custom_call_target="tpu_custom_call" | custom-call | flops 2307000064 | tf_op jit(solution)/shard_map/bring/pallas_call | solution.py:356
  7.9 4.0 %collective-permute-done.2.refs_2_ = bf16[2,512,256]{2,1,0:T(8,128)(2,1)S(1)} collective-permute-done((bf16[2,512,256]{2,1,0:T(8,128)(2,1)S(1)}, bf16[2,512,256]{2,1,0:T(8,128)(2,1)S(1)}, u32[]{:S(2)}, u32[]{:S(2)}) %collective-permute-start.2) | collective-permute-done | bytes 524320 | tf_op jit(solution)/shard_map/ppermute | solution.py:530
  13.1 1.3 %collective-permute-start.4 = (bf16[2,512,256]{2,1,0:T(8,128)(2,1)S(1)}, bf16[2,512,256]{2,1,0:T(8,128)(2,1)S(1)}, u32[]{:S(2)}, u32[]{:S(2)}) collective-permute-start(bf16[2,512,256]{2,1,0:T(8,128)(2,1)S(1)} %collective-permute-done.2.refs_2_), channel_id=1, source_target_pairs={{0,8},{2,6},{8,16},{10,2},{16,24},{18,10},{24,28},{26,18},{28,20},... | collective-permute-start | bytes 1572872 | tf_op jit(solution)/shard_map/ppermute | solution.py:530
  16.1 5.4 %collective-permute-done.4.refs_0_ = bf16[2,512,256]{2,1,0:T(8,128)(2,1)S(1)} collective-permute-done((bf16[2,512,256]{2,1,0:T(8,128)(2,1)S(1)}, bf16[2,512,256]{2,1,0:T(8,128)(2,1)S(1)}, u32[]{:S(2)}, u32[]{:S(2)}) %collective-permute-start.4) | collective-permute-done | bytes 524320 | tf_op jit(solution)/shard_map/ppermute | solution.py:530
  21.5 1.3 %collective-permute-start.5 = (bf16[2,512,256]{2,1,0:T(8,128)(2,1)S(1)}, bf16[2,512,256]{2,1,0:T(8,128)(2,1)S(1)}, u32[]{:S(2)}, u32[]{:S(2)}) collective-permute-start(bf16[2,512,256]{2,1,0:T(8,128)(2,1)S(1)} %collective-permute-done.4.refs_0_), channel_id=1, source_target_pairs={{0,8},{2,6},{8,16},{10,2},{16,24},{18,10},{24,28},{26,18},{28,20},... | collective-permute-start | bytes 1572872 | tf_op jit(solution)/shard_map/ppermute | solution.py:530
  22.8 4.3 %collective-permute-done.10.refs_1_ = bf16[2,512,256]{2,1,0:T(8,128)(2,1)S(1)} collective-permute-done((bf16[2,512,256]{2,1,0:T(8,128)(2,1)S(1)}, bf16[2,512,256]{2,1,0:T(8,128)(2,1)S(1)}, u32[]{:S(2)}, u32[]{:S(2)}) %collective-permute-start.10) | collective-permute-done | bytes 524320 | tf_op jit(solution)/shard_map/ppermute | solution.py:530
  29.6 3.1 %collective-permute-done.8.refs_2_ = bf16[512,512]{1,0:T(8,128)(2,1)S(1)} collective-permute-done((bf16[512,512]{1,0:T(8,128)(2,1)S(1)}, bf16[512,512]{1,0:T(8,128)(2,1)S(1)}, u32[]{:S(2)}, u32[]{:S(2)}) %collective-permute-start.8) | collective-permute-done | bytes 524320 | tf_op jit(solution)/shard_map/ppermute | solution.py:530
  33.6 4.8 %collective-permute-done.5.pair_ref.refs_0_ = bf16[2,512,256]{2,1,0:T(8,128)(2,1)S(1)} collective-permute-done((bf16[2,512,256]{2,1,0:T(8,128)(2,1)S(1)}, bf16[2,512,256]{2,1,0:T(8,128)(2,1)S(1)}, u32[]{:S(2)}, u32[]{:S(2)}) %collective-permute-start.5) | collective-permute-done | bytes 524320 | tf_op jit(solution)/shard_map/ppermute | solution.py:530
  38.3 1.3 %collective-permute-done.6.refs_1_ = bf16[2,512,256]{2,1,0:T(8,128)(2,1)S(1)} collective-permute-done((bf16[2,512,256]{2,1,0:T(8,128)(2,1)S(1)}, bf16[2,512,256]{2,1,0:T(8,128)(2,1)S(1)}, u32[]{:S(2)}, u32[]{:S(2)}) %collective-permute-start.6) | collective-permute-done | bytes 524320 | tf_op jit(solution)/shard_map/ppermute | solution.py:108
  41.0 1.5 %project.7.refs_2_ = f32[2,256,512]{2,1,0:T(8,128)S(1)} custom-call(s32[19]{0:T(128)S(1)} %stack.76.index_ref, bf16[256,8192]{1,0:T(8,128)(2,1)S(1)} %bring.1.own_ref, bf16[256,8192]{1,0:T(8,128)(2,1)S(1)} %collective-permute-done.3.other_ref, bf16[1,512,256]{2,1,0:T(8,128)(2,1)S(1)} %get-tuple-element.53.first_ref.refs_0_, ...), custom_call_target="tpu_custom_call" | custom-call | flops 2307000064 | tf_op jit(solution)/shard_map/project/pallas_call | solution.py:411
  42.5 1.4 %collective-permute-done.12.refs_0_ = bf16[2,512,256]{2,1,0:T(8,128)(2,1)S(1)} collective-permute-done((bf16[2,512,256]{2,1,0:T(8,128)(2,1)S(1)}, bf16[2,512,256]{2,1,0:T(8,128)(2,1)S(1)}, u32[]{:S(2)}, u32[]{:S(2)}) %collective-permute-start.12) | collective-permute-done | bytes 524320 | tf_op jit(solution)/shard_map/ppermute | solution.py:530
  43.9 1.3 %collective-permute-start.13 = (bf16[2,512,256]{2,1,0:T(8,128)(2,1)S(1)}, bf16[2,512,256]{2,1,0:T(8,128)(2,1)S(1)}, u32[]{:S(2)}, u32[]{:S(2)}) collective-permute-start(bf16[2,512,256]{2,1,0:T(8,128)(2,1)S(1)} %collective-permute-done.12.refs_0_), channel_id=1, source_target_pairs={{0,8},{2,6},{8,16},{10,2},{16,24},{18,10},{24,28},{26,18},{28,20},... | collective-permute-start | bytes 1572872 | tf_op jit(solution)/shard_map/ppermute | solution.py:530
  48.0 7.1 %collective-permute-done.15.refs_3_ = bf16[256,512]{1,0:T(8,128)(2,1)S(1)} collective-permute-done((bf16[256,512]{1,0:T(8,128)(2,1)S(1)}, bf16[256,512]{1,0:T(8,128)(2,1)S(1)}, u32[]{:S(2)}, u32[]{:S(2)}) %collective-permute-start.15) | collective-permute-done | bytes 262176 | tf_op jit(solution)/shard_map/ppermute | solution.py:530
  62.1 4.4 %collective-permute-done.17.refs_0_ = bf16[1,512,256]{2,1,0:T(8,128)(2,1)S(1)} collective-permute-done((bf16[1,512,256]{2,1,0:T(8,128)(2,1)S(1)}, bf16[1,512,256]{2,1,0:T(8,128)(2,1)S(1)}, u32[]{:S(2)}, u32[]{:S(2)}) %collective-permute-start.17) | collective-permute-done | bytes 262176 | tf_op jit(solution)/shard_map/ppermute | solution.py:530
  66.4 1.3 %collective-permute-start.18 = (bf16[512,512]{1,0:T(8,128)(2,1)S(1)}, bf16[512,512]{1,0:T(8,128)(2,1)S(1)}, u32[]{:S(2)}, u32[]{:S(2)}) collective-permute-start(bf16[512,512]{1,0:T(8,128)(2,1)S(1)} %collective-permute-done.9.refs_8_), channel_id=1, source_target_pairs={{0,8},{2,6},{8,16},{10,2},{16,24},{18,10},{24,28},{26,18},{28,20},... | collective-permute-start | bytes 1572872 | tf_op jit(solution)/shard_map/ppermute | solution.py:530
  67.7 1.5 %collective-permute-done.20.refs_4_ = bf16[256,512]{1,0:T(8,128)(2,1)S(1)} collective-permute-done((bf16[256,512]{1,0:T(8,128)(2,1)S(1)}, bf16[256,512]{1,0:T(8,128)(2,1)S(1)}, u32[]{:S(2)}, u32[]{:S(2)}) %collective-permute-start.20) | collective-permute-done | bytes 262176 | tf_op jit(solution)/shard_map/ppermute | solution.py:108
  70.0 1.7 %collective-permute-start.21 = (f32[256,256]{1,0:T(8,128)S(1)}, f32[256,256]{1,0:T(8,128)S(1)}, u32[]{:S(2)}, u32[]{:S(2)}) collective-permute-start(f32[256,256]{1,0:T(8,128)S(1)} %get-tuple-element.65), channel_id=1, source_target_pairs={{0,2},{2,0},{4,6},{6,4},{8,10},{10,8},{12,14},{14,12},{16,18},{18,... | collective-permute-start | bytes 786440 | tf_op jit(solution)/shard_map/ppermute | solution.py:104
  75.8 2.5 %collective-permute-start.22 = (f32[256,512]{1,0:T(8,128)S(1)}, f32[256,512]{1,0:T(8,128)S(1)}, u32[]{:S(2)}, u32[]{:S(2)}) collective-permute-start(f32[256,512]{1,0:T(8,128)S(1)} %get-tuple-element.70), channel_id=1, source_target_pairs={{0,2},{2,0},{4,6},{6,4},{8,10},{10,8},{12,14},{14,12},{16,18},{18,... | collective-permute-start | bytes 1572872 | tf_op jit(solution)/shard_map/ppermute | solution.py:104
  78.3 1.3 %collective-permute-done.26.refs_10_ = bf16[256,512]{1,0:T(8,128)(2,1)S(1)} collective-permute-done((bf16[256,512]{1,0:T(8,128)(2,1)S(1)}, bf16[256,512]{1,0:T(8,128)(2,1)S(1)}, u32[]{:S(2)}, u32[]{:S(2)}) %collective-permute-start.26) | collective-permute-done | bytes 262176 | tf_op jit(solution)/shard_map/ppermute | solution.py:108
  81.7 2.0 %collective-permute-done.27.beside_ref = bf16[256,256]{1,0:T(8,128)(2,1)S(1)} collective-permute-done((bf16[256,256]{1,0:T(8,128)(2,1)S(1)}, bf16[256,256]{1,0:T(8,128)(2,1)S(1)}, u32[]{:S(2)}, u32[]{:S(2)}) %collective-permute-start.27) | collective-permute-done | bytes 131104 | tf_op jit(solution)/shard_map/ppermute | solution.py:611
  84.4 2.0 %collective-permute-start.28 = (bf16[2,256,256]{2,1,0:T(8,128)(2,1)S(1)}, bf16[2,256,256]{2,1,0:T(8,128)(2,1)S(1)}, u32[]{:S(2)}, u32[]{:S(2)}) collective-permute-start(bf16[2,256,256]{2,1,0:T(8,128)(2,1)S(1)} %join_row.1.refs_2_), channel_id=1, source_target_pairs={{0,16},{4,20},{8,24},{12,28},{16,26},{20,30},{24,18},{28,22},{26,1... | collective-permute-start | bytes 786440 | tf_op jit(solution)/shard_map/ppermute | solution.py:618
  86.3 1.9 %collective-permute-start.29 = (bf16[2,256,256]{2,1,0:T(8,128)(2,1)S(1)}, bf16[2,256,256]{2,1,0:T(8,128)(2,1)S(1)}, u32[]{:S(2)}, u32[]{:S(2)}) collective-permute-start(bf16[2,256,256]{2,1,0:T(8,128)(2,1)S(1)} %join_row.1.refs_2_), channel_id=1, source_target_pairs={{0,8},{4,12},{8,16},{12,20},{16,24},{20,28},{24,26},{28,30},{26,18... | collective-permute-start | bytes 786440 | tf_op jit(solution)/shard_map/ppermute | solution.py:618
  88.3 1.7 %collective-permute-start.31 = (bf16[512,512]{1,0:T(8,128)(2,1)S(1)}, bf16[512,512]{1,0:T(8,128)(2,1)S(1)}, u32[]{:S(2)}, u32[]{:S(2)}) collective-permute-start(bf16[512,512]{1,0:T(8,128)(2,1)S(1)} %collective-permute-done.18.refs_14_), channel_id=1, source_target_pairs={{0,8},{2,6},{8,16},{10,2},{16,24},{18,10},{24,28},{26,18},{28,20},... | collective-permute-start | bytes 1572872 | tf_op jit(solution)/shard_map/ppermute | solution.py:530
  89.9 2.3 %collective-permute-start.35 = (bf16[256,512]{1,0:T(8,128)(2,1)S(1)}, bf16[256,512]{1,0:T(8,128)(2,1)S(1)}, u32[]{:S(2)}, u32[]{:S(2)}) collective-permute-start(bf16[256,512]{1,0:T(8,128)(2,1)S(1)} %collective-permute-done.20.refs_4_), channel_id=1, source_target_pairs={{0,2},{2,0},{4,6},{6,4},{8,10},{10,8},{12,14},{14,12},{16,18},{18,... | collective-permute-start | bytes 786440 | tf_op jit(solution)/shard_map/ppermute | solution.py:104
  92.2 3.0 %collective-permute-done.28.refs_0_ = bf16[2,256,256]{2,1,0:T(8,128)(2,1)S(1)} collective-permute-done((bf16[2,256,256]{2,1,0:T(8,128)(2,1)S(1)}, bf16[2,256,256]{2,1,0:T(8,128)(2,1)S(1)}, u32[]{:S(2)}, u32[]{:S(2)}) %collective-permute-start.28) | collective-permute-done | bytes 262176 | tf_op jit(solution)/shard_map/ppermute | solution.py:618
  95.3 2.9 %collective-permute-start.37 = (bf16[256,512]{1,0:T(8,128)(2,1)S(1)}, bf16[256,512]{1,0:T(8,128)(2,1)S(1)}, u32[]{:S(2)}, u32[]{:S(2)}) collective-permute-start(bf16[256,512]{1,0:T(8,128)(2,1)S(1)} %collective-permute-done.23.refs_9_), channel_id=1, source_target_pairs={{0,2},{2,0},{4,6},{6,4},{8,10},{10,8},{12,14},{14,12},{16,18},{18,... | collective-permute-start | bytes 786440 | tf_op jit(solution)/shard_map/ppermute | solution.py:104
  99.2 6.3 %collective-permute-start.36 = (bf16[512,512]{1,0:T(8,128)(2,1)S(1)}, bf16[512,512]{1,0:T(8,128)(2,1)S(1)}, u32[]{:S(2)}, u32[]{:S(2)}) collective-permute-start(bf16[512,512]{1,0:T(8,128)(2,1)S(1)} %collective-permute-done.9.refs_8_), channel_id=1, source_target_pairs={{0,2},{2,0},{4,6},{6,4},{8,10},{10,8},{12,14},{14,12},{16,18},{18,... | collective-permute-start | bytes 1572872 | tf_op jit(solution)/shard_map/ppermute | solution.py:104
  105.8 3.3 %attend.1.mixed_ref = bf16[256,512]{1,0:T(8,128)(2,1)S(1)} custom-call(s32[19]{0:T(128)S(1)} %stack.76.index_ref, bf16[256,512]{1,0:T(8,128)(2,1)S(1)} %rotate_sums.3.query_ref, s32[1,1280]{1,0:T(1,128)S(1)} %bitcast.29, bf16[2,256,256]{2,1,0:T(8,128)(2,1)S(1)} %collective-permute-done.28.refs_0_, bf16[2,256,256]{2,1,0:T(8,128)(2,1)S(1)} %collective-permute-done.29.refs_1_, ...), custom_call_target="tpu_custom_call" | custom-call | flops 2307000064 | tf_op jit(solution)/shard_map/attend/pallas_call | solution.py:254
  111.2 2.3 %collective-permute-done.41.refs_19_ = bf16[256,512]{1,0:T(8,128)(2,1)S(1)} collective-permute-done((bf16[256,512]{1,0:T(8,128)(2,1)S(1)}, bf16[256,512]{1,0:T(8,128)(2,1)S(1)}, u32[]{:S(2)}, u32[]{:S(2)}) %collective-permute-start.41) | collective-permute-done | bytes 262176 | tf_op jit(solution)/shard_map/ppermute | solution.py:104
  113.8 3.4 %columns_of.2.refs_2_ = bf16[256,8192]{1,0:T(8,128)(2,1)} custom-call(s32[19]{0:T(128)S(1)} %stack.76.index_ref, bf16[256,512]{1,0:T(8,128)(2,1)S(1)} %attend.1.mixed_ref, bf16[256,512]{1,0:T(8,128)(2,1)S(1)} %collective-permute-done.30.returned_ref, bf16[512,512]{1,0:T(8,128)(2,1)S(1)} %copy-done.1, ...), custom_call_target="tpu_custom_call" | custom-call | flops 2307000064 | tf_op jit(solution)/shard_map/columns_of/pallas_call | solution.py:468
  117.3 1.7 %columns_of.3 = bf16[256,8192]{1,0:T(8,128)(2,1)} custom-call(s32[19]{0:T(128)S(1)} %stack.76.index_ref, bf16[256,512]{1,0:T(8,128)(2,1)S(1)} %attend.1.mixed_ref, bf16[256,512]{1,0:T(8,128)(2,1)S(1)} %collective-permute-done.30.returned_ref, bf16[512,512]{1,0:T(8,128)(2,1)S(1)} %collective-permute-done.31.refs_0_, ...), custom_call_target="tpu_custom_call", output_to_operand_aliasing={{}: (5, {})} | custom-call | flops 2307000064 | tf_op jit(solution)/shard_map/columns_of/pallas_call | solution.py:468
  (87 shorter events, 32.5 us)
Async XLA Ops:
  3.5 8.4 %collective-permute-start.2 = (bf16[2,512,256]{2,1,0:T(8,128)(2,1)S(1)}, bf16[2,512,256]{2,1,0:T(8,128)(2,1)S(1)}, u32[]{:S(2)}, u32[]{:S(2)}) collective-permute-start(bf16[2,512,256]{2,1,0:T(8,128)(2,1)S(1)} %both_of.3), channel_id=1, source_target_pairs={{0,8},{2,6},{8,16},{10,2},{16,24},{18,10},{24,28},{26,18},{28,20},... | collective-permute-start | bytes 1572872 | tf_op jit(solution)/shard_map/ppermute | solution.py:530
  11.9 29.1 %collective-permute-start.3 = (bf16[256,8192]{1,0:T(8,128)(2,1)S(1)}, bf16[256,8192]{1,0:T(8,128)(2,1)S(1)}, u32[]{:S(2)}, u32[]{:S(2)}) collective-permute-start(bf16[256,8192]{1,0:T(8,128)(2,1)S(1)} %bring.1.own_ref), channel_id=1, source_target_pairs={{0,2},{2,0},{4,6},{6,4},{8,10},{10,8},{12,14},{14,12},{16,18},{18,... | collective-permute-start | bytes 12582920 | tf_op jit(solution)/shard_map/ppermute | solution.py:104
  13.1 8.3 %collective-permute-start.4 = (bf16[2,512,256]{2,1,0:T(8,128)(2,1)S(1)}, bf16[2,512,256]{2,1,0:T(8,128)(2,1)S(1)}, u32[]{:S(2)}, u32[]{:S(2)}) collective-permute-start(bf16[2,512,256]{2,1,0:T(8,128)(2,1)S(1)} %collective-permute-done.2.refs_2_), channel_id=1, source_target_pairs={{0,8},{2,6},{8,16},{10,2},{16,24},{18,10},{24,28},{26,18},{28,20},... | collective-permute-start | bytes 1572872 | tf_op jit(solution)/shard_map/ppermute | solution.py:530
  14.4 12.6 %collective-permute-start.10 = (bf16[2,512,256]{2,1,0:T(8,128)(2,1)S(1)}, bf16[2,512,256]{2,1,0:T(8,128)(2,1)S(1)}, u32[]{:S(2)}, u32[]{:S(2)}) collective-permute-start(bf16[2,512,256]{2,1,0:T(8,128)(2,1)S(1)} %both_of.2), channel_id=1, source_target_pairs={{0,8},{2,6},{8,16},{10,2},{16,24},{18,10},{24,28},{26,18},{28,20},... | collective-permute-start | bytes 1572872 | tf_op jit(solution)/shard_map/ppermute | solution.py:530
  14.7 13.8 %collective-permute-start.11 = (bf16[2,512,256]{2,1,0:T(8,128)(2,1)S(1)}, bf16[2,512,256]{2,1,0:T(8,128)(2,1)S(1)}, u32[]{:S(2)}, u32[]{:S(2)}) collective-permute-start(bf16[2,512,256]{2,1,0:T(8,128)(2,1)S(1)} %collective-permute-done.2.refs_2_), channel_id=1, source_target_pairs={{0,1},{1,0},{2,3},{3,2},{4,5},{5,4},{6,7},{7,6},{8,9},{9,8},{10,11... | collective-permute-start | bytes 1572872 | tf_op jit(solution)/shard_map/ppermute | solution.py:108
  15.9 16.8 %collective-permute-start.8 = (bf16[512,512]{1,0:T(8,128)(2,1)S(1)}, bf16[512,512]{1,0:T(8,128)(2,1)S(1)}, u32[]{:S(2)}, u32[]{:S(2)}) collective-permute-start(bf16[512,512]{1,0:T(8,128)(2,1)S(1)} %copy-done.1), channel_id=1, source_target_pairs={{0,8},{2,6},{8,16},{10,2},{16,24},{18,10},{24,28},{26,18},{28,20},... | collective-permute-start | bytes 1572872 | tf_op jit(solution)/shard_map/ppermute | solution.py:530
  21.5 16.9 %collective-permute-start.5 = (bf16[2,512,256]{2,1,0:T(8,128)(2,1)S(1)}, bf16[2,512,256]{2,1,0:T(8,128)(2,1)S(1)}, u32[]{:S(2)}, u32[]{:S(2)}) collective-permute-start(bf16[2,512,256]{2,1,0:T(8,128)(2,1)S(1)} %collective-permute-done.4.refs_0_), channel_id=1, source_target_pairs={{0,8},{2,6},{8,16},{10,2},{16,24},{18,10},{24,28},{26,18},{28,20},... | collective-permute-start | bytes 1572872 | tf_op jit(solution)/shard_map/ppermute | solution.py:530
  27.1 12.6 %collective-permute-start.6 = (bf16[2,512,256]{2,1,0:T(8,128)(2,1)S(1)}, bf16[2,512,256]{2,1,0:T(8,128)(2,1)S(1)}, u32[]{:S(2)}, u32[]{:S(2)}) collective-permute-start(bf16[2,512,256]{2,1,0:T(8,128)(2,1)S(1)} %collective-permute-done.4.refs_0_), channel_id=1, source_target_pairs={{0,1},{1,0},{2,3},{3,2},{4,5},{5,4},{6,7},{7,6},{8,9},{9,8},{10,11... | collective-permute-start | bytes 1572872 | tf_op jit(solution)/shard_map/ppermute | solution.py:108
  28.4 15.5 %collective-permute-start.12 = (bf16[2,512,256]{2,1,0:T(8,128)(2,1)S(1)}, bf16[2,512,256]{2,1,0:T(8,128)(2,1)S(1)}, u32[]{:S(2)}, u32[]{:S(2)}) collective-permute-start(bf16[2,512,256]{2,1,0:T(8,128)(2,1)S(1)} %collective-permute-done.10.refs_1_), channel_id=1, source_target_pairs={{0,8},{2,6},{8,16},{10,2},{16,24},{18,10},{24,28},{26,18},{28,20},... | collective-permute-start | bytes 1572872 | tf_op jit(solution)/shard_map/ppermute | solution.py:530
  32.7 13.8 %collective-permute-start.14 = (bf16[512,512]{1,0:T(8,128)(2,1)S(1)}, bf16[512,512]{1,0:T(8,128)(2,1)S(1)}, u32[]{:S(2)}, u32[]{:S(2)}) collective-permute-start(bf16[512,512]{1,0:T(8,128)(2,1)S(1)} %copy-done.1), channel_id=1, source_target_pairs={{0,2},{2,0},{4,6},{6,4},{8,10},{10,8},{12,14},{14,12},{16,18},{18,... | collective-permute-start | bytes 1572872 | tf_op jit(solution)/shard_map/ppermute | solution.py:104
  39.7 7.1 %collective-permute-start.7 = (bf16[1,512,256]{2,1,0:T(8,128)(2,1)S(1)}, bf16[1,512,256]{2,1,0:T(8,128)(2,1)S(1)}, u32[]{:S(2)}, u32[]{:S(2)}) collective-permute-start(bf16[1,512,256]{2,1,0:T(8,128)(2,1)S(1)} %first_of.2), channel_id=1, source_target_pairs={{0,8},{2,6},{8,16},{10,2},{16,24},{18,10},{24,28},{26,18},{28,20},... | collective-permute-start | bytes 786440 | tf_op jit(solution)/shard_map/ppermute | solution.py:530
  43.9 15.1 %collective-permute-start.13 = (bf16[2,512,256]{2,1,0:T(8,128)(2,1)S(1)}, bf16[2,512,256]{2,1,0:T(8,128)(2,1)S(1)}, u32[]{:S(2)}, u32[]{:S(2)}) collective-permute-start(bf16[2,512,256]{2,1,0:T(8,128)(2,1)S(1)} %collective-permute-done.12.refs_0_), channel_id=1, source_target_pairs={{0,8},{2,6},{8,16},{10,2},{16,24},{18,10},{24,28},{26,18},{28,20},... | collective-permute-start | bytes 1572872 | tf_op jit(solution)/shard_map/ppermute | solution.py:530
  45.2 14.1 %collective-permute-start.16 = (bf16[2,512,256]{2,1,0:T(8,128)(2,1)S(1)}, bf16[2,512,256]{2,1,0:T(8,128)(2,1)S(1)}, u32[]{:S(2)}, u32[]{:S(2)}) collective-permute-start(bf16[2,512,256]{2,1,0:T(8,128)(2,1)S(1)} %collective-permute-done.5.pair_ref.refs_0_), channel_id=1, source_target_pairs={{0,1},{1,0},{2,3},{3,2},{4,5},{5,4},{6,7},{7,6},{8,9},{9,8},{10,11... | collective-permute-start | bytes 1572872 | tf_op jit(solution)/shard_map/ppermute | solution.py:108
  46.5 8.7 %collective-permute-start.15 = (bf16[256,512]{1,0:T(8,128)(2,1)S(1)}, bf16[256,512]{1,0:T(8,128)(2,1)S(1)}, u32[]{:S(2)}, u32[]{:S(2)}) collective-permute-start(bf16[256,512]{1,0:T(8,128)(2,1)S(1)} %rows_near.1), channel_id=1, source_target_pairs={{0,8},{2,6},{8,16},{10,2},{16,24},{18,10},{24,28},{26,18},{28,20},... | collective-permute-start | bytes 786440 | tf_op jit(solution)/shard_map/ppermute | solution.py:530
  46.8 14.0 %collective-permute-start.9 = (bf16[512,512]{1,0:T(8,128)(2,1)S(1)}, bf16[512,512]{1,0:T(8,128)(2,1)S(1)}, u32[]{:S(2)}, u32[]{:S(2)}) collective-permute-start(bf16[512,512]{1,0:T(8,128)(2,1)S(1)} %collective-permute-done.8.refs_2_), channel_id=1, source_target_pairs={{0,8},{2,6},{8,16},{10,2},{16,24},{18,10},{24,28},{26,18},{28,20},... | collective-permute-start | bytes 1572872 | tf_op jit(solution)/shard_map/ppermute | solution.py:530
  55.2 16.6 %collective-permute-start.23 = (bf16[256,512]{1,0:T(8,128)(2,1)S(1)}, bf16[256,512]{1,0:T(8,128)(2,1)S(1)}, u32[]{:S(2)}, u32[]{:S(2)}) collective-permute-start(bf16[256,512]{1,0:T(8,128)(2,1)S(1)} %collective-permute-done.15.refs_3_), channel_id=1, source_target_pairs={{0,8},{2,6},{8,16},{10,2},{16,24},{18,10},{24,28},{26,18},{28,20},... | collective-permute-start | bytes 786440 | tf_op jit(solution)/shard_map/ppermute | solution.py:530
  56.5 15.3 %collective-permute-start.19 = (bf16[1,512,256]{2,1,0:T(8,128)(2,1)S(1)}, bf16[1,512,256]{2,1,0:T(8,128)(2,1)S(1)}, u32[]{:S(2)}, u32[]{:S(2)}) collective-permute-start(bf16[1,512,256]{2,1,0:T(8,128)(2,1)S(1)} %collective-permute-done.7.refs_0_), channel_id=1, source_target_pairs={{0,1},{1,0},{2,3},{3,2},{4,5},{5,4},{6,7},{7,6},{8,9},{9,8},{10,11... | collective-permute-start | bytes 786440 | tf_op jit(solution)/shard_map/ppermute | solution.py:108
  59.0 10.2 %collective-permute-start.20 = (bf16[256,512]{1,0:T(8,128)(2,1)S(1)}, bf16[256,512]{1,0:T(8,128)(2,1)S(1)}, u32[]{:S(2)}, u32[]{:S(2)}) collective-permute-start(bf16[256,512]{1,0:T(8,128)(2,1)S(1)} %collective-permute-done.15.refs_3_), channel_id=1, source_target_pairs={{0,1},{1,0},{2,3},{3,2},{4,5},{5,4},{6,7},{7,6},{8,9},{9,8},{10,11... | collective-permute-start | bytes 786440 | tf_op jit(solution)/shard_map/ppermute | solution.py:108
  59.3 7.1 %collective-permute-start.17 = (bf16[1,512,256]{2,1,0:T(8,128)(2,1)S(1)}, bf16[1,512,256]{2,1,0:T(8,128)(2,1)S(1)}, u32[]{:S(2)}, u32[]{:S(2)}) collective-permute-start(bf16[1,512,256]{2,1,0:T(8,128)(2,1)S(1)} %first_of.3), channel_id=1, source_target_pairs={{0,8},{2,6},{8,16},{10,2},{16,24},{18,10},{24,28},{26,18},{28,20},... | collective-permute-start | bytes 786440 | tf_op jit(solution)/shard_map/ppermute | solution.py:530
  66.4 8.3 %collective-permute-start.18 = (bf16[512,512]{1,0:T(8,128)(2,1)S(1)}, bf16[512,512]{1,0:T(8,128)(2,1)S(1)}, u32[]{:S(2)}, u32[]{:S(2)}) collective-permute-start(bf16[512,512]{1,0:T(8,128)(2,1)S(1)} %collective-permute-done.9.refs_8_), channel_id=1, source_target_pairs={{0,8},{2,6},{8,16},{10,2},{16,24},{18,10},{24,28},{26,18},{28,20},... | collective-permute-start | bytes 1572872 | tf_op jit(solution)/shard_map/ppermute | solution.py:530
  71.8 7.9 %collective-permute-start.26 = (bf16[256,512]{1,0:T(8,128)(2,1)S(1)}, bf16[256,512]{1,0:T(8,128)(2,1)S(1)}, u32[]{:S(2)}, u32[]{:S(2)}) collective-permute-start(bf16[256,512]{1,0:T(8,128)(2,1)S(1)} %collective-permute-done.23.refs_9_), channel_id=1, source_target_pairs={{0,1},{1,0},{2,3},{3,2},{4,5},{5,4},{6,7},{7,6},{8,9},{9,8},{10,11... | collective-permute-start | bytes 786440 | tf_op jit(solution)/shard_map/ppermute | solution.py:108
  73.0 7.5 %collective-permute-start.24 = (bf16[256,512]{1,0:T(8,128)(2,1)S(1)}, bf16[256,512]{1,0:T(8,128)(2,1)S(1)}, u32[]{:S(2)}, u32[]{:S(2)}) collective-permute-start(bf16[256,512]{1,0:T(8,128)(2,1)S(1)} %collective-permute-done.23.refs_9_), channel_id=1, source_target_pairs={{0,8},{2,6},{8,16},{10,2},{16,24},{18,10},{24,28},{26,18},{28,20},... | collective-permute-start | bytes 786440 | tf_op jit(solution)/shard_map/ppermute | solution.py:530
  75.8 29.7 %collective-permute-start.22 = (f32[256,512]{1,0:T(8,128)S(1)}, f32[256,512]{1,0:T(8,128)S(1)}, u32[]{:S(2)}, u32[]{:S(2)}) collective-permute-start(f32[256,512]{1,0:T(8,128)S(1)} %get-tuple-element.70), channel_id=1, source_target_pairs={{0,2},{2,0},{4,6},{6,4},{8,10},{10,8},{12,14},{14,12},{16,18},{18,... | collective-permute-start | bytes 1572872 | tf_op jit(solution)/shard_map/ppermute | solution.py:104
  79.6 8.6 %collective-permute-start.34 = (bf16[256,512]{1,0:T(8,128)(2,1)S(1)}, bf16[256,512]{1,0:T(8,128)(2,1)S(1)}, u32[]{:S(2)}, u32[]{:S(2)}) collective-permute-start(bf16[256,512]{1,0:T(8,128)(2,1)S(1)} %collective-permute-done.15.refs_3_), channel_id=1, source_target_pairs={{0,2},{2,0},{4,6},{6,4},{8,10},{10,8},{12,14},{14,12},{16,18},{18,... | collective-permute-start | bytes 786440 | tf_op jit(solution)/shard_map/ppermute | solution.py:104
  80.5 9.4 %collective-permute-start.25 = (bf16[256,512]{1,0:T(8,128)(2,1)S(1)}, bf16[256,512]{1,0:T(8,128)(2,1)S(1)}, u32[]{:S(2)}, u32[]{:S(2)}) collective-permute-start(bf16[256,512]{1,0:T(8,128)(2,1)S(1)} %collective-permute-done.24.refs_15_), channel_id=1, source_target_pairs={{0,1},{1,0},{2,3},{3,2},{4,5},{5,4},{6,7},{7,6},{8,9},{9,8},{10,11... | collective-permute-start | bytes 786440 | tf_op jit(solution)/shard_map/ppermute | solution.py:108
  84.4 10.9 %collective-permute-start.28 = (bf16[2,256,256]{2,1,0:T(8,128)(2,1)S(1)}, bf16[2,256,256]{2,1,0:T(8,128)(2,1)S(1)}, u32[]{:S(2)}, u32[]{:S(2)}) collective-permute-start(bf16[2,256,256]{2,1,0:T(8,128)(2,1)S(1)} %join_row.1.refs_2_), channel_id=1, source_target_pairs={{0,16},{4,20},{8,24},{12,28},{16,26},{20,30},{24,18},{28,22},{26,1... | collective-permute-start | bytes 786440 | tf_op jit(solution)/shard_map/ppermute | solution.py:618
  86.3 12.9 %collective-permute-start.29 = (bf16[2,256,256]{2,1,0:T(8,128)(2,1)S(1)}, bf16[2,256,256]{2,1,0:T(8,128)(2,1)S(1)}, u32[]{:S(2)}, u32[]{:S(2)}) collective-permute-start(bf16[2,256,256]{2,1,0:T(8,128)(2,1)S(1)} %join_row.1.refs_2_), channel_id=1, source_target_pairs={{0,8},{4,12},{8,16},{12,20},{16,24},{20,28},{24,26},{28,30},{26,18... | collective-permute-start | bytes 786440 | tf_op jit(solution)/shard_map/ppermute | solution.py:618
  88.3 21.9 %collective-permute-start.31 = (bf16[512,512]{1,0:T(8,128)(2,1)S(1)}, bf16[512,512]{1,0:T(8,128)(2,1)S(1)}, u32[]{:S(2)}, u32[]{:S(2)}) collective-permute-start(bf16[512,512]{1,0:T(8,128)(2,1)S(1)} %collective-permute-done.18.refs_14_), channel_id=1, source_target_pairs={{0,8},{2,6},{8,16},{10,2},{16,24},{18,10},{24,28},{26,18},{28,20},... | collective-permute-start | bytes 1572872 | tf_op jit(solution)/shard_map/ppermute | solution.py:530
  89.9 19.1 %collective-permute-start.35 = (bf16[256,512]{1,0:T(8,128)(2,1)S(1)}, bf16[256,512]{1,0:T(8,128)(2,1)S(1)}, u32[]{:S(2)}, u32[]{:S(2)}) collective-permute-start(bf16[256,512]{1,0:T(8,128)(2,1)S(1)} %collective-permute-done.20.refs_4_), channel_id=1, source_target_pairs={{0,2},{2,0},{4,6},{6,4},{8,10},{10,8},{12,14},{14,12},{16,18},{18,... | collective-permute-start | bytes 786440 | tf_op jit(solution)/shard_map/ppermute | solution.py:104
  95.3 14.4 %collective-permute-start.37 = (bf16[256,512]{1,0:T(8,128)(2,1)S(1)}, bf16[256,512]{1,0:T(8,128)(2,1)S(1)}, u32[]{:S(2)}, u32[]{:S(2)}) collective-permute-start(bf16[256,512]{1,0:T(8,128)(2,1)S(1)} %collective-permute-done.23.refs_9_), channel_id=1, source_target_pairs={{0,2},{2,0},{4,6},{6,4},{8,10},{10,8},{12,14},{14,12},{16,18},{18,... | collective-permute-start | bytes 786440 | tf_op jit(solution)/shard_map/ppermute | solution.py:104
  99.2 11.0 %collective-permute-start.36 = (bf16[512,512]{1,0:T(8,128)(2,1)S(1)}, bf16[512,512]{1,0:T(8,128)(2,1)S(1)}, u32[]{:S(2)}, u32[]{:S(2)}) collective-permute-start(bf16[512,512]{1,0:T(8,128)(2,1)S(1)} %collective-permute-done.9.refs_8_), channel_id=1, source_target_pairs={{0,2},{2,0},{4,6},{6,4},{8,10},{10,8},{12,14},{14,12},{16,18},{18,... | collective-permute-start | bytes 1572872 | tf_op jit(solution)/shard_map/ppermute | solution.py:104
  110.2 7.1 %collective-permute-start.32 = (bf16[512,512]{1,0:T(8,128)(2,1)S(1)}, bf16[512,512]{1,0:T(8,128)(2,1)S(1)}, u32[]{:S(2)}, u32[]{:S(2)}) collective-permute-start(bf16[512,512]{1,0:T(8,128)(2,1)S(1)} %collective-permute-done.31.refs_0_), channel_id=1, source_target_pairs={{0,2},{2,0},{4,6},{6,4},{8,10},{10,8},{12,14},{14,12},{16,18},{18,... | collective-permute-start | bytes 1572872 | tf_op jit(solution)/shard_map/ppermute | solution.py:104
  (12 other events, 45.6 us)

commit v8 on v7

--- a/solution.py
+++ b/solution.py
@@ -17,7 +17,7 @@
     "A0",
     "N0",
     "N1",
-    "C0",
+    "C0 N0",
     "T0",
     "B0 N1",
     "H0 C0",
@@ -26,29 +26,29 @@
     "C1 N1",
     "F1",
     "A1",
-    "N3",
-    "C2 N2 F1",
+    "N3 S0",
+    "C2 N2 F1 N1",
     "F2",
     "B1 N3",
     "X1",
-    "N4 F2",
-    "Q1 A1",
+    "N4",
+    "Q1",
     "C3 N3 F2 Q1",
     "F3",
     "A2 N4",
+    "K1 F2",
     "F4",
     "Q2 B1",
     "C4 N4 Q2 F3",
-    "K1",
     "K2 A2 Q2",
     "B2 N4",
     "X2 F4",
     "A3 C4 K2",
-    "B3 C4",
+    "B3",
     "K3 X1",
     "Q3 K3",
     "Q4 A3",
-    "R0 X2",
+    "R0 X2 Q3",
     "R1",
     "R2",
     "X3",
@@ -620,7 +620,7 @@
                 windows = [done["R2"], done["R1"], done["R0"]]
                 value = attend(index, tied(done["Q4"]), windows, key_seg, head_dim, micros)
             elif name == "M1":
-                value = core_swap(done["M0"], count)
+                value = core_swap(tied(done["M0"]), count)
             elif kind == "W":
                 value = [core_swap(tied(done[f"A{step}"]), count)]
                 if step < half:

time: 119 us -> 115 us (0.966)
  waiting for transfers between devices: 48.1 us -> 44.3 us
    ppermute x15, waiting for transfers between devices: 34.6 us -> 29.2 us  [ring(): return lax.ppermute(value, 'ctx', pairs)]
    ppermute x7, waiting for transfers between devices: 4.22 us -> 6.37 us  [plane_swap(): return lax.ppermute(value, 'dp', [(0, 1), (1, 0)])]
  transfers between devices with their start and end apart: 42 -> 42, of which waited for: 20 -> 20; matrix products, arithmetic and copies ran while one was open for 1% -> 1% of each run, Pallas kernels for 15% -> 16%
where the time goes in v8:
time: 115 us
  starting transfers between devices  46.9 us (41%)
  waiting for transfers between devices  44.3 us (39%)
  Pallas kernels  21.3 us (19%)
    ppermute x15, waiting for transfers between devices, ring(): return lax.ppermute(value, 'ctx', pairs)  29.2 us
    ppermute x17, starting transfers between devices, core_swap(): return lax.ppermute(value, 'ctx', [(i, i ^ 1) for i in range(count)])  21.4 us
    ppermute x15, starting transfers between devices, ring(): return lax.ppermute(value, 'ctx', pairs)  14.4 us
    pallas_call x7, Pallas kernels, project(): pl.pallas_call(functools.partial(project_kernel, slots, base, groups, tot...  8.38 us
    ppermute x7, starting transfers between devices, plane_swap(): return lax.ppermute(value, 'dp', [(0, 1), (1, 0)])  6.78 us
    ppermute x7, waiting for transfers between devices, plane_swap(): return lax.ppermute(value, 'dp', [(0, 1), (1, 0)])  6.37 us
    pallas_call x2, Pallas kernels, columns_of(): pl.pallas_call(functools.partial(columns_kernel, entries), in_specs=specs...  5.16 us
    ppermute x2, starting transfers between devices, run(): value = lax.ppermute(tied(done['R0']), 'ctx', sends)  4.01 us
  transfers between devices with their start and end apart: 42, of which 20 were waited for; matrix products, arithmetic and copies ran while one was open for 1% of the time, Pallas kernels for 16%

profile of v8, /device:TPU:19, one launch (start us, length us, event | category | flops | bytes accessed | tf_op | source)
XLA Modules:
  0.0 114.7 jit_solution(10699351025752607179)
XLA Ops:
  3.2 1.3 %collective-permute-start.2 = (bf16[2,512,256]{2,1,0:T(8,128)(2,1)S(1)}, bf16[2,512,256]{2,1,0:T(8,128)(2,1)S(1)}, u32[]{:S(2)}, u32[]{:S(2)}) collective-permute-start(bf16[2,512,256]{2,1,0:T(8,128)(2,1)S(1)} %both_of.2), channel_id=1, source_target_pairs={{0,8},{2,6},{8,16},{10,2},{16,24},{18,10},{24,28},{26,18},{28,20},... | collective-permute-start | bytes 1572872 | tf_op jit(solution)/shard_map/ppermute | solution.py:530
  6.1 2.3 %bring.1.own_ref = bf16[256,8192]{1,0:T(8,128)(2,1)S(1)} custom-call(bf16[256,8192]{1,0:T(8,128)(2,1)} %source_ref), custom_call_target="tpu_custom_call" | custom-call | flops 2307000064 | tf_op jit(solution)/shard_map/bring/pallas_call | solution.py:356
  8.4 3.2 %collective-permute-done.2.refs_2_ = bf16[2,512,256]{2,1,0:T(8,128)(2,1)S(1)} collective-permute-done((bf16[2,512,256]{2,1,0:T(8,128)(2,1)S(1)}, bf16[2,512,256]{2,1,0:T(8,128)(2,1)S(1)}, u32[]{:S(2)}, u32[]{:S(2)}) %collective-permute-start.2) | collective-permute-done | bytes 524320 | tf_op jit(solution)/shard_map/ppermute | solution.py:530
  12.8 1.3 %collective-permute-start.4 = (bf16[2,512,256]{2,1,0:T(8,128)(2,1)S(1)}, bf16[2,512,256]{2,1,0:T(8,128)(2,1)S(1)}, u32[]{:S(2)}, u32[]{:S(2)}) collective-permute-start(bf16[2,512,256]{2,1,0:T(8,128)(2,1)S(1)} %collective-permute-done.2.refs_2_), channel_id=1, source_target_pairs={{0,8},{2,6},{8,16},{10,2},{16,24},{18,10},{24,28},{26,18},{28,20},... | collective-permute-start | bytes 1572872 | tf_op jit(solution)/shard_map/ppermute | solution.py:530
  15.6 5.5 %collective-permute-done.4.refs_0_ = bf16[2,512,256]{2,1,0:T(8,128)(2,1)S(1)} collective-permute-done((bf16[2,512,256]{2,1,0:T(8,128)(2,1)S(1)}, bf16[2,512,256]{2,1,0:T(8,128)(2,1)S(1)}, u32[]{:S(2)}, u32[]{:S(2)}) %collective-permute-start.4) | collective-permute-done | bytes 524320 | tf_op jit(solution)/shard_map/ppermute | solution.py:530
  21.1 1.3 %collective-permute-start.5 = (bf16[2,512,256]{2,1,0:T(8,128)(2,1)S(1)}, bf16[2,512,256]{2,1,0:T(8,128)(2,1)S(1)}, u32[]{:S(2)}, u32[]{:S(2)}) collective-permute-start(bf16[2,512,256]{2,1,0:T(8,128)(2,1)S(1)} %collective-permute-done.4.refs_0_), channel_id=1, source_target_pairs={{0,8},{2,6},{8,16},{10,2},{16,24},{18,10},{24,28},{26,18},{28,20},... | collective-permute-start | bytes 1572872 | tf_op jit(solution)/shard_map/ppermute | solution.py:530
  22.4 4.3 %collective-permute-done.9.refs_1_ = bf16[2,512,256]{2,1,0:T(8,128)(2,1)S(1)} collective-permute-done((bf16[2,512,256]{2,1,0:T(8,128)(2,1)S(1)}, bf16[2,512,256]{2,1,0:T(8,128)(2,1)S(1)}, u32[]{:S(2)}, u32[]{:S(2)}) %collective-permute-start.9) | collective-permute-done | bytes 524320 | tf_op jit(solution)/shard_map/ppermute | solution.py:530
  26.7 1.4 %collective-permute-done.10.refs_3_ = bf16[2,512,256]{2,1,0:T(8,128)(2,1)S(1)} collective-permute-done((bf16[2,512,256]{2,1,0:T(8,128)(2,1)S(1)}, bf16[2,512,256]{2,1,0:T(8,128)(2,1)S(1)}, u32[]{:S(2)}, u32[]{:S(2)}) %collective-permute-start.10) | collective-permute-done | bytes 524320 | tf_op jit(solution)/shard_map/ppermute | solution.py:108
  29.8 1.7 %collective-permute-start.7 = (bf16[512,512]{1,0:T(8,128)(2,1)S(1)}, bf16[512,512]{1,0:T(8,128)(2,1)S(1)}, u32[]{:S(2)}, u32[]{:S(2)}) collective-permute-start(bf16[512,512]{1,0:T(8,128)(2,1)S(1)} %copy-done.1), channel_id=1, source_target_pairs={{0,8},{2,6},{8,16},{10,2},{16,24},{18,10},{24,28},{26,18},{28,20},... | collective-permute-start | bytes 1572872 | tf_op jit(solution)/shard_map/ppermute | solution.py:530
  32.3 1.3 %collective-permute-start.6 = (bf16[1,512,256]{2,1,0:T(8,128)(2,1)S(1)}, bf16[1,512,256]{2,1,0:T(8,128)(2,1)S(1)}, u32[]{:S(2)}, u32[]{:S(2)}) collective-permute-start(bf16[1,512,256]{2,1,0:T(8,128)(2,1)S(1)} %first_of.2), channel_id=1, source_target_pairs={{0,8},{2,6},{8,16},{10,2},{16,24},{18,10},{24,28},{26,18},{28,20},... | collective-permute-start | bytes 786440 | tf_op jit(solution)/shard_map/ppermute | solution.py:530
  33.7 1.5 %project.7.refs_2_ = f32[2,256,512]{2,1,0:T(8,128)S(1)} custom-call(s32[19]{0:T(128)S(1)} %stack.76.index_ref, bf16[256,8192]{1,0:T(8,128)(2,1)S(1)} %bring.1.own_ref, bf16[256,8192]{1,0:T(8,128)(2,1)S(1)} %collective-permute-done.3.other_ref, bf16[1,512,256]{2,1,0:T(8,128)(2,1)S(1)} %get-tuple-element.44.first_ref.refs_0_, ...), custom_call_target="tpu_custom_call" | custom-call | flops 2307000064 | tf_op jit(solution)/shard_map/project/pallas_call | solution.py:411
  35.2 2.7 %collective-permute-done.11.refs_0_ = bf16[2,512,256]{2,1,0:T(8,128)(2,1)S(1)} collective-permute-done((bf16[2,512,256]{2,1,0:T(8,128)(2,1)S(1)}, bf16[2,512,256]{2,1,0:T(8,128)(2,1)S(1)}, u32[]{:S(2)}, u32[]{:S(2)}) %collective-permute-start.11) | collective-permute-done | bytes 524320 | tf_op jit(solution)/shard_map/ppermute | solution.py:530
  37.9 3.5 %collective-permute-done.12.refs_1_ = bf16[2,512,256]{2,1,0:T(8,128)(2,1)S(1)} collective-permute-done((bf16[2,512,256]{2,1,0:T(8,128)(2,1)S(1)}, bf16[2,512,256]{2,1,0:T(8,128)(2,1)S(1)}, u32[]{:S(2)}, u32[]{:S(2)}) %collective-permute-start.12) | collective-permute-done | bytes 524320 | tf_op jit(solution)/shard_map/ppermute | solution.py:108
  43.6 2.8 %collective-permute-done.6.refs_0_ = bf16[1,512,256]{2,1,0:T(8,128)(2,1)S(1)} collective-permute-done((bf16[1,512,256]{2,1,0:T(8,128)(2,1)S(1)}, bf16[1,512,256]{2,1,0:T(8,128)(2,1)S(1)}, u32[]{:S(2)}, u32[]{:S(2)}) %collective-permute-start.6) | collective-permute-done | bytes 262176 | tf_op jit(solution)/shard_map/ppermute | solution.py:530
  47.7 7.1 %collective-permute-done.15.refs_3_ = bf16[256,512]{1,0:T(8,128)(2,1)S(1)} collective-permute-done((bf16[256,512]{1,0:T(8,128)(2,1)S(1)}, bf16[256,512]{1,0:T(8,128)(2,1)S(1)}, u32[]{:S(2)}, u32[]{:S(2)}) %collective-permute-start.15) | collective-permute-done | bytes 262176 | tf_op jit(solution)/shard_map/ppermute | solution.py:530
  57.4 1.4 %collective-permute-start.17 = (bf16[1,512,256]{2,1,0:T(8,128)(2,1)S(1)}, bf16[1,512,256]{2,1,0:T(8,128)(2,1)S(1)}, u32[]{:S(2)}, u32[]{:S(2)}) collective-permute-start(bf16[1,512,256]{2,1,0:T(8,128)(2,1)S(1)} %first_of.3), channel_id=1, source_target_pairs={{0,8},{2,6},{8,16},{10,2},{16,24},{18,10},{24,28},{26,18},{28,20},... | collective-permute-start | bytes 786440 | tf_op jit(solution)/shard_map/ppermute | solution.py:530
  61.7 1.5 %collective-permute-done.17.refs_0_ = bf16[1,512,256]{2,1,0:T(8,128)(2,1)S(1)} collective-permute-done((bf16[1,512,256]{2,1,0:T(8,128)(2,1)S(1)}, bf16[1,512,256]{2,1,0:T(8,128)(2,1)S(1)}, u32[]{:S(2)}, u32[]{:S(2)}) %collective-permute-start.17) | collective-permute-done | bytes 262176 | tf_op jit(solution)/shard_map/ppermute | solution.py:530
  63.2 1.3 %collective-permute-start.18 = (bf16[512,512]{1,0:T(8,128)(2,1)S(1)}, bf16[512,512]{1,0:T(8,128)(2,1)S(1)}, u32[]{:S(2)}, u32[]{:S(2)}) collective-permute-start(bf16[512,512]{1,0:T(8,128)(2,1)S(1)} %collective-permute-done.8.refs_8_), channel_id=1, source_target_pairs={{0,8},{2,6},{8,16},{10,2},{16,24},{18,10},{24,28},{26,18},{28,20},... | collective-permute-start | bytes 1572872 | tf_op jit(solution)/shard_map/ppermute | solution.py:530
  66.4 1.5 %collective-permute-done.19.refs_1_ = bf16[1,512,256]{2,1,0:T(8,128)(2,1)S(1)} collective-permute-done((bf16[1,512,256]{2,1,0:T(8,128)(2,1)S(1)}, bf16[1,512,256]{2,1,0:T(8,128)(2,1)S(1)}, u32[]{:S(2)}, u32[]{:S(2)}) %collective-permute-start.19) | collective-permute-done | bytes 262176 | tf_op jit(solution)/shard_map/ppermute | solution.py:108
  72.7 2.5 %collective-permute-start.22 = (f32[256,512]{1,0:T(8,128)S(1)}, f32[256,512]{1,0:T(8,128)S(1)}, u32[]{:S(2)}, u32[]{:S(2)}) collective-permute-start(f32[256,512]{1,0:T(8,128)S(1)} %get-tuple-element.71), channel_id=1, source_target_pairs={{0,2},{2,0},{4,6},{6,4},{8,10},{10,8},{12,14},{14,12},{16,18},{18,... | collective-permute-start | bytes 1572872 | tf_op jit(solution)/shard_map/ppermute | solution.py:104
  77.5 1.6 %collective-permute-done.27.beside_ref = bf16[256,256]{1,0:T(8,128)(2,1)S(1)} collective-permute-done((bf16[256,256]{1,0:T(8,128)(2,1)S(1)}, bf16[256,256]{1,0:T(8,128)(2,1)S(1)}, u32[]{:S(2)}, u32[]{:S(2)}) %collective-permute-start.27) | collective-permute-done | bytes 131104 | tf_op jit(solution)/shard_map/ppermute | solution.py:611
  79.6 2.1 %collective-permute-start.28 = (bf16[2,256,256]{2,1,0:T(8,128)(2,1)S(1)}, bf16[2,256,256]{2,1,0:T(8,128)(2,1)S(1)}, u32[]{:S(2)}, u32[]{:S(2)}) collective-permute-start(bf16[2,256,256]{2,1,0:T(8,128)(2,1)S(1)} %join_row.1.refs_2_), channel_id=1, source_target_pairs={{0,16},{4,20},{8,24},{12,28},{16,26},{20,30},{24,18},{28,22},{26,1... | collective-permute-start | bytes 786440 | tf_op jit(solution)/shard_map/ppermute | solution.py:618
  81.7 1.9 %collective-permute-start.29 = (bf16[2,256,256]{2,1,0:T(8,128)(2,1)S(1)}, bf16[2,256,256]{2,1,0:T(8,128)(2,1)S(1)}, u32[]{:S(2)}, u32[]{:S(2)}) collective-permute-start(bf16[2,256,256]{2,1,0:T(8,128)(2,1)S(1)} %join_row.1.refs_2_), channel_id=1, source_target_pairs={{0,8},{4,12},{8,16},{12,20},{16,24},{20,28},{24,26},{28,30},{26,18... | collective-permute-start | bytes 786440 | tf_op jit(solution)/shard_map/ppermute | solution.py:618
  83.7 1.7 %collective-permute-start.31 = (bf16[512,512]{1,0:T(8,128)(2,1)S(1)}, bf16[512,512]{1,0:T(8,128)(2,1)S(1)}, u32[]{:S(2)}, u32[]{:S(2)}) collective-permute-start(bf16[512,512]{1,0:T(8,128)(2,1)S(1)} %collective-permute-done.18.refs_14_), channel_id=1, source_target_pairs={{0,8},{2,6},{8,16},{10,2},{16,24},{18,10},{24,28},{26,18},{28,20},... | collective-permute-start | bytes 1572872 | tf_op jit(solution)/shard_map/ppermute | solution.py:530
  85.4 3.5 %collective-permute-start.35 = (bf16[256,512]{1,0:T(8,128)(2,1)S(1)}, bf16[256,512]{1,0:T(8,128)(2,1)S(1)}, u32[]{:S(2)}, u32[]{:S(2)}) collective-permute-start(bf16[256,512]{1,0:T(8,128)(2,1)S(1)} %collective-permute-done.20.refs_4_), channel_id=1, source_target_pairs={{0,2},{2,0},{4,6},{6,4},{8,10},{10,8},{12,14},{14,12},{16,18},{18,... | collective-permute-start | bytes 786440 | tf_op jit(solution)/shard_map/ppermute | solution.py:104
  88.9 3.2 %collective-permute-done.28.refs_0_ = bf16[2,256,256]{2,1,0:T(8,128)(2,1)S(1)} collective-permute-done((bf16[2,256,256]{2,1,0:T(8,128)(2,1)S(1)}, bf16[2,256,256]{2,1,0:T(8,128)(2,1)S(1)}, u32[]{:S(2)}, u32[]{:S(2)}) %collective-permute-start.28) | collective-permute-done | bytes 262176 | tf_op jit(solution)/shard_map/ppermute | solution.py:618
  92.0 2.2 %collective-permute-start.37 = (bf16[256,512]{1,0:T(8,128)(2,1)S(1)}, bf16[256,512]{1,0:T(8,128)(2,1)S(1)}, u32[]{:S(2)}, u32[]{:S(2)}) collective-permute-start(bf16[256,512]{1,0:T(8,128)(2,1)S(1)} %collective-permute-done.23.refs_9_), channel_id=1, source_target_pairs={{0,2},{2,0},{4,6},{6,4},{8,10},{10,8},{12,14},{14,12},{16,18},{18,... | collective-permute-start | bytes 786440 | tf_op jit(solution)/shard_map/ppermute | solution.py:104
  94.2 6.8 %collective-permute-start.38 = (bf16[256,512]{1,0:T(8,128)(2,1)S(1)}, bf16[256,512]{1,0:T(8,128)(2,1)S(1)}, u32[]{:S(2)}, u32[]{:S(2)}) collective-permute-start(bf16[256,512]{1,0:T(8,128)(2,1)S(1)} %collective-permute-done.26.refs_10_), channel_id=1, source_target_pairs={{0,2},{2,0},{4,6},{6,4},{8,10},{10,8},{12,14},{14,12},{16,18},{18,... | collective-permute-start | bytes 786440 | tf_op jit(solution)/shard_map/ppermute | solution.py:104
  101.3 3.3 %attend.1.mixed_ref = bf16[256,512]{1,0:T(8,128)(2,1)S(1)} custom-call(s32[19]{0:T(128)S(1)} %stack.76.index_ref, bf16[256,512]{1,0:T(8,128)(2,1)S(1)} %rotate_sums.3.query_ref, s32[1,1280]{1,0:T(1,128)S(1)} %bitcast.29, bf16[2,256,256]{2,1,0:T(8,128)(2,1)S(1)} %collective-permute-done.28.refs_0_, bf16[2,256,256]{2,1,0:T(8,128)(2,1)S(1)} %collective-permute-done.29.refs_1_, ...), custom_call_target="tpu_custom_call" | custom-call | flops 2307000064 | tf_op jit(solution)/shard_map/attend/pallas_call | solution.py:254
  106.8 2.1 %collective-permute-done.41.refs_19_ = bf16[256,512]{1,0:T(8,128)(2,1)S(1)} collective-permute-done((bf16[256,512]{1,0:T(8,128)(2,1)S(1)}, bf16[256,512]{1,0:T(8,128)(2,1)S(1)}, u32[]{:S(2)}, u32[]{:S(2)}) %collective-permute-start.41) | collective-permute-done | bytes 262176 | tf_op jit(solution)/shard_map/ppermute | solution.py:104
  109.3 3.4 %columns_of.2.refs_2_ = bf16[256,8192]{1,0:T(8,128)(2,1)} custom-call(s32[19]{0:T(128)S(1)} %stack.76.index_ref, bf16[256,512]{1,0:T(8,128)(2,1)S(1)} %attend.1.mixed_ref, bf16[256,512]{1,0:T(8,128)(2,1)S(1)} %collective-permute-done.30.returned_ref, bf16[512,512]{1,0:T(8,128)(2,1)S(1)} %copy-done.1, ...), custom_call_target="tpu_custom_call" | custom-call | flops 2307000064 | tf_op jit(solution)/shard_map/columns_of/pallas_call | solution.py:468
  112.8 1.7 %columns_of.3 = bf16[256,8192]{1,0:T(8,128)(2,1)} custom-call(s32[19]{0:T(128)S(1)} %stack.76.index_ref, bf16[256,512]{1,0:T(8,128)(2,1)S(1)} %attend.1.mixed_ref, bf16[256,512]{1,0:T(8,128)(2,1)S(1)} %collective-permute-done.30.returned_ref, bf16[512,512]{1,0:T(8,128)(2,1)S(1)} %collective-permute-done.31.refs_0_, ...), custom_call_target="tpu_custom_call", output_to_operand_aliasing={{}: (5, {})} | custom-call | flops 2307000064 | tf_op jit(solution)/shard_map/columns_of/pallas_call | solution.py:468
  (87 shorter events, 30.8 us)
Async XLA Ops:
  3.2 8.4 %collective-permute-start.2 = (bf16[2,512,256]{2,1,0:T(8,128)(2,1)S(1)}, bf16[2,512,256]{2,1,0:T(8,128)(2,1)S(1)}, u32[]{:S(2)}, u32[]{:S(2)}) collective-permute-start(bf16[2,512,256]{2,1,0:T(8,128)(2,1)S(1)} %both_of.2), channel_id=1, source_target_pairs={{0,8},{2,6},{8,16},{10,2},{16,24},{18,10},{24,28},{26,18},{28,20},... | collective-permute-start | bytes 1572872 | tf_op jit(solution)/shard_map/ppermute | solution.py:530
  11.5 9.6 %collective-permute-start.3 = (bf16[256,8192]{1,0:T(8,128)(2,1)S(1)}, bf16[256,8192]{1,0:T(8,128)(2,1)S(1)}, u32[]{:S(2)}, u32[]{:S(2)}) collective-permute-start(bf16[256,8192]{1,0:T(8,128)(2,1)S(1)} %bring.1.own_ref), channel_id=1, source_target_pairs={{0,2},{2,0},{4,6},{6,4},{8,10},{10,8},{12,14},{14,12},{16,18},{18,... | collective-permute-start | bytes 12582920 | tf_op jit(solution)/shard_map/ppermute | solution.py:104
  12.8 8.3 %collective-permute-start.4 = (bf16[2,512,256]{2,1,0:T(8,128)(2,1)S(1)}, bf16[2,512,256]{2,1,0:T(8,128)(2,1)S(1)}, u32[]{:S(2)}, u32[]{:S(2)}) collective-permute-start(bf16[2,512,256]{2,1,0:T(8,128)(2,1)S(1)} %collective-permute-done.2.refs_2_), channel_id=1, source_target_pairs={{0,8},{2,6},{8,16},{10,2},{16,24},{18,10},{24,28},{26,18},{28,20},... | collective-permute-start | bytes 1572872 | tf_op jit(solution)/shard_map/ppermute | solution.py:530
  14.1 12.6 %collective-permute-start.9 = (bf16[2,512,256]{2,1,0:T(8,128)(2,1)S(1)}, bf16[2,512,256]{2,1,0:T(8,128)(2,1)S(1)}, u32[]{:S(2)}, u32[]{:S(2)}) collective-permute-start(bf16[2,512,256]{2,1,0:T(8,128)(2,1)S(1)} %both_of.3), channel_id=1, source_target_pairs={{0,8},{2,6},{8,16},{10,2},{16,24},{18,10},{24,28},{26,18},{28,20},... | collective-permute-start | bytes 1572872 | tf_op jit(solution)/shard_map/ppermute | solution.py:530
  14.3 13.8 %collective-permute-start.10 = (bf16[2,512,256]{2,1,0:T(8,128)(2,1)S(1)}, bf16[2,512,256]{2,1,0:T(8,128)(2,1)S(1)}, u32[]{:S(2)}, u32[]{:S(2)}) collective-permute-start(bf16[2,512,256]{2,1,0:T(8,128)(2,1)S(1)} %collective-permute-done.2.refs_2_), channel_id=1, source_target_pairs={{0,1},{1,0},{2,3},{3,2},{4,5},{5,4},{6,7},{7,6},{8,9},{9,8},{10,11... | collective-permute-start | bytes 1572872 | tf_op jit(solution)/shard_map/ppermute | solution.py:108
  21.1 11.2 %collective-permute-start.5 = (bf16[2,512,256]{2,1,0:T(8,128)(2,1)S(1)}, bf16[2,512,256]{2,1,0:T(8,128)(2,1)S(1)}, u32[]{:S(2)}, u32[]{:S(2)}) collective-permute-start(bf16[2,512,256]{2,1,0:T(8,128)(2,1)S(1)} %collective-permute-done.4.refs_0_), channel_id=1, source_target_pairs={{0,8},{2,6},{8,16},{10,2},{16,24},{18,10},{24,28},{26,18},{28,20},... | collective-permute-start | bytes 1572872 | tf_op jit(solution)/shard_map/ppermute | solution.py:530
  28.1 9.9 %collective-permute-start.11 = (bf16[2,512,256]{2,1,0:T(8,128)(2,1)S(1)}, bf16[2,512,256]{2,1,0:T(8,128)(2,1)S(1)}, u32[]{:S(2)}, u32[]{:S(2)}) collective-permute-start(bf16[2,512,256]{2,1,0:T(8,128)(2,1)S(1)} %collective-permute-done.9.refs_1_), channel_id=1, source_target_pairs={{0,8},{2,6},{8,16},{10,2},{16,24},{18,10},{24,28},{26,18},{28,20},... | collective-permute-start | bytes 1572872 | tf_op jit(solution)/shard_map/ppermute | solution.py:530
  28.1 13.3 %collective-permute-start.12 = (bf16[2,512,256]{2,1,0:T(8,128)(2,1)S(1)}, bf16[2,512,256]{2,1,0:T(8,128)(2,1)S(1)}, u32[]{:S(2)}, u32[]{:S(2)}) collective-permute-start(bf16[2,512,256]{2,1,0:T(8,128)(2,1)S(1)} %collective-permute-done.4.refs_0_), channel_id=1, source_target_pairs={{0,1},{1,0},{2,3},{3,2},{4,5},{5,4},{6,7},{7,6},{8,9},{9,8},{10,11... | collective-permute-start | bytes 1572872 | tf_op jit(solution)/shard_map/ppermute | solution.py:108
  29.3 13.3 %collective-permute-start.14 = (bf16[512,512]{1,0:T(8,128)(2,1)S(1)}, bf16[512,512]{1,0:T(8,128)(2,1)S(1)}, u32[]{:S(2)}, u32[]{:S(2)}) collective-permute-start(bf16[512,512]{1,0:T(8,128)(2,1)S(1)} %copy-done.1), channel_id=1, source_target_pairs={{0,2},{2,0},{4,6},{6,4},{8,10},{10,8},{12,14},{14,12},{16,18},{18,... | collective-permute-start | bytes 1572872 | tf_op jit(solution)/shard_map/ppermute | solution.py:104
  29.8 13.8 %collective-permute-start.7 = (bf16[512,512]{1,0:T(8,128)(2,1)S(1)}, bf16[512,512]{1,0:T(8,128)(2,1)S(1)}, u32[]{:S(2)}, u32[]{:S(2)}) collective-permute-start(bf16[512,512]{1,0:T(8,128)(2,1)S(1)} %copy-done.1), channel_id=1, source_target_pairs={{0,8},{2,6},{8,16},{10,2},{16,24},{18,10},{24,28},{26,18},{28,20},... | collective-permute-start | bytes 1572872 | tf_op jit(solution)/shard_map/ppermute | solution.py:530
  32.3 14.0 %collective-permute-start.6 = (bf16[1,512,256]{2,1,0:T(8,128)(2,1)S(1)}, bf16[1,512,256]{2,1,0:T(8,128)(2,1)S(1)}, u32[]{:S(2)}, u32[]{:S(2)}) collective-permute-start(bf16[1,512,256]{2,1,0:T(8,128)(2,1)S(1)} %first_of.2), channel_id=1, source_target_pairs={{0,8},{2,6},{8,16},{10,2},{16,24},{18,10},{24,28},{26,18},{28,20},... | collective-permute-start | bytes 786440 | tf_op jit(solution)/shard_map/ppermute | solution.py:530
  41.4 15.9 %collective-permute-start.13 = (bf16[2,512,256]{2,1,0:T(8,128)(2,1)S(1)}, bf16[2,512,256]{2,1,0:T(8,128)(2,1)S(1)}, u32[]{:S(2)}, u32[]{:S(2)}) collective-permute-start(bf16[2,512,256]{2,1,0:T(8,128)(2,1)S(1)} %collective-permute-done.11.refs_0_), channel_id=1, source_target_pairs={{0,8},{2,6},{8,16},{10,2},{16,24},{18,10},{24,28},{26,18},{28,20},... | collective-permute-start | bytes 1572872 | tf_op jit(solution)/shard_map/ppermute | solution.py:530
  41.4 15.9 %collective-permute-start.16 = (bf16[2,512,256]{2,1,0:T(8,128)(2,1)S(1)}, bf16[2,512,256]{2,1,0:T(8,128)(2,1)S(1)}, u32[]{:S(2)}, u32[]{:S(2)}) collective-permute-start(bf16[2,512,256]{2,1,0:T(8,128)(2,1)S(1)} %collective-permute-done.5.pair_ref.refs_0_), channel_id=1, source_target_pairs={{0,1},{1,0},{2,3},{3,2},{4,5},{5,4},{6,7},{7,6},{8,9},{9,8},{10,11... | collective-permute-start | bytes 1572872 | tf_op jit(solution)/shard_map/ppermute | solution.py:108
  42.7 12.1 %collective-permute-start.15 = (bf16[256,512]{1,0:T(8,128)(2,1)S(1)}, bf16[256,512]{1,0:T(8,128)(2,1)S(1)}, u32[]{:S(2)}, u32[]{:S(2)}) collective-permute-start(bf16[256,512]{1,0:T(8,128)(2,1)S(1)} %rows_near.1), channel_id=1, source_target_pairs={{0,8},{2,6},{8,16},{10,2},{16,24},{18,10},{24,28},{26,18},{28,20},... | collective-permute-start | bytes 786440 | tf_op jit(solution)/shard_map/ppermute | solution.py:530
  46.4 14.0 %collective-permute-start.8 = (bf16[512,512]{1,0:T(8,128)(2,1)S(1)}, bf16[512,512]{1,0:T(8,128)(2,1)S(1)}, u32[]{:S(2)}, u32[]{:S(2)}) collective-permute-start(bf16[512,512]{1,0:T(8,128)(2,1)S(1)} %collective-permute-done.7.refs_2_), channel_id=1, source_target_pairs={{0,8},{2,6},{8,16},{10,2},{16,24},{18,10},{24,28},{26,18},{28,20},... | collective-permute-start | bytes 1572872 | tf_op jit(solution)/shard_map/ppermute | solution.py:530
  54.8 9.7 %collective-permute-start.20 = (bf16[256,512]{1,0:T(8,128)(2,1)S(1)}, bf16[256,512]{1,0:T(8,128)(2,1)S(1)}, u32[]{:S(2)}, u32[]{:S(2)}) collective-permute-start(bf16[256,512]{1,0:T(8,128)(2,1)S(1)} %collective-permute-done.15.refs_3_), channel_id=1, source_target_pairs={{0,1},{1,0},{2,3},{3,2},{4,5},{5,4},{6,7},{7,6},{8,9},{9,8},{10,11... | collective-permute-start | bytes 786440 | tf_op jit(solution)/shard_map/ppermute | solution.py:108
  57.4 5.9 %collective-permute-start.17 = (bf16[1,512,256]{2,1,0:T(8,128)(2,1)S(1)}, bf16[1,512,256]{2,1,0:T(8,128)(2,1)S(1)}, u32[]{:S(2)}, u32[]{:S(2)}) collective-permute-start(bf16[1,512,256]{2,1,0:T(8,128)(2,1)S(1)} %first_of.3), channel_id=1, source_target_pairs={{0,8},{2,6},{8,16},{10,2},{16,24},{18,10},{24,28},{26,18},{28,20},... | collective-permute-start | bytes 786440 | tf_op jit(solution)/shard_map/ppermute | solution.py:530
  59.8 8.1 %collective-permute-start.23 = (bf16[256,512]{1,0:T(8,128)(2,1)S(1)}, bf16[256,512]{1,0:T(8,128)(2,1)S(1)}, u32[]{:S(2)}, u32[]{:S(2)}) collective-permute-start(bf16[256,512]{1,0:T(8,128)(2,1)S(1)} %collective-permute-done.15.refs_3_), channel_id=1, source_target_pairs={{0,8},{2,6},{8,16},{10,2},{16,24},{18,10},{24,28},{26,18},{28,20},... | collective-permute-start | bytes 786440 | tf_op jit(solution)/shard_map/ppermute | solution.py:530
  60.1 7.8 %collective-permute-start.19 = (bf16[1,512,256]{2,1,0:T(8,128)(2,1)S(1)}, bf16[1,512,256]{2,1,0:T(8,128)(2,1)S(1)}, u32[]{:S(2)}, u32[]{:S(2)}) collective-permute-start(bf16[1,512,256]{2,1,0:T(8,128)(2,1)S(1)} %collective-permute-done.6.refs_0_), channel_id=1, source_target_pairs={{0,1},{1,0},{2,3},{3,2},{4,5},{5,4},{6,7},{7,6},{8,9},{9,8},{10,11... | collective-permute-start | bytes 786440 | tf_op jit(solution)/shard_map/ppermute | solution.py:108
  63.2 8.4 %collective-permute-start.18 = (bf16[512,512]{1,0:T(8,128)(2,1)S(1)}, bf16[512,512]{1,0:T(8,128)(2,1)S(1)}, u32[]{:S(2)}, u32[]{:S(2)}) collective-permute-start(bf16[512,512]{1,0:T(8,128)(2,1)S(1)} %collective-permute-done.8.refs_8_), channel_id=1, source_target_pairs={{0,8},{2,6},{8,16},{10,2},{16,24},{18,10},{24,28},{26,18},{28,20},... | collective-permute-start | bytes 1572872 | tf_op jit(solution)/shard_map/ppermute | solution.py:530
  67.9 7.3 %collective-permute-start.26 = (bf16[256,512]{1,0:T(8,128)(2,1)S(1)}, bf16[256,512]{1,0:T(8,128)(2,1)S(1)}, u32[]{:S(2)}, u32[]{:S(2)}) collective-permute-start(bf16[256,512]{1,0:T(8,128)(2,1)S(1)} %collective-permute-done.23.refs_9_), channel_id=1, source_target_pairs={{0,1},{1,0},{2,3},{3,2},{4,5},{5,4},{6,7},{7,6},{8,9},{9,8},{10,11... | collective-permute-start | bytes 786440 | tf_op jit(solution)/shard_map/ppermute | solution.py:108
  68.8 8.0 %collective-permute-start.24 = (bf16[256,512]{1,0:T(8,128)(2,1)S(1)}, bf16[256,512]{1,0:T(8,128)(2,1)S(1)}, u32[]{:S(2)}, u32[]{:S(2)}) collective-permute-start(bf16[256,512]{1,0:T(8,128)(2,1)S(1)} %collective-permute-done.23.refs_9_), channel_id=1, source_target_pairs={{0,8},{2,6},{8,16},{10,2},{16,24},{18,10},{24,28},{26,18},{28,20},... | collective-permute-start | bytes 786440 | tf_op jit(solution)/shard_map/ppermute | solution.py:530
  72.7 28.3 %collective-permute-start.22 = (f32[256,512]{1,0:T(8,128)S(1)}, f32[256,512]{1,0:T(8,128)S(1)}, u32[]{:S(2)}, u32[]{:S(2)}) collective-permute-start(f32[256,512]{1,0:T(8,128)S(1)} %get-tuple-element.71), channel_id=1, source_target_pairs={{0,2},{2,0},{4,6},{6,4},{8,10},{10,8},{12,14},{14,12},{16,18},{18,... | collective-permute-start | bytes 1572872 | tf_op jit(solution)/shard_map/ppermute | solution.py:104
  75.5 8.2 %collective-permute-start.34 = (bf16[256,512]{1,0:T(8,128)(2,1)S(1)}, bf16[256,512]{1,0:T(8,128)(2,1)S(1)}, u32[]{:S(2)}, u32[]{:S(2)}) collective-permute-start(bf16[256,512]{1,0:T(8,128)(2,1)S(1)} %collective-permute-done.15.refs_3_), channel_id=1, source_target_pairs={{0,2},{2,0},{4,6},{6,4},{8,10},{10,8},{12,14},{14,12},{16,18},{18,... | collective-permute-start | bytes 786440 | tf_op jit(solution)/shard_map/ppermute | solution.py:104
  76.7 8.6 %collective-permute-start.25 = (bf16[256,512]{1,0:T(8,128)(2,1)S(1)}, bf16[256,512]{1,0:T(8,128)(2,1)S(1)}, u32[]{:S(2)}, u32[]{:S(2)}) collective-permute-start(bf16[256,512]{1,0:T(8,128)(2,1)S(1)} %collective-permute-done.24.refs_15_), channel_id=1, source_target_pairs={{0,1},{1,0},{2,3},{3,2},{4,5},{5,4},{6,7},{7,6},{8,9},{9,8},{10,11... | collective-permute-start | bytes 786440 | tf_op jit(solution)/shard_map/ppermute | solution.py:108
  79.6 12.4 %collective-permute-start.28 = (bf16[2,256,256]{2,1,0:T(8,128)(2,1)S(1)}, bf16[2,256,256]{2,1,0:T(8,128)(2,1)S(1)}, u32[]{:S(2)}, u32[]{:S(2)}) collective-permute-start(bf16[2,256,256]{2,1,0:T(8,128)(2,1)S(1)} %join_row.1.refs_2_), channel_id=1, source_target_pairs={{0,16},{4,20},{8,24},{12,28},{16,26},{20,30},{24,18},{28,22},{26,1... | collective-permute-start | bytes 786440 | tf_op jit(solution)/shard_map/ppermute | solution.py:618
  81.7 12.5 %collective-permute-start.29 = (bf16[2,256,256]{2,1,0:T(8,128)(2,1)S(1)}, bf16[2,256,256]{2,1,0:T(8,128)(2,1)S(1)}, u32[]{:S(2)}, u32[]{:S(2)}) collective-permute-start(bf16[2,256,256]{2,1,0:T(8,128)(2,1)S(1)} %join_row.1.refs_2_), channel_id=1, source_target_pairs={{0,8},{4,12},{8,16},{12,20},{16,24},{20,28},{24,26},{28,30},{26,18... | collective-permute-start | bytes 786440 | tf_op jit(solution)/shard_map/ppermute | solution.py:618
  83.7 22.0 %collective-permute-start.31 = (bf16[512,512]{1,0:T(8,128)(2,1)S(1)}, bf16[512,512]{1,0:T(8,128)(2,1)S(1)}, u32[]{:S(2)}, u32[]{:S(2)}) collective-permute-start(bf16[512,512]{1,0:T(8,128)(2,1)S(1)} %collective-permute-done.18.refs_14_), channel_id=1, source_target_pairs={{0,8},{2,6},{8,16},{10,2},{16,24},{18,10},{24,28},{26,18},{28,20},... | collective-permute-start | bytes 1572872 | tf_op jit(solution)/shard_map/ppermute | solution.py:530
  85.4 19.2 %collective-permute-start.35 = (bf16[256,512]{1,0:T(8,128)(2,1)S(1)}, bf16[256,512]{1,0:T(8,128)(2,1)S(1)}, u32[]{:S(2)}, u32[]{:S(2)}) collective-permute-start(bf16[256,512]{1,0:T(8,128)(2,1)S(1)} %collective-permute-done.20.refs_4_), channel_id=1, source_target_pairs={{0,2},{2,0},{4,6},{6,4},{8,10},{10,8},{12,14},{14,12},{16,18},{18,... | collective-permute-start | bytes 786440 | tf_op jit(solution)/shard_map/ppermute | solution.py:104
  92.0 13.1 %collective-permute-start.37 = (bf16[256,512]{1,0:T(8,128)(2,1)S(1)}, bf16[256,512]{1,0:T(8,128)(2,1)S(1)}, u32[]{:S(2)}, u32[]{:S(2)}) collective-permute-start(bf16[256,512]{1,0:T(8,128)(2,1)S(1)} %collective-permute-done.23.refs_9_), channel_id=1, source_target_pairs={{0,2},{2,0},{4,6},{6,4},{8,10},{10,8},{12,14},{14,12},{16,18},{18,... | collective-permute-start | bytes 786440 | tf_op jit(solution)/shard_map/ppermute | solution.py:104
  94.2 11.0 %collective-permute-start.38 = (bf16[256,512]{1,0:T(8,128)(2,1)S(1)}, bf16[256,512]{1,0:T(8,128)(2,1)S(1)}, u32[]{:S(2)}, u32[]{:S(2)}) collective-permute-start(bf16[256,512]{1,0:T(8,128)(2,1)S(1)} %collective-permute-done.26.refs_10_), channel_id=1, source_target_pairs={{0,2},{2,0},{4,6},{6,4},{8,10},{10,8},{12,14},{14,12},{16,18},{18,... | collective-permute-start | bytes 786440 | tf_op jit(solution)/shard_map/ppermute | solution.py:104
  105.7 7.1 %collective-permute-start.32 = (bf16[512,512]{1,0:T(8,128)(2,1)S(1)}, bf16[512,512]{1,0:T(8,128)(2,1)S(1)}, u32[]{:S(2)}, u32[]{:S(2)}) collective-permute-start(bf16[512,512]{1,0:T(8,128)(2,1)S(1)} %collective-permute-done.31.refs_0_), channel_id=1, source_target_pairs={{0,2},{2,0},{4,6},{6,4},{8,10},{10,8},{12,14},{14,12},{16,18},{18,... | collective-permute-start | bytes 1572872 | tf_op jit(solution)/shard_map/ppermute | solution.py:104
  (12 other events, 57.5 us)

commit v9 on v8

--- a/solution.py
+++ b/solution.py
@@ -58,9 +58,8 @@
     "W1 M0",
     "W2",
     "W3",
+    "W4",
     "O0",
-    "W4",
-    "O1",
 )
 MICROS = {}
 PROJECTIONS = {
@@ -72,7 +71,7 @@
     "Q3": (3, 4, False),
     "Q4": (4, 5, True),
 }
-COLUMNS = ((0, 1, 2, 3), (4,))
+COLUMNS = ((0, 1, 2, 3, 4),)
 
 
 def step_shards(turn, half):
@@ -651,7 +650,7 @@
         cosine, sine, query_cosine, query_sine, key_seg = tables
         for entry in PLAN:
             run(*entry.split())
-        return done["O1"]
+        return done["O0"]
     else:
         index = jnp.stack(index).astype(jnp.int32)
         cosine, sine, query_cosine, query_sine, key_seg = tables

time: 115 us -> 113 us (0.983)
  Pallas kernels: 21.3 us -> 19.9 us
    pallas_call x2 -> x1, Pallas kernels: 5.16 us -> 3.74 us  [columns_of(): pl.pallas_call(functools.partial(columns_kernel, entries), in_specs=specs...]
    ppermute x17, starting transfers between devices: 21.4 us -> 20.1 us  [core_swap(): return lax.ppermute(value, 'ctx', [(i, i ^ 1) for i in range(count)])]
  transfers between devices with their start and end apart: 42 -> 42, of which waited for: 20 -> 20; matrix products, arithmetic and copies ran while one was open for 1% -> 1% of each run, Pallas kernels for 16% -> 13%
where the time goes in v9:
time: 113 us
  starting transfers between devices  45.9 us (41%)
  waiting for transfers between devices  45.4 us (40%)
  Pallas kernels  19.9 us (18%)
    ppermute x15, waiting for transfers between devices, ring(): return lax.ppermute(value, 'ctx', pairs)  29.2 us
    ppermute x17, starting transfers between devices, core_swap(): return lax.ppermute(value, 'ctx', [(i, i ^ 1) for i in range(count)])  20.1 us
    ppermute x15, starting transfers between devices, ring(): return lax.ppermute(value, 'ctx', pairs)  14.5 us
    pallas_call x7, Pallas kernels, project(): pl.pallas_call(functools.partial(project_kernel, slots, base, groups, tot...  8.38 us
    ppermute x7, starting transfers between devices, plane_swap(): return lax.ppermute(value, 'dp', [(0, 1), (1, 0)])  6.96 us
    ppermute x7, waiting for transfers between devices, plane_swap(): return lax.ppermute(value, 'dp', [(0, 1), (1, 0)])  6.37 us
    ppermute x2, starting transfers between devices, run(): value = lax.ppermute(tied(done['R0']), 'ctx', sends)  4.01 us
    ppermute x17, waiting for transfers between devices, core_swap(): return lax.ppermute(value, 'ctx', [(i, i ^ 1) for i in range(count)])  3.97 us
  transfers between devices with their start and end apart: 42, of which 20 were waited for; matrix products, arithmetic and copies ran while one was open for 1% of the time, Pallas kernels for 13%

profile of v9, /device:TPU:19, one launch (start us, length us, event | category | flops | bytes accessed | tf_op | source)
XLA Modules:
  0.0 113.3 jit_solution(9159862840483127683)
XLA Ops:
  3.2 1.3 %collective-permute-start.2 = (bf16[2,512,256]{2,1,0:T(8,128)(2,1)S(1)}, bf16[2,512,256]{2,1,0:T(8,128)(2,1)S(1)}, u32[]{:S(2)}, u32[]{:S(2)}) collective-permute-start(bf16[2,512,256]{2,1,0:T(8,128)(2,1)S(1)} %both_of.2), channel_id=1, source_target_pairs={{0,8},{2,6},{8,16},{10,2},{16,24},{18,10},{24,28},{26,18},{28,20},... | collective-permute-start | bytes 1572872 | tf_op jit(solution)/shard_map/ppermute | solution.py:529
  6.1 2.3 %bring.1.own_ref = bf16[256,8192]{1,0:T(8,128)(2,1)S(1)} custom-call(bf16[256,8192]{1,0:T(8,128)(2,1)} %source_ref), custom_call_target="tpu_custom_call" | custom-call | flops 2307000064 | tf_op jit(solution)/shard_map/bring/pallas_call | solution.py:355
  8.4 3.2 %collective-permute-done.2.refs_2_ = bf16[2,512,256]{2,1,0:T(8,128)(2,1)S(1)} collective-permute-done((bf16[2,512,256]{2,1,0:T(8,128)(2,1)S(1)}, bf16[2,512,256]{2,1,0:T(8,128)(2,1)S(1)}, u32[]{:S(2)}, u32[]{:S(2)}) %collective-permute-start.2) | collective-permute-done | bytes 524320 | tf_op jit(solution)/shard_map/ppermute | solution.py:529
  12.8 1.3 %collective-permute-start.4 = (bf16[2,512,256]{2,1,0:T(8,128)(2,1)S(1)}, bf16[2,512,256]{2,1,0:T(8,128)(2,1)S(1)}, u32[]{:S(2)}, u32[]{:S(2)}) collective-permute-start(bf16[2,512,256]{2,1,0:T(8,128)(2,1)S(1)} %collective-permute-done.2.refs_2_), channel_id=1, source_target_pairs={{0,8},{2,6},{8,16},{10,2},{16,24},{18,10},{24,28},{26,18},{28,20},... | collective-permute-start | bytes 1572872 | tf_op jit(solution)/shard_map/ppermute | solution.py:529
  15.6 5.5 %collective-permute-done.4.refs_0_ = bf16[2,512,256]{2,1,0:T(8,128)(2,1)S(1)} collective-permute-done((bf16[2,512,256]{2,1,0:T(8,128)(2,1)S(1)}, bf16[2,512,256]{2,1,0:T(8,128)(2,1)S(1)}, u32[]{:S(2)}, u32[]{:S(2)}) %collective-permute-start.4) | collective-permute-done | bytes 524320 | tf_op jit(solution)/shard_map/ppermute | solution.py:529
  21.1 1.3 %collective-permute-start.5 = (bf16[2,512,256]{2,1,0:T(8,128)(2,1)S(1)}, bf16[2,512,256]{2,1,0:T(8,128)(2,1)S(1)}, u32[]{:S(2)}, u32[]{:S(2)}) collective-permute-start(bf16[2,512,256]{2,1,0:T(8,128)(2,1)S(1)} %collective-permute-done.4.refs_0_), channel_id=1, source_target_pairs={{0,8},{2,6},{8,16},{10,2},{16,24},{18,10},{24,28},{26,18},{28,20},... | collective-permute-start | bytes 1572872 | tf_op jit(solution)/shard_map/ppermute | solution.py:529
  22.4 4.3 %collective-permute-done.9.refs_1_ = bf16[2,512,256]{2,1,0:T(8,128)(2,1)S(1)} collective-permute-done((bf16[2,512,256]{2,1,0:T(8,128)(2,1)S(1)}, bf16[2,512,256]{2,1,0:T(8,128)(2,1)S(1)}, u32[]{:S(2)}, u32[]{:S(2)}) %collective-permute-start.9) | collective-permute-done | bytes 524320 | tf_op jit(solution)/shard_map/ppermute | solution.py:529
  26.7 1.4 %collective-permute-done.10.refs_3_ = bf16[2,512,256]{2,1,0:T(8,128)(2,1)S(1)} collective-permute-done((bf16[2,512,256]{2,1,0:T(8,128)(2,1)S(1)}, bf16[2,512,256]{2,1,0:T(8,128)(2,1)S(1)}, u32[]{:S(2)}, u32[]{:S(2)}) %collective-permute-start.10) | collective-permute-done | bytes 524320 | tf_op jit(solution)/shard_map/ppermute | solution.py:107
  29.8 1.7 %collective-permute-start.7 = (bf16[512,512]{1,0:T(8,128)(2,1)S(1)}, bf16[512,512]{1,0:T(8,128)(2,1)S(1)}, u32[]{:S(2)}, u32[]{:S(2)}) collective-permute-start(bf16[512,512]{1,0:T(8,128)(2,1)S(1)} %copy-done.1), channel_id=1, source_target_pairs={{0,8},{2,6},{8,16},{10,2},{16,24},{18,10},{24,28},{26,18},{28,20},... | collective-permute-start | bytes 1572872 | tf_op jit(solution)/shard_map/ppermute | solution.py:529
  32.3 1.3 %collective-permute-start.6 = (bf16[1,512,256]{2,1,0:T(8,128)(2,1)S(1)}, bf16[1,512,256]{2,1,0:T(8,128)(2,1)S(1)}, u32[]{:S(2)}, u32[]{:S(2)}) collective-permute-start(bf16[1,512,256]{2,1,0:T(8,128)(2,1)S(1)} %first_of.2), channel_id=1, source_target_pairs={{0,8},{2,6},{8,16},{10,2},{16,24},{18,10},{24,28},{26,18},{28,20},... | collective-permute-start | bytes 786440 | tf_op jit(solution)/shard_map/ppermute | solution.py:529
  33.7 1.5 %project.7.refs_2_ = f32[2,256,512]{2,1,0:T(8,128)S(1)} custom-call(s32[19]{0:T(128)S(1)} %stack.76.index_ref, bf16[256,8192]{1,0:T(8,128)(2,1)S(1)} %bring.1.own_ref, bf16[256,8192]{1,0:T(8,128)(2,1)S(1)} %collective-permute-done.3.other_ref, bf16[1,512,256]{2,1,0:T(8,128)(2,1)S(1)} %get-tuple-element.44.first_ref.refs_0_, ...), custom_call_target="tpu_custom_call" | custom-call | flops 2307000064 | tf_op jit(solution)/shard_map/project/pallas_call | solution.py:410
  35.2 2.7 %collective-permute-done.11.refs_0_ = bf16[2,512,256]{2,1,0:T(8,128)(2,1)S(1)} collective-permute-done((bf16[2,512,256]{2,1,0:T(8,128)(2,1)S(1)}, bf16[2,512,256]{2,1,0:T(8,128)(2,1)S(1)}, u32[]{:S(2)}, u32[]{:S(2)}) %collective-permute-start.11) | collective-permute-done | bytes 524320 | tf_op jit(solution)/shard_map/ppermute | solution.py:529
  37.9 3.5 %collective-permute-done.12.refs_1_ = bf16[2,512,256]{2,1,0:T(8,128)(2,1)S(1)} collective-permute-done((bf16[2,512,256]{2,1,0:T(8,128)(2,1)S(1)}, bf16[2,512,256]{2,1,0:T(8,128)(2,1)S(1)}, u32[]{:S(2)}, u32[]{:S(2)}) %collective-permute-start.12) | collective-permute-done | bytes 524320 | tf_op jit(solution)/shard_map/ppermute | solution.py:107
  43.6 2.8 %collective-permute-done.6.refs_0_ = bf16[1,512,256]{2,1,0:T(8,128)(2,1)S(1)} collective-permute-done((bf16[1,512,256]{2,1,0:T(8,128)(2,1)S(1)}, bf16[1,512,256]{2,1,0:T(8,128)(2,1)S(1)}, u32[]{:S(2)}, u32[]{:S(2)}) %collective-permute-start.6) | collective-permute-done | bytes 262176 | tf_op jit(solution)/shard_map/ppermute | solution.py:529
  46.4 1.3 %collective-permute-start.8 = (bf16[512,512]{1,0:T(8,128)(2,1)S(1)}, bf16[512,512]{1,0:T(8,128)(2,1)S(1)}, u32[]{:S(2)}, u32[]{:S(2)}) collective-permute-start(bf16[512,512]{1,0:T(8,128)(2,1)S(1)} %collective-permute-done.7.refs_2_), channel_id=1, source_target_pairs={{0,8},{2,6},{8,16},{10,2},{16,24},{18,10},{24,28},{26,18},{28,20},... | collective-permute-start | bytes 1572872 | tf_op jit(solution)/shard_map/ppermute | solution.py:529
  47.7 7.1 %collective-permute-done.15.refs_3_ = bf16[256,512]{1,0:T(8,128)(2,1)S(1)} collective-permute-done((bf16[256,512]{1,0:T(8,128)(2,1)S(1)}, bf16[256,512]{1,0:T(8,128)(2,1)S(1)}, u32[]{:S(2)}, u32[]{:S(2)}) %collective-permute-start.15) | collective-permute-done | bytes 262176 | tf_op jit(solution)/shard_map/ppermute | solution.py:529
  57.4 1.4 %collective-permute-start.17 = (bf16[1,512,256]{2,1,0:T(8,128)(2,1)S(1)}, bf16[1,512,256]{2,1,0:T(8,128)(2,1)S(1)}, u32[]{:S(2)}, u32[]{:S(2)}) collective-permute-start(bf16[1,512,256]{2,1,0:T(8,128)(2,1)S(1)} %first_of.3), channel_id=1, source_target_pairs={{0,8},{2,6},{8,16},{10,2},{16,24},{18,10},{24,28},{26,18},{28,20},... | collective-permute-start | bytes 786440 | tf_op jit(solution)/shard_map/ppermute | solution.py:529
  61.7 1.5 %collective-permute-done.17.refs_0_ = bf16[1,512,256]{2,1,0:T(8,128)(2,1)S(1)} collective-permute-done((bf16[1,512,256]{2,1,0:T(8,128)(2,1)S(1)}, bf16[1,512,256]{2,1,0:T(8,128)(2,1)S(1)}, u32[]{:S(2)}, u32[]{:S(2)}) %collective-permute-start.17) | collective-permute-done | bytes 262176 | tf_op jit(solution)/shard_map/ppermute | solution.py:529
  63.2 1.3 %collective-permute-start.18 = (bf16[512,512]{1,0:T(8,128)(2,1)S(1)}, bf16[512,512]{1,0:T(8,128)(2,1)S(1)}, u32[]{:S(2)}, u32[]{:S(2)}) collective-permute-start(bf16[512,512]{1,0:T(8,128)(2,1)S(1)} %collective-permute-done.8.refs_8_), channel_id=1, source_target_pairs={{0,8},{2,6},{8,16},{10,2},{16,24},{18,10},{24,28},{26,18},{28,20},... | collective-permute-start | bytes 1572872 | tf_op jit(solution)/shard_map/ppermute | solution.py:529
  66.4 1.5 %collective-permute-done.19.refs_1_ = bf16[1,512,256]{2,1,0:T(8,128)(2,1)S(1)} collective-permute-done((bf16[1,512,256]{2,1,0:T(8,128)(2,1)S(1)}, bf16[1,512,256]{2,1,0:T(8,128)(2,1)S(1)}, u32[]{:S(2)}, u32[]{:S(2)}) %collective-permute-start.19) | collective-permute-done | bytes 262176 | tf_op jit(solution)/shard_map/ppermute | solution.py:107
  72.7 2.5 %collective-permute-start.22 = (f32[256,512]{1,0:T(8,128)S(1)}, f32[256,512]{1,0:T(8,128)S(1)}, u32[]{:S(2)}, u32[]{:S(2)}) collective-permute-start(f32[256,512]{1,0:T(8,128)S(1)} %get-tuple-element.71), channel_id=1, source_target_pairs={{0,2},{2,0},{4,6},{6,4},{8,10},{10,8},{12,14},{14,12},{16,18},{18,... | collective-permute-start | bytes 1572872 | tf_op jit(solution)/shard_map/ppermute | solution.py:103
  76.5 2.6 %collective-permute-done.27.beside_ref = bf16[256,256]{1,0:T(8,128)(2,1)S(1)} collective-permute-done((bf16[256,256]{1,0:T(8,128)(2,1)S(1)}, bf16[256,256]{1,0:T(8,128)(2,1)S(1)}, u32[]{:S(2)}, u32[]{:S(2)}) %collective-permute-start.27) | collective-permute-done | bytes 131104 | tf_op jit(solution)/shard_map/ppermute | solution.py:610
  79.7 2.1 %collective-permute-start.28 = (bf16[2,256,256]{2,1,0:T(8,128)(2,1)S(1)}, bf16[2,256,256]{2,1,0:T(8,128)(2,1)S(1)}, u32[]{:S(2)}, u32[]{:S(2)}) collective-permute-start(bf16[2,256,256]{2,1,0:T(8,128)(2,1)S(1)} %join_row.1.refs_2_), channel_id=1, source_target_pairs={{0,16},{4,20},{8,24},{12,28},{16,26},{20,30},{24,18},{28,22},{26,1... | collective-permute-start | bytes 786440 | tf_op jit(solution)/shard_map/ppermute | solution.py:617
  81.8 1.9 %collective-permute-start.29 = (bf16[2,256,256]{2,1,0:T(8,128)(2,1)S(1)}, bf16[2,256,256]{2,1,0:T(8,128)(2,1)S(1)}, u32[]{:S(2)}, u32[]{:S(2)}) collective-permute-start(bf16[2,256,256]{2,1,0:T(8,128)(2,1)S(1)} %join_row.1.refs_2_), channel_id=1, source_target_pairs={{0,8},{4,12},{8,16},{12,20},{16,24},{20,28},{24,26},{28,30},{26,18... | collective-permute-start | bytes 786440 | tf_op jit(solution)/shard_map/ppermute | solution.py:617
  83.7 1.8 %collective-permute-start.40 = (bf16[512,512]{1,0:T(8,128)(2,1)S(1)}, bf16[512,512]{1,0:T(8,128)(2,1)S(1)}, u32[]{:S(2)}, u32[]{:S(2)}) collective-permute-start(bf16[512,512]{1,0:T(8,128)(2,1)S(1)} %collective-permute-done.18.refs_14_), channel_id=1, source_target_pairs={{0,8},{2,6},{8,16},{10,2},{16,24},{18,10},{24,28},{26,18},{28,20},... | collective-permute-start | bytes 1572872 | tf_op jit(solution)/shard_map/ppermute | solution.py:529
  85.5 3.4 %collective-permute-start.33 = (bf16[256,512]{1,0:T(8,128)(2,1)S(1)}, bf16[256,512]{1,0:T(8,128)(2,1)S(1)}, u32[]{:S(2)}, u32[]{:S(2)}) collective-permute-start(bf16[256,512]{1,0:T(8,128)(2,1)S(1)} %collective-permute-done.20.refs_4_), channel_id=1, source_target_pairs={{0,2},{2,0},{4,6},{6,4},{8,10},{10,8},{12,14},{14,12},{16,18},{18,... | collective-permute-start | bytes 786440 | tf_op jit(solution)/shard_map/ppermute | solution.py:103
  88.9 3.2 %collective-permute-done.28.refs_0_ = bf16[2,256,256]{2,1,0:T(8,128)(2,1)S(1)} collective-permute-done((bf16[2,256,256]{2,1,0:T(8,128)(2,1)S(1)}, bf16[2,256,256]{2,1,0:T(8,128)(2,1)S(1)}, u32[]{:S(2)}, u32[]{:S(2)}) %collective-permute-start.28) | collective-permute-done | bytes 262176 | tf_op jit(solution)/shard_map/ppermute | solution.py:617
  92.1 2.1 %collective-permute-start.35 = (bf16[256,512]{1,0:T(8,128)(2,1)S(1)}, bf16[256,512]{1,0:T(8,128)(2,1)S(1)}, u32[]{:S(2)}, u32[]{:S(2)}) collective-permute-start(bf16[256,512]{1,0:T(8,128)(2,1)S(1)} %collective-permute-done.23.refs_9_), channel_id=1, source_target_pairs={{0,2},{2,0},{4,6},{6,4},{8,10},{10,8},{12,14},{14,12},{16,18},{18,... | collective-permute-start | bytes 786440 | tf_op jit(solution)/shard_map/ppermute | solution.py:103
  94.2 6.9 %collective-permute-start.36 = (bf16[256,512]{1,0:T(8,128)(2,1)S(1)}, bf16[256,512]{1,0:T(8,128)(2,1)S(1)}, u32[]{:S(2)}, u32[]{:S(2)}) collective-permute-start(bf16[256,512]{1,0:T(8,128)(2,1)S(1)} %collective-permute-done.26.refs_10_), channel_id=1, source_target_pairs={{0,2},{2,0},{4,6},{6,4},{8,10},{10,8},{12,14},{14,12},{16,18},{18,... | collective-permute-start | bytes 786440 | tf_op jit(solution)/shard_map/ppermute | solution.py:103
  101.4 3.3 %attend.1.mixed_ref = bf16[256,512]{1,0:T(8,128)(2,1)S(1)} custom-call(s32[19]{0:T(128)S(1)} %stack.76.index_ref, bf16[256,512]{1,0:T(8,128)(2,1)S(1)} %rotate_sums.3.query_ref, s32[1,1280]{1,0:T(1,128)S(1)} %bitcast.29, bf16[2,256,256]{2,1,0:T(8,128)(2,1)S(1)} %collective-permute-done.28.refs_0_, bf16[2,256,256]{2,1,0:T(8,128)(2,1)S(1)} %collective-permute-done.29.refs_1_, ...), custom_call_target="tpu_custom_call" | custom-call | flops 2307000064 | tf_op jit(solution)/shard_map/attend/pallas_call | solution.py:253
  106.9 2.1 %collective-permute-done.39.refs_19_ = bf16[256,512]{1,0:T(8,128)(2,1)S(1)} collective-permute-done((bf16[256,512]{1,0:T(8,128)(2,1)S(1)}, bf16[256,512]{1,0:T(8,128)(2,1)S(1)}, u32[]{:S(2)}, u32[]{:S(2)}) %collective-permute-start.39) | collective-permute-done | bytes 262176 | tf_op jit(solution)/shard_map/ppermute | solution.py:103
  109.4 3.7 %columns_of.1 = bf16[256,8192]{1,0:T(8,128)(2,1)} custom-call(s32[19]{0:T(128)S(1)} %stack.76.index_ref, bf16[256,512]{1,0:T(8,128)(2,1)S(1)} %attend.1.mixed_ref, bf16[256,512]{1,0:T(8,128)(2,1)S(1)} %collective-permute-done.30.returned_ref, bf16[512,512]{1,0:T(8,128)(2,1)S(1)} %copy-done.1, ...), custom_call_target="tpu_custom_call" | custom-call | flops 2307000064 | tf_op jit(solution)/shard_map/columns_of/pallas_call | solution.py:467
  (86 shorter events, 28.6 us)
Async XLA Ops:
  3.2 8.4 %collective-permute-start.2 = (bf16[2,512,256]{2,1,0:T(8,128)(2,1)S(1)}, bf16[2,512,256]{2,1,0:T(8,128)(2,1)S(1)}, u32[]{:S(2)}, u32[]{:S(2)}) collective-permute-start(bf16[2,512,256]{2,1,0:T(8,128)(2,1)S(1)} %both_of.2), channel_id=1, source_target_pairs={{0,8},{2,6},{8,16},{10,2},{16,24},{18,10},{24,28},{26,18},{28,20},... | collective-permute-start | bytes 1572872 | tf_op jit(solution)/shard_map/ppermute | solution.py:529
  11.5 9.6 %collective-permute-start.3 = (bf16[256,8192]{1,0:T(8,128)(2,1)S(1)}, bf16[256,8192]{1,0:T(8,128)(2,1)S(1)}, u32[]{:S(2)}, u32[]{:S(2)}) collective-permute-start(bf16[256,8192]{1,0:T(8,128)(2,1)S(1)} %bring.1.own_ref), channel_id=1, source_target_pairs={{0,2},{2,0},{4,6},{6,4},{8,10},{10,8},{12,14},{14,12},{16,18},{18,... | collective-permute-start | bytes 12582920 | tf_op jit(solution)/shard_map/ppermute | solution.py:103
  12.8 8.3 %collective-permute-start.4 = (bf16[2,512,256]{2,1,0:T(8,128)(2,1)S(1)}, bf16[2,512,256]{2,1,0:T(8,128)(2,1)S(1)}, u32[]{:S(2)}, u32[]{:S(2)}) collective-permute-start(bf16[2,512,256]{2,1,0:T(8,128)(2,1)S(1)} %collective-permute-done.2.refs_2_), channel_id=1, source_target_pairs={{0,8},{2,6},{8,16},{10,2},{16,24},{18,10},{24,28},{26,18},{28,20},... | collective-permute-start | bytes 1572872 | tf_op jit(solution)/shard_map/ppermute | solution.py:529
  14.1 12.6 %collective-permute-start.9 = (bf16[2,512,256]{2,1,0:T(8,128)(2,1)S(1)}, bf16[2,512,256]{2,1,0:T(8,128)(2,1)S(1)}, u32[]{:S(2)}, u32[]{:S(2)}) collective-permute-start(bf16[2,512,256]{2,1,0:T(8,128)(2,1)S(1)} %both_of.3), channel_id=1, source_target_pairs={{0,8},{2,6},{8,16},{10,2},{16,24},{18,10},{24,28},{26,18},{28,20},... | collective-permute-start | bytes 1572872 | tf_op jit(solution)/shard_map/ppermute | solution.py:529
  14.3 13.8 %collective-permute-start.10 = (bf16[2,512,256]{2,1,0:T(8,128)(2,1)S(1)}, bf16[2,512,256]{2,1,0:T(8,128)(2,1)S(1)}, u32[]{:S(2)}, u32[]{:S(2)}) collective-permute-start(bf16[2,512,256]{2,1,0:T(8,128)(2,1)S(1)} %collective-permute-done.2.refs_2_), channel_id=1, source_target_pairs={{0,1},{1,0},{2,3},{3,2},{4,5},{5,4},{6,7},{7,6},{8,9},{9,8},{10,11... | collective-permute-start | bytes 1572872 | tf_op jit(solution)/shard_map/ppermute | solution.py:107
  21.1 11.2 %collective-permute-start.5 = (bf16[2,512,256]{2,1,0:T(8,128)(2,1)S(1)}, bf16[2,512,256]{2,1,0:T(8,128)(2,1)S(1)}, u32[]{:S(2)}, u32[]{:S(2)}) collective-permute-start(bf16[2,512,256]{2,1,0:T(8,128)(2,1)S(1)} %collective-permute-done.4.refs_0_), channel_id=1, source_target_pairs={{0,8},{2,6},{8,16},{10,2},{16,24},{18,10},{24,28},{26,18},{28,20},... | collective-permute-start | bytes 1572872 | tf_op jit(solution)/shard_map/ppermute | solution.py:529
  28.1 9.9 %collective-permute-start.11 = (bf16[2,512,256]{2,1,0:T(8,128)(2,1)S(1)}, bf16[2,512,256]{2,1,0:T(8,128)(2,1)S(1)}, u32[]{:S(2)}, u32[]{:S(2)}) collective-permute-start(bf16[2,512,256]{2,1,0:T(8,128)(2,1)S(1)} %collective-permute-done.9.refs_1_), channel_id=1, source_target_pairs={{0,8},{2,6},{8,16},{10,2},{16,24},{18,10},{24,28},{26,18},{28,20},... | collective-permute-start | bytes 1572872 | tf_op jit(solution)/shard_map/ppermute | solution.py:529
  28.1 13.3 %collective-permute-start.12 = (bf16[2,512,256]{2,1,0:T(8,128)(2,1)S(1)}, bf16[2,512,256]{2,1,0:T(8,128)(2,1)S(1)}, u32[]{:S(2)}, u32[]{:S(2)}) collective-permute-start(bf16[2,512,256]{2,1,0:T(8,128)(2,1)S(1)} %collective-permute-done.4.refs_0_), channel_id=1, source_target_pairs={{0,1},{1,0},{2,3},{3,2},{4,5},{5,4},{6,7},{7,6},{8,9},{9,8},{10,11... | collective-permute-start | bytes 1572872 | tf_op jit(solution)/shard_map/ppermute | solution.py:107
  29.3 13.3 %collective-permute-start.14 = (bf16[512,512]{1,0:T(8,128)(2,1)S(1)}, bf16[512,512]{1,0:T(8,128)(2,1)S(1)}, u32[]{:S(2)}, u32[]{:S(2)}) collective-permute-start(bf16[512,512]{1,0:T(8,128)(2,1)S(1)} %copy-done.1), channel_id=1, source_target_pairs={{0,2},{2,0},{4,6},{6,4},{8,10},{10,8},{12,14},{14,12},{16,18},{18,... | collective-permute-start | bytes 1572872 | tf_op jit(solution)/shard_map/ppermute | solution.py:103
  29.8 13.8 %collective-permute-start.7 = (bf16[512,512]{1,0:T(8,128)(2,1)S(1)}, bf16[512,512]{1,0:T(8,128)(2,1)S(1)}, u32[]{:S(2)}, u32[]{:S(2)}) collective-permute-start(bf16[512,512]{1,0:T(8,128)(2,1)S(1)} %copy-done.1), channel_id=1, source_target_pairs={{0,8},{2,6},{8,16},{10,2},{16,24},{18,10},{24,28},{26,18},{28,20},... | collective-permute-start | bytes 1572872 | tf_op jit(solution)/shard_map/ppermute | solution.py:529
  32.3 14.0 %collective-permute-start.6 = (bf16[1,512,256]{2,1,0:T(8,128)(2,1)S(1)}, bf16[1,512,256]{2,1,0:T(8,128)(2,1)S(1)}, u32[]{:S(2)}, u32[]{:S(2)}) collective-permute-start(bf16[1,512,256]{2,1,0:T(8,128)(2,1)S(1)} %first_of.2), channel_id=1, source_target_pairs={{0,8},{2,6},{8,16},{10,2},{16,24},{18,10},{24,28},{26,18},{28,20},... | collective-permute-start | bytes 786440 | tf_op jit(solution)/shard_map/ppermute | solution.py:529
  41.4 15.9 %collective-permute-start.13 = (bf16[2,512,256]{2,1,0:T(8,128)(2,1)S(1)}, bf16[2,512,256]{2,1,0:T(8,128)(2,1)S(1)}, u32[]{:S(2)}, u32[]{:S(2)}) collective-permute-start(bf16[2,512,256]{2,1,0:T(8,128)(2,1)S(1)} %collective-permute-done.11.refs_0_), channel_id=1, source_target_pairs={{0,8},{2,6},{8,16},{10,2},{16,24},{18,10},{24,28},{26,18},{28,20},... | collective-permute-start | bytes 1572872 | tf_op jit(solution)/shard_map/ppermute | solution.py:529
  41.4 15.9 %collective-permute-start.16 = (bf16[2,512,256]{2,1,0:T(8,128)(2,1)S(1)}, bf16[2,512,256]{2,1,0:T(8,128)(2,1)S(1)}, u32[]{:S(2)}, u32[]{:S(2)}) collective-permute-start(bf16[2,512,256]{2,1,0:T(8,128)(2,1)S(1)} %collective-permute-done.5.pair_ref.refs_0_), channel_id=1, source_target_pairs={{0,1},{1,0},{2,3},{3,2},{4,5},{5,4},{6,7},{7,6},{8,9},{9,8},{10,11... | collective-permute-start | bytes 1572872 | tf_op jit(solution)/shard_map/ppermute | solution.py:107
  42.7 12.1 %collective-permute-start.15 = (bf16[256,512]{1,0:T(8,128)(2,1)S(1)}, bf16[256,512]{1,0:T(8,128)(2,1)S(1)}, u32[]{:S(2)}, u32[]{:S(2)}) collective-permute-start(bf16[256,512]{1,0:T(8,128)(2,1)S(1)} %rows_near.1), channel_id=1, source_target_pairs={{0,8},{2,6},{8,16},{10,2},{16,24},{18,10},{24,28},{26,18},{28,20},... | collective-permute-start | bytes 786440 | tf_op jit(solution)/shard_map/ppermute | solution.py:529
  46.4 14.0 %collective-permute-start.8 = (bf16[512,512]{1,0:T(8,128)(2,1)S(1)}, bf16[512,512]{1,0:T(8,128)(2,1)S(1)}, u32[]{:S(2)}, u32[]{:S(2)}) collective-permute-start(bf16[512,512]{1,0:T(8,128)(2,1)S(1)} %collective-permute-done.7.refs_2_), channel_id=1, source_target_pairs={{0,8},{2,6},{8,16},{10,2},{16,24},{18,10},{24,28},{26,18},{28,20},... | collective-permute-start | bytes 1572872 | tf_op jit(solution)/shard_map/ppermute | solution.py:529
  54.8 9.7 %collective-permute-start.20 = (bf16[256,512]{1,0:T(8,128)(2,1)S(1)}, bf16[256,512]{1,0:T(8,128)(2,1)S(1)}, u32[]{:S(2)}, u32[]{:S(2)}) collective-permute-start(bf16[256,512]{1,0:T(8,128)(2,1)S(1)} %collective-permute-done.15.refs_3_), channel_id=1, source_target_pairs={{0,1},{1,0},{2,3},{3,2},{4,5},{5,4},{6,7},{7,6},{8,9},{9,8},{10,11... | collective-permute-start | bytes 786440 | tf_op jit(solution)/shard_map/ppermute | solution.py:107
  57.4 5.9 %collective-permute-start.17 = (bf16[1,512,256]{2,1,0:T(8,128)(2,1)S(1)}, bf16[1,512,256]{2,1,0:T(8,128)(2,1)S(1)}, u32[]{:S(2)}, u32[]{:S(2)}) collective-permute-start(bf16[1,512,256]{2,1,0:T(8,128)(2,1)S(1)} %first_of.3), channel_id=1, source_target_pairs={{0,8},{2,6},{8,16},{10,2},{16,24},{18,10},{24,28},{26,18},{28,20},... | collective-permute-start | bytes 786440 | tf_op jit(solution)/shard_map/ppermute | solution.py:529
  59.8 8.1 %collective-permute-start.23 = (bf16[256,512]{1,0:T(8,128)(2,1)S(1)}, bf16[256,512]{1,0:T(8,128)(2,1)S(1)}, u32[]{:S(2)}, u32[]{:S(2)}) collective-permute-start(bf16[256,512]{1,0:T(8,128)(2,1)S(1)} %collective-permute-done.15.refs_3_), channel_id=1, source_target_pairs={{0,8},{2,6},{8,16},{10,2},{16,24},{18,10},{24,28},{26,18},{28,20},... | collective-permute-start | bytes 786440 | tf_op jit(solution)/shard_map/ppermute | solution.py:529
  60.1 7.8 %collective-permute-start.19 = (bf16[1,512,256]{2,1,0:T(8,128)(2,1)S(1)}, bf16[1,512,256]{2,1,0:T(8,128)(2,1)S(1)}, u32[]{:S(2)}, u32[]{:S(2)}) collective-permute-start(bf16[1,512,256]{2,1,0:T(8,128)(2,1)S(1)} %collective-permute-done.6.refs_0_), channel_id=1, source_target_pairs={{0,1},{1,0},{2,3},{3,2},{4,5},{5,4},{6,7},{7,6},{8,9},{9,8},{10,11... | collective-permute-start | bytes 786440 | tf_op jit(solution)/shard_map/ppermute | solution.py:107
  63.2 8.4 %collective-permute-start.18 = (bf16[512,512]{1,0:T(8,128)(2,1)S(1)}, bf16[512,512]{1,0:T(8,128)(2,1)S(1)}, u32[]{:S(2)}, u32[]{:S(2)}) collective-permute-start(bf16[512,512]{1,0:T(8,128)(2,1)S(1)} %collective-permute-done.8.refs_8_), channel_id=1, source_target_pairs={{0,8},{2,6},{8,16},{10,2},{16,24},{18,10},{24,28},{26,18},{28,20},... | collective-permute-start | bytes 1572872 | tf_op jit(solution)/shard_map/ppermute | solution.py:529
  67.9 7.4 %collective-permute-start.26 = (bf16[256,512]{1,0:T(8,128)(2,1)S(1)}, bf16[256,512]{1,0:T(8,128)(2,1)S(1)}, u32[]{:S(2)}, u32[]{:S(2)}) collective-permute-start(bf16[256,512]{1,0:T(8,128)(2,1)S(1)} %collective-permute-done.23.refs_9_), channel_id=1, source_target_pairs={{0,1},{1,0},{2,3},{3,2},{4,5},{5,4},{6,7},{7,6},{8,9},{9,8},{10,11... | collective-permute-start | bytes 786440 | tf_op jit(solution)/shard_map/ppermute | solution.py:107
  68.8 6.8 %collective-permute-start.24 = (bf16[256,512]{1,0:T(8,128)(2,1)S(1)}, bf16[256,512]{1,0:T(8,128)(2,1)S(1)}, u32[]{:S(2)}, u32[]{:S(2)}) collective-permute-start(bf16[256,512]{1,0:T(8,128)(2,1)S(1)} %collective-permute-done.23.refs_9_), channel_id=1, source_target_pairs={{0,8},{2,6},{8,16},{10,2},{16,24},{18,10},{24,28},{26,18},{28,20},... | collective-permute-start | bytes 786440 | tf_op jit(solution)/shard_map/ppermute | solution.py:529
  72.7 28.4 %collective-permute-start.22 = (f32[256,512]{1,0:T(8,128)S(1)}, f32[256,512]{1,0:T(8,128)S(1)}, u32[]{:S(2)}, u32[]{:S(2)}) collective-permute-start(f32[256,512]{1,0:T(8,128)S(1)} %get-tuple-element.71), channel_id=1, source_target_pairs={{0,2},{2,0},{4,6},{6,4},{8,10},{10,8},{12,14},{14,12},{16,18},{18,... | collective-permute-start | bytes 1572872 | tf_op jit(solution)/shard_map/ppermute | solution.py:103
  75.2 8.5 %collective-permute-start.32 = (bf16[256,512]{1,0:T(8,128)(2,1)S(1)}, bf16[256,512]{1,0:T(8,128)(2,1)S(1)}, u32[]{:S(2)}, u32[]{:S(2)}) collective-permute-start(bf16[256,512]{1,0:T(8,128)(2,1)S(1)} %collective-permute-done.15.refs_3_), channel_id=1, source_target_pairs={{0,2},{2,0},{4,6},{6,4},{8,10},{10,8},{12,14},{14,12},{16,18},{18,... | collective-permute-start | bytes 786440 | tf_op jit(solution)/shard_map/ppermute | solution.py:103
  75.6 9.9 %collective-permute-start.25 = (bf16[256,512]{1,0:T(8,128)(2,1)S(1)}, bf16[256,512]{1,0:T(8,128)(2,1)S(1)}, u32[]{:S(2)}, u32[]{:S(2)}) collective-permute-start(bf16[256,512]{1,0:T(8,128)(2,1)S(1)} %collective-permute-done.24.refs_15_), channel_id=1, source_target_pairs={{0,1},{1,0},{2,3},{3,2},{4,5},{5,4},{6,7},{7,6},{8,9},{9,8},{10,11... | collective-permute-start | bytes 786440 | tf_op jit(solution)/shard_map/ppermute | solution.py:107
  79.7 12.4 %collective-permute-start.28 = (bf16[2,256,256]{2,1,0:T(8,128)(2,1)S(1)}, bf16[2,256,256]{2,1,0:T(8,128)(2,1)S(1)}, u32[]{:S(2)}, u32[]{:S(2)}) collective-permute-start(bf16[2,256,256]{2,1,0:T(8,128)(2,1)S(1)} %join_row.1.refs_2_), channel_id=1, source_target_pairs={{0,16},{4,20},{8,24},{12,28},{16,26},{20,30},{24,18},{28,22},{26,1... | collective-permute-start | bytes 786440 | tf_op jit(solution)/shard_map/ppermute | solution.py:617
  81.8 12.4 %collective-permute-start.29 = (bf16[2,256,256]{2,1,0:T(8,128)(2,1)S(1)}, bf16[2,256,256]{2,1,0:T(8,128)(2,1)S(1)}, u32[]{:S(2)}, u32[]{:S(2)}) collective-permute-start(bf16[2,256,256]{2,1,0:T(8,128)(2,1)S(1)} %join_row.1.refs_2_), channel_id=1, source_target_pairs={{0,8},{4,12},{8,16},{12,20},{16,24},{20,28},{24,26},{28,30},{26,18... | collective-permute-start | bytes 786440 | tf_op jit(solution)/shard_map/ppermute | solution.py:617
  83.7 22.0 %collective-permute-start.40 = (bf16[512,512]{1,0:T(8,128)(2,1)S(1)}, bf16[512,512]{1,0:T(8,128)(2,1)S(1)}, u32[]{:S(2)}, u32[]{:S(2)}) collective-permute-start(bf16[512,512]{1,0:T(8,128)(2,1)S(1)} %collective-permute-done.18.refs_14_), channel_id=1, source_target_pairs={{0,8},{2,6},{8,16},{10,2},{16,24},{18,10},{24,28},{26,18},{28,20},... | collective-permute-start | bytes 1572872 | tf_op jit(solution)/shard_map/ppermute | solution.py:529
  85.5 19.1 %collective-permute-start.33 = (bf16[256,512]{1,0:T(8,128)(2,1)S(1)}, bf16[256,512]{1,0:T(8,128)(2,1)S(1)}, u32[]{:S(2)}, u32[]{:S(2)}) collective-permute-start(bf16[256,512]{1,0:T(8,128)(2,1)S(1)} %collective-permute-done.20.refs_4_), channel_id=1, source_target_pairs={{0,2},{2,0},{4,6},{6,4},{8,10},{10,8},{12,14},{14,12},{16,18},{18,... | collective-permute-start | bytes 786440 | tf_op jit(solution)/shard_map/ppermute | solution.py:103
  92.1 13.1 %collective-permute-start.35 = (bf16[256,512]{1,0:T(8,128)(2,1)S(1)}, bf16[256,512]{1,0:T(8,128)(2,1)S(1)}, u32[]{:S(2)}, u32[]{:S(2)}) collective-permute-start(bf16[256,512]{1,0:T(8,128)(2,1)S(1)} %collective-permute-done.23.refs_9_), channel_id=1, source_target_pairs={{0,2},{2,0},{4,6},{6,4},{8,10},{10,8},{12,14},{14,12},{16,18},{18,... | collective-permute-start | bytes 786440 | tf_op jit(solution)/shard_map/ppermute | solution.py:103
  94.2 11.1 %collective-permute-start.36 = (bf16[256,512]{1,0:T(8,128)(2,1)S(1)}, bf16[256,512]{1,0:T(8,128)(2,1)S(1)}, u32[]{:S(2)}, u32[]{:S(2)}) collective-permute-start(bf16[256,512]{1,0:T(8,128)(2,1)S(1)} %collective-permute-done.26.refs_10_), channel_id=1, source_target_pairs={{0,2},{2,0},{4,6},{6,4},{8,10},{10,8},{12,14},{14,12},{16,18},{18,... | collective-permute-start | bytes 786440 | tf_op jit(solution)/shard_map/ppermute | solution.py:103
  101.1 5.7 %collective-permute-start.34 = (bf16[512,512]{1,0:T(8,128)(2,1)S(1)}, bf16[512,512]{1,0:T(8,128)(2,1)S(1)}, u32[]{:S(2)}, u32[]{:S(2)}) collective-permute-start(bf16[512,512]{1,0:T(8,128)(2,1)S(1)} %collective-permute-done.8.refs_8_), channel_id=1, source_target_pairs={{0,2},{2,0},{4,6},{6,4},{8,10},{10,8},{12,14},{14,12},{16,18},{18,... | collective-permute-start | bytes 1572872 | tf_op jit(solution)/shard_map/ppermute | solution.py:103
  (12 other events, 55.5 us)
